TPU v7x, 32 devices: a whole 2x2x4 slice. The times are simulated.
32 devices in a mesh: graph: 4 (over z), config: 8 (over y, x, core).
Axes of the slice: x: 2, y: 2, z: 4, core: 2. Of those that a mesh axis runs over, the one named last changes fastest.
Arguments:
- features: bfloat16 [16, 2048, 128], P('config', 'graph'), may hold values from -6 to 6
- cotangent: bfloat16 [16, 2048, 128], P(None, ('graph', 'config')), may hold values from -6 to 6
- sage_weight: bfloat16 [2, 128, 128], replicated, may hold values from -0.5 to 0.5
- attn_weight: bfloat16 [4, 128, 128], replicated, may hold values from -0.5 to 0.5
- tile_vals: bfloat16 [48, 128, 128], P('graph'), may hold values from -0.375 to 0.375
- tile_dst: int32 [48], P('graph'), may hold values from 0 to 3
- tile_src: int32 [48], P('graph'), may hold values from 0 to 3
- tile_count: int32 [4], P('graph'), may hold values from 3 to 12, as said below
- hub_ids: int32 [32], P('graph'), may hold values from 0 to 2047, as said below
- hub_weight: bfloat16 [2048, 32], P('graph'), may hold values from -1 to 1
Outputs:
- layer_out: bfloat16 [16, 2048, 128], P(None, ('graph', 'config'))
- grad_features: bfloat16 [16, 2048, 128], P('config', 'graph')
- grad_weights: float32 [4, 6, 128, 128], P('graph')
Inputs may be any that keep to these rules, and one draw needn't show every extreme that they name: Slot t of slab g (t counted within the slab) is live when t < tile_count[g]; some slab has all 12 slots live. `hub_ids`: entries g * 8 to (g+1) * 8 - 1 are distinct nodes of slab g.
All inputs are finite; a program needn't handle non-finite values.
Results may differ from a plain program's by a relative error of at most 0.024.
Values may be sent and summed in bfloat16 or wider, within the bound.
No kernel may reach another device: no remote copies, remote signals or barrier semaphores. Data moves between devices by JAX's collectives and lax.ppermute only.
A program may use at most 64 MiB of HBM per device.

v0:
```python
import functools
import math

import jax
import jax.numpy as jnp
from jax import lax
from jax.experimental import pallas as pl
from jax.experimental.pallas import tpu as pltpu
from jax.sharding import PartitionSpec as P

HEADS = 4
CAP = 20.0
SUB = 8

BF = jnp.bfloat16
F32 = jnp.float32
VMEM = pl.BlockSpec(memory_space=pltpu.VMEM)
SMEM = pl.BlockSpec(memory_space=pltpu.SMEM)
LIMIT = 48 * 1024 * 1024


def dot(a, b):
    return jnp.dot(a, b, preferred_element_type=F32)


def dot_nt(a, b):
    return lax.dot_general(a, b, (((1,), (1,)), ((), ())), preferred_element_type=F32)


def call(kernel, outs, operands, specs, scratch=(), flops=0, size=0, name=None):
    return pl.pallas_call(
        kernel,
        out_shape=outs,
        in_specs=specs,
        out_specs=jax.tree.map(lambda _: VMEM, outs),
        scratch_shapes=list(scratch),
        compiler_params=pltpu.CompilerParams(vmem_limit_bytes=LIMIT),
        cost_estimate=pl.CostEstimate(flops=flops, bytes_accessed=size, transcendentals=0),
        name=name,
    )(*operands)


def hub_pick(ids, feats, out):
    layouts, nodes, _ = feats.shape
    hubs = out.shape[1]
    row = lax.broadcasted_iota(jnp.int32, (hubs, nodes), 0)
    col = lax.broadcasted_iota(jnp.int32, (hubs, nodes), 1)
    want = jnp.zeros((hubs, nodes), jnp.int32)
    for j in range(hubs):
        want = jnp.where(row == j, lax.rem(ids[j], nodes), want)
    hot = jnp.where(col == want, 1.0, 0.0).astype(BF)
    for l in range(layouts):
        out[l] = dot(hot, feats[l]).astype(BF)


def adjacency(src, dst, count, tiles, feats, weight, adj, adj_t, summed, pre_self):
    slots, tile, _ = tiles.shape
    layouts, nodes, _ = feats.shape
    adj[...] = jnp.zeros(adj.shape, F32)
    for t in range(slots):

        @pl.when(t < count[0])
        def _():
            at = pl.ds(pl.multiple_of(dst[t] * tile, tile), tile)
            block = tiles[t].astype(F32)
            col = src[t]
            for s in range(nodes // tile):

                @pl.when(col == s)
                def _():
                    adj[at, pl.ds(s * tile, tile)] += block

    dense = adj[...].astype(BF)
    adj_t[...] = adj[...].T.astype(BF)
    wide = jnp.concatenate([feats[l] for l in range(layouts)], axis=1)
    summed[...] = dot(dense, wide)
    for l in range(layouts):
        pre_self[l] = dot(feats[l], weight[0])


def sage_out(ranks, pieces, summed, pre_self, hub_weight, weight, hidden, agg, pre, hub_all):
    layouts, nodes, width = pre_self.shape
    shares, groups, _, _ = hidden.shape
    hubs = pieces[0].shape[1]
    me = lax.axis_index("graph")
    for s, piece in enumerate(pieces):
        at = pl.ds(pl.multiple_of(lax.rem(me + ranks - s, ranks) * hubs, hubs), hubs)
        for l in range(layouts):
            hub_all[at, l * width : (l + 1) * width] = piece[l].astype(F32)
    total = summed[...] + dot(hub_weight[...], hub_all[...].astype(BF))
    acts = []
    for l in range(layouts):
        mine = total[:, l * width : (l + 1) * width].astype(BF)
        agg[l] = mine
        value = pre_self[l] + dot(mine, weight[1])
        pre[l] = value
        act = value / (1.0 + jnp.exp(-value))
        acts.append(act.reshape(shares, groups, SUB, width))
    both = jnp.concatenate(acts, axis=2)
    hidden[...] = both.astype(BF)


def prepare(cot, attn, weight, feats, agg, pre, hub_weight, cot_g, gmix, slope, rows_t, w_back, hub_t):
    layouts, nodes, width = cot.shape
    groups = cot_g.shape[0]
    for p in range(groups // 2):
        block = cot[:, 2 * SUB * p : 2 * SUB * (p + 1), :].astype(F32)
        for h in range(2):
            rows = block[:, SUB * h : SUB * (h + 1), :].reshape(layouts * SUB, width).astype(BF)
            cot_g[2 * p + h] = rows
            gmix[2 * p + h] = dot_nt(rows, attn[3]).astype(BF)
    for l in range(feats.shape[0]):
        value = pre[l]
        sig = 1.0 / (1.0 + jnp.exp(-value))
        slope[l] = sig * (1.0 + value * (1.0 - sig))
        at = slice(l * feats.shape[1], (l + 1) * feats.shape[1])
        rows_t[0:width, at] = feats[l].T
        rows_t[width : 2 * width, at] = agg[l].T
    w_back[:, 0:width] = weight[0].T
    w_back[:, width : 2 * width] = weight[1].T
    hub_t[...] = hub_weight[...].T


def attend(hidden, cot_g, gmix, attn, grad_hidden, mixed, grads):
    shares, groups, depth, width = hidden.shape
    rows = shares * depth
    head = width // HEADS
    scale = 1.0 / math.sqrt(head)
    w_all = jnp.concatenate([attn[0], attn[1], attn[2]], axis=1)
    lane = lax.broadcasted_iota(jnp.int32, (rows, width), 1) // head
    r = lax.broadcasted_iota(jnp.int32, (rows, rows), 0)
    c = lax.broadcasted_iota(jnp.int32, (rows, rows), 1)
    same = (r % SUB) == (c % SUB)
    zero = jnp.zeros((rows, width), BF)

    def by_head(x):
        return [jnp.where(lane == e, x, zero) for e in range(HEADS)]

    total_w = jnp.zeros((width, 3 * width), F32)
    total_o = jnp.zeros((width, width), F32)
    for g in range(groups):
        hid = hidden[:, g].reshape(rows, width)
        qkv = dot(hid, w_all).astype(BF)
        q, k, v = (qkv[:, i * width : (i + 1) * width] for i in range(3))
        gm = gmix[g]
        k_t, v_t = k.T, v.T
        scores = dot_nt(jnp.concatenate(by_head(k), axis=0), q)
        d_probs = dot_nt(jnp.concatenate(by_head(v), axis=0), gm)
        probs, d_scores, mix_t, dq_t = [], [], [], []
        for e in range(HEADS):
            t = jnp.tanh(scores[e * rows : (e + 1) * rows] * (scale / CAP))
            w = jnp.where(same, jnp.exp(CAP * t), 0.0)
            a = w * (1.0 / jnp.sum(w, axis=0, keepdims=True))
            z = a * d_probs[e * rows : (e + 1) * rows]
            zs = jnp.sum(z, axis=0, keepdims=True)
            ds = ((z - a * zs) * (scale - scale * (t * t))).astype(BF)
            p = a.astype(BF)
            at = slice(e * head, (e + 1) * head)
            mix_t.append(dot(v_t[at], p))
            dq_t.append(dot(k_t[at], ds))
            probs.append(p)
            d_scores.append(ds)
        mix_t = jnp.concatenate(mix_t, axis=0).astype(BF)
        dq = jnp.concatenate(dq_t, axis=0).astype(BF).T
        dk = dot(jnp.concatenate(d_scores, axis=1), jnp.concatenate(by_head(q), axis=0)).astype(BF)
        dv = dot(jnp.concatenate(probs, axis=1), jnp.concatenate(by_head(gm), axis=0)).astype(BF)
        d_all = jnp.concatenate([dq, dk, dv], axis=1)
        back = cot_g[g].astype(F32) + dot_nt(d_all, w_all)
        grad_hidden[:, g] = back.astype(BF).reshape(shares, depth, width)
        mixed[g] = mix_t.T
        total_w += dot(hid.T, d_all)
        total_o += dot(mix_t, cot_g[g])
    for i in range(3):
        grads[i] = total_w[:, i * width : (i + 1) * width].astype(BF)
    grads[3] = total_o.astype(BF)


def outputs(hidden, mixed, attn, out):
    shares, groups, depth, width = hidden.shape
    rows = shares * depth
    layouts = rows // SUB
    for p in range(groups // 2):
        pair = []
        for g in (2 * p, 2 * p + 1):
            both = hidden[:, g].reshape(rows, width).astype(F32) + dot(mixed[g], attn[3])
            pair.append(both.reshape(layouts, SUB, width))
        out[:, 2 * SUB * p : 2 * SUB * (p + 1), :] = jnp.concatenate(pair, axis=1).astype(BF)


def sage_back(grad_hidden, slope, rows_t, w_back, hub_t, adj_t, totals, hub_part, grads):
    shares, groups, depth, width = grad_hidden.shape
    layouts, nodes, _ = slope.shape
    parts = grad_hidden[...].astype(F32).reshape(shares, groups, layouts, SUB, width)
    grad_pre, grad_agg, grad_self = [], [], []
    for l in range(layouts):
        gpre = (parts[:, :, l].reshape(nodes, width) * slope[l]).astype(BF)
        both = dot(gpre, w_back[...])
        grad_pre.append(gpre)
        grad_self.append(both[:, 0:width].astype(BF).astype(F32))
        grad_agg.append(both[:, width : 2 * width].astype(BF))
    wide = jnp.concatenate(grad_agg, axis=1)
    part = dot(hub_t[...], wide).astype(BF)
    for l in range(layouts):
        hub_part[:, l] = part[:, l * width : (l + 1) * width].reshape(
            hub_part.shape[0], hub_part.shape[2], width
        )
    back = dot(adj_t[...], wide)
    for l in range(layouts):
        totals[l] = grad_self[l] + back[:, l * width : (l + 1) * width]
    both = dot(rows_t[...], jnp.concatenate(grad_pre, axis=0))
    grads[0] = both[0:width].astype(BF)
    grads[1] = both[width : 2 * width].astype(BF)


def finish(ids, totals, hub_parts, out, work):
    layouts, nodes, width = totals.shape
    hubs = hub_parts.shape[2]
    work[...] = totals[...]
    summed = jnp.sum(hub_parts[...].astype(F32), axis=0)
    for l in range(layouts):
        for j in range(hubs):
            at = pl.ds(lax.rem(ids[j], nodes), 1)
            work[l, at, :] += summed[l, j : j + 1, :]
    out[...] = work[...].astype(BF)


def add_parts(parts, out):
    out[...] = jnp.sum(parts[...].astype(F32), axis=0).astype(BF)


def scaled(gathered, out, *, scale):
    out[...] = gathered[...].astype(F32) * scale


def local(
    features,
    cotangent,
    sage_weight,
    attn_weight,
    tile_vals,
    tile_dst,
    tile_src,
    tile_count,
    hub_ids,
    hub_weight,
):
    layout_dev, node_dev, width = features.shape
    ranks = lax.axis_size("graph")
    shares = lax.axis_size("config")
    share = node_dev // shares
    groups = share // SUB
    layouts = layout_dev * shares
    rows = layouts * SUB
    depth = layout_dev * SUB
    hub_dev = hub_ids.shape[0]
    hubs = hub_weight.shape[1]

    def shape(dims, kind=BF):
        return jax.ShapeDtypeStruct(dims, kind)

    mine = call(hub_pick, shape((layout_dev, hub_dev, width)), (hub_ids, features), [SMEM, VMEM], name="hub_pick")
    pieces = [mine]
    for s in range(1, ranks):
        pieces.append(lax.ppermute(mine, "graph", [(i, (i + s) % ranks) for i in range(ranks)]))

    adj_t, summed, pre_self = call(
        lambda src, dst, count, tiles, feats, weight, adj_t, summed, pre_self, adj: adjacency(
            src, dst, count, tiles, feats, weight, adj, adj_t, summed, pre_self
        ),
        (
            shape((node_dev, node_dev)),
            shape((node_dev, layout_dev * width), F32),
            shape((layout_dev, node_dev, width), F32),
        ),
        (tile_src, tile_dst, tile_count, tile_vals, features, sage_weight),
        [SMEM, SMEM, SMEM, VMEM, VMEM, VMEM],
        [pltpu.VMEM((node_dev, node_dev), F32)],
        flops=10**9,
        size=2**21,
        name="adjacency",
    )

    def sage_kernel(*refs):
        sage_out(ranks, refs[:ranks], *refs[ranks:])

    hidden, agg, pre = call(
        sage_kernel,
        (
            shape((shares, groups, depth, width)),
            shape((layout_dev, node_dev, width)),
            shape((layout_dev, node_dev, width), F32),
        ),
        (*pieces, summed, pre_self, hub_weight, sage_weight),
        [VMEM] * (ranks + 4),
        [pltpu.VMEM((hubs, layout_dev * width), F32)],
        name="sage_out",
    )
    hidden_in = lax.all_to_all(hidden, "config", split_axis=0, concat_axis=0, tiled=True)

    cot_g, gmix, slope, rows_t, w_back, hub_t = call(
        prepare,
        (
            shape((groups, rows, width)),
            shape((groups, rows, width)),
            shape((layout_dev, node_dev, width), F32),
            shape((2 * width, layout_dev * node_dev)),
            shape((width, 2 * width)),
            shape((hubs, node_dev)),
        ),
        (cotangent, attn_weight, sage_weight, features, agg, pre, hub_weight),
        [VMEM] * 7,
        flops=10**9,
        size=2**21,
        name="prepare",
    )

    grad_hidden, mixed, attn_grads = call(
        attend,
        (
            shape((shares, groups, depth, width)),
            shape((groups, rows, width)),
            shape((4, width, width)),
        ),
        (hidden_in, cot_g, gmix, attn_weight),
        [VMEM] * 4,
        name="attend",
    )
    grad_in = lax.all_to_all(grad_hidden, "config", split_axis=0, concat_axis=0, tiled=True)

    output = call(
        outputs,
        shape((layouts, share, width)),
        (hidden_in, mixed, attn_weight),
        [VMEM] * 3,
        flops=10**9,
        size=2**21,
        name="outputs",
    )

    totals, hub_part, sage_grads = call(
        sage_back,
        (
            shape((layout_dev, node_dev, width), F32),
            shape((ranks, layout_dev, hub_dev, width)),
            shape((2, width, width)),
        ),
        (grad_in, slope, rows_t, w_back, hub_t, adj_t),
        [VMEM] * 6,
        name="sage_back",
    )

    hub_parts = lax.all_to_all(hub_part, "graph", split_axis=0, concat_axis=0, tiled=True)
    partial_grads = jnp.concatenate([sage_grads, attn_grads], axis=0)
    count = partial_grads.shape[0]
    slices = partial_grads.reshape(shares, count * width // shares, width)
    received = lax.all_to_all(slices, "config", split_axis=0, concat_axis=0, tiled=True)
    own = call(add_parts, shape(received.shape[1:]), (received,), [VMEM], name="add_parts")
    gathered = lax.all_to_all(
        jnp.broadcast_to(own[None], received.shape), "config", split_axis=0, concat_axis=0, tiled=True
    )
    grad_features = call(
        finish,
        shape((layout_dev, node_dev, width)),
        (hub_ids, totals, hub_parts),
        [SMEM, VMEM, VMEM],
        [pltpu.VMEM((layout_dev, node_dev, width), F32)],
        name="finish",
    )
    scale = 1.0 / math.sqrt(layouts * node_dev)
    weights = call(
        functools.partial(scaled, scale=scale),
        shape((count, width, width), F32),
        (gathered.reshape(count, width, width),),
        [VMEM],
        name="scaled",
    )
    return (output, grad_features, weights[None])


def solution(mesh):
    return jax.shard_map(
        local,
        mesh=mesh,
        in_specs=(
            P("config", "graph", None),
            P(None, ("graph", "config"), None),
            P(),
            P(),
            P("graph", None, None),
            P("graph"),
            P("graph"),
            P("graph"),
            P("graph"),
            P("graph", None),
        ),
        out_specs=(
            P(None, ("graph", "config"), None),
            P("config", "graph", None),
            P("graph", None, None, None),
        ),
        check_vma=False,
    )
```

profile of v0, /device:TPU:0, one launch (start us, length us, event | category | flops | bytes accessed | tf_op | source)
XLA Modules:
  0.0 72.3 jit_solution(1862636923599819178)
XLA Ops:
  0.6 0.0 copy-start
  0.6 0.9 %copy-done = bf16[2,512,128]{2,1,0:T(8,128)(2,1)S(1)} copy-done((bf16[2,512,128]{2,1,0:T(8,128)(2,1)S(1)}, bf16[2,512,128]{2,1,0:T(8,128)(2,1)}, u32[]{:S(2)}) %copy-start) | copy-done | bytes 262168
  1.6 0.7 copy-done.5
  2.2 0.0 copy-start.1
  2.2 0.7 hub_pick.1.refs_0_
  2.9 0.0 copy-start.13
  2.9 0.0 copy-start.14
  2.9 5.1 %collective-permute-start.2 = (bf16[2,8,128]{2,1,0:T(8,128)(2,1)S(1)}, bf16[2,8,128]{2,1,0:T(8,128)(2,1)S(1)}, u32[]{:S(2)}, u32[]{:S(2)}) collective-permute-start(bf16[2,8,128]{2,1,0:T(8,128)(2,1)S(1)} %hub_pick.1.refs_0_), channel_id=1, source_target_pairs={{0,24},{8,0},{16,8},{24,16},{1,25},{9,1},{17,9},{25,17},{2,26},{10... | collective-permute-start | bytes 12296 | tf_op jit(solution)/shard_map/ppermute | solution.py:264
  8.0 0.0 collective-permute-start.1
  8.0 1.0 %collective-permute-start = (bf16[2,8,128]{2,1,0:T(8,128)(2,1)S(1)}, bf16[2,8,128]{2,1,0:T(8,128)(2,1)S(1)}, u32[]{:S(2)}, u32[]{:S(2)}) collective-permute-start(bf16[2,8,128]{2,1,0:T(8,128)(2,1)S(1)} %hub_pick.1.refs_0_), channel_id=1, source_target_pairs={{0,8},{8,16},{16,24},{24,0},{1,9},{9,17},{17,25},{25,1},{2,10},{10... | collective-permute-start | bytes 12296 | tf_op jit(solution)/shard_map/ppermute | solution.py:264
  9.7 0.0 copy-done.1
  9.7 0.0 copy-done.13
  9.7 0.0 copy-done.14
  9.7 0.0 copy-start.3
  9.7 0.8 %copy-done.3 = bf16[2,128,128]{2,1,0:T(8,128)(2,1)S(1)} copy-done((bf16[2,128,128]{2,1,0:T(8,128)(2,1)S(1)}, bf16[2,128,128]{2,1,0:T(8,128)(2,1)}, u32[]{:S(2)}) %copy-start.3) | copy-done | bytes 65560
  10.6 1.0 %copy-done.9 = bf16[12,128,128]{2,1,0:T(8,128)(2,1)S(1)} copy-done((bf16[12,128,128]{2,1,0:T(8,128)(2,1)S(1)}, bf16[12,128,128]{2,1,0:T(8,128)(2,1)}, u32[]{:S(2)}) %copy-start.9) | copy-done | bytes 393240
  11.6 1.4 %adjacency.1 = (bf16[512,512]{1,0:T(8,128)(2,1)S(1)}, f32[512,256]{1,0:T(8,128)S(1)}, f32[2,512,128]{2,1,0:T(8,128)S(1)}) custom-call(s32[12]{0:T(128)S(1)} %copy-done.13, s32[12]{0:T(128)S(1)} %copy-done.14, s32[1]{0:T(128)S(6)} %copy.15.count, bf16[12,128,128]{2,1,0:T(8,128)(2,1)S(1)} %copy-done.9, bf16[2,512,128]{2,1,0:T(8,128)(2,1)S(1)} %copy-done.1, ...), custom_call_target="tpu_custom_call" | custom-call | flops 1000000000 | bytes 2097152 | tf_op jit(solution)/shard_map/adjacency/pallas_call | solution.py:31
  13.0 0.0 copy-done.15
  13.0 0.0 copy-start.4
  13.0 0.1 copy.13.refs_6_.hub_weight
  13.2 0.0 collective-permute-done.2.refs_3_
  13.2 0.0 collective-permute-done.1.refs_2_
  13.2 0.3 collective-permute-done.refs_1_
  13.4 0.4 copy-done.4
  13.9 1.2 %sage_out.1 = (bf16[8,8,16,128]{3,2,1,0:T(8,128)(2,1)}, bf16[2,512,128]{2,1,0:T(8,128)(2,1)S(1)}, f32[2,512,128]{2,1,0:T(8,128)S(1)}) custom-call(bf16[2,8,128]{2,1,0:T(8,128)(2,1)S(1)} %hub_pick.1.refs_0_, bf16[2,8,128]{2,1,0:T(8,128)(2,1)S(1)} %collective-permute-done.refs_1_, bf16[2,8,128]{2,1,0:T(8,128)(2,1)S(1)} %collective-permute-done.1.refs_2_, ...), custom_call_target="tpu_custom_call" | custom-call | tf_op jit(solution)/shard_map/sage_out/pallas_call | solution.py:31
  15.0 0.7 copy-done.11
  15.7 3.9 %all-to-all-start = ((bf16[8,8,16,128]{3,2,1,0:T(8,128)(2,1)}), bf16[8,8,16,128]{3,2,1,0:T(8,128)(2,1)S(1)}, u32[]{:S(2)}, u32[]{:S(2)}) async-start(bf16[8,8,16,128]{3,2,1,0:T(8,128)(2,1)} %get-tuple-element.23), calls=%async_computation | async-start | bytes 524288 | tf_op jit(solution)/shard_map/all_to_all | solution.py:298
  19.6 0.0 copy-done.7
  19.6 0.0 copy-done.2
  19.6 0.0 copy-done.10
  19.6 0.0 copy-start.8
  19.6 1.0 %copy-done.8 = f32[2,512,128]{2,1,0:T(8,128)S(1)} copy-done((f32[2,512,128]{2,1,0:T(8,128)S(1)}, f32[2,512,128]{2,1,0:T(8,128)}, u32[]{:S(2)}) %copy-start.8) | copy-done | bytes 524312
  20.7 0.9 %copy-done.12 = bf16[2,512,128]{2,1,0:T(8,128)(2,1)S(1)} copy-done((bf16[2,512,128]{2,1,0:T(8,128)(2,1)S(1)}, bf16[2,512,128]{2,1,0:T(8,128)(2,1)}, u32[]{:S(2)}) %copy-start.12) | copy-done | bytes 262168
  21.6 0.4 prepare.1
  22.1 4.5 %all-to-all-done.hidden = bf16[8,8,16,128]{3,2,1,0:T(8,128)(2,1)S(1)} async-done(((bf16[8,8,16,128]{3,2,1,0:T(8,128)(2,1)}), bf16[8,8,16,128]{3,2,1,0:T(8,128)(2,1)S(1)}, u32[]{:S(2)}, u32[]{:S(2)}) %all-to-all-start) | async-done | bytes 262176 | tf_op jit(solution)/shard_map/all_to_all | solution.py:298
  26.5 5.8 %attend.1 = (bf16[8,8,16,128]{3,2,1,0:T(8,128)(2,1)S(1)}, bf16[8,128,128]{2,1,0:T(8,128)(2,1)S(1)}, bf16[4,128,128]{2,1,0:T(8,128)(2,1)S(1)}) custom-call(bf16[8,8,16,128]{3,2,1,0:T(8,128)(2,1)S(1)} %all-to-all-done.hidden, bf16[8,128,128]{2,1,0:T(8,128)(2,1)S(1)} %get-tuple-element.26.cot_g, bf16[8,128,128]{2,1,0:T(8,128)(2,1)S(1)} %get-tuple-element.27.gmix, ...), custom_call_target="tpu_custom_call" | custom-call | tf_op jit(solution)/shard_map/attend/pallas_call | solution.py:31
  32.4 9.3 %all_to_all.25.grad_hidden = bf16[8,8,16,128]{3,2,1,0:T(8,128)(2,1)S(1)} all-to-all(bf16[8,8,16,128]{3,2,1,0:T(8,128)(2,1)S(1)} %get-tuple-element.29), channel_id=1, replica_groups=mesh['graph'=4,'config'=8] {'config'}, dimensions={0} | all-to-all | bytes 524288 | tf_op jit(solution)/shard_map/all_to_all | solution.py:328
  41.7 1.3 %sage_back.1 = (f32[2,512,128]{2,1,0:T(8,128)S(1)}, bf16[4,2,8,128]{3,2,1,0:T(8,128)(2,1)}, bf16[2,128,128]{2,1,0:T(8,128)(2,1)S(1)}) custom-call(bf16[8,8,16,128]{3,2,1,0:T(8,128)(2,1)S(1)} %all_to_all.25.grad_hidden, f32[2,512,128]{2,1,0:T(8,128)S(1)} %get-tuple-element.30.slope, bf16[256,1024]{1,0:T(8,128)(2,1)S(1)} %get-tuple-element.31.rows_t, ...), custom_call_target="tpu_custom_call" | custom-call | tf_op jit(solution)/shard_map/sage_back/pallas_call | solution.py:31
  43.0 8.6 %all_to_all.26.parts = bf16[8,96,128]{2,1,0:T(8,128)(2,1)S(1)} all-to-all(bf16[8,96,128]{2,1,0:T(8,128)(2,1)S(1)} %bitcast.4), channel_id=1, replica_groups=mesh['graph'=4,'config'=8] {'config'}, dimensions={0} | all-to-all | bytes 393216 | tf_op jit(solution)/shard_map/all_to_all | solution.py:356
  51.6 4.0 %all-to-all-start.2 = ((bf16[4,2,8,128]{3,2,1,0:T(8,128)(2,1)}), bf16[4,2,8,128]{3,2,1,0:T(8,128)(2,1)S(1)}, u32[]{:S(2)}, u32[]{:S(2)}) async-start(bf16[4,2,8,128]{3,2,1,0:T(8,128)(2,1)} %get-tuple-element.36), calls=%async_computation.2 | async-start | bytes 32768 | tf_op jit(solution)/shard_map/all_to_all | solution.py:352
  55.7 5.6 %all-to-all-done.2.hub_parts = bf16[4,2,8,128]{3,2,1,0:T(8,128)(2,1)S(1)} async-done(((bf16[4,2,8,128]{3,2,1,0:T(8,128)(2,1)}), bf16[4,2,8,128]{3,2,1,0:T(8,128)(2,1)S(1)}, u32[]{:S(2)}, u32[]{:S(2)}) %all-to-all-start.2) | async-done | bytes 16416 | tf_op jit(solution)/shard_map/all_to_all | solution.py:352
  61.3 0.7 broadcast_in_dim.4
  62.0 3.4 %all-to-all-start.4 = ((bf16[8,96,128]{2,1,0:T(8,128)(2,1)}), bf16[8,96,128]{2,1,0:T(8,128)(2,1)S(1)}, u32[]{:S(2)}, u32[]{:S(2)}) async-start(bf16[8,96,128]{2,1,0:T(8,128)(2,1)} %broadcast_in_dim.4), calls=%async_computation.4 | async-start | bytes 393216 | tf_op jit(solution)/shard_map/all_to_all | solution.py:358
  65.4 0.9 %outputs.1 = bf16[16,64,128]{2,1,0:T(8,128)(2,1)} custom-call(bf16[8,8,16,128]{3,2,1,0:T(8,128)(2,1)S(1)} %all-to-all-done.hidden, bf16[8,128,128]{2,1,0:T(8,128)(2,1)S(1)} %get-tuple-element.28.mixed, bf16[4,128,128]{2,1,0:T(8,128)(2,1)S(1)} %copy-done.2), custom_call_target="tpu_custom_call" | custom-call | flops 1000000000 | bytes 2097152 | tf_op jit(solution)/shard_map/outputs/pallas_call | solution.py:31
  66.3 0.7 copy-done.6
  67.0 1.3 %finish.1 = bf16[2,512,128]{2,1,0:T(8,128)(2,1)} custom-call(s32[8]{0:T(128)S(1)} %copy-done.6, f32[2,512,128]{2,1,0:T(8,128)S(1)} %get-tuple-element.35.totals, bf16[4,2,8,128]{3,2,1,0:T(8,128)(2,1)S(1)} %all-to-all-done.2.hub_parts), custom_call_target="tpu_custom_call" | custom-call | tf_op jit(solution)/shard_map/finish/pallas_call | solution.py:31
  68.3 3.2 %all-to-all-done.4 = bf16[8,96,128]{2,1,0:T(8,128)(2,1)S(1)} async-done(((bf16[8,96,128]{2,1,0:T(8,128)(2,1)}), bf16[8,96,128]{2,1,0:T(8,128)(2,1)S(1)}, u32[]{:S(2)}, u32[]{:S(2)}) %all-to-all-start.4) | async-done | bytes 196640 | tf_op jit(solution)/shard_map/all_to_all | solution.py:358
  71.6 0.8 %scaled.1 = f32[6,128,128]{2,1,0:T(8,128)} custom-call(bf16[6,128,128]{2,1,0:T(8,128)(2,1)S(1)} %bitcast.3), custom_call_target="tpu_custom_call" | custom-call | tf_op jit(solution)/shard_map/scaled/pallas_call | solution.py:31
  (11 shorter events, 0.1 us)
Async XLA Ops:
  0.6 1.0 %copy-start = (bf16[2,512,128]{2,1,0:T(8,128)(2,1)S(1)}, bf16[2,512,128]{2,1,0:T(8,128)(2,1)}, u32[]{:S(2)}) copy-start(bf16[2,512,128]{2,1,0:T(8,128)(2,1)} %feats.5) | copy-start | bytes 786436
  1.6 0.7 copy-start.5
  2.2 7.5 %copy-start.1 = (bf16[2,512,128]{2,1,0:T(8,128)(2,1)S(1)}, bf16[2,512,128]{2,1,0:T(8,128)(2,1)}, u32[]{:S(2)}) copy-start(bf16[2,512,128]{2,1,0:T(8,128)(2,1)} %feats.5) | copy-start | bytes 786436
  2.9 6.8 %copy-start.13 = (s32[12]{0:T(128)S(1)}, s32[12]{0:T(128)}, u32[]{:S(2)}) copy-start(s32[12]{0:T(128)} %src.1) | copy-start | bytes 148
  2.9 6.8 %copy-start.14 = (s32[12]{0:T(128)S(1)}, s32[12]{0:T(128)}, u32[]{:S(2)}) copy-start(s32[12]{0:T(128)} %dst.1) | copy-start | bytes 148
  2.9 10.2 %collective-permute-start.2 = (bf16[2,8,128]{2,1,0:T(8,128)(2,1)S(1)}, bf16[2,8,128]{2,1,0:T(8,128)(2,1)S(1)}, u32[]{:S(2)}, u32[]{:S(2)}) collective-permute-start(bf16[2,8,128]{2,1,0:T(8,128)(2,1)S(1)} %hub_pick.1.refs_0_), channel_id=1, source_target_pairs={{0,24},{8,0},{16,8},{24,16},{1,25},{9,1},{17,9},{25,17},{2,26},{10... | collective-permute-start | bytes 12296 | tf_op jit(solution)/shard_map/ppermute | solution.py:264
  8.0 5.1 %collective-permute-start.1 = (bf16[2,8,128]{2,1,0:T(8,128)(2,1)S(1)}, bf16[2,8,128]{2,1,0:T(8,128)(2,1)S(1)}, u32[]{:S(2)}, u32[]{:S(2)}) collective-permute-start(bf16[2,8,128]{2,1,0:T(8,128)(2,1)S(1)} %hub_pick.1.refs_0_), channel_id=1, source_target_pairs={{0,16},{8,24},{16,0},{24,8},{1,17},{9,25},{17,1},{25,9},{2,18},{10... | collective-permute-start | bytes 12296 | tf_op jit(solution)/shard_map/ppermute | solution.py:264
  8.0 5.4 %collective-permute-start = (bf16[2,8,128]{2,1,0:T(8,128)(2,1)S(1)}, bf16[2,8,128]{2,1,0:T(8,128)(2,1)S(1)}, u32[]{:S(2)}, u32[]{:S(2)}) collective-permute-start(bf16[2,8,128]{2,1,0:T(8,128)(2,1)S(1)} %hub_pick.1.refs_0_), channel_id=1, source_target_pairs={{0,8},{8,16},{16,24},{24,0},{1,9},{9,17},{17,25},{25,1},{2,10},{10... | collective-permute-start | bytes 12296 | tf_op jit(solution)/shard_map/ppermute | solution.py:264
  9.7 0.8 %copy-start.3 = (bf16[2,128,128]{2,1,0:T(8,128)(2,1)S(1)}, bf16[2,128,128]{2,1,0:T(8,128)(2,1)}, u32[]{:S(2)}) copy-start(bf16[2,128,128]{2,1,0:T(8,128)(2,1)} %weight.3) | copy-start | bytes 196612
  10.6 1.0 %copy-start.9 = (bf16[12,128,128]{2,1,0:T(8,128)(2,1)S(1)}, bf16[12,128,128]{2,1,0:T(8,128)(2,1)}, u32[]{:S(2)}) copy-start(bf16[12,128,128]{2,1,0:T(8,128)(2,1)} %tiles.1) | copy-start | bytes 1179652
  11.6 1.4 %copy-start.15 = (bf16[512,32]{0,1:T(8,128)(2,1)S(1)}, bf16[512,32]{0,1:T(8,128)(2,1)}, u32[]{:S(2)}) copy-start(bf16[512,32]{0,1:T(8,128)(2,1)} %param.19) | copy-start | bytes 98308
  13.0 0.8 %copy-start.4 = (bf16[2,128,128]{2,1,0:T(8,128)(2,1)S(1)}, bf16[2,128,128]{2,1,0:T(8,128)(2,1)}, u32[]{:S(2)}) copy-start(bf16[2,128,128]{2,1,0:T(8,128)(2,1)} %weight.3) | copy-start | bytes 196612
  15.0 0.7 copy-start.11
  15.7 3.9 %copy-start.7 = (f32[2,512,128]{2,1,0:T(8,128)}, f32[2,512,128]{2,1,0:T(8,128)S(1)}, u32[]{:S(2)}) copy-start(f32[2,512,128]{2,1,0:T(8,128)S(1)} %get-tuple-element.25.pre) | copy-start | bytes 1572868
  15.7 3.9 %copy-start.2 = (bf16[4,128,128]{2,1,0:T(8,128)(2,1)S(1)}, bf16[4,128,128]{2,1,0:T(8,128)(2,1)}, u32[]{:S(2)}) copy-start(bf16[4,128,128]{2,1,0:T(8,128)(2,1)} %attn.5) | copy-start | bytes 393220
  15.7 3.9 %copy-start.10 = (bf16[16,64,128]{2,1,0:T(8,128)(2,1)S(1)}, bf16[16,64,128]{2,1,0:T(8,128)(2,1)}, u32[]{:S(2)}) copy-start(bf16[16,64,128]{2,1,0:T(8,128)(2,1)} %cot.1) | copy-start | bytes 786436
  15.7 10.8 %all-to-all-start = ((bf16[8,8,16,128]{3,2,1,0:T(8,128)(2,1)}), bf16[8,8,16,128]{3,2,1,0:T(8,128)(2,1)S(1)}, u32[]{:S(2)}, u32[]{:S(2)}) async-start(bf16[8,8,16,128]{3,2,1,0:T(8,128)(2,1)} %get-tuple-element.23), calls=%async_computation | async-start | bytes 524288 | tf_op jit(solution)/shard_map/all_to_all | solution.py:298
  19.6 1.0 %copy-start.8 = (f32[2,512,128]{2,1,0:T(8,128)S(1)}, f32[2,512,128]{2,1,0:T(8,128)}, u32[]{:S(2)}) copy-start(f32[2,512,128]{2,1,0:T(8,128)} %copy-done.7) | copy-start | bytes 1572868
  20.7 0.9 %copy-start.12 = (bf16[2,512,128]{2,1,0:T(8,128)(2,1)S(1)}, bf16[2,512,128]{2,1,0:T(8,128)(2,1)}, u32[]{:S(2)}) copy-start(bf16[2,512,128]{2,1,0:T(8,128)(2,1)} %copy-done.11) | copy-start | bytes 786436
  51.6 9.7 %all-to-all-start.2 = ((bf16[4,2,8,128]{3,2,1,0:T(8,128)(2,1)}), bf16[4,2,8,128]{3,2,1,0:T(8,128)(2,1)S(1)}, u32[]{:S(2)}, u32[]{:S(2)}) async-start(bf16[4,2,8,128]{3,2,1,0:T(8,128)(2,1)} %get-tuple-element.36), calls=%async_computation.2 | async-start | bytes 32768 | tf_op jit(solution)/shard_map/all_to_all | solution.py:352
  62.0 9.6 %all-to-all-start.4 = ((bf16[8,96,128]{2,1,0:T(8,128)(2,1)}), bf16[8,96,128]{2,1,0:T(8,128)(2,1)S(1)}, u32[]{:S(2)}, u32[]{:S(2)}) async-start(bf16[8,96,128]{2,1,0:T(8,128)(2,1)} %broadcast_in_dim.4), calls=%async_computation.4 | async-start | bytes 393216 | tf_op jit(solution)/shard_map/all_to_all | solution.py:358
  66.3 0.7 copy-start.6
where the time goes:
time: 73 us; the launch traced here: 72.3 us
  blocking collectives  18 us (25%)
  starting transfers between devices  17.4 us (24%)
  Pallas kernels  13.9 us (19%)
  waiting for transfers between devices  13.6 us (19%)
  local copies, waits for them, and re-layouts  8.04 us (11%)
  between operations  1.44 us (2%)
    pallas_call x10, Pallas kernels, call(): pl.pallas_call(kernel, out_shape=outs, in_specs=specs, out_specs=jax.tree...  13.9 us
    all_to_all x1, blocking collectives, local(): lax.all_to_all(grad_hidden, 'config', split_axis=0, concat_axis=0, tiled=...  9.35 us
    all_to_all x1, blocking collectives, local(): lax.all_to_all(slices, 'config', split_axis=0, concat_axis=0, tiled=True)  8.63 us
    unnamed x33, local copies, waits for them, and re-layouts  7.33 us
    ppermute x3, starting transfers between devices, local(): lax.ppermute(mine, 'graph', [(i, (i + s) % ranks) for i in range(ranks)])  6.11 us
    all_to_all x1, waiting for transfers between devices, local(): lax.all_to_all(hub_part, 'graph', split_axis=0, concat_axis=0, tiled=True)  5.58 us
    all_to_all x1, waiting for transfers between devices, local(): lax.all_to_all(hidden, 'config', split_axis=0, concat_axis=0, tiled=True)  4.47 us
    all_to_all x1, starting transfers between devices, local(): lax.all_to_all(hub_part, 'graph', split_axis=0, concat_axis=0, tiled=True)  4.05 us
  transfers between devices with their start and end apart: 6, of which 4 were waited for; matrix products, arithmetic and copies ran while one was open for 0% of the time, Pallas kernels for 6%

commit v1 on v0

v1 whole, which is shorter than its diff:
```python
import functools
import math

import jax
import jax.numpy as jnp
from jax import lax
from jax.experimental import pallas as pl
from jax.experimental.pallas import tpu as pltpu
from jax.sharding import PartitionSpec as P

HEADS = 4
CAP = 20.0
SUB = 8

BF = jnp.bfloat16
F32 = jnp.float32
VMEM = pl.BlockSpec(memory_space=pltpu.VMEM)
HBM = pl.BlockSpec(memory_space=pltpu.HBM)
LIMIT = 24 * 1024 * 1024


def dot(a, b):
    return jnp.dot(a, b, preferred_element_type=F32)


def dot_nt(a, b):
    return lax.dot_general(a, b, (((1,), (1,)), ((), ())), preferred_element_type=F32)


def dot_tn(a, b):
    return lax.dot_general(a, b, (((0,), (0,)), ((), ())), preferred_element_type=F32)


def shape(dims, kind=BF):
    return jax.ShapeDtypeStruct(dims, kind)


def call(kernel, outs, operands, specs, scratch=(), hidden=False, name=None):
    cost = {}
    if hidden:
        cost["cost_estimate"] = pl.CostEstimate(flops=10**9, bytes_accessed=2**21, transcendentals=0)
    return pl.pallas_call(
        kernel,
        out_shape=outs,
        in_specs=specs,
        out_specs=jax.tree.map(lambda _: VMEM, outs),
        scratch_shapes=list(scratch),
        compiler_params=pltpu.CompilerParams(vmem_limit_bytes=LIMIT),
        name=name,
        **cost,
    )(*operands)


def fetch(pairs, sems):
    copies = [pltpu.make_async_copy(a, b, sems.at[i]) for i, (a, b) in enumerate(pairs)]
    for copy in copies:
        copy.start()
    return copies


def swapped(x, axis, mask):
    count = lax.axis_size(axis)
    return lax.ppermute(x, axis, [(i, i ^ mask) for i in range(count)])


def hub_pick(ids, feats, out, kept, ids_s, sems):
    copies = fetch([(ids, ids_s)] + [(feats.at[l], kept.at[l]) for l in range(feats.shape[0])], sems)
    layouts, nodes, _ = feats.shape
    hubs = out.shape[1]
    row = lax.broadcasted_iota(jnp.int32, (hubs, nodes), 0)
    col = lax.broadcasted_iota(jnp.int32, (hubs, nodes), 1)
    want = jnp.zeros((hubs, nodes), jnp.int32)
    copies[0].wait()
    for j in range(hubs):
        want = jnp.where(row == j, lax.rem(ids_s[j], nodes), want)
    hot = jnp.where(col == want, 1.0, 0.0).astype(BF)
    for l in range(layouts):
        copies[1 + l].wait()
        out[l] = dot(hot, kept[l]).astype(BF)


def adjacency(src, dst, count, tiles, weight, hub_t, feats, adj_t, summed, pre_self, weight_v, hub_v, *scratch):
    src_s, dst_s, count_s, tiles_v, adj, sems = scratch
    copies = fetch(
        [(src, src_s), (dst, dst_s), (count, count_s), (weight, weight_v), (tiles, tiles_v), (hub_t, hub_v)], sems
    )
    slots, tile, _ = tiles.shape
    layouts, nodes, _ = feats.shape
    adj[...] = jnp.zeros(adj.shape, F32)
    for i in range(4):
        copies[i].wait()
    for l in range(layouts):
        pre_self[l] = dot(feats[l], weight_v[0])
    copies[4].wait()
    for t in range(slots):

        @pl.when(t < count_s[0])
        def _():
            at = pl.ds(pl.multiple_of(dst_s[t] * tile, tile), tile)
            block = tiles_v[t].astype(F32)
            col = src_s[t]
            for s in range(nodes // tile):

                @pl.when(col == s)
                def _():
                    adj[at, pl.ds(s * tile, tile)] += block

    dense = adj[...].astype(BF)
    wide = jnp.concatenate([feats[l] for l in range(layouts)], axis=1)
    summed[...] = dot(dense, wide)
    adj_t[...] = dense.T
    copies[5].wait()


def sage_out(*refs):
    pieces, (summed, pre_self, hub_t, weight, own, other, agg, pre, hub_all, ready) = refs[:-10], refs[-10:]
    layouts, nodes, width = pre_self.shape
    shares, groups, _, _ = ready.shape
    hubs = pieces[0].shape[1]
    slab = lax.axis_index("graph")
    for s, piece in enumerate(pieces):
        at = pl.ds(pl.multiple_of(lax.bitwise_xor(slab, s) * hubs, hubs), hubs)
        for l in range(layouts):
            hub_all[at, l * width : (l + 1) * width] = piece[l].astype(F32)
    total = summed[...] + dot_tn(hub_t[...], hub_all[...].astype(BF))
    acts = []
    for l in range(layouts):
        mine = total[:, l * width : (l + 1) * width].astype(BF)
        agg[l] = mine
        value = pre_self[l] + dot(mine, weight[1])
        pre[l] = value
        act = value / (1.0 + jnp.exp(-value))
        acts.append(act.reshape(shares, groups, SUB, width))
    ready[...] = jnp.concatenate(acts, axis=2).astype(BF)
    hand_out(ready, own, other)


def hand_out(ready, own, other):
    me = lax.axis_index("config")
    for s in range(own.shape[0]):
        own[s] = ready[lax.bitwise_xor(me, 2 * s)]
        other[s] = ready[lax.bitwise_xor(me, 2 * s + 1)]


def arrivals(own, other, received):
    found = [(0, own[0]), (1, other[0])]
    for s, both in enumerate(received):
        found.append((2 * s + 2, both[0]))
        found.append((2 * s + 3, both[1]))
    return found


def prepare(cot, attn, weight, feats, agg, pre, cot_g, gmix, slope, rows_t, w_back, attn_v, cot_v, sems):
    copies = fetch([(attn, attn_v), (cot, cot_v)], sems)
    width = cot.shape[2]
    layouts = cot.shape[0]
    groups = cot_g.shape[0]
    for l in range(feats.shape[0]):
        value = pre[l]
        sig = 1.0 / (1.0 + jnp.exp(-value))
        slope[l] = sig * (1.0 + value * (1.0 - sig))
        at = slice(l * feats.shape[1], (l + 1) * feats.shape[1])
        rows_t[0:width, at] = feats[l].T
        rows_t[width : 2 * width, at] = agg[l].T
    w_back[:, 0:width] = weight[0].T
    w_back[:, width : 2 * width] = weight[1].T
    copies[0].wait()
    copies[1].wait()
    for p in range(groups // 2):
        block = cot_v[:, 2 * SUB * p : 2 * SUB * (p + 1), :].astype(F32)
        for h in range(2):
            rows = block[:, SUB * h : SUB * (h + 1), :].reshape(layouts * SUB, width).astype(BF)
            cot_g[2 * p + h] = rows
            gmix[2 * p + h] = dot_nt(rows, attn_v[3]).astype(BF)


def attend(*refs):
    (own, other), received = refs[:2], refs[2:-13]
    cot_g, gmix, attn, own_out, other_out, hid_out, mixed, grads_own, grads_other = refs[-13:-4]
    hidden, ready, grads, _ = refs[-4:]
    me = lax.axis_index("config")
    groups, shares, depth, width = hidden.shape
    rows = shares * depth
    head = width // HEADS
    scale = 1.0 / math.sqrt(head)
    for mask, block in arrivals(own, other, received):
        hidden[:, lax.bitwise_xor(me, mask)] = block
    w_all = jnp.concatenate([attn[0], attn[1], attn[2]], axis=1)
    lane = lax.broadcasted_iota(jnp.int32, (rows, width), 1) // head
    r = lax.broadcasted_iota(jnp.int32, (rows, rows), 0)
    c = lax.broadcasted_iota(jnp.int32, (rows, rows), 1)
    same = (r % SUB) == (c % SUB)
    zero = jnp.zeros((rows, width), BF)

    def by_head(x):
        return [jnp.where(lane == e, x, zero) for e in range(HEADS)]

    total_w = jnp.zeros((width, 3 * width), F32)
    total_o = jnp.zeros((width, width), F32)
    for g in range(groups):
        hid = hidden[g].reshape(rows, width)
        hid_out[g] = hid
        qkv = dot(hid, w_all).astype(BF)
        q, k, v = (qkv[:, i * width : (i + 1) * width] for i in range(3))
        gm = gmix[g]
        k_t, v_t = k.T, v.T
        scores = dot_nt(jnp.concatenate(by_head(k), axis=0), q)
        d_probs = dot_nt(jnp.concatenate(by_head(v), axis=0), gm)
        probs, d_scores, mix_t, dq_t = [], [], [], []
        for e in range(HEADS):
            t = jnp.tanh(scores[e * rows : (e + 1) * rows] * (scale / CAP))
            w = jnp.where(same, jnp.exp(CAP * t), 0.0)
            a = w * (1.0 / jnp.sum(w, axis=0, keepdims=True))
            z = a * d_probs[e * rows : (e + 1) * rows]
            zs = jnp.sum(z, axis=0, keepdims=True)
            ds = ((z - a * zs) * (scale - scale * (t * t))).astype(BF)
            p = a.astype(BF)
            at = slice(e * head, (e + 1) * head)
            mix_t.append(dot(v_t[at], p))
            dq_t.append(dot(k_t[at], ds))
            probs.append(p)
            d_scores.append(ds)
        mix_t = jnp.concatenate(mix_t, axis=0).astype(BF)
        dq = jnp.concatenate(dq_t, axis=0).astype(BF).T
        dk = dot(jnp.concatenate(d_scores, axis=1), jnp.concatenate(by_head(q), axis=0)).astype(BF)
        dv = dot(jnp.concatenate(probs, axis=1), jnp.concatenate(by_head(gm), axis=0)).astype(BF)
        d_all = jnp.concatenate([dq, dk, dv], axis=1)
        back = cot_g[g].astype(F32) + dot_nt(d_all, w_all)
        ready[:, g] = back.astype(BF).reshape(shares, depth, width)
        mixed[g] = mix_t.T
        total_w += dot(hid.T, d_all)
        total_o += dot(mix_t, cot_g[g])
    hand_out(ready, own_out, other_out)
    for i in range(3):
        grads[i] = total_w[:, i * width : (i + 1) * width].astype(BF)
    grads[3] = total_o.astype(BF)
    core = lax.rem(me, 2)
    half = grads_own.shape[0]
    grads_own[...] = grads[pl.ds(core * half, half)]
    grads_other[...] = grads[pl.ds((1 - core) * half, half)]


def outputs(hidden, mixed, attn, out):
    groups, rows, width = hidden.shape
    layouts = rows // SUB
    for p in range(groups // 2):
        pair = []
        for g in (2 * p, 2 * p + 1):
            both = hidden[g].astype(F32) + dot(mixed[g], attn[3])
            pair.append(both.reshape(layouts, SUB, width))
        out[:, 2 * SUB * p : 2 * SUB * (p + 1), :] = jnp.concatenate(pair, axis=1).astype(BF)


def sage_back(ranks, *refs):
    (own, other), received = refs[:2], refs[2 : -9 - ranks]
    slope, rows_t, w_back, hub_t, wide, self_out, grads = refs[-9 - ranks : -2 - ranks]
    hub_out, (parts, hub_sum) = refs[-2 - ranks : -2], refs[-2:]
    me = lax.axis_index("config")
    shares, groups, layouts, _, width = parts.shape
    nodes = slope.shape[1]
    for mask, block in arrivals(own, other, received):
        parts[lax.bitwise_xor(me, mask)] = block.astype(F32).reshape(parts.shape[1:])
    grad_pre, grad_agg = [], []
    for l in range(layouts):
        gpre = (parts[:, :, l].reshape(nodes, width) * slope[l]).astype(BF)
        both = dot(gpre, w_back[...]).astype(BF)
        grad_pre.append(gpre)
        self_out[l] = both[:, 0:width]
        grad_agg.append(both[:, width : 2 * width])
    spread = jnp.concatenate(grad_agg, axis=1)
    wide[...] = spread
    hub_sum[...] = dot(hub_t[...], spread)
    slab = lax.axis_index("graph")
    hubs = hub_out[0].shape[1]
    for s in range(ranks):
        at = pl.ds(pl.multiple_of(lax.bitwise_xor(slab, s) * hubs, hubs), hubs)
        for l in range(layouts):
            hub_out[s][l] = hub_sum[at, l * width : (l + 1) * width].astype(BF)
    both = dot(rows_t[...], jnp.concatenate(grad_pre, axis=0))
    grads[0] = both[0:width].astype(BF)
    grads[1] = both[width : 2 * width].astype(BF)


def chip_order(chip, parts, work):
    for s, part in enumerate(parts):
        work[lax.bitwise_xor(chip, s)] = part[...].astype(F32)
    total = work[0]
    for s in range(1, len(parts)):
        total = total + work[s]
    return total


def tile_back(adj_t, wide, grad_self, *refs):
    parts, (totals, half, work) = refs[:-3], refs[-3:]
    layouts, _, width = totals.shape
    back = dot(adj_t[...], wide[...])
    for l in range(layouts):
        totals[l] = grad_self[l].astype(F32) + back[:, l * width : (l + 1) * width]
    half[...] = chip_order(lax.axis_index("config") // 2, parts, work).astype(BF)


def finish(ranks, scale, ids, totals, half, half_other, *refs):
    hub_parts, chips = refs[:ranks], refs[ranks:-6]
    out, weights, ids_s, rows, work, sems = refs[-6:]
    copies = fetch([(ids, ids_s)], sems)
    me = lax.axis_index("config")
    layouts, nodes, width = totals.shape
    weights[0:2] = chip_order(me // 2, chips, work) * scale
    count = half.shape[0]
    core = lax.rem(me, 2)
    weights[pl.ds(2 + core * count, count)] = half[...].astype(F32) * scale
    weights[pl.ds(2 + (1 - core) * count, count)] = half_other[...].astype(F32) * scale
    summed = hub_parts[0][...].astype(F32)
    for part in hub_parts[1:]:
        summed = summed + part[...].astype(F32)
    rows[...] = totals[...]
    copies[0].wait()
    for l in range(layouts):
        for j in range(ids.shape[0]):
            at = pl.ds(lax.rem(ids_s[j], nodes), 1)
            rows[l, at, :] += summed[l, j : j + 1, :]
    out[...] = rows[...].astype(BF)


def exchange(own, other):
    other = swapped(other, "config", 1)
    received = [
        swapped(jnp.stack([own[s], other[s]]), "config", 2 * s) for s in range(1, own.shape[0])
    ]
    return (own, other, *received)


def chips_of(x):
    return [x] + [swapped(x, "config", mask) for mask in range(2, lax.axis_size("config"), 2)]


def local(
    features,
    cotangent,
    sage_weight,
    attn_weight,
    tile_vals,
    tile_dst,
    tile_src,
    tile_count,
    hub_ids,
    hub_weight,
):
    layout_dev, node_dev, width = features.shape
    ranks = lax.axis_size("graph")
    shares = lax.axis_size("config")
    chips = shares // 2
    share = node_dev // shares
    groups = share // SUB
    layouts = layout_dev * shares
    rows = layouts * SUB
    depth = layout_dev * SUB
    hub_dev = hub_ids.shape[0]
    hubs = hub_weight.shape[1]
    slots = tile_vals.shape[0]
    slab = (layout_dev, node_dev, width)
    spread = (node_dev, layout_dev * width)
    dma = pltpu.SemaphoreType.DMA

    mine, feats = call(
        hub_pick,
        (shape((layout_dev, hub_dev, width)), shape(slab)),
        (hub_ids, features),
        [HBM, HBM],
        [pltpu.SMEM((hub_dev,), jnp.int32), dma((1 + layout_dev,))],
        name="hub_pick",
    )
    pieces = [mine] + [swapped(mine, "graph", s) for s in range(1, ranks)]

    adj_t, summed, pre_self, sage_w, hub_t = call(
        adjacency,
        (
            shape((node_dev, node_dev)),
            shape(spread, F32),
            shape(slab, F32),
            shape(sage_weight.shape),
            shape((hubs, node_dev)),
        ),
        (tile_src, tile_dst, tile_count, tile_vals, sage_weight, hub_weight.T, feats),
        [HBM] * 6 + [VMEM],
        [
            pltpu.SMEM((slots,), jnp.int32),
            pltpu.SMEM((slots,), jnp.int32),
            pltpu.SMEM((1,), jnp.int32),
            pltpu.VMEM(tile_vals.shape, BF),
            pltpu.VMEM((node_dev, node_dev), F32),
            dma((6,)),
        ],
        hidden=True,
        name="adjacency",
    )

    own, other, agg, pre = call(
        sage_out,
        (
            shape((chips, groups, depth, width)),
            shape((chips, groups, depth, width)),
            shape(slab),
            shape(slab, F32),
        ),
        (*pieces, summed, pre_self, hub_t, sage_w),
        [VMEM] * (ranks + 4),
        [pltpu.VMEM((hubs, layout_dev * width), F32), pltpu.VMEM((shares, groups, depth, width), BF)],
        name="sage_out",
    )
    hidden_in = exchange(own, other)

    cot_g, gmix, slope, rows_t, w_back, attn = call(
        prepare,
        (
            shape((groups, rows, width)),
            shape((groups, rows, width)),
            shape(slab, F32),
            shape((2 * width, layout_dev * node_dev)),
            shape((width, 2 * width)),
            shape(attn_weight.shape),
        ),
        (cotangent, attn_weight, sage_w, feats, agg, pre),
        [HBM] * 2 + [VMEM] * 4,
        [pltpu.VMEM((layouts, share, width), BF), dma((2,))],
        hidden=True,
        name="prepare",
    )

    half = (attn_weight.shape[0] // 2, width, width)
    own, other, hidden, mixed, grads_own, grads_other = call(
        attend,
        (
            shape((chips, groups, depth, width)),
            shape((chips, groups, depth, width)),
            shape((groups, rows, width)),
            shape((groups, rows, width)),
            shape(half),
            shape(half),
        ),
        (*hidden_in, cot_g, gmix, attn),
        [VMEM] * (len(hidden_in) + 3),
        [
            pltpu.VMEM((groups, shares, depth, width), BF),
            pltpu.VMEM((shares, groups, depth, width), BF),
            pltpu.VMEM(attn_weight.shape, BF),
            pltpu.VMEM((8, width), F32),
        ],
        name="attend",
    )
    grad_in = exchange(own, other)
    half_parts = chips_of(grads_own + swapped(grads_other, "config", 1))

    output = call(
        outputs,
        shape((layouts, share, width)),
        (hidden, mixed, attn),
        [VMEM] * 3,
        hidden=True,
        name="outputs",
    )

    wide, grad_self, sage_grads, *hub_parts = call(
        functools.partial(sage_back, ranks),
        (
            shape(spread),
            shape(slab),
            shape(sage_weight.shape),
            *[shape((layout_dev, hub_dev, width)) for _ in range(ranks)],
        ),
        (*grad_in, slope, rows_t, w_back, hub_t),
        [VMEM] * (len(grad_in) + 4),
        [
            pltpu.VMEM((shares, groups, layout_dev, SUB, width), F32),
            pltpu.VMEM((hubs, layout_dev * width), F32),
        ],
        name="sage_back",
    )
    hub_parts = [swapped(part, "graph", s) if s else part for s, part in enumerate(hub_parts)]
    sage_parts = chips_of(sage_grads + swapped(sage_grads, "config", 1))

    totals, half_own = call(
        tile_back,
        (shape(slab, F32), shape(half)),
        (adj_t, wide, grad_self, *half_parts),
        [VMEM] * (3 + chips),
        [pltpu.VMEM((chips, *half), F32)],
        hidden=True,
        name="tile_back",
    )
    half_other = swapped(half_own, "config", 1)

    grad_features, weights = call(
        functools.partial(finish, ranks, 1.0 / math.sqrt(layouts * node_dev)),
        (shape(slab), shape((6, width, width), F32)),
        (hub_ids, totals, half_own, half_other, *hub_parts, *sage_parts),
        [HBM] + [VMEM] * (3 + ranks + chips),
        [
            pltpu.SMEM((hub_dev,), jnp.int32),
            pltpu.VMEM(slab, F32),
            pltpu.VMEM((chips, *sage_weight.shape), F32),
            dma((1,)),
        ],
        name="finish",
    )
    return (output, grad_features, weights[None])


def solution(mesh):
    return jax.shard_map(
        local,
        mesh=mesh,
        in_specs=(
            P("config", "graph", None),
            P(None, ("graph", "config"), None),
            P(),
            P(),
            P("graph", None, None),
            P("graph"),
            P("graph"),
            P("graph"),
            P("graph"),
            P("graph", None),
        ),
        out_specs=(
            P(None, ("graph", "config"), None),
            P("config", "graph", None),
            P("graph", None, None, None),
        ),
        check_vma=False,
    )
```

time: 73 us -> 54.1 us (0.74)
  blocking collectives: 18 us -> 0 us
  starting transfers between devices: 17.4 us -> 26 us
  local copies, waits for them, and re-layouts: 8.04 us -> 3.93 us
  waiting for transfers between devices: 13.6 us -> 9.63 us
  Pallas kernels: 13.9 us -> 12.8 us
    ppermute x3 -> x23, starting transfers between devices: 6.11 us -> 26 us  [swapped(): return lax.ppermute(x, axis, [(i, i ^ mask) for i in range(count)])]
    all_to_all x2 -> x0, blocking collectives: 18 us -> none  [the longest x1 9.35 us: local(): lax.all_to_all(grad_hidden, 'config', split_axis=0, concat_axis=0, tiled=...]
    all_to_all x3 -> x0, waiting for transfers between devices: 13.3 us -> none  [the longest x1 5.58 us: local(): lax.all_to_all(hub_part, 'graph', split_axis=0, concat_axis=0, tiled=True)]
    all_to_all x3 -> x0, starting transfers between devices: 11.3 us -> none  [the longest x1 4.05 us: local(): lax.all_to_all(hub_part, 'graph', split_axis=0, concat_axis=0, tiled=True)]
    ppermute x3 -> x23, waiting for transfers between devices: 0.28 us -> 9.63 us  [swapped(): return lax.ppermute(x, axis, [(i, i ^ mask) for i in range(count)])]
    unnamed x33 -> x20, local copies, waits for them, and re-layouts: 7.33 us -> 3.9 us
    pallas_call x10 -> x9, Pallas kernels: 13.9 us -> 12.8 us  [call(): pl.pallas_call(kernel, out_shape=outs, in_specs=specs, out_specs=jax.tree...]
  transfers between devices with their start and end apart: 6 -> 23, of which waited for: 4 -> 10; matrix products, arithmetic and copies ran while one was open for 0% -> 0% of each run, Pallas kernels for 6% -> 8%
where the time goes in v1:
time: 54.1 us; the launch traced here: 54 us
  starting transfers between devices  26 us (48%)
  Pallas kernels  12.8 us (24%)
  waiting for transfers between devices  9.63 us (18%)
  local copies, waits for them, and re-layouts  3.93 us (7%)
  between operations  1.5 us (3%)
    ppermute x23, starting transfers between devices, swapped(): return lax.ppermute(x, axis, [(i, i ^ mask) for i in range(count)])  26 us
    pallas_call x9, Pallas kernels, call(): pl.pallas_call(kernel, out_shape=outs, in_specs=specs, out_specs=jax.tree...  12.8 us
    ppermute x23, waiting for transfers between devices, swapped(): return lax.ppermute(x, axis, [(i, i ^ mask) for i in range(count)])  9.63 us
    unnamed x20, local copies, waits for them, and re-layouts  3.9 us
  transfers between devices with their start and end apart: 23, of which 10 were waited for; matrix products, arithmetic and copies ran while one was open for 0% of the time, Pallas kernels for 8%

profile of v1, /device:TPU:0, one launch (start us, length us, event | category | flops | bytes accessed | tf_op | source)
XLA Modules:
  0.0 54.0 jit_solution(555585260384617738)
XLA Ops:
  0.6 0.9 %copy-done = bf16[2,512,128]{2,1,0:T(8,128)(2,1)S(1)} copy-done((bf16[2,512,128]{2,1,0:T(8,128)(2,1)S(1)}, bf16[2,512,128]{2,1,0:T(8,128)(2,1)}, u32[]{:S(2)}) %copy-start) | copy-done | bytes 262168
  1.6 0.7 %copy-done.1 = s32[8]{0:T(128)S(1)} copy-done((s32[8]{0:T(128)S(1)}, s32[8]{0:T(128)}, u32[]{:S(2)}) %copy-start.1) | copy-done | bytes 56
  2.2 0.9 %hub_pick.1 = (bf16[2,8,128]{2,1,0:T(8,128)(2,1)S(1)}, bf16[2,512,128]{2,1,0:T(8,128)(2,1)S(1)}) custom-call(s32[8]{0:T(128)S(1)} %copy-done.1, bf16[2,512,128]{2,1,0:T(8,128)(2,1)S(1)} %copy-done), custom_call_target="tpu_custom_call" | custom-call | tf_op jit(solution)/shard_map/hub_pick/pallas_call | solution.py:42
  3.1 3.1 %collective-permute-start = (bf16[2,8,128]{2,1,0:T(8,128)(2,1)S(1)}, bf16[2,8,128]{2,1,0:T(8,128)(2,1)S(1)}, u32[]{:S(2)}, u32[]{:S(2)}) collective-permute-start(bf16[2,8,128]{2,1,0:T(8,128)(2,1)S(1)} %get-tuple-element.37.refs_0_), channel_id=1, source_target_pairs={{0,8},{8,0},{16,24},{24,16},{1,9},{9,1},{17,25},{25,17},{2,10},{10... | collective-permute-start | bytes 12296 | tf_op jit(solution)/shard_map/ppermute | solution.py:63
  6.2 2.6 %collective-permute-start.1 = (bf16[2,8,128]{2,1,0:T(8,128)(2,1)S(1)}, bf16[2,8,128]{2,1,0:T(8,128)(2,1)S(1)}, u32[]{:S(2)}, u32[]{:S(2)}) collective-permute-start(bf16[2,8,128]{2,1,0:T(8,128)(2,1)S(1)} %get-tuple-element.37.refs_0_), channel_id=1, source_target_pairs={{0,16},{8,24},{16,0},{24,8},{1,17},{9,25},{17,1},{25,9},{2,18},{10... | collective-permute-start | bytes 12296 | tf_op jit(solution)/shard_map/ppermute | solution.py:63
  9.5 0.0 copy-start.9
  9.5 0.6 %copy-done.8 = s32[12]{0:T(128)S(1)} copy-done((s32[12]{0:T(128)S(1)}, s32[12]{0:T(128)}, u32[]{:S(2)}) %copy-start.8) | copy-done | bytes 72
  10.1 0.0 copy-done.9
  10.1 1.0 %copy-done.3 = bf16[12,128,128]{2,1,0:T(8,128)(2,1)S(1)} copy-done((bf16[12,128,128]{2,1,0:T(8,128)(2,1)S(1)}, bf16[12,128,128]{2,1,0:T(8,128)(2,1)}, u32[]{:S(2)}) %copy-start.3) | copy-done | bytes 393240
  11.1 1.6 %adjacency.1 = (bf16[512,512]{1,0:T(8,128)(2,1)S(1)}, f32[512,256]{1,0:T(8,128)S(1)}, f32[2,512,128]{2,1,0:T(8,128)S(1)}, bf16[2,128,128]{2,1,0:T(8,128)(2,1)S(1)}, bf16[32,512]{1,0:T(8,128)(2,1)S(1)}) custom-call(s32[12]{0:T(128)S(1)} %copy-done.8, s32[12]{0:T(128)S(1)} %copy-done.9, s32[1]{0:T(128)S(6)} %copy.13.count, ...), custom_call_target="tpu_custom_call" | custom-call | flops 1000000000 | bytes 2097152 | tf_op jit(solution)/shard_map/adjacency/pallas_call | solution.py:42
  12.7 1.5 %collective-permute-done.2.refs_3_ = bf16[2,8,128]{2,1,0:T(8,128)(2,1)S(1)} collective-permute-done((bf16[2,8,128]{2,1,0:T(8,128)(2,1)S(1)}, bf16[2,8,128]{2,1,0:T(8,128)(2,1)S(1)}, u32[]{:S(2)}, u32[]{:S(2)}) %collective-permute-start.2) | collective-permute-done | bytes 4128 | tf_op jit(solution)/shard_map/ppermute | solution.py:63
  14.2 0.5 sage_out.1
  14.7 0.1 collective-permute-start.3
  14.8 1.3 %collective-permute-done.3.refs_1_ = bf16[4,8,16,128]{3,2,1,0:T(8,128)(2,1)S(1)} collective-permute-done((bf16[4,8,16,128]{3,2,1,0:T(8,128)(2,1)S(1)}, bf16[4,8,16,128]{3,2,1,0:T(8,128)(2,1)S(1)}, u32[]{:S(2)}, u32[]{:S(2)}) %collective-permute-start.3) | collective-permute-done | bytes 131104 | tf_op jit(solution)/shard_map/ppermute | solution.py:63
  16.2 2.5 %collective-permute-start.6 = (bf16[2,8,16,128]{3,2,1,0:T(8,128)(2,1)S(1)}, bf16[2,8,16,128]{3,2,1,0:T(8,128)(2,1)S(1)}, u32[]{:S(2)}, u32[]{:S(2)}) collective-permute-start(bf16[2,8,16,128]{3,2,1,0:T(8,128)(2,1)S(1)} %pad_maximum_fusion.2), channel_id=1, source_target_pairs={{0,6},{1,7},{2,4},{3,5},{4,2},{5,3},{6,0},{7,1},{8,14},{9,15},{10,... | collective-permute-start | bytes 196616 | tf_op jit(solution)/shard_map/ppermute | solution.py:63
  18.7 0.6 %collective-permute-start.5 = (bf16[2,8,16,128]{3,2,1,0:T(8,128)(2,1)S(1)}, bf16[2,8,16,128]{3,2,1,0:T(8,128)(2,1)S(1)}, u32[]{:S(2)}, u32[]{:S(2)}) collective-permute-start(bf16[2,8,16,128]{3,2,1,0:T(8,128)(2,1)S(1)} %pad_maximum_fusion.1), channel_id=1, source_target_pairs={{0,4},{1,5},{2,6},{3,7},{4,0},{5,1},{6,2},{7,3},{8,12},{9,13},{10,... | collective-permute-start | bytes 196616 | tf_op jit(solution)/shard_map/ppermute | solution.py:63
  19.3 0.6 %collective-permute-start.4 = (bf16[2,8,16,128]{3,2,1,0:T(8,128)(2,1)S(1)}, bf16[2,8,16,128]{3,2,1,0:T(8,128)(2,1)S(1)}, u32[]{:S(2)}, u32[]{:S(2)}) collective-permute-start(bf16[2,8,16,128]{3,2,1,0:T(8,128)(2,1)S(1)} %pad_maximum_fusion), channel_id=1, source_target_pairs={{0,2},{1,3},{2,0},{3,1},{4,6},{5,7},{6,4},{7,5},{8,10},{9,11},{10,... | collective-permute-start | bytes 196616 | tf_op jit(solution)/shard_map/ppermute | solution.py:63
  19.9 0.8 %prepare.1 = (bf16[8,128,128]{2,1,0:T(8,128)(2,1)S(1)}, bf16[8,128,128]{2,1,0:T(8,128)(2,1)S(1)}, f32[2,512,128]{2,1,0:T(8,128)S(1)}, bf16[256,1024]{1,0:T(8,128...) custom-call(bf16[16,64,128]{2,1,0:T(8,128)(2,1)S(1)} %copy-done.4, ...), custom_call_target="tpu_custom_call" | custom-call | flops 1000000000 | bytes 2097152 | tf_op jit(solution)/shard_map/prepare/pallas_call | solution.py:42
  20.7 0.7 %collective-permute-done.6.refs_4_ = bf16[2,8,16,128]{3,2,1,0:T(8,128)(2,1)S(1)} collective-permute-done((bf16[2,8,16,128]{3,2,1,0:T(8,128)(2,1)S(1)}, bf16[2,8,16,128]{3,2,1,0:T(8,128)(2,1)S(1)}, u32[]{:S(2)}, u32[]{:S(2)}) %collective-permute-start.6) | collective-permute-done | bytes 65568 | tf_op jit(solution)/shard_map/ppermute | solution.py:63
  21.4 1.6 %collective-permute-done.5.refs_3_ = bf16[2,8,16,128]{3,2,1,0:T(8,128)(2,1)S(1)} collective-permute-done((bf16[2,8,16,128]{3,2,1,0:T(8,128)(2,1)S(1)}, bf16[2,8,16,128]{3,2,1,0:T(8,128)(2,1)S(1)}, u32[]{:S(2)}, u32[]{:S(2)}) %collective-permute-start.5) | collective-permute-done | bytes 65568 | tf_op jit(solution)/shard_map/ppermute | solution.py:63
  23.0 0.6 %collective-permute-done.4.refs_2_ = bf16[2,8,16,128]{3,2,1,0:T(8,128)(2,1)S(1)} collective-permute-done((bf16[2,8,16,128]{3,2,1,0:T(8,128)(2,1)S(1)}, bf16[2,8,16,128]{3,2,1,0:T(8,128)(2,1)S(1)}, u32[]{:S(2)}, u32[]{:S(2)}) %collective-permute-start.4) | collective-permute-done | bytes 65568 | tf_op jit(solution)/shard_map/ppermute | solution.py:63
  23.6 5.9 %attend.1 = (bf16[4,8,16,128]{3,2,1,0:T(8,128)(2,1)S(1)}, bf16[4,8,16,128]{3,2,1,0:T(8,128)(2,1)S(1)}, bf16[8,128,128]{2,1,0:T(8,128)(2,1)S(1)}, bf16[8,128,128]...) custom-call(bf16[4,8,16,128]{3,2,1,0:T(8,128)(2,1)S(1)} %get-tuple-element.43.refs_0_, ...), custom_call_target="tpu_custom_call" | custom-call | tf_op jit(solution)/shard_map/attend/pallas_call | solution.py:42
  29.5 0.1 collective-permute-start.7
  29.5 0.5 collective-permute-start.11
  30.0 0.8 %collective-permute-done.7.refs_1_ = bf16[4,8,16,128]{3,2,1,0:T(8,128)(2,1)S(1)} collective-permute-done((bf16[4,8,16,128]{3,2,1,0:T(8,128)(2,1)S(1)}, bf16[4,8,16,128]{3,2,1,0:T(8,128)(2,1)S(1)}, u32[]{:S(2)}, u32[]{:S(2)}) %collective-permute-start.7) | collective-permute-done | bytes 131104 | tf_op jit(solution)/shard_map/ppermute | solution.py:63
  30.9 1.6 %collective-permute-start.10 = (bf16[2,8,16,128]{3,2,1,0:T(8,128)(2,1)S(1)}, bf16[2,8,16,128]{3,2,1,0:T(8,128)(2,1)S(1)}, u32[]{:S(2)}, u32[]{:S(2)}) collective-permute-start(bf16[2,8,16,128]{3,2,1,0:T(8,128)(2,1)S(1)} %pad_maximum_fusion.5), channel_id=1, source_target_pairs={{0,6},{1,7},{2,4},{3,5},{4,2},{5,3},{6,0},{7,1},{8,14},{9,15},{10,... | collective-permute-start | bytes 196616 | tf_op jit(solution)/shard_map/ppermute | solution.py:63
  32.5 0.7 %collective-permute-start.9 = (bf16[2,8,16,128]{3,2,1,0:T(8,128)(2,1)S(1)}, bf16[2,8,16,128]{3,2,1,0:T(8,128)(2,1)S(1)}, u32[]{:S(2)}, u32[]{:S(2)}) collective-permute-start(bf16[2,8,16,128]{3,2,1,0:T(8,128)(2,1)S(1)} %pad_maximum_fusion.4), channel_id=1, source_target_pairs={{0,4},{1,5},{2,6},{3,7},{4,0},{5,1},{6,2},{7,3},{8,12},{9,13},{10,... | collective-permute-start | bytes 196616 | tf_op jit(solution)/shard_map/ppermute | solution.py:63
  33.1 1.5 %collective-permute-start.8 = (bf16[2,8,16,128]{3,2,1,0:T(8,128)(2,1)S(1)}, bf16[2,8,16,128]{3,2,1,0:T(8,128)(2,1)S(1)}, u32[]{:S(2)}, u32[]{:S(2)}) collective-permute-start(bf16[2,8,16,128]{3,2,1,0:T(8,128)(2,1)S(1)} %pad_maximum_fusion.3), channel_id=1, source_target_pairs={{0,2},{1,3},{2,0},{3,1},{4,6},{5,7},{6,4},{7,5},{8,10},{9,11},{10,... | collective-permute-start | bytes 196616 | tf_op jit(solution)/shard_map/ppermute | solution.py:63
  34.6 0.7 %collective-permute-start.12 = (bf16[2,128,128]{2,1,0:T(8,128)(2,1)S(1)}, bf16[2,128,128]{2,1,0:T(8,128)(2,1)S(1)}, u32[]{:S(2)}, u32[]{:S(2)}) collective-permute-start(bf16[2,128,128]{2,1,0:T(8,128)(2,1)S(1)} %add.6.refs_0_), channel_id=1, source_target_pairs={{0,2},{1,3},{2,0},{3,1},{4,6},{5,7},{6,4},{7,5},{8,10},{9,11},{10,... | collective-permute-start | bytes 196616 | tf_op jit(solution)/shard_map/ppermute | solution.py:63
  35.3 1.4 %collective-permute-start.13 = (bf16[2,128,128]{2,1,0:T(8,128)(2,1)S(1)}, bf16[2,128,128]{2,1,0:T(8,128)(2,1)S(1)}, u32[]{:S(2)}, u32[]{:S(2)}) collective-permute-start(bf16[2,128,128]{2,1,0:T(8,128)(2,1)S(1)} %add.6.refs_0_), channel_id=1, source_target_pairs={{0,4},{1,5},{2,6},{3,7},{4,0},{5,1},{6,2},{7,3},{8,12},{9,13},{10,... | collective-permute-start | bytes 196616 | tf_op jit(solution)/shard_map/ppermute | solution.py:63
  36.8 1.4 %collective-permute-start.14 = (bf16[2,128,128]{2,1,0:T(8,128)(2,1)S(1)}, bf16[2,128,128]{2,1,0:T(8,128)(2,1)S(1)}, u32[]{:S(2)}, u32[]{:S(2)}) collective-permute-start(bf16[2,128,128]{2,1,0:T(8,128)(2,1)S(1)} %add.6.refs_0_), channel_id=1, source_target_pairs={{0,6},{1,7},{2,4},{3,5},{4,2},{5,3},{6,0},{7,1},{8,14},{9,15},{10,... | collective-permute-start | bytes 196616 | tf_op jit(solution)/shard_map/ppermute | solution.py:63
  38.2 0.6 %sage_back.1 = (bf16[512,256]{1,0:T(8,128)(2,1)S(1)}, bf16[2,512,128]{2,1,0:T(8,128)(2,1)S(1)}, bf16[2,128,128]{2,1,0:T(8,128)(2,1)S(1)}, bf16[2,8,128]{2,1,0:T(...) custom-call(bf16[4,8,16,128]{3,2,1,0:T(8,128)(2,1)S(1)} %get-tuple-e, ...), custom_call_target="tpu_custom_call" | custom-call | tf_op jit(solution)/shard_map/sage_back/pallas_call | solution.py:42
  38.8 0.1 collective-permute-start.19
  38.9 0.1 collective-permute-start.16
  38.9 0.3 collective-permute-done.12.refs_1_
  39.2 2.6 %collective-permute-start.17 = (bf16[2,8,128]{2,1,0:T(8,128)(2,1)S(1)}, bf16[2,8,128]{2,1,0:T(8,128)(2,1)S(1)}, u32[]{:S(2)}, u32[]{:S(2)}) collective-permute-start(bf16[2,8,128]{2,1,0:T(8,128)(2,1)S(1)} %get-tuple-element.66), channel_id=1, source_target_pairs={{0,16},{8,24},{16,0},{24,8},{1,17},{9,25},{17,1},{25,9},{2,18},{10... | collective-permute-start | bytes 12296 | tf_op jit(solution)/shard_map/ppermute | solution.py:63
  41.8 0.1 collective-permute-done.14.refs_3_
  41.9 0.3 tile_back.1
  42.2 0.1 collective-permute-start.15
  42.3 2.4 %collective-permute-start.18 = (bf16[2,8,128]{2,1,0:T(8,128)(2,1)S(1)}, bf16[2,8,128]{2,1,0:T(8,128)(2,1)S(1)}, u32[]{:S(2)}, u32[]{:S(2)}) collective-permute-start(bf16[2,8,128]{2,1,0:T(8,128)(2,1)S(1)} %get-tuple-element.67), channel_id=1, source_target_pairs={{0,24},{8,16},{16,8},{24,0},{1,25},{9,17},{17,9},{25,1},{2,26},{10... | collective-permute-start | bytes 12296 | tf_op jit(solution)/shard_map/ppermute | solution.py:63
  44.7 1.6 %collective-permute-start.20 = (bf16[2,128,128]{2,1,0:T(8,128)(2,1)S(1)}, bf16[2,128,128]{2,1,0:T(8,128)(2,1)S(1)}, u32[]{:S(2)}, u32[]{:S(2)}) collective-permute-start(bf16[2,128,128]{2,1,0:T(8,128)(2,1)S(1)} %add.7.refs_4_), channel_id=1, source_target_pairs={{0,2},{1,3},{2,0},{3,1},{4,6},{5,7},{6,4},{7,5},{8,10},{9,11},{10,... | collective-permute-start | bytes 196616 | tf_op jit(solution)/shard_map/ppermute | solution.py:63
  46.3 0.5 collective-permute-start.21
  46.8 1.5 %collective-permute-start.22 = (bf16[2,128,128]{2,1,0:T(8,128)(2,1)S(1)}, bf16[2,128,128]{2,1,0:T(8,128)(2,1)S(1)}, u32[]{:S(2)}, u32[]{:S(2)}) collective-permute-start(bf16[2,128,128]{2,1,0:T(8,128)(2,1)S(1)} %add.7.refs_4_), channel_id=1, source_target_pairs={{0,6},{1,7},{2,4},{3,5},{4,2},{5,3},{6,0},{7,1},{8,14},{9,15},{10,... | collective-permute-start | bytes 196616 | tf_op jit(solution)/shard_map/ppermute | solution.py:63
  48.3 0.9 %outputs.1 = bf16[16,64,128]{2,1,0:T(8,128)(2,1)} custom-call(bf16[8,128,128]{2,1,0:T(8,128)(2,1)S(1)} %get-tuple-element.50.hidden, bf16[8,128,128]{2,1,0:T(8,128)(2,1)S(1)} %get-tuple-element.51.mixed, bf16[4,128,128]{2,1,0:T(8,128)(2,1)S(1)} %get-tuple-element.49.refs_7_.attn), custom_call_target="tpu_custom_call" | custom-call | flops 1000000000 | bytes 2097152 | tf_op jit(solution)/shard_map/outputs/pallas_call | solution.py:42
  49.2 2.0 %collective-permute-done.21.refs_6_ = bf16[2,128,128]{2,1,0:T(8,128)(2,1)S(1)} collective-permute-done((bf16[2,128,128]{2,1,0:T(8,128)(2,1)S(1)}, bf16[2,128,128]{2,1,0:T(8,128)(2,1)S(1)}, u32[]{:S(2)}, u32[]{:S(2)}) %collective-permute-start.21) | collective-permute-done | bytes 65568 | tf_op jit(solution)/shard_map/ppermute | solution.py:63
  51.3 0.7 %collective-permute-done.22.refs_7_ = bf16[2,128,128]{2,1,0:T(8,128)(2,1)S(1)} collective-permute-done((bf16[2,128,128]{2,1,0:T(8,128)(2,1)S(1)}, bf16[2,128,128]{2,1,0:T(8,128)(2,1)S(1)}, u32[]{:S(2)}, u32[]{:S(2)}) %collective-permute-start.22) | collective-permute-done | bytes 65568 | tf_op jit(solution)/shard_map/ppermute | solution.py:63
  52.0 0.7 %copy-done.2 = s32[8]{0:T(128)S(1)} copy-done((s32[8]{0:T(128)S(1)}, s32[8]{0:T(128)}, u32[]{:S(2)}) %copy-start.2) | copy-done | bytes 56
  52.6 1.4 %finish.1 = (bf16[2,512,128]{2,1,0:T(8,128)(2,1)}, f32[6,128,128]{2,1,0:T(8,128)}) custom-call(s32[8]{0:T(128)S(1)} %copy-done.2, f32[2,512,128]{2,1,0:T(8,128)S(1)} %get-tuple-element.62.totals, bf16[2,128,128]{2,1,0:T(8,128)(2,1)S(1)} %get-tuple-element.63.half, bf16[2,128,128]{2,1,0:T(8,128)(2,1)S(1)} %collective-permute-done.15.half_other, ...), custom_call_target="tpu_custom_call" | custom-call | tf_op jit(solution)/shard_map/finish/pallas_call | solution.py:42
  (39 shorter events, 0.2 us)
Async XLA Ops:
  0.6 1.0 %copy-start = (bf16[2,512,128]{2,1,0:T(8,128)(2,1)S(1)}, bf16[2,512,128]{2,1,0:T(8,128)(2,1)}, u32[]{:S(2)}) copy-start(bf16[2,512,128]{2,1,0:T(8,128)(2,1)} %feats.1) | copy-start | bytes 786436
  1.6 0.7 %copy-start.1 = (s32[8]{0:T(128)S(1)}, s32[8]{0:T(128)}, u32[]{:S(2)}) copy-start(s32[8]{0:T(128)} %ids.3) | copy-start | bytes 100
  2.2 7.2 %copy-start.6 = (bf16[2,128,128]{2,1,0:T(8,128)(2,1)S(1)}, bf16[2,128,128]{2,1,0:T(8,128)(2,1)}, u32[]{:S(2)}) copy-start(bf16[2,128,128]{2,1,0:T(8,128)(2,1)} %weight.1) | copy-start | bytes 196612
  2.2 7.2 %copy-start.7 = (bf16[512,32]{0,1:T(8,128)(2,1)S(1)}, bf16[512,32]{0,1:T(8,128)(2,1)}, u32[]{:S(2)}) copy-start(bf16[512,32]{0,1:T(8,128)(2,1)} %param.19) | copy-start | bytes 98308
  3.1 9.6 %collective-permute-start = (bf16[2,8,128]{2,1,0:T(8,128)(2,1)S(1)}, bf16[2,8,128]{2,1,0:T(8,128)(2,1)S(1)}, u32[]{:S(2)}, u32[]{:S(2)}) collective-permute-start(bf16[2,8,128]{2,1,0:T(8,128)(2,1)S(1)} %get-tuple-element.37.refs_0_), channel_id=1, source_target_pairs={{0,8},{8,0},{16,24},{24,16},{1,9},{9,1},{17,25},{25,17},{2,10},{10... | collective-permute-start | bytes 12296 | tf_op jit(solution)/shard_map/ppermute | solution.py:63
  6.2 6.5 %collective-permute-start.1 = (bf16[2,8,128]{2,1,0:T(8,128)(2,1)S(1)}, bf16[2,8,128]{2,1,0:T(8,128)(2,1)S(1)}, u32[]{:S(2)}, u32[]{:S(2)}) collective-permute-start(bf16[2,8,128]{2,1,0:T(8,128)(2,1)S(1)} %get-tuple-element.37.refs_0_), channel_id=1, source_target_pairs={{0,16},{8,24},{16,0},{24,8},{1,17},{9,25},{17,1},{25,9},{2,18},{10... | collective-permute-start | bytes 12296 | tf_op jit(solution)/shard_map/ppermute | solution.py:63
  8.8 5.4 %collective-permute-start.2 = (bf16[2,8,128]{2,1,0:T(8,128)(2,1)S(1)}, bf16[2,8,128]{2,1,0:T(8,128)(2,1)S(1)}, u32[]{:S(2)}, u32[]{:S(2)}) collective-permute-start(bf16[2,8,128]{2,1,0:T(8,128)(2,1)S(1)} %get-tuple-element.37.refs_0_), channel_id=1, source_target_pairs={{0,24},{8,16},{16,8},{24,0},{1,25},{9,17},{17,9},{25,1},{2,26},{10... | collective-permute-start | bytes 12296 | tf_op jit(solution)/shard_map/ppermute | solution.py:63
  9.4 0.7 %copy-start.8 = (s32[12]{0:T(128)S(1)}, s32[12]{0:T(128)}, u32[]{:S(2)}) copy-start(s32[12]{0:T(128)} %src.1) | copy-start | bytes 148
  9.5 0.7 %copy-start.9 = (s32[12]{0:T(128)S(1)}, s32[12]{0:T(128)}, u32[]{:S(2)}) copy-start(s32[12]{0:T(128)} %dst.1) | copy-start | bytes 148
  10.1 1.0 %copy-start.3 = (bf16[12,128,128]{2,1,0:T(8,128)(2,1)S(1)}, bf16[12,128,128]{2,1,0:T(8,128)(2,1)}, u32[]{:S(2)}) copy-start(bf16[12,128,128]{2,1,0:T(8,128)(2,1)} %tiles.1) | copy-start | bytes 1179652
  14.7 1.4 %collective-permute-start.3 = (bf16[4,8,16,128]{3,2,1,0:T(8,128)(2,1)S(1)}, bf16[4,8,16,128]{3,2,1,0:T(8,128)(2,1)S(1)}, u32[]{:S(2)}, u32[]{:S(2)}) collective-permute-start(bf16[4,8,16,128]{3,2,1,0:T(8,128)(2,1)S(1)} %get-tuple-element.44), channel_id=1, source_target_pairs={{0,1},{1,0},{2,3},{3,2},{4,5},{5,4},{6,7},{7,6},{8,9},{9,8},{10,11... | collective-permute-start | bytes 393224 | tf_op jit(solution)/shard_map/ppermute | solution.py:63
  14.8 5.0 %copy-start.4 = (bf16[16,64,128]{2,1,0:T(8,128)(2,1)S(1)}, bf16[16,64,128]{2,1,0:T(8,128)(2,1)}, u32[]{:S(2)}) copy-start(bf16[16,64,128]{2,1,0:T(8,128)(2,1)} %cot.1) | copy-start | bytes 786436
  16.2 5.2 %collective-permute-start.6 = (bf16[2,8,16,128]{3,2,1,0:T(8,128)(2,1)S(1)}, bf16[2,8,16,128]{3,2,1,0:T(8,128)(2,1)S(1)}, u32[]{:S(2)}, u32[]{:S(2)}) collective-permute-start(bf16[2,8,16,128]{3,2,1,0:T(8,128)(2,1)S(1)} %pad_maximum_fusion.2), channel_id=1, source_target_pairs={{0,6},{1,7},{2,4},{3,5},{4,2},{5,3},{6,0},{7,1},{8,14},{9,15},{10,... | collective-permute-start | bytes 196616 | tf_op jit(solution)/shard_map/ppermute | solution.py:63
  18.7 1.2 %copy-start.5 = (bf16[4,128,128]{2,1,0:T(8,128)(2,1)S(1)}, bf16[4,128,128]{2,1,0:T(8,128)(2,1)}, u32[]{:S(2)}) copy-start(bf16[4,128,128]{2,1,0:T(8,128)(2,1)} %attn.1) | copy-start | bytes 393220
  18.7 4.3 %collective-permute-start.5 = (bf16[2,8,16,128]{3,2,1,0:T(8,128)(2,1)S(1)}, bf16[2,8,16,128]{3,2,1,0:T(8,128)(2,1)S(1)}, u32[]{:S(2)}, u32[]{:S(2)}) collective-permute-start(bf16[2,8,16,128]{3,2,1,0:T(8,128)(2,1)S(1)} %pad_maximum_fusion.1), channel_id=1, source_target_pairs={{0,4},{1,5},{2,6},{3,7},{4,0},{5,1},{6,2},{7,3},{8,12},{9,13},{10,... | collective-permute-start | bytes 196616 | tf_op jit(solution)/shard_map/ppermute | solution.py:63
  19.3 4.3 %collective-permute-start.4 = (bf16[2,8,16,128]{3,2,1,0:T(8,128)(2,1)S(1)}, bf16[2,8,16,128]{3,2,1,0:T(8,128)(2,1)S(1)}, u32[]{:S(2)}, u32[]{:S(2)}) collective-permute-start(bf16[2,8,16,128]{3,2,1,0:T(8,128)(2,1)S(1)} %pad_maximum_fusion), channel_id=1, source_target_pairs={{0,2},{1,3},{2,0},{3,1},{4,6},{5,7},{6,4},{7,5},{8,10},{9,11},{10,... | collective-permute-start | bytes 196616 | tf_op jit(solution)/shard_map/ppermute | solution.py:63
  29.5 1.4 %collective-permute-start.7 = (bf16[4,8,16,128]{3,2,1,0:T(8,128)(2,1)S(1)}, bf16[4,8,16,128]{3,2,1,0:T(8,128)(2,1)S(1)}, u32[]{:S(2)}, u32[]{:S(2)}) collective-permute-start(bf16[4,8,16,128]{3,2,1,0:T(8,128)(2,1)S(1)} %get-tuple-element.54), channel_id=1, source_target_pairs={{0,1},{1,0},{2,3},{3,2},{4,5},{5,4},{6,7},{7,6},{8,9},{9,8},{10,11... | collective-permute-start | bytes 393224 | tf_op jit(solution)/shard_map/ppermute | solution.py:63
  29.5 5.1 %collective-permute-start.11 = (bf16[2,128,128]{2,1,0:T(8,128)(2,1)S(1)}, bf16[2,128,128]{2,1,0:T(8,128)(2,1)S(1)}, u32[]{:S(2)}, u32[]{:S(2)}) collective-permute-start(bf16[2,128,128]{2,1,0:T(8,128)(2,1)S(1)} %get-tuple-element.61), channel_id=1, source_target_pairs={{0,1},{1,0},{2,3},{3,2},{4,5},{5,4},{6,7},{7,6},{8,9},{9,8},{10,11... | collective-permute-start | bytes 196616 | tf_op jit(solution)/shard_map/ppermute | solution.py:63
  30.9 5.8 %collective-permute-start.10 = (bf16[2,8,16,128]{3,2,1,0:T(8,128)(2,1)S(1)}, bf16[2,8,16,128]{3,2,1,0:T(8,128)(2,1)S(1)}, u32[]{:S(2)}, u32[]{:S(2)}) collective-permute-start(bf16[2,8,16,128]{3,2,1,0:T(8,128)(2,1)S(1)} %pad_maximum_fusion.5), channel_id=1, source_target_pairs={{0,6},{1,7},{2,4},{3,5},{4,2},{5,3},{6,0},{7,1},{8,14},{9,15},{10,... | collective-permute-start | bytes 196616 | tf_op jit(solution)/shard_map/ppermute | solution.py:63
  32.5 5.7 %collective-permute-start.9 = (bf16[2,8,16,128]{3,2,1,0:T(8,128)(2,1)S(1)}, bf16[2,8,16,128]{3,2,1,0:T(8,128)(2,1)S(1)}, u32[]{:S(2)}, u32[]{:S(2)}) collective-permute-start(bf16[2,8,16,128]{3,2,1,0:T(8,128)(2,1)S(1)} %pad_maximum_fusion.4), channel_id=1, source_target_pairs={{0,4},{1,5},{2,6},{3,7},{4,0},{5,1},{6,2},{7,3},{8,12},{9,13},{10,... | collective-permute-start | bytes 196616 | tf_op jit(solution)/shard_map/ppermute | solution.py:63
  33.1 5.0 %collective-permute-start.8 = (bf16[2,8,16,128]{3,2,1,0:T(8,128)(2,1)S(1)}, bf16[2,8,16,128]{3,2,1,0:T(8,128)(2,1)S(1)}, u32[]{:S(2)}, u32[]{:S(2)}) collective-permute-start(bf16[2,8,16,128]{3,2,1,0:T(8,128)(2,1)S(1)} %pad_maximum_fusion.3), channel_id=1, source_target_pairs={{0,2},{1,3},{2,0},{3,1},{4,6},{5,7},{6,4},{7,5},{8,10},{9,11},{10,... | collective-permute-start | bytes 196616 | tf_op jit(solution)/shard_map/ppermute | solution.py:63
  34.6 4.6 %collective-permute-start.12 = (bf16[2,128,128]{2,1,0:T(8,128)(2,1)S(1)}, bf16[2,128,128]{2,1,0:T(8,128)(2,1)S(1)}, u32[]{:S(2)}, u32[]{:S(2)}) collective-permute-start(bf16[2,128,128]{2,1,0:T(8,128)(2,1)S(1)} %add.6.refs_0_), channel_id=1, source_target_pairs={{0,2},{1,3},{2,0},{3,1},{4,6},{5,7},{6,4},{7,5},{8,10},{9,11},{10,... | collective-permute-start | bytes 196616 | tf_op jit(solution)/shard_map/ppermute | solution.py:63
  35.3 6.5 %collective-permute-start.13 = (bf16[2,128,128]{2,1,0:T(8,128)(2,1)S(1)}, bf16[2,128,128]{2,1,0:T(8,128)(2,1)S(1)}, u32[]{:S(2)}, u32[]{:S(2)}) collective-permute-start(bf16[2,128,128]{2,1,0:T(8,128)(2,1)S(1)} %add.6.refs_0_), channel_id=1, source_target_pairs={{0,4},{1,5},{2,6},{3,7},{4,0},{5,1},{6,2},{7,3},{8,12},{9,13},{10,... | collective-permute-start | bytes 196616 | tf_op jit(solution)/shard_map/ppermute | solution.py:63
  36.8 5.2 %collective-permute-start.14 = (bf16[2,128,128]{2,1,0:T(8,128)(2,1)S(1)}, bf16[2,128,128]{2,1,0:T(8,128)(2,1)S(1)}, u32[]{:S(2)}, u32[]{:S(2)}) collective-permute-start(bf16[2,128,128]{2,1,0:T(8,128)(2,1)S(1)} %add.6.refs_0_), channel_id=1, source_target_pairs={{0,6},{1,7},{2,4},{3,5},{4,2},{5,3},{6,0},{7,1},{8,14},{9,15},{10,... | collective-permute-start | bytes 196616 | tf_op jit(solution)/shard_map/ppermute | solution.py:63
  38.8 5.9 %collective-permute-start.19 = (bf16[2,128,128]{2,1,0:T(8,128)(2,1)S(1)}, bf16[2,128,128]{2,1,0:T(8,128)(2,1)S(1)}, u32[]{:S(2)}, u32[]{:S(2)}) collective-permute-start(bf16[2,128,128]{2,1,0:T(8,128)(2,1)S(1)} %get-tuple-element.68), channel_id=1, source_target_pairs={{0,1},{1,0},{2,3},{3,2},{4,5},{5,4},{6,7},{7,6},{8,9},{9,8},{10,11... | collective-permute-start | bytes 196616 | tf_op jit(solution)/shard_map/ppermute | solution.py:63
  38.9 7.4 %collective-permute-start.16 = (bf16[2,8,128]{2,1,0:T(8,128)(2,1)S(1)}, bf16[2,8,128]{2,1,0:T(8,128)(2,1)S(1)}, u32[]{:S(2)}, u32[]{:S(2)}) collective-permute-start(bf16[2,8,128]{2,1,0:T(8,128)(2,1)S(1)} %get-tuple-element.65), channel_id=1, source_target_pairs={{0,8},{8,0},{16,24},{24,16},{1,9},{9,1},{17,25},{25,17},{2,10},{10... | collective-permute-start | bytes 12296 | tf_op jit(solution)/shard_map/ppermute | solution.py:63
  39.2 7.6 %collective-permute-start.17 = (bf16[2,8,128]{2,1,0:T(8,128)(2,1)S(1)}, bf16[2,8,128]{2,1,0:T(8,128)(2,1)S(1)}, u32[]{:S(2)}, u32[]{:S(2)}) collective-permute-start(bf16[2,8,128]{2,1,0:T(8,128)(2,1)S(1)} %get-tuple-element.66), channel_id=1, source_target_pairs={{0,16},{8,24},{16,0},{24,8},{1,17},{9,25},{17,1},{25,9},{2,18},{10... | collective-permute-start | bytes 12296 | tf_op jit(solution)/shard_map/ppermute | solution.py:63
  42.2 7.0 %collective-permute-start.15 = (bf16[2,128,128]{2,1,0:T(8,128)(2,1)S(1)}, bf16[2,128,128]{2,1,0:T(8,128)(2,1)S(1)}, u32[]{:S(2)}, u32[]{:S(2)}) collective-permute-start(bf16[2,128,128]{2,1,0:T(8,128)(2,1)S(1)} %get-tuple-element.63.half), channel_id=1, source_target_pairs={{0,1},{1,0},{2,3},{3,2},{4,5},{5,4},{6,7},{7,6},{8,9},{9,8},{10,11... | collective-permute-start | bytes 196616 | tf_op jit(solution)/shard_map/ppermute | solution.py:63
  42.3 6.9 %collective-permute-start.18 = (bf16[2,8,128]{2,1,0:T(8,128)(2,1)S(1)}, bf16[2,8,128]{2,1,0:T(8,128)(2,1)S(1)}, u32[]{:S(2)}, u32[]{:S(2)}) collective-permute-start(bf16[2,8,128]{2,1,0:T(8,128)(2,1)S(1)} %get-tuple-element.67), channel_id=1, source_target_pairs={{0,24},{8,16},{16,8},{24,0},{1,25},{9,17},{17,9},{25,1},{2,26},{10... | collective-permute-start | bytes 12296 | tf_op jit(solution)/shard_map/ppermute | solution.py:63
  44.7 4.5 %collective-permute-start.20 = (bf16[2,128,128]{2,1,0:T(8,128)(2,1)S(1)}, bf16[2,128,128]{2,1,0:T(8,128)(2,1)S(1)}, u32[]{:S(2)}, u32[]{:S(2)}) collective-permute-start(bf16[2,128,128]{2,1,0:T(8,128)(2,1)S(1)} %add.7.refs_4_), channel_id=1, source_target_pairs={{0,2},{1,3},{2,0},{3,1},{4,6},{5,7},{6,4},{7,5},{8,10},{9,11},{10,... | collective-permute-start | bytes 196616 | tf_op jit(solution)/shard_map/ppermute | solution.py:63
  46.3 5.0 %collective-permute-start.21 = (bf16[2,128,128]{2,1,0:T(8,128)(2,1)S(1)}, bf16[2,128,128]{2,1,0:T(8,128)(2,1)S(1)}, u32[]{:S(2)}, u32[]{:S(2)}) collective-permute-start(bf16[2,128,128]{2,1,0:T(8,128)(2,1)S(1)} %add.7.refs_4_), channel_id=1, source_target_pairs={{0,4},{1,5},{2,6},{3,7},{4,0},{5,1},{6,2},{7,3},{8,12},{9,13},{10,... | collective-permute-start | bytes 196616 | tf_op jit(solution)/shard_map/ppermute | solution.py:63
  46.8 5.2 %collective-permute-start.22 = (bf16[2,128,128]{2,1,0:T(8,128)(2,1)S(1)}, bf16[2,128,128]{2,1,0:T(8,128)(2,1)S(1)}, u32[]{:S(2)}, u32[]{:S(2)}) collective-permute-start(bf16[2,128,128]{2,1,0:T(8,128)(2,1)S(1)} %add.7.refs_4_), channel_id=1, source_target_pairs={{0,6},{1,7},{2,4},{3,5},{4,2},{5,3},{6,0},{7,1},{8,14},{9,15},{10,... | collective-permute-start | bytes 196616 | tf_op jit(solution)/shard_map/ppermute | solution.py:63
  52.0 0.7 %copy-start.2 = (s32[8]{0:T(128)S(1)}, s32[8]{0:T(128)}, u32[]{:S(2)}) copy-start(s32[8]{0:T(128)} %ids.3) | copy-start | bytes 100

commit v2 on v1

v2 whole, which is shorter than its diff:
```python
import functools
import math

import jax
import jax.numpy as jnp
from jax import lax
from jax.experimental import pallas as pl
from jax.experimental.pallas import tpu as pltpu
from jax.sharding import PartitionSpec as P

HEADS = 4
CAP = 20.0
SUB = 8

BF = jnp.bfloat16
F32 = jnp.float32
VMEM = pl.BlockSpec(memory_space=pltpu.VMEM)
HBM = pl.BlockSpec(memory_space=pltpu.HBM)
LIMIT = 24 * 1024 * 1024


def dot(a, b):
    return jnp.dot(a, b, preferred_element_type=F32)


def dot_nt(a, b):
    return lax.dot_general(a, b, (((1,), (1,)), ((), ())), preferred_element_type=F32)


def dot_tn(a, b):
    return lax.dot_general(a, b, (((0,), (0,)), ((), ())), preferred_element_type=F32)


def shape(dims, kind=BF):
    return jax.ShapeDtypeStruct(dims, kind)


def call(kernel, outs, operands, specs, scratch=(), micros=1.0, name=None):
    return pl.pallas_call(
        kernel,
        out_shape=outs,
        in_specs=specs,
        out_specs=jax.tree.map(lambda _: VMEM, outs),
        scratch_shapes=list(scratch),
        compiler_params=pltpu.CompilerParams(vmem_limit_bytes=LIMIT),
        cost_estimate=pl.CostEstimate(
            flops=int(micros * 10**9), bytes_accessed=int(micros * 2**21), transcendentals=0
        ),
        name=name,
    )(*operands)


def fetch(pairs, sems):
    copies = [pltpu.make_async_copy(a, b, sems.at[i]) for i, (a, b) in enumerate(pairs)]
    for copy in copies:
        copy.start()
    return copies


def swapped(x, axis, mask):
    count = lax.axis_size(axis)
    return lax.ppermute(x, axis, [(i, i ^ mask) for i in range(count)])


def hub_pick(ints, feats, out, ints_s, sems):
    copies = fetch([(ints, ints_s)], sems)
    layouts, nodes, _ = feats.shape
    hubs = out.shape[1]
    row = lax.broadcasted_iota(jnp.int32, (hubs, nodes), 0)
    col = lax.broadcasted_iota(jnp.int32, (hubs, nodes), 1)
    want = jnp.zeros((hubs, nodes), jnp.int32)
    copies[0].wait()
    for j in range(hubs):
        want = jnp.where(row == j, lax.rem(ints_s[j], nodes), want)
    hot = jnp.where(col == want, 1.0, 0.0).astype(BF)
    for l in range(layouts):
        out[l] = dot(hot, feats[l]).astype(BF)


def adjacency(first, ints, tiles, weight, feats, adj_t, summed, pre_self, ints_s, adj, sems):
    copies = fetch([(ints, ints_s)], sems)
    slots, tile, _ = tiles.shape
    layouts, nodes, _ = feats.shape
    adj[...] = jnp.zeros(adj.shape, F32)
    for l in range(layouts):
        pre_self[l] = dot(feats[l], weight[0])
    copies[0].wait()
    for t in range(slots):

        @pl.when(t < ints_s[first + 2 * slots])
        def _():
            at = pl.ds(pl.multiple_of(ints_s[first + t] * tile, tile), tile)
            block = tiles[t].astype(F32)
            col = ints_s[first + slots + t]
            for s in range(nodes // tile):

                @pl.when(col == s)
                def _():
                    adj[at, pl.ds(s * tile, tile)] += block

    dense = adj[...].astype(BF)
    wide = jnp.concatenate([feats[l] for l in range(layouts)], axis=1)
    summed[...] = dot(dense, wide)
    adj_t[...] = dense.T


def sage_out(*refs):
    pieces, (summed, pre_self, hub_t, weight, own, other, agg, pre, hub_all, ready) = refs[:-10], refs[-10:]
    layouts, nodes, width = pre_self.shape
    shares, groups, _, _ = ready.shape
    hubs = pieces[0].shape[1]
    slab = lax.axis_index("graph")
    for s, piece in enumerate(pieces):
        at = pl.ds(pl.multiple_of(lax.bitwise_xor(slab, s) * hubs, hubs), hubs)
        for l in range(layouts):
            hub_all[at, l * width : (l + 1) * width] = piece[l].astype(F32)
    total = summed[...] + dot_tn(hub_t[...], hub_all[...].astype(BF))
    acts = []
    for l in range(layouts):
        mine = total[:, l * width : (l + 1) * width].astype(BF)
        agg[l] = mine
        value = pre_self[l] + dot(mine, weight[1])
        pre[l] = value
        act = value / (1.0 + jnp.exp(-value))
        acts.append(act.reshape(shares, groups, SUB, width))
    ready[...] = jnp.concatenate(acts, axis=2).astype(BF)
    hand_out(ready, own, other)


def hand_out(ready, own, other):
    me = lax.axis_index("config")
    for s in range(own.shape[0]):
        own[s] = ready[lax.bitwise_xor(me, 2 * s)]
        other[s] = ready[lax.bitwise_xor(me, 2 * s + 1)]


def arrivals(own, other, received):
    found = [(0, own[0]), (1, other[0])]
    for s, both in enumerate(received):
        found.append((2 * s + 2, both[0]))
        found.append((2 * s + 3, both[1]))
    return found


def prepare(cot, attn, weight, feats, agg, pre, cot_g, gmix, slope, rows_t, w_back):
    layouts, _, width = cot.shape
    groups = cot_g.shape[0]
    for l in range(feats.shape[0]):
        value = pre[l]
        sig = 1.0 / (1.0 + jnp.exp(-value))
        slope[l] = sig * (1.0 + value * (1.0 - sig))
        at = slice(l * feats.shape[1], (l + 1) * feats.shape[1])
        rows_t[0:width, at] = feats[l].T
        rows_t[width : 2 * width, at] = agg[l].T
    w_back[:, 0:width] = weight[0].T
    w_back[:, width : 2 * width] = weight[1].T
    for p in range(groups // 2):
        block = cot[:, 2 * SUB * p : 2 * SUB * (p + 1), :].astype(F32)
        for h in range(2):
            rows = block[:, SUB * h : SUB * (h + 1), :].reshape(layouts * SUB, width).astype(BF)
            cot_g[2 * p + h] = rows
            gmix[2 * p + h] = dot_nt(rows, attn[3]).astype(BF)


def attend(*refs):
    (own, other), received = refs[:2], refs[2:-12]
    cot_g, gmix, attn, own_out, other_out, hid_out, mixed_t, grads_own, grads_other = refs[-12:-3]
    hidden, ready, grads = refs[-3:]
    me = lax.axis_index("config")
    groups, shares, depth, width = hidden.shape
    rows = shares * depth
    head = width // HEADS
    scale = 1.0 / math.sqrt(head)
    for mask, block in arrivals(own, other, received):
        hidden[:, lax.bitwise_xor(me, mask)] = block
    w_all = jnp.concatenate([attn[0], attn[1], attn[2]], axis=1)
    lane = lax.broadcasted_iota(jnp.int32, (rows, width), 1) // head
    r = lax.broadcasted_iota(jnp.int32, (rows, HEADS * rows), 0)
    c = lax.broadcasted_iota(jnp.int32, (rows, HEADS * rows), 1)
    same = (r % SUB) == (c % SUB)
    zero = jnp.zeros((rows, width), BF)
    gap = jnp.zeros((head, rows), BF)

    def by_head(x):
        return jnp.concatenate([jnp.where(lane == e, x, zero) for e in range(HEADS)], axis=0)

    flat = hidden[...].reshape(groups * rows, width)
    hid_out[...] = flat.reshape(groups, rows, width)
    qkv = dot(flat, w_all).astype(BF)
    inputs = []
    for g in range(groups):
        q, k, v = (qkv[g * rows : (g + 1) * rows, i * width : (i + 1) * width] for i in range(3))
        inputs.append((k, v, k.T, v.T, by_head(q), by_head(gmix[g])))
    products = [(dot_nt(k, qm), dot_nt(v, gm)) for k, v, _, _, qm, gm in inputs]
    weighted = []
    for scores, d_probs in products:
        t = jnp.tanh(scores * (scale / CAP))
        w = jnp.where(same, jnp.exp2(t * (CAP * math.log2(math.e))), 0.0)
        a = w * (1.0 / jnp.sum(w, axis=0, keepdims=True))
        z = a * d_probs
        zs = jnp.sum(z, axis=0, keepdims=True)
        weighted.append((a.astype(BF), ((z - a * zs) * (scale - scale * (t * t))).astype(BF)))
    d_all, mix_t = [], []
    for (k, v, k_t, v_t, qm, gm), (p, ds) in zip(inputs, weighted):
        mix, dq = [], []
        for e in range(HEADS):
            at, span = slice(e * head, (e + 1) * head), slice(e * rows, (e + 1) * rows)
            left = jnp.concatenate(
                [jnp.concatenate([v_t[at], gap], axis=1), jnp.concatenate([gap, k_t[at]], axis=1)], axis=0
            )
            both = dot(left, jnp.concatenate([p[:, span], ds[:, span]], axis=0))
            mix.append(both[:head])
            dq.append(both[head:])
        mix_t.append(jnp.concatenate(mix, axis=0).astype(BF))
        dq = jnp.concatenate(dq, axis=0).astype(BF).T
        d_all.append(jnp.concatenate([dq, dot(ds, qm).astype(BF), dot(p, gm).astype(BF)], axis=1))
    d_all = jnp.concatenate(d_all, axis=0)
    mix_t = jnp.concatenate(mix_t, axis=1)
    mixed_t[...] = mix_t
    cots = cot_g[...].reshape(groups * rows, width)
    back = (cots.astype(F32) + dot_nt(d_all, w_all)).astype(BF).reshape(groups, shares, depth, width)
    for g in range(groups):
        ready[:, g] = back[g]
    hand_out(ready, own_out, other_out)
    total = dot(flat.T, d_all)
    for i in range(3):
        grads[i] = total[:, i * width : (i + 1) * width].astype(BF)
    grads[3] = dot(mix_t, cots).astype(BF)
    core = lax.rem(me, 2)
    half = grads_own.shape[0]
    grads_own[...] = grads[pl.ds(core * half, half)]
    grads_other[...] = grads[pl.ds((1 - core) * half, half)]


def outputs(hidden, mixed_t, attn, out):
    groups, rows, width = hidden.shape
    layouts = rows // SUB
    projected = dot_tn(mixed_t[...], attn[3])
    for p in range(groups // 2):
        pair = []
        for g in (2 * p, 2 * p + 1):
            both = hidden[g].astype(F32) + projected[g * rows : (g + 1) * rows]
            pair.append(both.reshape(layouts, SUB, width))
        out[:, 2 * SUB * p : 2 * SUB * (p + 1), :] = jnp.concatenate(pair, axis=1).astype(BF)


def sage_back(*refs):
    (own, other), received = refs[:2], refs[2:-10]
    slope, rows_t, w_back, hub_t, wide, self_out, grads, hub_out, parts, hub_sum = refs[-10:]
    me = lax.axis_index("config")
    layouts, width = parts.shape[2], parts.shape[4]
    nodes = slope.shape[1]
    for mask, block in arrivals(own, other, received):
        parts[lax.bitwise_xor(me, mask)] = block[...].astype(F32).reshape(parts.shape[1:])
    grad_pre, grad_agg = [], []
    for l in range(layouts):
        gpre = (parts[:, :, l].reshape(nodes, width) * slope[l]).astype(BF)
        both = dot(gpre, w_back[...]).astype(BF)
        grad_pre.append(gpre)
        self_out[l] = both[:, 0:width]
        grad_agg.append(both[:, width : 2 * width])
    spread = jnp.concatenate(grad_agg, axis=1)
    wide[...] = spread
    hub_sum[...] = dot(hub_t[...], spread)
    slab = lax.axis_index("graph")
    ranks, _, hubs, _ = hub_out.shape
    for s in range(ranks):
        at = pl.ds(pl.multiple_of(lax.bitwise_xor(slab, s) * hubs, hubs), hubs)
        for l in range(layouts):
            hub_out[s, l] = hub_sum[at, l * width : (l + 1) * width].astype(BF)
    both = dot(rows_t[...], jnp.concatenate(grad_pre, axis=0))
    grads[0] = both[0:width].astype(BF)
    grads[1] = both[width : 2 * width].astype(BF)


def tile_back(adj_t, wide, grad_self, totals):
    back = dot(adj_t[...], wide[...])
    layouts, _, width = totals.shape
    for l in range(layouts):
        totals[l] = grad_self[l].astype(F32) + back[:, l * width : (l + 1) * width]


def finish(ints, totals, hub_own, hub_in, out, ints_s, rows, sems):
    copies = fetch([(ints, ints_s)], sems)
    layouts, nodes, _ = totals.shape
    hubs = hub_own.shape[-2]
    summed = [hub_own[0, l].astype(F32) + hub_in[0, l].astype(F32) for l in range(layouts)]
    rows[...] = totals[...]
    copies[0].wait()
    for l in range(layouts):
        for j in range(hubs):
            at = pl.ds(lax.rem(ints_s[j], nodes), 1)
            rows[l, at, :] += summed[l][j : j + 1, :]
    out[...] = rows[...].astype(BF)


def weights_out(scale, sage, sage_in, half, half_in, out):
    first = sage.shape[0]
    count = half.shape[0]
    core = lax.rem(lax.axis_index("config"), 2)
    out[0:first] = (sage[...].astype(F32) + sage_in[...].astype(F32)) * scale
    out[pl.ds(first + core * count, count)] = half[...].astype(F32) * scale
    out[pl.ds(first + (1 - core) * count, count)] = half_in[...].astype(F32) * scale


def exchange(own, other):
    other = swapped(other, "config", 1)
    received = [
        swapped(jnp.stack([own[s], other[s]]), "config", 2 * s) for s in range(1, own.shape[0])
    ]
    return (own, other, *received)


def local(
    features,
    cotangent,
    sage_weight,
    attn_weight,
    tile_vals,
    tile_dst,
    tile_src,
    tile_count,
    hub_ids,
    hub_weight,
):
    layout_dev, node_dev, width = features.shape
    ranks = lax.axis_size("graph")
    shares = lax.axis_size("config")
    chips = shares // 2
    share = node_dev // shares
    groups = share // SUB
    layouts = layout_dev * shares
    rows = layouts * SUB
    depth = layout_dev * SUB
    hub_dev = hub_ids.shape[0]
    hubs = hub_weight.shape[1]
    slab = (layout_dev, node_dev, width)
    spread = (node_dev, layout_dev * width)
    dma = pltpu.SemaphoreType.DMA
    ints = jnp.concatenate([hub_ids, tile_dst, tile_src, tile_count])
    ints_s = pltpu.SMEM(ints.shape, jnp.int32)
    hub_t = hub_weight.T

    mine = call(
        hub_pick,
        shape((layout_dev, hub_dev, width)),
        (ints, features),
        [VMEM] * 2,
        [ints_s, dma((1,))],
        name="hub_pick",
    )
    pieces = [mine] + [swapped(mine, "graph", s) for s in range(1, ranks)]

    adj_t, summed, pre_self = call(
        functools.partial(adjacency, hub_dev),
        (shape((node_dev, node_dev)), shape(spread, F32), shape(slab, F32)),
        (ints, tile_vals, sage_weight, features),
        [VMEM] * 4,
        [ints_s, pltpu.VMEM((node_dev, node_dev), F32), dma((1,))],
        name="adjacency",
    )

    own, other, agg, pre = call(
        sage_out,
        (
            shape((chips, groups, depth, width)),
            shape((chips, groups, depth, width)),
            shape(slab),
            shape(slab, F32),
        ),
        (*pieces, summed, pre_self, hub_t, sage_weight),
        [VMEM] * (ranks + 4),
        [pltpu.VMEM((hubs, layout_dev * width), F32), pltpu.VMEM((shares, groups, depth, width), BF)],
        name="sage_out",
    )
    hidden_in = exchange(own, other)

    cot_g, gmix, slope, rows_t, w_back = call(
        prepare,
        (
            shape((groups, rows, width)),
            shape((groups, rows, width)),
            shape(slab, F32),
            shape((2 * width, layout_dev * node_dev)),
            shape((width, 2 * width)),
        ),
        (cotangent, attn_weight, sage_weight, features, agg, pre),
        [VMEM] * 6,
        name="prepare",
    )

    half = (attn_weight.shape[0] // 2, width, width)
    own, other, hidden, mixed_t, grads_own, grads_other = call(
        attend,
        (
            shape((chips, groups, depth, width)),
            shape((chips, groups, depth, width)),
            shape((groups, rows, width)),
            shape((width, groups * rows)),
            shape(half),
            shape(half),
        ),
        (*hidden_in, cot_g, gmix, attn_weight),
        [VMEM] * (len(hidden_in) + 3),
        [
            pltpu.VMEM((groups, shares, depth, width), BF),
            pltpu.VMEM((shares, groups, depth, width), BF),
            pltpu.VMEM(attn_weight.shape, BF),
        ],
        micros=4.0,
        name="attend",
    )
    grad_in = exchange(own, other)
    masks = [1 << i for i in range(1, shares.bit_length() - 1)]
    half_sum = grads_own + swapped(grads_other, "config", 1)
    for mask in masks[:-1]:
        half_sum = half_sum + swapped(half_sum, "config", mask)

    output = call(
        outputs,
        shape((layouts, share, width)),
        (hidden, mixed_t, attn_weight),
        [VMEM] * 3,
        name="outputs",
    )

    wide, grad_self, sage_sum, hub_sum = call(
        sage_back,
        (
            shape(spread),
            shape(slab),
            shape(sage_weight.shape),
            shape((ranks, layout_dev, hub_dev, width)),
        ),
        (*grad_in, slope, rows_t, w_back, hub_t),
        [VMEM] * (len(grad_in) + 4),
        [
            pltpu.VMEM((shares, groups, layout_dev, SUB, width), F32),
            pltpu.VMEM((hubs, layout_dev * width), F32),
        ],
        name="sage_back",
    )
    while hub_sum.shape[0] > 2:
        keep = hub_sum.shape[0] // 2
        hub_sum = hub_sum[:keep] + swapped(hub_sum[keep:], "graph", keep)
    hub_in = swapped(hub_sum[1:], "graph", 1)

    sage_sum = sage_sum + swapped(sage_sum, "config", 1)
    first = sage_sum.shape[0]
    both = jnp.concatenate([sage_sum, half_sum], axis=0)
    both = both + swapped(both, "config", masks[-1])
    sage_sum, half_sum = both[:first], both[first:]
    half_in = swapped(half_sum, "config", 1)
    for mask in masks[:-2]:
        sage_sum = sage_sum + swapped(sage_sum, "config", mask)
    sage_in = swapped(sage_sum, "config", masks[-2])

    totals = call(
        tile_back,
        shape(slab, F32),
        (adj_t, wide, grad_self),
        [VMEM] * 3,
        name="tile_back",
    )
    grad_features = call(
        finish,
        shape(slab),
        (ints, totals, hub_sum, hub_in),
        [VMEM] * 4,
        [ints_s, pltpu.VMEM(slab, F32), dma((1,))],
        name="finish",
    )
    weights = call(
        functools.partial(weights_out, 1.0 / math.sqrt(layouts * node_dev)),
        shape((first + attn_weight.shape[0], width, width), F32),
        (sage_sum, sage_in, half_sum, half_in),
        [VMEM] * 4,
        name="weights_out",
    )
    return (output, grad_features, weights[None])


def solution(mesh):
    return jax.shard_map(
        local,
        mesh=mesh,
        in_specs=(
            P("config", "graph", None),
            P(None, ("graph", "config"), None),
            P(),
            P(),
            P("graph", None, None),
            P("graph"),
            P("graph"),
            P("graph"),
            P("graph"),
            P("graph", None),
        ),
        out_specs=(
            P(None, ("graph", "config"), None),
            P("config", "graph", None),
            P("graph", None, None, None),
        ),
        check_vma=False,
    )
```

time: 54.1 us -> 50.5 us (0.933)
  waiting for transfers between devices: 9.63 us -> 18.9 us
  starting transfers between devices: 26 us -> 18.8 us
  Pallas kernels: 12.8 us -> 9.8 us
  local copies, waits for them, and re-layouts: 3.93 us -> 1.05 us
    ppermute x23 -> x19, waiting for transfers between devices: 9.63 us -> 18.9 us  [swapped(): return lax.ppermute(x, axis, [(i, i ^ mask) for i in range(count)])]
    ppermute x23 -> x19, starting transfers between devices: 26 us -> 18.8 us  [swapped(): return lax.ppermute(x, axis, [(i, i ^ mask) for i in range(count)])]
    pallas_call x9 -> x10, Pallas kernels: 12.8 us -> 9.8 us  [call(): pl.pallas_call(kernel, out_shape=outs, in_specs=specs, out_specs=jax.tree...]
    unnamed x20, local copies, waits for them, and re-layouts: 3.9 us -> 1 us
  transfers between devices with their start and end apart: 23 -> 19, of which waited for: 10 -> 12; matrix products, arithmetic and copies ran while one was open for 0% -> 0% of each run, Pallas kernels for 8% -> 9%
where the time goes in v2:
time: 50.5 us; the launch traced here: 50.3 us
  waiting for transfers between devices  18.9 us (37%)
  starting transfers between devices  18.8 us (37%)
  Pallas kernels  9.8 us (19%)
  between operations  1.57 us (3%)
  local copies, waits for them, and re-layouts  1.05 us (2%)
    ppermute x19, waiting for transfers between devices, swapped(): return lax.ppermute(x, axis, [(i, i ^ mask) for i in range(count)])  18.9 us
    ppermute x19, starting transfers between devices, swapped(): return lax.ppermute(x, axis, [(i, i ^ mask) for i in range(count)])  18.8 us
    pallas_call x10, Pallas kernels, call(): pl.pallas_call(kernel, out_shape=outs, in_specs=specs, out_specs=jax.tree...  9.8 us
  transfers between devices with their start and end apart: 19, of which 12 were waited for; matrix products, arithmetic and copies ran while one was open for 0% of the time, Pallas kernels for 9%

profile of v2, /device:TPU:0, one launch (start us, length us, event | category | flops | bytes accessed | tf_op | source)
XLA Modules:
  0.0 50.3 jit_solution(7460473379253950831)
XLA Ops:
  1.4 0.1 pad_add_fusion.ints
  1.4 0.9 %copy-done.1 = bf16[2,512,128]{2,1,0:T(8,128)(2,1)S(1)} copy-done((bf16[2,512,128]{2,1,0:T(8,128)(2,1)S(1)}, bf16[2,512,128]{2,1,0:T(8,128)(2,1)}, u32[]{:S(2)}) %copy-start.1) | copy-done | bytes 262168
  2.4 0.7 %hub_pick.1.refs_0_ = bf16[2,8,128]{2,1,0:T(8,128)(2,1)S(1)} custom-call(s32[33]{0:T(128)S(1)} %pad_add_fusion.ints, bf16[2,512,128]{2,1,0:T(8,128)(2,1)S(1)} %copy-done.1), custom_call_target="tpu_custom_call" | custom-call | flops 1000000000 | bytes 2097152 | tf_op jit(solution)/shard_map/hub_pick/pallas_call | solution.py:39
  3.1 0.0 copy-start.6
  3.1 5.1 %collective-permute-start.2 = (bf16[2,8,128]{2,1,0:T(8,128)(2,1)S(1)}, bf16[2,8,128]{2,1,0:T(8,128)(2,1)S(1)}, u32[]{:S(2)}, u32[]{:S(2)}) collective-permute-start(bf16[2,8,128]{2,1,0:T(8,128)(2,1)S(1)} %hub_pick.1.refs_0_), channel_id=1, source_target_pairs={{0,24},{8,16},{16,8},{24,0},{1,25},{9,17},{17,9},{25,1},{2,26},{10... | collective-permute-start | bytes 12296 | tf_op jit(solution)/shard_map/ppermute | solution.py:62
  8.2 0.0 collective-permute-start.1
  8.2 0.6 %collective-permute-start = (bf16[2,8,128]{2,1,0:T(8,128)(2,1)S(1)}, bf16[2,8,128]{2,1,0:T(8,128)(2,1)S(1)}, u32[]{:S(2)}, u32[]{:S(2)}) collective-permute-start(bf16[2,8,128]{2,1,0:T(8,128)(2,1)S(1)} %hub_pick.1.refs_0_), channel_id=1, source_target_pairs={{0,8},{8,0},{16,24},{24,16},{1,9},{9,1},{17,25},{25,17},{2,10},{10... | collective-permute-start | bytes 12296 | tf_op jit(solution)/shard_map/ppermute | solution.py:62
  8.9 1.3 %adjacency.1 = (bf16[512,512]{1,0:T(8,128)(2,1)S(1)}, f32[512,256]{1,0:T(8,128)S(1)}, f32[2,512,128]{2,1,0:T(8,128)S(1)}) custom-call(s32[33]{0:T(128)S(1)} %pad_add_fusion.ints, bf16[12,128,128]{2,1,0:T(8,128)(2,1)S(1)} %copy-done, bf16[2,128,128]{2,1,0:T(8,128)(2,1)S(1)} %copy-done.5, bf16[2,512,128]{2,1,0:T(8,128)(2,1)S(1)} %copy-done.1), custom_call_target="tpu_custom_call" | custom-call | flops 1000000000 | bytes 2097152 | tf_op jit(solution)/shard_map/adjacency/pallas_call | solution.py:39
  10.2 0.0 collective-permute-done.2.refs_3_
  10.2 2.5 %collective-permute-done.1.refs_2_ = bf16[2,8,128]{2,1,0:T(8,128)(2,1)S(1)} collective-permute-done((bf16[2,8,128]{2,1,0:T(8,128)(2,1)S(1)}, bf16[2,8,128]{2,1,0:T(8,128)(2,1)S(1)}, u32[]{:S(2)}, u32[]{:S(2)}) %collective-permute-start.1) | collective-permute-done | bytes 4128 | tf_op jit(solution)/shard_map/ppermute | solution.py:62
  12.7 0.0 collective-permute-done.refs_1_
  12.7 0.5 %sage_out.1 = (bf16[4,8,16,128]{3,2,1,0:T(8,128)(2,1)S(1)}, bf16[4,8,16,128]{3,2,1,0:T(8,128)(2,1)S(1)}, bf16[2,512,128]{2,1,0:T(8,128)(2,1)S(1)}, f32[2,512,128]{2,1,0:T(8,128)S(1)}) custom-call(bf16[2,8,128]{2,1,0:T(8,128)(2,1)S(1)} %hub_pick.1.refs_0_, bf16[2,8,128]{2,1,0:T(8,128)(2,1)S(1)} %collective-permute-done.refs_1_, ...), custom_call_target="tpu_custom_call" | custom-call | flops 1000000000 | bytes 2097152 | tf_op jit(solution)/shard_map/sage_out/pallas_call | solution.py:39
  13.3 0.1 collective-permute-start.3
  13.4 0.0 copy-start.4
  13.4 0.0 copy-start.2
  13.4 0.0 copy-start.3
  13.4 1.3 %collective-permute-done.3.refs_1_ = bf16[4,8,16,128]{3,2,1,0:T(8,128)(2,1)S(1)} collective-permute-done((bf16[4,8,16,128]{3,2,1,0:T(8,128)(2,1)S(1)}, bf16[4,8,16,128]{3,2,1,0:T(8,128)(2,1)S(1)}, u32[]{:S(2)}, u32[]{:S(2)}) %collective-permute-start.3) | collective-permute-done | bytes 131104 | tf_op jit(solution)/shard_map/ppermute | solution.py:62
  14.7 1.6 %collective-permute-start.4 = (bf16[2,8,16,128]{3,2,1,0:T(8,128)(2,1)S(1)}, bf16[2,8,16,128]{3,2,1,0:T(8,128)(2,1)S(1)}, u32[]{:S(2)}, u32[]{:S(2)}) collective-permute-start(bf16[2,8,16,128]{3,2,1,0:T(8,128)(2,1)S(1)} %pad_maximum_fusion.1), channel_id=1, source_target_pairs={{0,2},{1,3},{2,0},{3,1},{4,6},{5,7},{6,4},{7,5},{8,10},{9,11},{10,... | collective-permute-start | bytes 196616 | tf_op jit(solution)/shard_map/ppermute | solution.py:62
  16.3 1.6 %collective-permute-start.5 = (bf16[2,8,16,128]{3,2,1,0:T(8,128)(2,1)S(1)}, bf16[2,8,16,128]{3,2,1,0:T(8,128)(2,1)S(1)}, u32[]{:S(2)}, u32[]{:S(2)}) collective-permute-start(bf16[2,8,16,128]{3,2,1,0:T(8,128)(2,1)S(1)} %pad_maximum_fusion.2), channel_id=1, source_target_pairs={{0,4},{1,5},{2,6},{3,7},{4,0},{5,1},{6,2},{7,3},{8,12},{9,13},{10,... | collective-permute-start | bytes 196616 | tf_op jit(solution)/shard_map/ppermute | solution.py:62
  17.9 0.5 %collective-permute-start.6 = (bf16[2,8,16,128]{3,2,1,0:T(8,128)(2,1)S(1)}, bf16[2,8,16,128]{3,2,1,0:T(8,128)(2,1)S(1)}, u32[]{:S(2)}, u32[]{:S(2)}) collective-permute-start(bf16[2,8,16,128]{3,2,1,0:T(8,128)(2,1)S(1)} %pad_maximum_fusion.3), channel_id=1, source_target_pairs={{0,6},{1,7},{2,4},{3,5},{4,2},{5,3},{6,0},{7,1},{8,14},{9,15},{10,... | collective-permute-start | bytes 196616 | tf_op jit(solution)/shard_map/ppermute | solution.py:62
  18.4 0.5 prepare.1
  18.9 0.2 collective-permute-done.4.refs_2_
  19.1 1.6 %collective-permute-done.5.refs_3_ = bf16[2,8,16,128]{3,2,1,0:T(8,128)(2,1)S(1)} collective-permute-done((bf16[2,8,16,128]{3,2,1,0:T(8,128)(2,1)S(1)}, bf16[2,8,16,128]{3,2,1,0:T(8,128)(2,1)S(1)}, u32[]{:S(2)}, u32[]{:S(2)}) %collective-permute-start.5) | collective-permute-done | bytes 65568 | tf_op jit(solution)/shard_map/ppermute | solution.py:62
  20.6 2.5 %collective-permute-done.6.refs_4_ = bf16[2,8,16,128]{3,2,1,0:T(8,128)(2,1)S(1)} collective-permute-done((bf16[2,8,16,128]{3,2,1,0:T(8,128)(2,1)S(1)}, bf16[2,8,16,128]{3,2,1,0:T(8,128)(2,1)S(1)}, u32[]{:S(2)}, u32[]{:S(2)}) %collective-permute-start.6) | collective-permute-done | bytes 65568 | tf_op jit(solution)/shard_map/ppermute | solution.py:62
  23.1 2.8 %attend.1 = (bf16[4,8,16,128]{3,2,1,0:T(8,128)(2,1)S(1)}, bf16[4,8,16,128]{3,2,1,0:T(8,128)(2,1)S(1)}, bf16[8,128,128]{2,1,0:T(8,128)(2,1)S(1)}, bf16[128,1024]{...) custom-call(bf16[4,8,16,128]{3,2,1,0:T(8,128)(2,1)S(1)} %get-tuple-element.27.refs_0_, ...), custom_call_target="tpu_custom_call" | custom-call | flops 4000000000 | bytes 8388608 | tf_op jit(solution)/shard_map/attend/pallas_call | solution.py:39
  25.9 0.1 collective-permute-start.14
  26.0 0.5 collective-permute-start.7
  26.5 0.7 %collective-permute-done.14 = bf16[2,128,128]{2,1,0:T(8,128)(2,1)S(1)} collective-permute-done((bf16[2,128,128]{2,1,0:T(8,128)(2,1)S(1)}, bf16[2,128,128]{2,1,0:T(8,128)(2,1)S(1)}, u32[]{:S(2)}, u32[]{:S(2)}) %collective-permute-start.14) | collective-permute-done | bytes 65568 | tf_op jit(solution)/shard_map/ppermute | solution.py:62
  27.3 0.6 %collective-permute-start.15 = (bf16[2,128,128]{2,1,0:T(8,128)(2,1)S(1)}, bf16[2,128,128]{2,1,0:T(8,128)(2,1)S(1)}, u32[]{:S(2)}, u32[]{:S(2)}) collective-permute-start(bf16[2,128,128]{2,1,0:T(8,128)(2,1)S(1)} %add.17), channel_id=1, source_target_pairs={{0,2},{1,3},{2,0},{3,1},{4,6},{5,7},{6,4},{7,5},{8,10},{9,11},{10,... | collective-permute-start | bytes 196616 | tf_op jit(solution)/shard_map/ppermute | solution.py:62
  27.9 1.6 %collective-permute-start.8 = (bf16[2,8,16,128]{3,2,1,0:T(8,128)(2,1)S(1)}, bf16[2,8,16,128]{3,2,1,0:T(8,128)(2,1)S(1)}, u32[]{:S(2)}, u32[]{:S(2)}) collective-permute-start(bf16[2,8,16,128]{3,2,1,0:T(8,128)(2,1)S(1)} %pad_maximum_fusion.4), channel_id=1, source_target_pairs={{0,2},{1,3},{2,0},{3,1},{4,6},{5,7},{6,4},{7,5},{8,10},{9,11},{10,... | collective-permute-start | bytes 196616 | tf_op jit(solution)/shard_map/ppermute | solution.py:62
  29.5 0.6 %collective-permute-start.9 = (bf16[2,8,16,128]{3,2,1,0:T(8,128)(2,1)S(1)}, bf16[2,8,16,128]{3,2,1,0:T(8,128)(2,1)S(1)}, u32[]{:S(2)}, u32[]{:S(2)}) collective-permute-start(bf16[2,8,16,128]{3,2,1,0:T(8,128)(2,1)S(1)} %pad_maximum_fusion.5), channel_id=1, source_target_pairs={{0,4},{1,5},{2,6},{3,7},{4,0},{5,1},{6,2},{7,3},{8,12},{9,13},{10,... | collective-permute-start | bytes 196616 | tf_op jit(solution)/shard_map/ppermute | solution.py:62
  30.1 1.5 %collective-permute-start.10 = (bf16[2,8,16,128]{3,2,1,0:T(8,128)(2,1)S(1)}, bf16[2,8,16,128]{3,2,1,0:T(8,128)(2,1)S(1)}, u32[]{:S(2)}, u32[]{:S(2)}) collective-permute-start(bf16[2,8,16,128]{3,2,1,0:T(8,128)(2,1)S(1)} %pad_maximum_fusion.6), channel_id=1, source_target_pairs={{0,6},{1,7},{2,4},{3,5},{4,2},{5,3},{6,0},{7,1},{8,14},{9,15},{10,... | collective-permute-start | bytes 196616 | tf_op jit(solution)/shard_map/ppermute | solution.py:62
  31.6 1.0 %outputs.1 = bf16[16,64,128]{2,1,0:T(8,128)(2,1)} custom-call(bf16[8,128,128]{2,1,0:T(8,128)(2,1)S(1)} %get-tuple-element.33.hidden, bf16[128,1024]{1,0:T(8,128)(2,1)S(1)} %get-tuple-element.34.mixed_t, bf16[4,128,128]{2,1,0:T(8,128)(2,1)S(1)} %copy-done.4), custom_call_target="tpu_custom_call" | custom-call | flops 1000000000 | bytes 2097152 | tf_op jit(solution)/shard_map/outputs/pallas_call | solution.py:39
  32.6 0.3 collective-permute-done.8.refs_2_
  32.9 1.4 %collective-permute-done.9.refs_3_ = bf16[2,8,16,128]{3,2,1,0:T(8,128)(2,1)S(1)} collective-permute-done((bf16[2,8,16,128]{3,2,1,0:T(8,128)(2,1)S(1)}, bf16[2,8,16,128]{3,2,1,0:T(8,128)(2,1)S(1)}, u32[]{:S(2)}, u32[]{:S(2)}) %collective-permute-start.9) | collective-permute-done | bytes 65568 | tf_op jit(solution)/shard_map/ppermute | solution.py:62
  34.3 0.9 %collective-permute-done.10.refs_4_ = bf16[2,8,16,128]{3,2,1,0:T(8,128)(2,1)S(1)} collective-permute-done((bf16[2,8,16,128]{3,2,1,0:T(8,128)(2,1)S(1)}, bf16[2,8,16,128]{3,2,1,0:T(8,128)(2,1)S(1)}, u32[]{:S(2)}, u32[]{:S(2)}) %collective-permute-start.10) | collective-permute-done | bytes 65568 | tf_op jit(solution)/shard_map/ppermute | solution.py:62
  35.3 0.6 %sage_back.1 = (bf16[512,256]{1,0:T(8,128)(2,1)S(1)}, bf16[2,512,128]{2,1,0:T(8,128)(2,1)S(1)}, bf16[2,128,128]{2,1,0:T(8,128)(2,1)S(1)}, bf16[4,2,8,128]{3,2,1,0:T(8,128)(2,1)S(1)}) custom-call(bf16[4,8,16,128]{3,2,1,0:T(8,128)(2,1)S(1)} %get-tuple-element.36.refs_0_, bf16[4,8,16,128]{3,2,1,0:T(8,128)(2,1)S(1)} %collective-permute-done.7.refs_1_, ...), custom_call_target="tpu_custom_call" | custom-call | flops 1000000000 | bytes 2097152 | tf_op jit(solution)/shard_map/sage_back/pallas_call | solution.py:39
  35.9 2.1 %collective-permute-start.11 = (bf16[2,2,8,128]{3,2,1,0:T(8,128)(2,1)S(1)}, bf16[2,2,8,128]{3,2,1,0:T(8,128)(2,1)S(1)}, u32[]{:S(2)}, u32[]{:S(2)}) collective-permute-start(bf16[2,2,8,128]{3,2,1,0:T(8,128)(2,1)S(1)} %slice.64), channel_id=1, source_target_pairs={{0,16},{8,24},{16,0},{24,8},{1,17},{9,25},{17,1},{25,9},{2,18},{10... | collective-permute-start | bytes 24584 | tf_op jit(solution)/shard_map/ppermute | solution.py:62
  38.0 0.3 tile_back.1.totals
  38.3 0.9 %collective-permute-done.13 = bf16[2,128,128]{2,1,0:T(8,128)(2,1)S(1)} collective-permute-done((bf16[2,128,128]{2,1,0:T(8,128)(2,1)S(1)}, bf16[2,128,128]{2,1,0:T(8,128)(2,1)S(1)}, u32[]{:S(2)}, u32[]{:S(2)}) %collective-permute-start.13) | collective-permute-done | bytes 65568 | tf_op jit(solution)/shard_map/ppermute | solution.py:62
  39.3 1.6 %collective-permute-start.16 = (bf16[4,128,128]{2,1,0:T(8,128)(2,1)S(1)}, bf16[4,128,128]{2,1,0:T(8,128)(2,1)S(1)}, u32[]{:S(2)}, u32[]{:S(2)}) collective-permute-start(bf16[4,128,128]{2,1,0:T(8,128)(2,1)S(1)} %pad_maximum_fusion), channel_id=1, source_target_pairs={{0,4},{1,5},{2,6},{3,7},{4,0},{5,1},{6,2},{7,3},{8,12},{9,13},{10,... | collective-permute-start | bytes 393224 | tf_op jit(solution)/shard_map/ppermute | solution.py:62
  40.9 0.1 collective-permute-start.12
  41.0 4.0 %collective-permute-done.16 = bf16[4,128,128]{2,1,0:T(8,128)(2,1)S(1)} collective-permute-done((bf16[4,128,128]{2,1,0:T(8,128)(2,1)S(1)}, bf16[4,128,128]{2,1,0:T(8,128)(2,1)S(1)}, u32[]{:S(2)}, u32[]{:S(2)}) %collective-permute-start.16) | collective-permute-done | bytes 131104 | tf_op jit(solution)/shard_map/ppermute | solution.py:62
  44.9 0.1 collective-permute-start.18
  45.0 0.6 %collective-permute-start.17 = (bf16[2,128,128]{2,1,0:T(8,128)(2,1)S(1)}, bf16[2,128,128]{2,1,0:T(8,128)(2,1)S(1)}, u32[]{:S(2)}, u32[]{:S(2)}) collective-permute-start(bf16[2,128,128]{2,1,0:T(8,128)(2,1)S(1)} %get-tuple-element.48.sage), channel_id=1, source_target_pairs={{0,2},{1,3},{2,0},{3,1},{4,6},{5,7},{6,4},{7,5},{8,10},{9,11},{10,... | collective-permute-start | bytes 196616 | tf_op jit(solution)/shard_map/ppermute | solution.py:62
  45.6 1.3 %finish.1 = bf16[2,512,128]{2,1,0:T(8,128)(2,1)} custom-call(s32[33]{0:T(128)S(1)} %pad_add_fusion.ints, f32[2,512,128]{2,1,0:T(8,128)S(1)} %tile_back.1.totals, bf16[2,2,8,128]{3,2,1,0:T(8,128)(2,1)S(1)} %slice_add_fusion.hub_own, bf16[1,2,8,128]{3,2,1,0:T(8,128)(2,1)S(1)} %collective-permute-done.12.hub_in), custom_call_target="tpu_custom_call" | custom-call | flops 1000000000 | bytes 2097152 | tf_op jit(solution)/shard_map/finish/pallas_call | solution.py:39
  47.0 2.6 %collective-permute-done.17.sage_in = bf16[2,128,128]{2,1,0:T(8,128)(2,1)S(1)} collective-permute-done((bf16[2,128,128]{2,1,0:T(8,128)(2,1)S(1)}, bf16[2,128,128]{2,1,0:T(8,128)(2,1)S(1)}, u32[]{:S(2)}, u32[]{:S(2)}) %collective-permute-start.17) | collective-permute-done | bytes 65568 | tf_op jit(solution)/shard_map/ppermute | solution.py:62
  49.5 0.8 %weights_out.1 = f32[6,128,128]{2,1,0:T(8,128)} custom-call(bf16[2,128,128]{2,1,0:T(8,128)(2,1)S(1)} %get-tuple-element.48.sage, bf16[2,128,128]{2,1,0:T(8,128)(2,1)S(1)} %collective-permute-done.17.sage_in, bf16[2,128,128]{2,1,0:T(8,128)(2,1)S(1)} %get-tuple-element.47.half, bf16[2,128,128]{2,1,0:T(8,128)(2,1)S(1)} %collective-permute-done.18.half_in), custom_call_target="tpu_custom_call" | custom-call | flops 1000000000 | bytes 2097152 | tf_op jit(solution)/shard_map/weights_out/pallas_call | solution.py:39
  (40 shorter events, 0.2 us)
Async XLA Ops:
  0.6 0.7 %copy-start.9 = (s32[8]{0:T(128)S(1)}, s32[8]{0:T(128)}, u32[]{:S(2)}) copy-start(s32[8]{0:T(128)} %param.18) | copy-start | bytes 100
  0.6 0.7 %copy-start.7 = (s32[12]{0:T(128)S(1)}, s32[12]{0:T(128)}, u32[]{:S(2)}) copy-start(s32[12]{0:T(128)} %param.16) | copy-start | bytes 148
  0.7 0.7 %copy-start.8 = (s32[12]{0:T(128)S(1)}, s32[12]{0:T(128)}, u32[]{:S(2)}) copy-start(s32[12]{0:T(128)} %param.15) | copy-start | bytes 148
  1.4 1.0 %copy-start.1 = (bf16[2,512,128]{2,1,0:T(8,128)(2,1)S(1)}, bf16[2,512,128]{2,1,0:T(8,128)(2,1)}, u32[]{:S(2)}) copy-start(bf16[2,512,128]{2,1,0:T(8,128)(2,1)} %feats.5) | copy-start | bytes 786436
  2.4 6.5 %copy-start = (bf16[12,128,128]{2,1,0:T(8,128)(2,1)S(1)}, bf16[12,128,128]{2,1,0:T(8,128)(2,1)}, u32[]{:S(2)}) copy-start(bf16[12,128,128]{2,1,0:T(8,128)(2,1)} %tiles.1) | copy-start | bytes 1179652
  2.4 6.5 %copy-start.5 = (bf16[2,128,128]{2,1,0:T(8,128)(2,1)S(1)}, bf16[2,128,128]{2,1,0:T(8,128)(2,1)}, u32[]{:S(2)}) copy-start(bf16[2,128,128]{2,1,0:T(8,128)(2,1)} %weight.3) | copy-start | bytes 196612
  3.1 9.6 %copy-start.6 = (bf16[512,32]{0,1:T(8,128)(2,1)S(1)}, bf16[512,32]{0,1:T(8,128)(2,1)}, u32[]{:S(2)}) copy-start(bf16[512,32]{0,1:T(8,128)(2,1)} %param.19) | copy-start | bytes 98308
  3.1 7.1 %collective-permute-start.2 = (bf16[2,8,128]{2,1,0:T(8,128)(2,1)S(1)}, bf16[2,8,128]{2,1,0:T(8,128)(2,1)S(1)}, u32[]{:S(2)}, u32[]{:S(2)}) collective-permute-start(bf16[2,8,128]{2,1,0:T(8,128)(2,1)S(1)} %hub_pick.1.refs_0_), channel_id=1, source_target_pairs={{0,24},{8,16},{16,8},{24,0},{1,25},{9,17},{17,9},{25,1},{2,26},{10... | collective-permute-start | bytes 12296 | tf_op jit(solution)/shard_map/ppermute | solution.py:62
  8.2 4.5 %collective-permute-start.1 = (bf16[2,8,128]{2,1,0:T(8,128)(2,1)S(1)}, bf16[2,8,128]{2,1,0:T(8,128)(2,1)S(1)}, u32[]{:S(2)}, u32[]{:S(2)}) collective-permute-start(bf16[2,8,128]{2,1,0:T(8,128)(2,1)S(1)} %hub_pick.1.refs_0_), channel_id=1, source_target_pairs={{0,16},{8,24},{16,0},{24,8},{1,17},{9,25},{17,1},{25,9},{2,18},{10... | collective-permute-start | bytes 12296 | tf_op jit(solution)/shard_map/ppermute | solution.py:62
  8.2 4.5 %collective-permute-start = (bf16[2,8,128]{2,1,0:T(8,128)(2,1)S(1)}, bf16[2,8,128]{2,1,0:T(8,128)(2,1)S(1)}, u32[]{:S(2)}, u32[]{:S(2)}) collective-permute-start(bf16[2,8,128]{2,1,0:T(8,128)(2,1)S(1)} %hub_pick.1.refs_0_), channel_id=1, source_target_pairs={{0,8},{8,0},{16,24},{24,16},{1,9},{9,1},{17,25},{25,17},{2,10},{10... | collective-permute-start | bytes 12296 | tf_op jit(solution)/shard_map/ppermute | solution.py:62
  13.3 1.4 %collective-permute-start.3 = (bf16[4,8,16,128]{3,2,1,0:T(8,128)(2,1)S(1)}, bf16[4,8,16,128]{3,2,1,0:T(8,128)(2,1)S(1)}, u32[]{:S(2)}, u32[]{:S(2)}) collective-permute-start(bf16[4,8,16,128]{3,2,1,0:T(8,128)(2,1)S(1)} %get-tuple-element.28), channel_id=1, source_target_pairs={{0,1},{1,0},{2,3},{3,2},{4,5},{5,4},{6,7},{7,6},{8,9},{9,8},{10,11... | collective-permute-start | bytes 393224 | tf_op jit(solution)/shard_map/ppermute | solution.py:62
  13.4 5.1 %copy-start.4 = (bf16[4,128,128]{2,1,0:T(8,128)(2,1)S(1)}, bf16[4,128,128]{2,1,0:T(8,128)(2,1)}, u32[]{:S(2)}) copy-start(bf16[4,128,128]{2,1,0:T(8,128)(2,1)} %attn.3) | copy-start | bytes 393220
  13.4 5.0 %copy-start.2 = (bf16[2,512,128]{2,1,0:T(8,128)(2,1)S(1)}, bf16[2,512,128]{2,1,0:T(8,128)(2,1)}, u32[]{:S(2)}) copy-start(bf16[2,512,128]{2,1,0:T(8,128)(2,1)} %feats.5) | copy-start | bytes 786436
  13.4 5.0 %copy-start.3 = (bf16[16,64,128]{2,1,0:T(8,128)(2,1)S(1)}, bf16[16,64,128]{2,1,0:T(8,128)(2,1)}, u32[]{:S(2)}) copy-start(bf16[16,64,128]{2,1,0:T(8,128)(2,1)} %cot.1) | copy-start | bytes 786436
  14.7 4.3 %collective-permute-start.4 = (bf16[2,8,16,128]{3,2,1,0:T(8,128)(2,1)S(1)}, bf16[2,8,16,128]{3,2,1,0:T(8,128)(2,1)S(1)}, u32[]{:S(2)}, u32[]{:S(2)}) collective-permute-start(bf16[2,8,16,128]{3,2,1,0:T(8,128)(2,1)S(1)} %pad_maximum_fusion.1), channel_id=1, source_target_pairs={{0,2},{1,3},{2,0},{3,1},{4,6},{5,7},{6,4},{7,5},{8,10},{9,11},{10,... | collective-permute-start | bytes 196616 | tf_op jit(solution)/shard_map/ppermute | solution.py:62
  16.3 4.3 %collective-permute-start.5 = (bf16[2,8,16,128]{3,2,1,0:T(8,128)(2,1)S(1)}, bf16[2,8,16,128]{3,2,1,0:T(8,128)(2,1)S(1)}, u32[]{:S(2)}, u32[]{:S(2)}) collective-permute-start(bf16[2,8,16,128]{3,2,1,0:T(8,128)(2,1)S(1)} %pad_maximum_fusion.2), channel_id=1, source_target_pairs={{0,4},{1,5},{2,6},{3,7},{4,0},{5,1},{6,2},{7,3},{8,12},{9,13},{10,... | collective-permute-start | bytes 196616 | tf_op jit(solution)/shard_map/ppermute | solution.py:62
  17.9 5.2 %collective-permute-start.6 = (bf16[2,8,16,128]{3,2,1,0:T(8,128)(2,1)S(1)}, bf16[2,8,16,128]{3,2,1,0:T(8,128)(2,1)S(1)}, u32[]{:S(2)}, u32[]{:S(2)}) collective-permute-start(bf16[2,8,16,128]{3,2,1,0:T(8,128)(2,1)S(1)} %pad_maximum_fusion.3), channel_id=1, source_target_pairs={{0,6},{1,7},{2,4},{3,5},{4,2},{5,3},{6,0},{7,1},{8,14},{9,15},{10,... | collective-permute-start | bytes 196616 | tf_op jit(solution)/shard_map/ppermute | solution.py:62
  25.9 1.3 %collective-permute-start.14 = (bf16[2,128,128]{2,1,0:T(8,128)(2,1)S(1)}, bf16[2,128,128]{2,1,0:T(8,128)(2,1)S(1)}, u32[]{:S(2)}, u32[]{:S(2)}) collective-permute-start(bf16[2,128,128]{2,1,0:T(8,128)(2,1)S(1)} %get-tuple-element.46), channel_id=1, source_target_pairs={{0,1},{1,0},{2,3},{3,2},{4,5},{5,4},{6,7},{7,6},{8,9},{9,8},{10,11... | collective-permute-start | bytes 196616 | tf_op jit(solution)/shard_map/ppermute | solution.py:62
  26.0 1.9 %collective-permute-start.7 = (bf16[4,8,16,128]{3,2,1,0:T(8,128)(2,1)S(1)}, bf16[4,8,16,128]{3,2,1,0:T(8,128)(2,1)S(1)}, u32[]{:S(2)}, u32[]{:S(2)}) collective-permute-start(bf16[4,8,16,128]{3,2,1,0:T(8,128)(2,1)S(1)} %get-tuple-element.37), channel_id=1, source_target_pairs={{0,1},{1,0},{2,3},{3,2},{4,5},{5,4},{6,7},{7,6},{8,9},{9,8},{10,11... | collective-permute-start | bytes 393224 | tf_op jit(solution)/shard_map/ppermute | solution.py:62
  27.3 5.3 %collective-permute-start.15 = (bf16[2,128,128]{2,1,0:T(8,128)(2,1)S(1)}, bf16[2,128,128]{2,1,0:T(8,128)(2,1)S(1)}, u32[]{:S(2)}, u32[]{:S(2)}) collective-permute-start(bf16[2,128,128]{2,1,0:T(8,128)(2,1)S(1)} %add.17), channel_id=1, source_target_pairs={{0,2},{1,3},{2,0},{3,1},{4,6},{5,7},{6,4},{7,5},{8,10},{9,11},{10,... | collective-permute-start | bytes 196616 | tf_op jit(solution)/shard_map/ppermute | solution.py:62
  27.9 5.0 %collective-permute-start.8 = (bf16[2,8,16,128]{3,2,1,0:T(8,128)(2,1)S(1)}, bf16[2,8,16,128]{3,2,1,0:T(8,128)(2,1)S(1)}, u32[]{:S(2)}, u32[]{:S(2)}) collective-permute-start(bf16[2,8,16,128]{3,2,1,0:T(8,128)(2,1)S(1)} %pad_maximum_fusion.4), channel_id=1, source_target_pairs={{0,2},{1,3},{2,0},{3,1},{4,6},{5,7},{6,4},{7,5},{8,10},{9,11},{10,... | collective-permute-start | bytes 196616 | tf_op jit(solution)/shard_map/ppermute | solution.py:62
  29.5 4.8 %collective-permute-start.9 = (bf16[2,8,16,128]{3,2,1,0:T(8,128)(2,1)S(1)}, bf16[2,8,16,128]{3,2,1,0:T(8,128)(2,1)S(1)}, u32[]{:S(2)}, u32[]{:S(2)}) collective-permute-start(bf16[2,8,16,128]{3,2,1,0:T(8,128)(2,1)S(1)} %pad_maximum_fusion.5), channel_id=1, source_target_pairs={{0,4},{1,5},{2,6},{3,7},{4,0},{5,1},{6,2},{7,3},{8,12},{9,13},{10,... | collective-permute-start | bytes 196616 | tf_op jit(solution)/shard_map/ppermute | solution.py:62
  30.1 5.2 %collective-permute-start.10 = (bf16[2,8,16,128]{3,2,1,0:T(8,128)(2,1)S(1)}, bf16[2,8,16,128]{3,2,1,0:T(8,128)(2,1)S(1)}, u32[]{:S(2)}, u32[]{:S(2)}) collective-permute-start(bf16[2,8,16,128]{3,2,1,0:T(8,128)(2,1)S(1)} %pad_maximum_fusion.6), channel_id=1, source_target_pairs={{0,6},{1,7},{2,4},{3,5},{4,2},{5,3},{6,0},{7,1},{8,14},{9,15},{10,... | collective-permute-start | bytes 196616 | tf_op jit(solution)/shard_map/ppermute | solution.py:62
  35.9 5.0 %collective-permute-start.11 = (bf16[2,2,8,128]{3,2,1,0:T(8,128)(2,1)S(1)}, bf16[2,2,8,128]{3,2,1,0:T(8,128)(2,1)S(1)}, u32[]{:S(2)}, u32[]{:S(2)}) collective-permute-start(bf16[2,2,8,128]{3,2,1,0:T(8,128)(2,1)S(1)} %slice.64), channel_id=1, source_target_pairs={{0,16},{8,24},{16,0},{24,8},{1,17},{9,25},{17,1},{25,9},{2,18},{10... | collective-permute-start | bytes 24584 | tf_op jit(solution)/shard_map/ppermute | solution.py:62
  38.0 1.3 %collective-permute-start.13 = (bf16[2,128,128]{2,1,0:T(8,128)(2,1)S(1)}, bf16[2,128,128]{2,1,0:T(8,128)(2,1)S(1)}, u32[]{:S(2)}, u32[]{:S(2)}) collective-permute-start(bf16[2,128,128]{2,1,0:T(8,128)(2,1)S(1)} %get-tuple-element.44), channel_id=1, source_target_pairs={{0,1},{1,0},{2,3},{3,2},{4,5},{5,4},{6,7},{7,6},{8,9},{9,8},{10,11... | collective-permute-start | bytes 196616 | tf_op jit(solution)/shard_map/ppermute | solution.py:62
  39.3 5.6 %collective-permute-start.16 = (bf16[4,128,128]{2,1,0:T(8,128)(2,1)S(1)}, bf16[4,128,128]{2,1,0:T(8,128)(2,1)S(1)}, u32[]{:S(2)}, u32[]{:S(2)}) collective-permute-start(bf16[4,128,128]{2,1,0:T(8,128)(2,1)S(1)} %pad_maximum_fusion), channel_id=1, source_target_pairs={{0,4},{1,5},{2,6},{3,7},{4,0},{5,1},{6,2},{7,3},{8,12},{9,13},{10,... | collective-permute-start | bytes 393224 | tf_op jit(solution)/shard_map/ppermute | solution.py:62
  40.9 4.8 %collective-permute-start.12 = (bf16[1,2,8,128]{3,2,1,0:T(8,128)(2,1)S(1)}, bf16[1,2,8,128]{3,2,1,0:T(8,128)(2,1)S(1)}, u32[]{:S(2)}, u32[]{:S(2)}) collective-permute-start(bf16[1,2,8,128]{3,2,1,0:T(8,128)(2,1)S(1)} %slice.74), channel_id=1, source_target_pairs={{0,8},{8,0},{16,24},{24,16},{1,9},{9,1},{17,25},{25,17},{2,10},{10... | collective-permute-start | bytes 12296 | tf_op jit(solution)/shard_map/ppermute | solution.py:62
  44.9 2.0 %collective-permute-start.18 = (bf16[2,128,128]{2,1,0:T(8,128)(2,1)S(1)}, bf16[2,128,128]{2,1,0:T(8,128)(2,1)S(1)}, u32[]{:S(2)}, u32[]{:S(2)}) collective-permute-start(bf16[2,128,128]{2,1,0:T(8,128)(2,1)S(1)} %get-tuple-element.47.half), channel_id=1, source_target_pairs={{0,1},{1,0},{2,3},{3,2},{4,5},{5,4},{6,7},{7,6},{8,9},{9,8},{10,11... | collective-permute-start | bytes 196616 | tf_op jit(solution)/shard_map/ppermute | solution.py:62
  45.0 4.5 %collective-permute-start.17 = (bf16[2,128,128]{2,1,0:T(8,128)(2,1)S(1)}, bf16[2,128,128]{2,1,0:T(8,128)(2,1)S(1)}, u32[]{:S(2)}, u32[]{:S(2)}) collective-permute-start(bf16[2,128,128]{2,1,0:T(8,128)(2,1)S(1)} %get-tuple-element.48.sage), channel_id=1, source_target_pairs={{0,2},{1,3},{2,0},{3,1},{4,6},{5,7},{6,4},{7,5},{8,10},{9,11},{10,... | collective-permute-start | bytes 196616 | tf_op jit(solution)/shard_map/ppermute | solution.py:62

commit v3 on v2

--- a/solution.py
+++ b/solution.py
@@ -17,6 +17,7 @@
 VMEM = pl.BlockSpec(memory_space=pltpu.VMEM)
 HBM = pl.BlockSpec(memory_space=pltpu.HBM)
 LIMIT = 24 * 1024 * 1024
+WHOLE = 56 * 1024 * 1024
 
 
 def dot(a, b):
@@ -35,14 +36,14 @@
     return jax.ShapeDtypeStruct(dims, kind)
 
 
-def call(kernel, outs, operands, specs, scratch=(), micros=1.0, name=None):
+def call(kernel, outs, operands, specs, scratch=(), micros=1.0, limit=LIMIT, name=None):
     return pl.pallas_call(
         kernel,
         out_shape=outs,
         in_specs=specs,
         out_specs=jax.tree.map(lambda _: VMEM, outs),
         scratch_shapes=list(scratch),
-        compiler_params=pltpu.CompilerParams(vmem_limit_bytes=LIMIT),
+        compiler_params=pltpu.CompilerParams(vmem_limit_bytes=limit),
         cost_estimate=pl.CostEstimate(
             flops=int(micros * 10**9), bytes_accessed=int(micros * 2**21), transcendentals=0
         ),
@@ -62,19 +63,20 @@
     return lax.ppermute(x, axis, [(i, i ^ mask) for i in range(count)])
 
 
-def hub_pick(ints, feats, out, ints_s, sems):
-    copies = fetch([(ints, ints_s)], sems)
+def hub_pick(ids, feats, out, ids_s, feats_v, sems):
     layouts, nodes, _ = feats.shape
+    copies = fetch([(ids, ids_s)] + [(feats.at[l], feats_v.at[l]) for l in range(layouts)], sems)
     hubs = out.shape[1]
     row = lax.broadcasted_iota(jnp.int32, (hubs, nodes), 0)
     col = lax.broadcasted_iota(jnp.int32, (hubs, nodes), 1)
     want = jnp.zeros((hubs, nodes), jnp.int32)
     copies[0].wait()
     for j in range(hubs):
-        want = jnp.where(row == j, lax.rem(ints_s[j], nodes), want)
+        want = jnp.where(row == j, lax.rem(ids_s[j], nodes), want)
     hot = jnp.where(col == want, 1.0, 0.0).astype(BF)
     for l in range(layouts):
-        out[l] = dot(hot, feats[l]).astype(BF)
+        copies[1 + l].wait()
+        out[l] = dot(hot, feats_v[l]).astype(BF)
 
 
 def adjacency(first, ints, tiles, weight, feats, adj_t, summed, pre_self, ints_s, adj, sems):
@@ -232,7 +234,8 @@
     grads_other[...] = grads[pl.ds((1 - core) * half, half)]
 
 
-def outputs(hidden, mixed_t, attn, out):
+def outputs(hidden, mixed_t, attn, mine, theirs, out, half):
+    half[...] = add(mine, theirs)
     groups, rows, width = hidden.shape
     layouts = rows // SUB
     projected = dot_tn(mixed_t[...], attn[3])
@@ -278,6 +281,15 @@
     layouts, _, width = totals.shape
     for l in range(layouts):
         totals[l] = grad_self[l].astype(F32) + back[:, l * width : (l + 1) * width]
+
+
+def add(a, b):
+    return (a[...].astype(F32) + b[...].astype(F32)).astype(BF)
+
+
+def join(sage, sage_in, half, half_in, sage_sum, half_sum):
+    sage_sum[...] = add(sage, sage_in)
+    half_sum[...] = add(half, half_in)
 
 
 def finish(ints, totals, hub_own, hub_in, out, ints_s, rows, sems):
@@ -344,9 +356,10 @@
     mine = call(
         hub_pick,
         shape((layout_dev, hub_dev, width)),
-        (ints, features),
-        [VMEM] * 2,
-        [ints_s, dma((1,))],
+        (hub_ids, features),
+        [HBM] * 2,
+        [pltpu.SMEM((hub_dev,), jnp.int32), pltpu.VMEM(slab, BF), dma((1 + layout_dev,))],
+        limit=WHOLE,
         name="hub_pick",
     )
     pieces = [mine] + [swapped(mine, "graph", s) for s in range(1, ranks)]
@@ -411,16 +424,11 @@
         name="attend",
     )
     grad_in = exchange(own, other)
-    masks = [1 << i for i in range(1, shares.bit_length() - 1)]
-    half_sum = grads_own + swapped(grads_other, "config", 1)
-    for mask in masks[:-1]:
-        half_sum = half_sum + swapped(half_sum, "config", mask)
-
-    output = call(
+    output, half_sum = call(
         outputs,
-        shape((layouts, share, width)),
-        (hidden, mixed_t, attn_weight),
-        [VMEM] * 3,
+        (shape((layouts, share, width)), shape(half)),
+        (hidden, mixed_t, attn_weight, grads_own, swapped(grads_other, "config", 1)),
+        [VMEM] * 5,
         name="outputs",
     )
 
@@ -445,15 +453,20 @@
         hub_sum = hub_sum[:keep] + swapped(hub_sum[keep:], "graph", keep)
     hub_in = swapped(hub_sum[1:], "graph", 1)
 
-    sage_sum = sage_sum + swapped(sage_sum, "config", 1)
-    first = sage_sum.shape[0]
-    both = jnp.concatenate([sage_sum, half_sum], axis=0)
-    both = both + swapped(both, "config", masks[-1])
-    sage_sum, half_sum = both[:first], both[first:]
-    half_in = swapped(half_sum, "config", 1)
-    for mask in masks[:-2]:
-        sage_sum = sage_sum + swapped(sage_sum, "config", mask)
-    sage_in = swapped(sage_sum, "config", masks[-2])
+    masks = [1 << i for i in range(1, shares.bit_length() - 1)]
+    half_in = swapped(half_sum, "config", masks[0])
+    sage_in = swapped(sage_sum, "config", 1)
+    for mask, later in zip(masks, masks[1:] + [1]):
+        sage_sum, half_sum = call(
+            join,
+            (shape(sage_weight.shape), shape(half)),
+            (sage_sum, sage_in, half_sum, half_in),
+            [VMEM] * 4,
+            micros=0.1,
+            name="join",
+        )
+        sage_in = swapped(sage_sum, "config", mask)
+        half_in = swapped(half_sum, "config", later)
 
     totals = call(
         tile_back,
@@ -472,7 +485,7 @@
     )
     weights = call(
         functools.partial(weights_out, 1.0 / math.sqrt(layouts * node_dev)),
-        shape((first + attn_weight.shape[0], width, width), F32),
+        shape((sage_weight.shape[0] + attn_weight.shape[0], width, width), F32),
         (sage_sum, sage_in, half_sum, half_in),
         [VMEM] * 4,
         name="weights_out",

time: 50.5 us -> 49.4 us (0.978)
  waiting for transfers between devices: 18.9 us -> 13.9 us
  starting transfers between devices: 18.8 us -> 22.7 us
  Pallas kernels: 9.8 us -> 10.8 us
  local copies, waits for them, and re-layouts: 1.05 us -> 0.09 us
    ppermute x19 -> x20, waiting for transfers between devices: 18.9 us -> 13.9 us  [swapped(): return lax.ppermute(x, axis, [(i, i ^ mask) for i in range(count)])]
    ppermute x19 -> x20, starting transfers between devices: 18.8 us -> 22.7 us  [swapped(): return lax.ppermute(x, axis, [(i, i ^ mask) for i in range(count)])]
    pallas_call x10 -> x12, Pallas kernels: 9.8 us -> 10.8 us  [call(): pl.pallas_call(kernel, out_shape=outs, in_specs=specs, out_specs=jax.tree...]
    unnamed x20, local copies, waits for them, and re-layouts: 1 us -> 0.05 us
  transfers between devices with their start and end apart: 19 -> 20, of which waited for: 12 -> 11; matrix products, arithmetic and copies ran while one was open for 0% -> 0% of each run, Pallas kernels for 9% -> 10%
where the time goes in v3:
time: 49.4 us; the launch traced here: 49.2 us
  starting transfers between devices  22.7 us (46%)
  waiting for transfers between devices  13.9 us (28%)
  Pallas kernels  10.8 us (22%)
  between operations  1.53 us (3%)
    ppermute x20, starting transfers between devices, swapped(): return lax.ppermute(x, axis, [(i, i ^ mask) for i in range(count)])  22.7 us
    ppermute x20, waiting for transfers between devices, swapped(): return lax.ppermute(x, axis, [(i, i ^ mask) for i in range(count)])  13.9 us
    pallas_call x12, Pallas kernels, call(): pl.pallas_call(kernel, out_shape=outs, in_specs=specs, out_specs=jax.tree...  10.8 us
  transfers between devices with their start and end apart: 20, of which 11 were waited for; matrix products, arithmetic and copies ran while one was open for 0% of the time, Pallas kernels for 10%

profile of v3, /device:TPU:0, one launch (start us, length us, event | category | flops | bytes accessed | tf_op | source)
XLA Modules:
  0.0 49.2 jit_solution(10168607631265798492)
XLA Ops:
  0.7 1.9 %hub_pick.1.refs_0_ = bf16[2,8,128]{2,1,0:T(8,128)(2,1)} custom-call(s32[8]{0:T(128)} %ids.1, bf16[2,512,128]{2,1,0:T(8,128)(2,1)} %feats.5), custom_call_target="tpu_custom_call" | custom-call | flops 1000000000 | bytes 2097152 | tf_op jit(solution)/shard_map/hub_pick/pallas_call | solution.py:40
  2.5 0.0 copy-start.7
  2.5 0.0 copy-start.8
  2.6 0.0 copy-start.9
  2.6 5.1 %collective-permute-start.2 = (bf16[2,8,128]{2,1,0:T(8,128)(2,1)}, bf16[2,8,128]{2,1,0:T(8,128)(2,1)S(1)}, u32[]{:S(2)}, u32[]{:S(2)}) collective-permute-start(bf16[2,8,128]{2,1,0:T(8,128)(2,1)} %hub_pick.1.refs_0_), channel_id=1, source_target_pairs={{0,24},{8,16},{16,8},{24,0},{1,25},{9,17},{17,9},{25,1},{2,26},{10... | collective-permute-start | bytes 12296 | tf_op jit(solution)/shard_map/ppermute | solution.py:63
  7.7 0.0 collective-permute-start.1
  7.7 0.6 %collective-permute-start = (bf16[2,8,128]{2,1,0:T(8,128)(2,1)}, bf16[2,8,128]{2,1,0:T(8,128)(2,1)S(1)}, u32[]{:S(2)}, u32[]{:S(2)}) collective-permute-start(bf16[2,8,128]{2,1,0:T(8,128)(2,1)} %hub_pick.1.refs_0_), channel_id=1, source_target_pairs={{0,8},{8,0},{16,24},{24,16},{1,9},{9,1},{17,25},{25,17},{2,10},{10... | collective-permute-start | bytes 12296 | tf_op jit(solution)/shard_map/ppermute | solution.py:63
  9.0 0.1 pad_add_fusion.ints
  9.1 0.0 copy-start.5
  9.1 1.1 %adjacency.1 = (bf16[512,512]{1,0:T(8,128)(2,1)S(1)}, f32[512,256]{1,0:T(8,128)S(1)}, f32[2,512,128]{2,1,0:T(8,128)S(1)}) custom-call(s32[33]{0:T(128)S(1)} %pad_add_fusion.ints, bf16[12,128,128]{2,1,0:T(8,128)(2,1)S(1)} %copy-done, bf16[2,128,128]{2,1,0:T(8,128)(2,1)S(1)} %copy-done.4, bf16[2,512,128]{2,1,0:T(8,128)(2,1)S(1)} %copy-done.1), custom_call_target="tpu_custom_call" | custom-call | flops 1000000000 | bytes 2097152 | tf_op jit(solution)/shard_map/adjacency/pallas_call | solution.py:40
  10.2 0.0 copy-start.6
  10.2 0.0 collective-permute-done.2.refs_3_
  10.2 2.2 %collective-permute-done.1.refs_2_ = bf16[2,8,128]{2,1,0:T(8,128)(2,1)S(1)} collective-permute-done((bf16[2,8,128]{2,1,0:T(8,128)(2,1)}, bf16[2,8,128]{2,1,0:T(8,128)(2,1)S(1)}, u32[]{:S(2)}, u32[]{:S(2)}) %collective-permute-start.1) | collective-permute-done | bytes 4128 | tf_op jit(solution)/shard_map/ppermute | solution.py:63
  12.4 0.5 %sage_out.1 = (bf16[4,8,16,128]{3,2,1,0:T(8,128)(2,1)S(1)}, bf16[4,8,16,128]{3,2,1,0:T(8,128)(2,1)S(1)}, bf16[2,512,128]{2,1,0:T(8,128)(2,1)S(1)}, f32[2,512,128]{2,1,0:T(8,128)S(1)}) custom-call(bf16[2,8,128]{2,1,0:T(8,128)(2,1)S(1)} %copy-done.6, bf16[2,8,128]{2,1,0:T(8,128)(2,1)S(1)} %collective-permute-done.refs_1_, ...), custom_call_target="tpu_custom_call" | custom-call | flops 1000000000 | bytes 2097152 | tf_op jit(solution)/shard_map/sage_out/pallas_call | solution.py:40
  12.9 0.1 collective-permute-start.3
  13.0 0.0 copy-start.2
  13.1 1.3 %collective-permute-done.3.refs_1_ = bf16[4,8,16,128]{3,2,1,0:T(8,128)(2,1)S(1)} collective-permute-done((bf16[4,8,16,128]{3,2,1,0:T(8,128)(2,1)S(1)}, bf16[4,8,16,128]{3,2,1,0:T(8,128)(2,1)S(1)}, u32[]{:S(2)}, u32[]{:S(2)}) %collective-permute-start.3) | collective-permute-done | bytes 131104 | tf_op jit(solution)/shard_map/ppermute | solution.py:63
  14.4 1.6 %collective-permute-start.4 = (bf16[2,8,16,128]{3,2,1,0:T(8,128)(2,1)S(1)}, bf16[2,8,16,128]{3,2,1,0:T(8,128)(2,1)S(1)}, u32[]{:S(2)}, u32[]{:S(2)}) collective-permute-start(bf16[2,8,16,128]{3,2,1,0:T(8,128)(2,1)S(1)} %pad_maximum_fusion), channel_id=1, source_target_pairs={{0,2},{1,3},{2,0},{3,1},{4,6},{5,7},{6,4},{7,5},{8,10},{9,11},{10,... | collective-permute-start | bytes 196616 | tf_op jit(solution)/shard_map/ppermute | solution.py:63
  16.0 1.6 %collective-permute-start.5 = (bf16[2,8,16,128]{3,2,1,0:T(8,128)(2,1)S(1)}, bf16[2,8,16,128]{3,2,1,0:T(8,128)(2,1)S(1)}, u32[]{:S(2)}, u32[]{:S(2)}) collective-permute-start(bf16[2,8,16,128]{3,2,1,0:T(8,128)(2,1)S(1)} %pad_maximum_fusion.1), channel_id=1, source_target_pairs={{0,4},{1,5},{2,6},{3,7},{4,0},{5,1},{6,2},{7,3},{8,12},{9,13},{10,... | collective-permute-start | bytes 196616 | tf_op jit(solution)/shard_map/ppermute | solution.py:63
  17.6 0.5 %collective-permute-start.6 = (bf16[2,8,16,128]{3,2,1,0:T(8,128)(2,1)S(1)}, bf16[2,8,16,128]{3,2,1,0:T(8,128)(2,1)S(1)}, u32[]{:S(2)}, u32[]{:S(2)}) collective-permute-start(bf16[2,8,16,128]{3,2,1,0:T(8,128)(2,1)S(1)} %pad_maximum_fusion.2), channel_id=1, source_target_pairs={{0,6},{1,7},{2,4},{3,5},{4,2},{5,3},{6,0},{7,1},{8,14},{9,15},{10,... | collective-permute-start | bytes 196616 | tf_op jit(solution)/shard_map/ppermute | solution.py:63
  18.1 0.5 prepare.1
  18.6 0.1 collective-permute-done.4.refs_2_
  18.7 1.6 %collective-permute-done.5.refs_3_ = bf16[2,8,16,128]{3,2,1,0:T(8,128)(2,1)S(1)} collective-permute-done((bf16[2,8,16,128]{3,2,1,0:T(8,128)(2,1)S(1)}, bf16[2,8,16,128]{3,2,1,0:T(8,128)(2,1)S(1)}, u32[]{:S(2)}, u32[]{:S(2)}) %collective-permute-start.5) | collective-permute-done | bytes 65568 | tf_op jit(solution)/shard_map/ppermute | solution.py:63
  20.3 2.5 %collective-permute-done.6.refs_4_ = bf16[2,8,16,128]{3,2,1,0:T(8,128)(2,1)S(1)} collective-permute-done((bf16[2,8,16,128]{3,2,1,0:T(8,128)(2,1)S(1)}, bf16[2,8,16,128]{3,2,1,0:T(8,128)(2,1)S(1)}, u32[]{:S(2)}, u32[]{:S(2)}) %collective-permute-start.6) | collective-permute-done | bytes 65568 | tf_op jit(solution)/shard_map/ppermute | solution.py:63
  22.8 2.8 %attend.1 = (bf16[4,8,16,128]{3,2,1,0:T(8,128)(2,1)S(1)}, bf16[4,8,16,128]{3,2,1,0:T(8,128)(2,1)S(1)}, bf16[8,128,128]{2,1,0:T(8,128)(2,1)S(1)}, bf16[128,1024]{...) custom-call(bf16[4,8,16,128]{3,2,1,0:T(8,128)(2,1)S(1)} %get-tuple-element.33.refs_0_, ...), custom_call_target="tpu_custom_call" | custom-call | flops 4000000000 | bytes 8388608 | tf_op jit(solution)/shard_map/attend/pallas_call | solution.py:40
  25.6 0.1 collective-permute-start.7
  25.7 0.5 %collective-permute-start.8 = (bf16[4,8,16,128]{3,2,1,0:T(8,128)(2,1)S(1)}, bf16[4,8,16,128]{3,2,1,0:T(8,128)(2,1)S(1)}, u32[]{:S(2)}, u32[]{:S(2)}) collective-permute-start(bf16[4,8,16,128]{3,2,1,0:T(8,128)(2,1)S(1)} %get-tuple-element.46), channel_id=1, source_target_pairs={{0,1},{1,0},{2,3},{3,2},{4,5},{5,4},{6,7},{7,6},{8,9},{9,8},{10,11... | collective-permute-start | bytes 393224 | tf_op jit(solution)/shard_map/ppermute | solution.py:63
  26.2 1.0 %collective-permute-done.8.refs_1_ = bf16[4,8,16,128]{3,2,1,0:T(8,128)(2,1)S(1)} collective-permute-done((bf16[4,8,16,128]{3,2,1,0:T(8,128)(2,1)S(1)}, bf16[4,8,16,128]{3,2,1,0:T(8,128)(2,1)S(1)}, u32[]{:S(2)}, u32[]{:S(2)}) %collective-permute-start.8) | collective-permute-done | bytes 131104 | tf_op jit(solution)/shard_map/ppermute | solution.py:63
  27.2 0.6 %collective-permute-start.9 = (bf16[2,8,16,128]{3,2,1,0:T(8,128)(2,1)S(1)}, bf16[2,8,16,128]{3,2,1,0:T(8,128)(2,1)S(1)}, u32[]{:S(2)}, u32[]{:S(2)}) collective-permute-start(bf16[2,8,16,128]{3,2,1,0:T(8,128)(2,1)S(1)} %pad_maximum_fusion.3), channel_id=1, source_target_pairs={{0,2},{1,3},{2,0},{3,1},{4,6},{5,7},{6,4},{7,5},{8,10},{9,11},{10,... | collective-permute-start | bytes 196616 | tf_op jit(solution)/shard_map/ppermute | solution.py:63
  27.8 0.6 %collective-permute-start.10 = (bf16[2,8,16,128]{3,2,1,0:T(8,128)(2,1)S(1)}, bf16[2,8,16,128]{3,2,1,0:T(8,128)(2,1)S(1)}, u32[]{:S(2)}, u32[]{:S(2)}) collective-permute-start(bf16[2,8,16,128]{3,2,1,0:T(8,128)(2,1)S(1)} %pad_maximum_fusion.4), channel_id=1, source_target_pairs={{0,4},{1,5},{2,6},{3,7},{4,0},{5,1},{6,2},{7,3},{8,12},{9,13},{10,... | collective-permute-start | bytes 196616 | tf_op jit(solution)/shard_map/ppermute | solution.py:63
  28.4 2.5 %collective-permute-start.11 = (bf16[2,8,16,128]{3,2,1,0:T(8,128)(2,1)S(1)}, bf16[2,8,16,128]{3,2,1,0:T(8,128)(2,1)S(1)}, u32[]{:S(2)}, u32[]{:S(2)}) collective-permute-start(bf16[2,8,16,128]{3,2,1,0:T(8,128)(2,1)S(1)} %pad_maximum_fusion.5), channel_id=1, source_target_pairs={{0,6},{1,7},{2,4},{3,5},{4,2},{5,3},{6,0},{7,1},{8,14},{9,15},{10,... | collective-permute-start | bytes 196616 | tf_op jit(solution)/shard_map/ppermute | solution.py:63
  30.9 0.0 collective-permute-done.7.theirs
  30.9 1.0 %outputs.1 = (bf16[16,64,128]{2,1,0:T(8,128)(2,1)}, bf16[2,128,128]{2,1,0:T(8,128)(2,1)S(1)}) custom-call(bf16[8,128,128]{2,1,0:T(8,128)(2,1)S(1)} %get-tuple-element.39.hidden, bf16[128,1024]{1,0:T(8,128)(2,1)S(1)} %get-tuple-element.40.mixed_t, bf16[4,128,128]{2,1,0:T(8,128)(2,1)S(1)} %copy-done.3, bf16[2,128,128]{2,1,0:T(8,128)(2,1)S(1)} %get-tuple-element.41.mine, ...), custom_call_target="tpu_custom_call" | custom-call | flops 1000000000 | bytes 2097152 | tf_op jit(solution)/shard_map/outputs/pallas_call | solution.py:40
  31.9 0.5 %collective-permute-start.15 = (bf16[2,128,128]{2,1,0:T(8,128)(2,1)S(1)}, bf16[2,128,128]{2,1,0:T(8,128)(2,1)S(1)}, u32[]{:S(2)}, u32[]{:S(2)}) collective-permute-start(bf16[2,128,128]{2,1,0:T(8,128)(2,1)S(1)} %get-tuple-element.54.half), channel_id=1, source_target_pairs={{0,2},{1,3},{2,0},{3,1},{4,6},{5,7},{6,4},{7,5},{8,10},{9,11},{10,... | collective-permute-start | bytes 196616 | tf_op jit(solution)/shard_map/ppermute | solution.py:63
  32.4 0.4 collective-permute-done.10.refs_3_
  32.9 0.8 %collective-permute-done.11.refs_4_ = bf16[2,8,16,128]{3,2,1,0:T(8,128)(2,1)S(1)} collective-permute-done((bf16[2,8,16,128]{3,2,1,0:T(8,128)(2,1)S(1)}, bf16[2,8,16,128]{3,2,1,0:T(8,128)(2,1)S(1)}, u32[]{:S(2)}, u32[]{:S(2)}) %collective-permute-start.11) | collective-permute-done | bytes 65568 | tf_op jit(solution)/shard_map/ppermute | solution.py:63
  33.6 0.6 %sage_back.1 = (bf16[512,256]{1,0:T(8,128)(2,1)S(1)}, bf16[2,512,128]{2,1,0:T(8,128)(2,1)S(1)}, bf16[2,128,128]{2,1,0:T(8,128)(2,1)S(1)}, bf16[4,2,8,128]{3,2,1,0:T(8,128)(2,1)S(1)}) custom-call(bf16[4,8,16,128]{3,2,1,0:T(8,128)(2,1)S(1)} %get-tuple-element.45.refs_0_, bf16[4,8,16,128]{3,2,1,0:T(8,128)(2,1)S(1)} %collective-permute-done.8.refs_1_, ...), custom_call_target="tpu_custom_call" | custom-call | flops 1000000000 | bytes 2097152 | tf_op jit(solution)/shard_map/sage_back/pallas_call | solution.py:40
  34.2 2.1 %collective-permute-start.12 = (bf16[2,2,8,128]{3,2,1,0:T(8,128)(2,1)S(1)}, bf16[2,2,8,128]{3,2,1,0:T(8,128)(2,1)S(1)}, u32[]{:S(2)}, u32[]{:S(2)}) collective-permute-start(bf16[2,2,8,128]{3,2,1,0:T(8,128)(2,1)S(1)} %slice.58), channel_id=1, source_target_pairs={{0,16},{8,24},{16,0},{24,8},{1,17},{9,25},{17,1},{25,9},{2,18},{10... | collective-permute-start | bytes 24584 | tf_op jit(solution)/shard_map/ppermute | solution.py:63
  36.3 0.3 tile_back.1.totals
  36.6 0.9 %collective-permute-done.14.sage_in = bf16[2,128,128]{2,1,0:T(8,128)(2,1)S(1)} collective-permute-done((bf16[2,128,128]{2,1,0:T(8,128)(2,1)S(1)}, bf16[2,128,128]{2,1,0:T(8,128)(2,1)S(1)}, u32[]{:S(2)}, u32[]{:S(2)}) %collective-permute-start.14) | collective-permute-done | bytes 65568 | tf_op jit(solution)/shard_map/ppermute | solution.py:63
  37.6 2.2 %collective-permute-start.16 = (bf16[2,128,128]{2,1,0:T(8,128)(2,1)S(1)}, bf16[2,128,128]{2,1,0:T(8,128)(2,1)S(1)}, u32[]{:S(2)}, u32[]{:S(2)}) collective-permute-start(bf16[2,128,128]{2,1,0:T(8,128)(2,1)S(1)} %get-tuple-element.55.sage), channel_id=1, source_target_pairs={{0,2},{1,3},{2,0},{3,1},{4,6},{5,7},{6,4},{7,5},{8,10},{9,11},{10,... | collective-permute-start | bytes 196616 | tf_op jit(solution)/shard_map/ppermute | solution.py:63
  39.8 1.5 %collective-permute-start.17 = (bf16[2,128,128]{2,1,0:T(8,128)(2,1)S(1)}, bf16[2,128,128]{2,1,0:T(8,128)(2,1)S(1)}, u32[]{:S(2)}, u32[]{:S(2)}) collective-permute-start(bf16[2,128,128]{2,1,0:T(8,128)(2,1)S(1)} %get-tuple-element.56.half), channel_id=1, source_target_pairs={{0,4},{1,5},{2,6},{3,7},{4,0},{5,1},{6,2},{7,3},{8,12},{9,13},{10,... | collective-permute-start | bytes 196616 | tf_op jit(solution)/shard_map/ppermute | solution.py:63
  41.3 1.0 %collective-permute-start.13 = (bf16[1,2,8,128]{3,2,1,0:T(8,128)(2,1)S(1)}, bf16[1,2,8,128]{3,2,1,0:T(8,128)(2,1)S(1)}, u32[]{:S(2)}, u32[]{:S(2)}) collective-permute-start(bf16[1,2,8,128]{3,2,1,0:T(8,128)(2,1)S(1)} %slice.66), channel_id=1, source_target_pairs={{0,8},{8,0},{16,24},{24,16},{1,9},{9,1},{17,25},{25,17},{2,10},{10... | collective-permute-start | bytes 12296 | tf_op jit(solution)/shard_map/ppermute | solution.py:63
  42.4 1.7 %collective-permute-done.17.half_in = bf16[2,128,128]{2,1,0:T(8,128)(2,1)S(1)} collective-permute-done((bf16[2,128,128]{2,1,0:T(8,128)(2,1)S(1)}, bf16[2,128,128]{2,1,0:T(8,128)(2,1)S(1)}, u32[]{:S(2)}, u32[]{:S(2)}) %collective-permute-start.17) | collective-permute-done | bytes 65568 | tf_op jit(solution)/shard_map/ppermute | solution.py:63
  44.1 1.6 %collective-permute-start.18 = (bf16[2,128,128]{2,1,0:T(8,128)(2,1)S(1)}, bf16[2,128,128]{2,1,0:T(8,128)(2,1)S(1)}, u32[]{:S(2)}, u32[]{:S(2)}) collective-permute-start(bf16[2,128,128]{2,1,0:T(8,128)(2,1)S(1)} %get-tuple-element.57.sage), channel_id=1, source_target_pairs={{0,4},{1,5},{2,6},{3,7},{4,0},{5,1},{6,2},{7,3},{8,12},{9,13},{10,... | collective-permute-start | bytes 196616 | tf_op jit(solution)/shard_map/ppermute | solution.py:63
  45.7 1.3 %finish.1 = bf16[2,512,128]{2,1,0:T(8,128)(2,1)} custom-call(s32[33]{0:T(128)S(1)} %pad_add_fusion.ints, f32[2,512,128]{2,1,0:T(8,128)S(1)} %tile_back.1.totals, bf16[2,2,8,128]{3,2,1,0:T(8,128)(2,1)S(1)} %slice_add_fusion.hub_own, bf16[1,2,8,128]{3,2,1,0:T(8,128)(2,1)S(1)} %collective-permute-done.13.hub_in), custom_call_target="tpu_custom_call" | custom-call | flops 1000000000 | bytes 2097152 | tf_op jit(solution)/shard_map/finish/pallas_call | solution.py:40
  47.0 1.4 %collective-permute-done.18.sage_in = bf16[2,128,128]{2,1,0:T(8,128)(2,1)S(1)} collective-permute-done((bf16[2,128,128]{2,1,0:T(8,128)(2,1)S(1)}, bf16[2,128,128]{2,1,0:T(8,128)(2,1)S(1)}, u32[]{:S(2)}, u32[]{:S(2)}) %collective-permute-start.18) | collective-permute-done | bytes 65568 | tf_op jit(solution)/shard_map/ppermute | solution.py:63
  48.4 0.8 %weights_out.1 = f32[6,128,128]{2,1,0:T(8,128)} custom-call(bf16[2,128,128]{2,1,0:T(8,128)(2,1)S(1)} %get-tuple-element.57.sage, bf16[2,128,128]{2,1,0:T(8,128)(2,1)S(1)} %collective-permute-done.18.sage_in, bf16[2,128,128]{2,1,0:T(8,128)(2,1)S(1)} %get-tuple-element.58.half, bf16[2,128,128]{2,1,0:T(8,128)(2,1)S(1)} %collective-permute-done.19.half_in), custom_call_target="tpu_custom_call" | custom-call | flops 1000000000 | bytes 2097152 | tf_op jit(solution)/shard_map/weights_out/pallas_call | solution.py:40
  (38 shorter events, 0.2 us)
Async XLA Ops:
  0.6 8.5 %copy-start.1 = (bf16[2,512,128]{2,1,0:T(8,128)(2,1)S(1)}, bf16[2,512,128]{2,1,0:T(8,128)(2,1)}, u32[]{:S(2)}) copy-start(bf16[2,512,128]{2,1,0:T(8,128)(2,1)} %feats.5) | copy-start | bytes 786436
  0.6 8.4 %copy-start.4 = (bf16[2,128,128]{2,1,0:T(8,128)(2,1)S(1)}, bf16[2,128,128]{2,1,0:T(8,128)(2,1)}, u32[]{:S(2)}) copy-start(bf16[2,128,128]{2,1,0:T(8,128)(2,1)} %weight.3) | copy-start | bytes 196612
  0.7 8.4 %copy-start = (bf16[12,128,128]{2,1,0:T(8,128)(2,1)S(1)}, bf16[12,128,128]{2,1,0:T(8,128)(2,1)}, u32[]{:S(2)}) copy-start(bf16[12,128,128]{2,1,0:T(8,128)(2,1)} %tiles.1) | copy-start | bytes 1179652
  2.5 6.4 %copy-start.7 = (s32[8]{0:T(128)S(1)}, s32[8]{0:T(128)}, u32[]{:S(2)}) copy-start(s32[8]{0:T(128)} %ids.1) | copy-start | bytes 100
  2.5 6.4 %copy-start.8 = (s32[12]{0:T(128)S(1)}, s32[12]{0:T(128)}, u32[]{:S(2)}) copy-start(s32[12]{0:T(128)} %param.16) | copy-start | bytes 148
  2.6 6.4 %copy-start.9 = (s32[12]{0:T(128)S(1)}, s32[12]{0:T(128)}, u32[]{:S(2)}) copy-start(s32[12]{0:T(128)} %param.15) | copy-start | bytes 148
  2.6 7.6 %collective-permute-start.2 = (bf16[2,8,128]{2,1,0:T(8,128)(2,1)}, bf16[2,8,128]{2,1,0:T(8,128)(2,1)S(1)}, u32[]{:S(2)}, u32[]{:S(2)}) collective-permute-start(bf16[2,8,128]{2,1,0:T(8,128)(2,1)} %hub_pick.1.refs_0_), channel_id=1, source_target_pairs={{0,24},{8,16},{16,8},{24,0},{1,25},{9,17},{17,9},{25,1},{2,26},{10... | collective-permute-start | bytes 12296 | tf_op jit(solution)/shard_map/ppermute | solution.py:63
  7.7 4.7 %collective-permute-start.1 = (bf16[2,8,128]{2,1,0:T(8,128)(2,1)}, bf16[2,8,128]{2,1,0:T(8,128)(2,1)S(1)}, u32[]{:S(2)}, u32[]{:S(2)}) collective-permute-start(bf16[2,8,128]{2,1,0:T(8,128)(2,1)} %hub_pick.1.refs_0_), channel_id=1, source_target_pairs={{0,16},{8,24},{16,0},{24,8},{1,17},{9,25},{17,1},{25,9},{2,18},{10... | collective-permute-start | bytes 12296 | tf_op jit(solution)/shard_map/ppermute | solution.py:63
  7.7 4.7 %collective-permute-start = (bf16[2,8,128]{2,1,0:T(8,128)(2,1)}, bf16[2,8,128]{2,1,0:T(8,128)(2,1)S(1)}, u32[]{:S(2)}, u32[]{:S(2)}) collective-permute-start(bf16[2,8,128]{2,1,0:T(8,128)(2,1)} %hub_pick.1.refs_0_), channel_id=1, source_target_pairs={{0,8},{8,0},{16,24},{24,16},{1,9},{9,1},{17,25},{25,17},{2,10},{10... | collective-permute-start | bytes 12296 | tf_op jit(solution)/shard_map/ppermute | solution.py:63
  9.1 3.3 %copy-start.5 = (bf16[512,32]{0,1:T(8,128)(2,1)S(1)}, bf16[512,32]{0,1:T(8,128)(2,1)}, u32[]{:S(2)}) copy-start(bf16[512,32]{0,1:T(8,128)(2,1)} %param.19) | copy-start | bytes 98308
  10.2 2.2 %copy-start.6 = (bf16[2,8,128]{2,1,0:T(8,128)(2,1)S(1)}, bf16[2,8,128]{2,1,0:T(8,128)(2,1)}, u32[]{:S(2)}) copy-start(bf16[2,8,128]{2,1,0:T(8,128)(2,1)} %hub_pick.1.refs_0_) | copy-start | bytes 12292
  12.9 1.4 %collective-permute-start.3 = (bf16[4,8,16,128]{3,2,1,0:T(8,128)(2,1)S(1)}, bf16[4,8,16,128]{3,2,1,0:T(8,128)(2,1)S(1)}, u32[]{:S(2)}, u32[]{:S(2)}) collective-permute-start(bf16[4,8,16,128]{3,2,1,0:T(8,128)(2,1)S(1)} %get-tuple-element.34), channel_id=1, source_target_pairs={{0,1},{1,0},{2,3},{3,2},{4,5},{5,4},{6,7},{7,6},{8,9},{9,8},{10,11... | collective-permute-start | bytes 393224 | tf_op jit(solution)/shard_map/ppermute | solution.py:63
  13.0 5.0 %copy-start.2 = (bf16[16,64,128]{2,1,0:T(8,128)(2,1)S(1)}, bf16[16,64,128]{2,1,0:T(8,128)(2,1)}, u32[]{:S(2)}) copy-start(bf16[16,64,128]{2,1,0:T(8,128)(2,1)} %cot.1) | copy-start | bytes 786436
  14.4 4.3 %collective-permute-start.4 = (bf16[2,8,16,128]{3,2,1,0:T(8,128)(2,1)S(1)}, bf16[2,8,16,128]{3,2,1,0:T(8,128)(2,1)S(1)}, u32[]{:S(2)}, u32[]{:S(2)}) collective-permute-start(bf16[2,8,16,128]{3,2,1,0:T(8,128)(2,1)S(1)} %pad_maximum_fusion), channel_id=1, source_target_pairs={{0,2},{1,3},{2,0},{3,1},{4,6},{5,7},{6,4},{7,5},{8,10},{9,11},{10,... | collective-permute-start | bytes 196616 | tf_op jit(solution)/shard_map/ppermute | solution.py:63
  15.9 2.1 %copy-start.3 = (bf16[4,128,128]{2,1,0:T(8,128)(2,1)S(1)}, bf16[4,128,128]{2,1,0:T(8,128)(2,1)}, u32[]{:S(2)}) copy-start(bf16[4,128,128]{2,1,0:T(8,128)(2,1)} %attn.3) | copy-start | bytes 393220
  16.0 4.3 %collective-permute-start.5 = (bf16[2,8,16,128]{3,2,1,0:T(8,128)(2,1)S(1)}, bf16[2,8,16,128]{3,2,1,0:T(8,128)(2,1)S(1)}, u32[]{:S(2)}, u32[]{:S(2)}) collective-permute-start(bf16[2,8,16,128]{3,2,1,0:T(8,128)(2,1)S(1)} %pad_maximum_fusion.1), channel_id=1, source_target_pairs={{0,4},{1,5},{2,6},{3,7},{4,0},{5,1},{6,2},{7,3},{8,12},{9,13},{10,... | collective-permute-start | bytes 196616 | tf_op jit(solution)/shard_map/ppermute | solution.py:63
  17.6 5.2 %collective-permute-start.6 = (bf16[2,8,16,128]{3,2,1,0:T(8,128)(2,1)S(1)}, bf16[2,8,16,128]{3,2,1,0:T(8,128)(2,1)S(1)}, u32[]{:S(2)}, u32[]{:S(2)}) collective-permute-start(bf16[2,8,16,128]{3,2,1,0:T(8,128)(2,1)S(1)} %pad_maximum_fusion.2), channel_id=1, source_target_pairs={{0,6},{1,7},{2,4},{3,5},{4,2},{5,3},{6,0},{7,1},{8,14},{9,15},{10,... | collective-permute-start | bytes 196616 | tf_op jit(solution)/shard_map/ppermute | solution.py:63
  25.6 5.3 %collective-permute-start.7 = (bf16[2,128,128]{2,1,0:T(8,128)(2,1)S(1)}, bf16[2,128,128]{2,1,0:T(8,128)(2,1)S(1)}, u32[]{:S(2)}, u32[]{:S(2)}) collective-permute-start(bf16[2,128,128]{2,1,0:T(8,128)(2,1)S(1)} %get-tuple-element.42), channel_id=1, source_target_pairs={{0,1},{1,0},{2,3},{3,2},{4,5},{5,4},{6,7},{7,6},{8,9},{9,8},{10,11... | collective-permute-start | bytes 196616 | tf_op jit(solution)/shard_map/ppermute | solution.py:63
  25.7 1.5 %collective-permute-start.8 = (bf16[4,8,16,128]{3,2,1,0:T(8,128)(2,1)S(1)}, bf16[4,8,16,128]{3,2,1,0:T(8,128)(2,1)S(1)}, u32[]{:S(2)}, u32[]{:S(2)}) collective-permute-start(bf16[4,8,16,128]{3,2,1,0:T(8,128)(2,1)S(1)} %get-tuple-element.46), channel_id=1, source_target_pairs={{0,1},{1,0},{2,3},{3,2},{4,5},{5,4},{6,7},{7,6},{8,9},{9,8},{10,11... | collective-permute-start | bytes 393224 | tf_op jit(solution)/shard_map/ppermute | solution.py:63
  27.2 5.2 %collective-permute-start.9 = (bf16[2,8,16,128]{3,2,1,0:T(8,128)(2,1)S(1)}, bf16[2,8,16,128]{3,2,1,0:T(8,128)(2,1)S(1)}, u32[]{:S(2)}, u32[]{:S(2)}) collective-permute-start(bf16[2,8,16,128]{3,2,1,0:T(8,128)(2,1)S(1)} %pad_maximum_fusion.3), channel_id=1, source_target_pairs={{0,2},{1,3},{2,0},{3,1},{4,6},{5,7},{6,4},{7,5},{8,10},{9,11},{10,... | collective-permute-start | bytes 196616 | tf_op jit(solution)/shard_map/ppermute | solution.py:63
  27.8 5.0 %collective-permute-start.10 = (bf16[2,8,16,128]{3,2,1,0:T(8,128)(2,1)S(1)}, bf16[2,8,16,128]{3,2,1,0:T(8,128)(2,1)S(1)}, u32[]{:S(2)}, u32[]{:S(2)}) collective-permute-start(bf16[2,8,16,128]{3,2,1,0:T(8,128)(2,1)S(1)} %pad_maximum_fusion.4), channel_id=1, source_target_pairs={{0,4},{1,5},{2,6},{3,7},{4,0},{5,1},{6,2},{7,3},{8,12},{9,13},{10,... | collective-permute-start | bytes 196616 | tf_op jit(solution)/shard_map/ppermute | solution.py:63
  28.4 5.2 %collective-permute-start.11 = (bf16[2,8,16,128]{3,2,1,0:T(8,128)(2,1)S(1)}, bf16[2,8,16,128]{3,2,1,0:T(8,128)(2,1)S(1)}, u32[]{:S(2)}, u32[]{:S(2)}) collective-permute-start(bf16[2,8,16,128]{3,2,1,0:T(8,128)(2,1)S(1)} %pad_maximum_fusion.5), channel_id=1, source_target_pairs={{0,6},{1,7},{2,4},{3,5},{4,2},{5,3},{6,0},{7,1},{8,14},{9,15},{10,... | collective-permute-start | bytes 196616 | tf_op jit(solution)/shard_map/ppermute | solution.py:63
  31.9 4.7 %collective-permute-start.15 = (bf16[2,128,128]{2,1,0:T(8,128)(2,1)S(1)}, bf16[2,128,128]{2,1,0:T(8,128)(2,1)S(1)}, u32[]{:S(2)}, u32[]{:S(2)}) collective-permute-start(bf16[2,128,128]{2,1,0:T(8,128)(2,1)S(1)} %get-tuple-element.54.half), channel_id=1, source_target_pairs={{0,2},{1,3},{2,0},{3,1},{4,6},{5,7},{6,4},{7,5},{8,10},{9,11},{10,... | collective-permute-start | bytes 196616 | tf_op jit(solution)/shard_map/ppermute | solution.py:63
  34.2 7.1 %collective-permute-start.12 = (bf16[2,2,8,128]{3,2,1,0:T(8,128)(2,1)S(1)}, bf16[2,2,8,128]{3,2,1,0:T(8,128)(2,1)S(1)}, u32[]{:S(2)}, u32[]{:S(2)}) collective-permute-start(bf16[2,2,8,128]{3,2,1,0:T(8,128)(2,1)S(1)} %slice.58), channel_id=1, source_target_pairs={{0,16},{8,24},{16,0},{24,8},{1,17},{9,25},{17,1},{25,9},{2,18},{10... | collective-permute-start | bytes 24584 | tf_op jit(solution)/shard_map/ppermute | solution.py:63
  36.3 1.3 %collective-permute-start.14 = (bf16[2,128,128]{2,1,0:T(8,128)(2,1)S(1)}, bf16[2,128,128]{2,1,0:T(8,128)(2,1)S(1)}, u32[]{:S(2)}, u32[]{:S(2)}) collective-permute-start(bf16[2,128,128]{2,1,0:T(8,128)(2,1)S(1)} %get-tuple-element.53.sage), channel_id=1, source_target_pairs={{0,1},{1,0},{2,3},{3,2},{4,5},{5,4},{6,7},{7,6},{8,9},{9,8},{10,11... | collective-permute-start | bytes 196616 | tf_op jit(solution)/shard_map/ppermute | solution.py:63
  37.6 4.8 %collective-permute-start.16 = (bf16[2,128,128]{2,1,0:T(8,128)(2,1)S(1)}, bf16[2,128,128]{2,1,0:T(8,128)(2,1)S(1)}, u32[]{:S(2)}, u32[]{:S(2)}) collective-permute-start(bf16[2,128,128]{2,1,0:T(8,128)(2,1)S(1)} %get-tuple-element.55.sage), channel_id=1, source_target_pairs={{0,2},{1,3},{2,0},{3,1},{4,6},{5,7},{6,4},{7,5},{8,10},{9,11},{10,... | collective-permute-start | bytes 196616 | tf_op jit(solution)/shard_map/ppermute | solution.py:63
  39.8 4.3 %collective-permute-start.17 = (bf16[2,128,128]{2,1,0:T(8,128)(2,1)S(1)}, bf16[2,128,128]{2,1,0:T(8,128)(2,1)S(1)}, u32[]{:S(2)}, u32[]{:S(2)}) collective-permute-start(bf16[2,128,128]{2,1,0:T(8,128)(2,1)S(1)} %get-tuple-element.56.half), channel_id=1, source_target_pairs={{0,4},{1,5},{2,6},{3,7},{4,0},{5,1},{6,2},{7,3},{8,12},{9,13},{10,... | collective-permute-start | bytes 196616 | tf_op jit(solution)/shard_map/ppermute | solution.py:63
  41.3 4.4 %collective-permute-start.13 = (bf16[1,2,8,128]{3,2,1,0:T(8,128)(2,1)S(1)}, bf16[1,2,8,128]{3,2,1,0:T(8,128)(2,1)S(1)}, u32[]{:S(2)}, u32[]{:S(2)}) collective-permute-start(bf16[1,2,8,128]{3,2,1,0:T(8,128)(2,1)S(1)} %slice.66), channel_id=1, source_target_pairs={{0,8},{8,0},{16,24},{24,16},{1,9},{9,1},{17,25},{25,17},{2,10},{10... | collective-permute-start | bytes 12296 | tf_op jit(solution)/shard_map/ppermute | solution.py:63
  44.1 4.3 %collective-permute-start.18 = (bf16[2,128,128]{2,1,0:T(8,128)(2,1)S(1)}, bf16[2,128,128]{2,1,0:T(8,128)(2,1)S(1)}, u32[]{:S(2)}, u32[]{:S(2)}) collective-permute-start(bf16[2,128,128]{2,1,0:T(8,128)(2,1)S(1)} %get-tuple-element.57.sage), channel_id=1, source_target_pairs={{0,4},{1,5},{2,6},{3,7},{4,0},{5,1},{6,2},{7,3},{8,12},{9,13},{10,... | collective-permute-start | bytes 196616 | tf_op jit(solution)/shard_map/ppermute | solution.py:63
  45.7 2.7 %collective-permute-start.19 = (bf16[2,128,128]{2,1,0:T(8,128)(2,1)S(1)}, bf16[2,128,128]{2,1,0:T(8,128)(2,1)S(1)}, u32[]{:S(2)}, u32[]{:S(2)}) collective-permute-start(bf16[2,128,128]{2,1,0:T(8,128)(2,1)S(1)} %get-tuple-element.58.half), channel_id=1, source_target_pairs={{0,1},{1,0},{2,3},{3,2},{4,5},{5,4},{6,7},{7,6},{8,9},{9,8},{10,11... | collective-permute-start | bytes 196616 | tf_op jit(solution)/shard_map/ppermute | solution.py:63

commit v4 on v3

v4 whole, which is shorter than its diff:
```python
import functools
import math

import jax
import jax.numpy as jnp
from jax import lax
from jax.experimental import pallas as pl
from jax.experimental.pallas import tpu as pltpu
from jax.sharding import PartitionSpec as P

HEADS = 4
CAP = 20.0
SUB = 8

BF = jnp.bfloat16
F32 = jnp.float32
VMEM = pl.BlockSpec(memory_space=pltpu.VMEM)
ANY = pl.BlockSpec(memory_space=pl.ANY)
HBM = pl.BlockSpec(memory_space=pltpu.HBM)
LIMIT = 24 * 1024 * 1024
WHOLE = 56 * 1024 * 1024


def dot(a, b):
    return jnp.dot(a, b, preferred_element_type=F32)


def dot_nt(a, b):
    return lax.dot_general(a, b, (((1,), (1,)), ((), ())), preferred_element_type=F32)


def dot_tn(a, b):
    return lax.dot_general(a, b, (((0,), (0,)), ((), ())), preferred_element_type=F32)


def shape(dims, kind=BF):
    return jax.ShapeDtypeStruct(dims, kind)


def call(kernel, outs, operands, specs, scratch=(), micros=1.0, limit=LIMIT, outs_at=VMEM, name=None):
    return pl.pallas_call(
        kernel,
        out_shape=outs,
        in_specs=specs,
        out_specs=jax.tree.map(lambda _: outs_at, outs),
        scratch_shapes=list(scratch),
        compiler_params=pltpu.CompilerParams(vmem_limit_bytes=limit),
        cost_estimate=pl.CostEstimate(
            flops=int(micros * 10**9), bytes_accessed=int(micros * 2**21), transcendentals=0
        ),
        name=name,
    )(*operands)


def fetch(pairs, sems):
    copies = [pltpu.make_async_copy(a, b, sems.at[i]) for i, (a, b) in enumerate(pairs)]
    for copy in copies:
        copy.start()
    return copies


def swapped(x, axis, mask):
    count = lax.axis_size(axis)
    return lax.ppermute(x, axis, [(i, i ^ mask) for i in range(count)])


def one_hot(ids, hubs, nodes):
    row = lax.broadcasted_iota(jnp.int32, (hubs, nodes), 0)
    col = lax.broadcasted_iota(jnp.int32, (hubs, nodes), 1)
    want = jnp.zeros((hubs, nodes), jnp.int32)
    for j in range(hubs):
        want = jnp.where(row == j, lax.rem(ids[j], nodes), want)
    return jnp.where(col == want, 1.0, 0.0).astype(BF)


def hub_pick(ids, feats, out, ids_s, feats_v, sems):
    layouts, nodes, _ = feats.shape
    copies = fetch([(ids, ids_s)] + [(feats.at[l], feats_v.at[l]) for l in range(layouts)], sems)
    copies[0].wait()
    hot = one_hot(ids_s, out.shape[1], nodes)
    for l in range(layouts):
        copies[1 + l].wait()
        out[l] = dot(hot, feats_v[l]).astype(BF)


def core_rows(ref, lead, core):
    block = ref[lead + (slice(None), pl.ds(core, 1))]
    return block.reshape(block.shape[0] * block.shape[2], block.shape[3])


def adjacency(first, ints, tiles, weight, feats, other, whole, summed, pre_self, chosen, mine, hot, ints_s, adj, dense, sems):
    copies = fetch([(ints, ints_s)], sems)
    slots, tile, _ = tiles.shape
    layouts, chips, cores, share, width = feats.shape
    nodes = chips * cores * share
    core = lax.rem(lax.axis_index("config"), 2)
    adj[...] = jnp.zeros(adj.shape, F32)
    for l in range(2 * layouts):
        chosen[l] = core_rows((feats, other)[l // layouts], (l % layouts,), core)
        pre_self[l] = dot(chosen[l], weight[0])
    copies[0].wait()
    for t in range(slots):

        @pl.when(t < ints_s[first + 2 * slots])
        def _():
            at = pl.ds(pl.multiple_of(ints_s[first + t] * tile, tile), tile)
            block = tiles[t].astype(F32)
            col = ints_s[first + slots + t]
            for s in range(nodes // tile):

                @pl.when(col == s)
                def _():
                    adj[at, pl.ds(s * tile, tile)] += block

    whole[...] = adj[...].astype(BF)
    dense[...] = whole[...].reshape(dense.shape)
    wide = [x[l].reshape(nodes, width) for x in (feats, other) for l in range(layouts)]
    summed[...] = dot(core_rows(dense, (), core), jnp.concatenate(wide, axis=1))
    hot[...] = one_hot(ints_s, mine.shape[1], nodes)
    for l in range(layouts):
        mine[l] = dot(hot[...], wide[l]).astype(BF)


def sage_out(*refs):
    hub_rows, (summed, pre_self, hub_weight, weight) = refs[:2], refs[2:6]
    blocks, (agg, pre, ready) = refs[6:-3], refs[-3:]
    layouts, nodes, width = pre_self.shape
    chips, groups, _, _ = ready.shape
    me = lax.axis_index("config")
    hub_all = jnp.concatenate([x[...] for x in hub_rows], axis=1)
    total = summed[...] + dot(core_rows(hub_weight, (), lax.rem(me, 2)), hub_all)
    acts = []
    for l in range(layouts):
        mine = total[:, l * width : (l + 1) * width].astype(BF)
        agg[l] = mine
        value = pre_self[l] + dot(mine, weight[1])
        pre[l] = value
        act = value / (1.0 + jnp.exp(-value))
        acts.append(act.reshape(chips, groups, SUB, width))
    ready[...] = jnp.concatenate(acts, axis=2).astype(BF)
    for s, block in enumerate(blocks):
        block[...] = ready[lax.bitwise_xor(me // 2, s)]


def prepare(cot, attn, weight, feats, agg, pre, adj, cot_g, gmix, slope, rows_t, w_back, adj_t):
    layouts, _, width = cot.shape
    groups = cot_g.shape[0]
    adj_t[...] = adj[...].T
    for l in range(feats.shape[0]):
        value = pre[l]
        sig = 1.0 / (1.0 + jnp.exp(-value))
        slope[l] = sig * (1.0 + value * (1.0 - sig))
        at = slice(l * feats.shape[1], (l + 1) * feats.shape[1])
        rows_t[0:width, at] = feats[l].T
        rows_t[width : 2 * width, at] = agg[l].T
    w_back[:, 0:width] = weight[0].T
    w_back[:, width : 2 * width] = weight[1].T
    for p in range(groups // 2):
        block = cot[:, 2 * SUB * p : 2 * SUB * (p + 1), :].astype(F32)
        for h in range(2):
            rows = block[:, SUB * h : SUB * (h + 1), :].reshape(layouts * SUB, width).astype(BF)
            cot_g[2 * p + h] = rows
            gmix[2 * p + h] = dot_nt(rows, attn[3]).astype(BF)


def attend(*refs):
    hidden, ready, grads, pieces = refs[-4:]
    groups, shares, depth, width = hidden.shape
    chips = shares // 2
    blocks, (cot_g, gmix, attn) = refs[:chips], refs[chips : chips + 3]
    outs, (hid_out, mixed_t) = refs[chips + 3 : -6], refs[-6:-4]
    me = lax.axis_index("config")
    rows = shares * depth
    head = width // HEADS
    scale = 1.0 / math.sqrt(head)
    for s, block in enumerate(blocks):
        for core in range(2):
            hidden[:, lax.bitwise_xor(me, 2 * s + core)] = block[:, core * depth : (core + 1) * depth]
    w_all = jnp.concatenate([attn[0], attn[1], attn[2]], axis=1)
    lane = lax.broadcasted_iota(jnp.int32, (rows, width), 1) // head
    r = lax.broadcasted_iota(jnp.int32, (rows, HEADS * rows), 0)
    c = lax.broadcasted_iota(jnp.int32, (rows, HEADS * rows), 1)
    same = (r % SUB) == (c % SUB)
    zero = jnp.zeros((rows, width), BF)
    gap = jnp.zeros((head, rows), BF)

    def by_head(x):
        return jnp.concatenate([jnp.where(lane == e, x, zero) for e in range(HEADS)], axis=0)

    flat = hidden[...].reshape(groups * rows, width)
    hid_out[...] = flat.reshape(groups, rows, width)
    qkv = dot(flat, w_all).astype(BF)
    inputs = []
    for g in range(groups):
        q, k, v = (qkv[g * rows : (g + 1) * rows, i * width : (i + 1) * width] for i in range(3))
        inputs.append((k, v, k.T, v.T, by_head(q), by_head(gmix[g])))
    products = [(dot_nt(k, qm), dot_nt(v, gm)) for k, v, _, _, qm, gm in inputs]
    weighted = []
    for scores, d_probs in products:
        t = jnp.tanh(scores * (scale / CAP))
        w = jnp.where(same, jnp.exp2(t * (CAP * math.log2(math.e))), 0.0)
        a = w * (1.0 / jnp.sum(w, axis=0, keepdims=True))
        z = a * d_probs
        zs = jnp.sum(z, axis=0, keepdims=True)
        weighted.append((a.astype(BF), ((z - a * zs) * (scale - scale * (t * t))).astype(BF)))
    d_all, mix_t = [], []
    for (k, v, k_t, v_t, qm, gm), (p, ds) in zip(inputs, weighted):
        mix, dq = [], []
        for e in range(HEADS):
            at, span = slice(e * head, (e + 1) * head), slice(e * rows, (e + 1) * rows)
            left = jnp.concatenate(
                [jnp.concatenate([v_t[at], gap], axis=1), jnp.concatenate([gap, k_t[at]], axis=1)], axis=0
            )
            both = dot(left, jnp.concatenate([p[:, span], ds[:, span]], axis=0))
            mix.append(both[:head])
            dq.append(both[head:])
        mix_t.append(jnp.concatenate(mix, axis=0).astype(BF))
        dq = jnp.concatenate(dq, axis=0).astype(BF).T
        d_all.append(jnp.concatenate([dq, dot(ds, qm).astype(BF), dot(p, gm).astype(BF)], axis=1))
    d_all = jnp.concatenate(d_all, axis=0)
    mix_t = jnp.concatenate(mix_t, axis=1)
    mixed_t[...] = mix_t
    cots = cot_g[...].reshape(groups * rows, width)
    back = (cots.astype(F32) + dot_nt(d_all, w_all)).astype(BF).reshape(groups, shares, depth, width)
    for g in range(groups):
        ready[:, g] = back[g]
    total = dot(flat.T, d_all)
    for i in range(3):
        grads[i] = total[:, i * width : (i + 1) * width].astype(BF)
    grads[3] = dot(mix_t, cots).astype(BF)
    shared = grads[...].reshape(chips, -1, width)
    pieces[...] = shared
    count = groups * 2 * depth
    for s, block in enumerate(outs):
        pair = [ready[lax.bitwise_xor(me, 2 * s + core)] for core in range(2)]
        block[0:count] = jnp.concatenate(pair, axis=1).reshape(count, width)
        block[count:] = pieces[lax.bitwise_xor(me // 2, s)]


def outputs(hidden, mixed_t, attn, _, out, done):
    done[...] = jnp.zeros(done.shape, F32)
    groups, rows, width = hidden.shape
    layouts = rows // SUB
    projected = dot_tn(mixed_t[...], attn[3])
    for p in range(groups // 2):
        pair = []
        for g in (2 * p, 2 * p + 1):
            both = hidden[g].astype(F32) + projected[g * rows : (g + 1) * rows]
            pair.append(both.reshape(layouts, SUB, width))
        out[:, 2 * SUB * p : 2 * SUB * (p + 1), :] = jnp.concatenate(pair, axis=1).astype(BF)


def sage_back(*refs):
    parts, hub_sum = refs[-2:]
    chips, _, layouts, _, width = parts.shape
    blocks, (slope, rows_t, w_back, hub_weight) = refs[:chips], refs[chips : chips + 4]
    mine, theirs, sums, hub_mine, hub_theirs = refs[chips + 5 : -2]
    me = lax.axis_index("config")
    nodes = slope.shape[1]
    count = parts.shape[1] * layouts * SUB
    for s, block in enumerate(blocks):
        parts[lax.bitwise_xor(me // 2, s)] = block[0:count].astype(F32).reshape(parts.shape[1:])
    sums[2 * width :] = sum(block[count:].astype(F32) for block in blocks).astype(BF)
    half = layouts // 2
    grad_pre, grad_agg = [], []
    for l in range(layouts):
        gpre = (parts[:, :, l].reshape(nodes, width) * slope[l]).astype(BF)
        (mine, theirs)[l // half][l % half] = gpre
        grad_pre.append(gpre)
        grad_agg.append(dot(gpre, w_back[:, width : 2 * width]).astype(BF))
    both = dot(rows_t[...], jnp.concatenate(grad_pre, axis=0))
    sums[0 : 2 * width] = both.astype(BF)
    hub_sum[...] = dot_tn(core_rows(hub_weight, (), lax.rem(me, 2)), jnp.concatenate(grad_agg, axis=1))
    slab = lax.axis_index("graph")
    ranks, _, hubs, _ = hub_mine.shape
    for s in range(ranks):
        at = pl.ds(pl.multiple_of(lax.bitwise_xor(slab, s) * hubs, hubs), hubs)
        for l in range(layouts):
            (hub_mine, hub_theirs)[l // half][s, l % half] = hub_sum[at, l * width : (l + 1) * width].astype(BF)


def tile_back(adj_t, w_back, mine, theirs, totals, whole):
    layouts, nodes, width = totals.shape
    core = lax.rem(lax.axis_index("config"), 2)
    for l in range(layouts):
        for part, at in ((mine, core), (theirs, 1 - core)):
            whole[l, :, pl.ds(at, 1)] = part[l].reshape(whole.shape[1], 1, whole.shape[3], width)
    grad_self, grad_agg = [], []
    for l in range(layouts):
        both = dot(whole[l].reshape(nodes, width), w_back[...]).astype(BF)
        grad_self.append(both[:, 0:width])
        grad_agg.append(both[:, width : 2 * width])
    back = dot(adj_t[...], jnp.concatenate(grad_agg, axis=1))
    for l in range(layouts):
        totals[l] = grad_self[l].astype(F32) + back[:, l * width : (l + 1) * width]


def add(a, b):
    return (a[...].astype(F32) + b[...].astype(F32)).astype(BF)


def join(*refs):
    pairs = len(refs) // 3
    for i in range(pairs):
        refs[2 * pairs + i][...] = add(refs[2 * i], refs[2 * i + 1])


def joined(*operands):
    return call(
        join,
        [shape(x.shape) for x in operands[::2]],
        operands,
        [VMEM] * len(operands),
        micros=0.1,
        name="join",
    )


def by_slab(*refs):
    pieces, (rows, work) = refs[:-2], refs[-2:]
    layouts, hubs, width = pieces[0].shape
    slab = lax.axis_index("graph")
    for s, piece in enumerate(pieces):
        at = pl.ds(pl.multiple_of(lax.bitwise_xor(slab, s) * hubs, hubs), hubs)
        for l in range(layouts):
            work[at, l * width : (l + 1) * width] = piece[l].astype(F32)
    rows[...] = work[...].astype(BF)


def finish(hot, totals, hub_own, hub_in, _, out, work, sems):
    layouts, nodes, width = totals.shape
    summed = [hub_own[0, l].astype(F32) + hub_in[0, l].astype(F32) for l in range(layouts)]
    upper = [x.astype(BF) for x in summed]
    lower = [(x - y.astype(F32)).astype(BF) for x, y in zip(summed, upper)]
    twice = jnp.concatenate([hot[...], hot[...]], axis=0)
    copies = []
    for l in range(layouts):
        added = dot_tn(twice, jnp.concatenate([upper[l], lower[l]], axis=0))
        work[l] = (totals[l] + added).astype(BF)
        copies.append(pltpu.make_async_copy(work.at[l], out.at[l], sems.at[l]))
        copies[l].start()
    for copy in copies:
        copy.wait()


def weights_out(scale, *refs):
    sums, (out, done, work) = refs[:-3], refs[-3:]
    done[...] = jnp.zeros(done.shape, F32)
    width = out.shape[1]
    first = 2 * width
    share = sums[0].shape[0] - first
    chip = lax.axis_index("config") // 2
    for s, part in enumerate(sums):
        at = lax.bitwise_xor(chip, s)
        work[at] = part[0:first].astype(F32)
        out[pl.ds(pl.multiple_of(first + at * share, share), share)] = part[first:].astype(F32) * scale
    total = work[0]
    for s in range(1, len(sums)):
        total = total + work[s]
    out[0:first] = total * scale


def exchange(blocks):
    return [swapped(block, "config", 2 * s) if s else block for s, block in enumerate(blocks)]


def local(
    features,
    cotangent,
    sage_weight,
    attn_weight,
    tile_vals,
    tile_dst,
    tile_src,
    tile_count,
    hub_ids,
    hub_weight,
):
    layout_dev, node_dev, width = features.shape
    ranks = lax.axis_size("graph")
    shares = lax.axis_size("config")
    chips = shares // 2
    share = node_dev // shares
    groups = share // SUB
    layouts = layout_dev * shares
    rows = layouts * SUB
    depth = 2 * layout_dev * SUB
    hub_dev = hub_ids.shape[0]
    hubs = hub_weight.shape[1]
    slab = (layout_dev, node_dev, width)
    part = (2 * layout_dev, node_dev // 2, width)
    block = (groups, depth, width)
    dma = pltpu.SemaphoreType.DMA
    ints = jnp.concatenate([hub_ids, tile_dst, tile_src, tile_count])
    ints_s = pltpu.SMEM(ints.shape, jnp.int32)
    hub_weight = hub_weight.reshape(chips, 2, share, hubs)
    by_core = (layout_dev, chips, 2, share, width)

    mine = call(
        hub_pick,
        shape((layout_dev, hub_dev, width)),
        (hub_ids, features),
        [HBM] * 2,
        [pltpu.SMEM((hub_dev,), jnp.int32), pltpu.VMEM(slab, BF), dma((1 + layout_dev,))],
        limit=WHOLE,
        name="hub_pick",
    )
    pieces = [swapped(mine, "graph", s) for s in range(1, ranks)]
    other = swapped(features, "config", 1)

    adj, summed, pre_self, feats, mine, hot = call(
        functools.partial(adjacency, hub_dev),
        (
            shape((node_dev, node_dev)),
            shape((part[1], part[0] * width), F32),
            shape(part, F32),
            shape(part),
            shape(mine.shape),
            shape((hub_dev, node_dev)),
        ),
        (ints, tile_vals, sage_weight, features.reshape(by_core), other.reshape(by_core)),
        [VMEM] * 5,
        [
            ints_s,
            pltpu.VMEM((node_dev, node_dev), F32),
            pltpu.VMEM((chips, 2, share, node_dev), BF),
            dma((1,)),
        ],
        name="adjacency",
    )

    hub_rows = call(
        by_slab,
        shape((hubs, layout_dev * width)),
        (mine, *pieces),
        [VMEM] * ranks,
        [pltpu.VMEM((hubs, layout_dev * width), F32)],
        micros=0.1,
        name="by_slab",
    )
    hub_rows = (hub_rows, swapped(hub_rows, "config", 1))

    *blocks, agg, pre = call(
        sage_out,
        (*[shape(block)] * chips, shape(part), shape(part, F32)),
        (*hub_rows, summed, pre_self, hub_weight, sage_weight),
        [VMEM] * 6,
        [pltpu.VMEM((chips, *block), BF)],
        name="sage_out",
    )
    hidden_in = exchange(blocks)

    cot_g, gmix, slope, rows_t, w_back, adj_t = call(
        prepare,
        (
            shape((groups, rows, width)),
            shape((groups, rows, width)),
            shape(part, F32),
            shape((2 * width, part[0] * part[1])),
            shape((width, 2 * width)),
            shape((node_dev, node_dev)),
        ),
        (cotangent, attn_weight, sage_weight, feats, agg, pre, adj),
        [VMEM] * 7,
        name="prepare",
    )

    share_rows = attn_weight.shape[0] * width // chips
    back = (groups * depth + share_rows, width)
    *blocks, hidden, mixed_t = call(
        attend,
        (
            *[shape(back)] * chips,
            shape((groups, rows, width)),
            shape((width, groups * rows)),
        ),
        (*hidden_in, cot_g, gmix, attn_weight),
        [VMEM] * (len(hidden_in) + 3),
        [
            pltpu.VMEM((groups, shares, depth // 2, width), BF),
            pltpu.VMEM((shares, groups, depth // 2, width), BF),
            pltpu.VMEM(attn_weight.shape, BF),
            pltpu.VMEM((chips, share_rows, width), BF),
        ],
        micros=4.0,
        name="attend",
    )
    grad_in = exchange(blocks)
    token = shape((SUB, width), F32)
    output, shown = call(
        outputs,
        (shape((layouts, share, width)), token),
        (hidden, mixed_t, attn_weight, grad_in[1]),
        [VMEM] * 3 + [ANY],
        name="outputs",
    )

    hub_shape = (ranks, layout_dev, hub_dev, width)
    mine = (layout_dev, node_dev // 2, width)
    mine, theirs, sums, hub_sum, hub_theirs = call(
        sage_back,
        (shape(mine), shape(mine), shape((2 * width + share_rows, width)), shape(hub_shape), shape(hub_shape)),
        (*grad_in, slope, rows_t, w_back, hub_weight, shown),
        [VMEM] * (chips + 4) + [ANY],
        [
            pltpu.VMEM((chips, groups, 2 * layout_dev, SUB, width), F32),
            pltpu.VMEM((hubs, part[0] * width), F32),
        ],
        name="sage_back",
    )
    hub_in = swapped(hub_theirs, "config", 1)
    theirs = swapped(theirs, "config", 1)
    sums, hub_sum = joined(sums, swapped(sums, "config", 1), hub_sum, hub_in)
    sums = [swapped(sums, "config", 2 * s) if s else sums for s in range(chips)]
    totals = call(
        tile_back,
        shape(slab, F32),
        (adj_t, w_back, mine, theirs),
        [VMEM] * 4,
        [pltpu.VMEM(by_core, BF)],
        name="tile_back",
    )
    while hub_sum.shape[0] > 2:
        keep = hub_sum.shape[0] // 2
        hub_sum = hub_sum[:keep] + swapped(hub_sum[keep:], "graph", keep)
    hub_in = swapped(hub_sum[1:], "graph", 1)
    count = sage_weight.shape[0] + attn_weight.shape[0]
    weights, summed = call(
        functools.partial(weights_out, 1.0 / math.sqrt(layouts * node_dev)),
        (shape((count * width, width), F32), token),
        sums,
        [VMEM] * chips,
        [pltpu.VMEM((chips, 2 * width, width), F32)],
        name="weights_out",
    )
    grad_features = call(
        finish,
        shape(slab),
        (hot, totals, hub_sum, hub_in, summed),
        [VMEM] * 4 + [ANY],
        [pltpu.VMEM(slab, BF), dma((layout_dev,))],
        outs_at=HBM,
        name="finish",
    )
    return (output, grad_features, weights.reshape(1, count, width, width))


def solution(mesh):
    return jax.shard_map(
        local,
        mesh=mesh,
        in_specs=(
            P("config", "graph", None),
            P(None, ("graph", "config"), None),
            P(),
            P(),
            P("graph", None, None),
            P("graph"),
            P("graph"),
            P("graph"),
            P("graph"),
            P("graph", None),
        ),
        out_specs=(
            P(None, ("graph", "config"), None),
            P("config", "graph", None),
            P("graph", None, None, None),
        ),
        check_vma=False,
    )
```

time: 49.4 us -> 46.2 us (0.935)
  starting transfers between devices: 22.7 us -> 19.8 us
  local copies, waits for them, and re-layouts: 0.09 us -> 0.82 us
  waiting for transfers between devices: 13.9 us -> 13.3 us
    ppermute x20 -> x19, starting transfers between devices: 22.7 us -> 19.8 us  [swapped(): return lax.ppermute(x, axis, [(i, i ^ mask) for i in range(count)])]
    unnamed x20 -> x19, local copies, waits for them, and re-layouts: 0.05 us -> 0.82 us
    ppermute x20 -> x19, waiting for transfers between devices: 13.9 us -> 13.3 us  [swapped(): return lax.ppermute(x, axis, [(i, i ^ mask) for i in range(count)])]
  transfers between devices with their start and end apart: 20 -> 19, of which waited for: 11 -> 11; matrix products, arithmetic and copies ran while one was open for 0% -> 0% of each run, Pallas kernels for 10% -> 13%
where the time goes in v4:
time: 46.2 us; the launch traced here: 46 us
  starting transfers between devices  19.8 us (43%)
  waiting for transfers between devices  13.3 us (29%)
  Pallas kernels  10.5 us (23%)
  between operations  1.48 us (3%)
  local copies, waits for them, and re-layouts  0.82 us (2%)
    ppermute x19, starting transfers between devices, swapped(): return lax.ppermute(x, axis, [(i, i ^ mask) for i in range(count)])  19.8 us
    ppermute x19, waiting for transfers between devices, swapped(): return lax.ppermute(x, axis, [(i, i ^ mask) for i in range(count)])  13.3 us
    pallas_call x12, Pallas kernels, call(): pl.pallas_call(kernel, out_shape=outs, in_specs=specs, out_specs=jax.tree...  10.5 us
  transfers between devices with their start and end apart: 19, of which 11 were waited for; matrix products, arithmetic and copies ran while one was open for 0% of the time, Pallas kernels for 13%

profile of v4, /device:TPU:0, one launch (start us, length us, event | category | flops | bytes accessed | tf_op | source)
XLA Modules:
  0.0 46.0 jit_solution(2540174218167769469)
XLA Ops:
  0.7 0.5 %collective-permute-start = (bf16[2,512,128]{2,1,0:T(8,128)(2,1)}, bf16[2,512,128]{2,1,0:T(8,128)(2,1)S(1)}, u32[]{:S(2)}, u32[]{:S(2)}) collective-permute-start(bf16[2,512,128]{2,1,0:T(8,128)(2,1)} %feats.1), channel_id=1, source_target_pairs={{0,1},{1,0},{2,3},{3,2},{4,5},{5,4},{6,7},{7,6},{8,9},{9,8},{10,11... | collective-permute-start | bytes 786440 | tf_op jit(solution)/shard_map/ppermute | solution.py:64
  1.2 1.8 %hub_pick.1 = bf16[2,8,128]{2,1,0:T(8,128)(2,1)} custom-call(s32[8]{0:T(128)} %ids.1, bf16[2,512,128]{2,1,0:T(8,128)(2,1)} %feats.1), custom_call_target="tpu_custom_call" | custom-call | flops 1000000000 | bytes 2097152 | tf_op jit(solution)/shard_map/hub_pick/pallas_call | solution.py:41
  3.0 0.0 copy-start.6
  3.0 0.0 copy-start.7
  3.0 0.0 copy-start.8
  3.0 4.7 %collective-permute-start.3 = (bf16[2,8,128]{2,1,0:T(8,128)(2,1)}, bf16[2,8,128]{2,1,0:T(8,128)(2,1)S(1)}, u32[]{:S(2)}, u32[]{:S(2)}) collective-permute-start(bf16[2,8,128]{2,1,0:T(8,128)(2,1)} %hub_pick.1), channel_id=1, source_target_pairs={{0,24},{8,16},{16,8},{24,0},{1,25},{9,17},{17,9},{25,1},{2,26},{10... | collective-permute-start | bytes 12296 | tf_op jit(solution)/shard_map/ppermute | solution.py:64
  7.8 0.6 %collective-permute-start.1 = (bf16[2,8,128]{2,1,0:T(8,128)(2,1)}, bf16[2,8,128]{2,1,0:T(8,128)(2,1)S(1)}, u32[]{:S(2)}, u32[]{:S(2)}) collective-permute-start(bf16[2,8,128]{2,1,0:T(8,128)(2,1)} %hub_pick.1), channel_id=1, source_target_pairs={{0,8},{8,0},{16,24},{24,16},{1,9},{9,1},{17,25},{25,17},{2,10},{10... | collective-permute-start | bytes 12296 | tf_op jit(solution)/shard_map/ppermute | solution.py:64
  9.1 0.1 pad_add_fusion.ints
  9.2 0.0 collective-permute-done
  9.2 1.2 %adjacency.1 = (bf16[512,512]{1,0:T(8,128)(2,1)S(1)}, f32[256,512]{1,0:T(8,128)S(1)}, f32[4,256,128]{2,1,0:T(8,128)S(1)}, bf16[4,256,128]{2,1,0:T(8,128)(2,1)S(1...) custom-call(s32[33]{0:T(128)S(1)} %pad_add_fusion.ints, bf16[12,128,128]{2,1,0:T(8,128)(2,1)S(1)} %copy-done, ...), custom_call_target="tpu_custom_call" | custom-call | flops 1000000000 | bytes 2097152 | tf_op jit(solution)/shard_map/adjacency/pallas_call | solution.py:41
  10.4 0.0 collective-permute-done.3.refs_3_
  10.4 2.1 %collective-permute-done.2.refs_2_ = bf16[2,8,128]{2,1,0:T(8,128)(2,1)S(1)} collective-permute-done((bf16[2,8,128]{2,1,0:T(8,128)(2,1)}, bf16[2,8,128]{2,1,0:T(8,128)(2,1)S(1)}, u32[]{:S(2)}, u32[]{:S(2)}) %collective-permute-start.2) | collective-permute-done | bytes 4128 | tf_op jit(solution)/shard_map/ppermute | solution.py:64
  12.5 0.0 collective-permute-done.1.refs_1_
  12.5 0.1 collective-permute-start.4
  12.6 0.7 %copy-done.5 = bf16[512,32]{0,1:T(8,128)(2,1)S(1)} copy-done((bf16[512,32]{0,1:T(8,128)(2,1)S(1)}, bf16[512,32]{0,1:T(8,128)(2,1)}, u32[]{:S(2)}) %copy-start.5) | copy-done | bytes 32792
  13.2 0.1 copy.13
  13.4 0.4 collective-permute-done.4.refs_1_
  13.8 0.4 sage_out.1
  14.2 1.6 %collective-permute-start.5 = (bf16[8,32,128]{2,1,0:T(8,128)(2,1)S(1)}, bf16[8,32,128]{2,1,0:T(8,128)(2,1)S(1)}, u32[]{:S(2)}, u32[]{:S(2)}) collective-permute-start(bf16[8,32,128]{2,1,0:T(8,128)(2,1)S(1)} %get-tuple-element.42), channel_id=1, source_target_pairs={{0,2},{1,3},{2,0},{3,1},{4,6},{5,7},{6,4},{7,5},{8,10},{9,11},{10,... | collective-permute-start | bytes 196616 | tf_op jit(solution)/shard_map/ppermute | solution.py:64
  15.8 1.5 %collective-permute-start.6 = (bf16[8,32,128]{2,1,0:T(8,128)(2,1)S(1)}, bf16[8,32,128]{2,1,0:T(8,128)(2,1)S(1)}, u32[]{:S(2)}, u32[]{:S(2)}) collective-permute-start(bf16[8,32,128]{2,1,0:T(8,128)(2,1)S(1)} %get-tuple-element.43), channel_id=1, source_target_pairs={{0,4},{1,5},{2,6},{3,7},{4,0},{5,1},{6,2},{7,3},{8,12},{9,13},{10,... | collective-permute-start | bytes 196616 | tf_op jit(solution)/shard_map/ppermute | solution.py:64
  17.3 0.5 %collective-permute-start.7 = (bf16[8,32,128]{2,1,0:T(8,128)(2,1)S(1)}, bf16[8,32,128]{2,1,0:T(8,128)(2,1)S(1)}, u32[]{:S(2)}, u32[]{:S(2)}) collective-permute-start(bf16[8,32,128]{2,1,0:T(8,128)(2,1)S(1)} %get-tuple-element.44), channel_id=1, source_target_pairs={{0,6},{1,7},{2,4},{3,5},{4,2},{5,3},{6,0},{7,1},{8,14},{9,15},{10,... | collective-permute-start | bytes 196616 | tf_op jit(solution)/shard_map/ppermute | solution.py:64
  17.8 0.5 %prepare.1 = (bf16[8,128,128]{2,1,0:T(8,128)(2,1)S(1)}, bf16[8,128,128]{2,1,0:T(8,128)(2,1)S(1)}, f32[4,256,128]{2,1,0:T(8,128)S(1)}, bf16[256,1024]{1,0:T(8,128...) custom-call(bf16[16,64,128]{2,1,0:T(8,128)(2,1)S(1)} %copy-done.2, ...), custom_call_target="tpu_custom_call" | custom-call | flops 1000000000 | bytes 2097152 | tf_op jit(solution)/shard_map/prepare/pallas_call | solution.py:41
  18.3 0.3 collective-permute-done.5.refs_1_
  18.5 1.5 %collective-permute-done.6.refs_2_ = bf16[8,32,128]{2,1,0:T(8,128)(2,1)S(1)} collective-permute-done((bf16[8,32,128]{2,1,0:T(8,128)(2,1)S(1)}, bf16[8,32,128]{2,1,0:T(8,128)(2,1)S(1)}, u32[]{:S(2)}, u32[]{:S(2)}) %collective-permute-start.6) | collective-permute-done | bytes 65568 | tf_op jit(solution)/shard_map/ppermute | solution.py:64
  20.0 2.4 %collective-permute-done.7.refs_3_ = bf16[8,32,128]{2,1,0:T(8,128)(2,1)S(1)} collective-permute-done((bf16[8,32,128]{2,1,0:T(8,128)(2,1)S(1)}, bf16[8,32,128]{2,1,0:T(8,128)(2,1)S(1)}, u32[]{:S(2)}, u32[]{:S(2)}) %collective-permute-start.7) | collective-permute-done | bytes 65568 | tf_op jit(solution)/shard_map/ppermute | solution.py:64
  22.4 2.8 %attend.1 = (bf16[384,128]{1,0:T(8,128)(2,1)S(1)}, bf16[384,128]{1,0:T(8,128)(2,1)S(1)}, bf16[384,128]{1,0:T(8,128)(2,1)S(1)}, bf16[384,128]{1,0:T(8,128)(2,1)S(...) custom-call(bf16[8,32,128]{2,1,0:T(8,128)(2,1)S(1)} %get-tuple-element.41.refs_0_, ...), custom_call_target="tpu_custom_call" | custom-call | flops 4000000000 | bytes 8388608 | tf_op jit(solution)/shard_map/attend/pallas_call | solution.py:41
  25.3 0.6 %collective-permute-start.8 = (bf16[384,128]{1,0:T(8,128)(2,1)S(1)}, bf16[384,128]{1,0:T(8,128)(2,1)S(1)}, u32[]{:S(2)}, u32[]{:S(2)}) collective-permute-start(bf16[384,128]{1,0:T(8,128)(2,1)S(1)} %get-tuple-element.53), channel_id=1, source_target_pairs={{0,2},{1,3},{2,0},{3,1},{4,6},{5,7},{6,4},{7,5},{8,10},{9,11},{10,... | collective-permute-start | bytes 294920 | tf_op jit(solution)/shard_map/ppermute | solution.py:64
  25.9 0.5 %collective-permute-start.9 = (bf16[384,128]{1,0:T(8,128)(2,1)S(1)}, bf16[384,128]{1,0:T(8,128)(2,1)S(1)}, u32[]{:S(2)}, u32[]{:S(2)}) collective-permute-start(bf16[384,128]{1,0:T(8,128)(2,1)S(1)} %get-tuple-element.59), channel_id=1, source_target_pairs={{0,4},{1,5},{2,6},{3,7},{4,0},{5,1},{6,2},{7,3},{8,12},{9,13},{10,... | collective-permute-start | bytes 294920 | tf_op jit(solution)/shard_map/ppermute | solution.py:64
  26.4 2.4 %collective-permute-start.10 = (bf16[384,128]{1,0:T(8,128)(2,1)S(1)}, bf16[384,128]{1,0:T(8,128)(2,1)S(1)}, u32[]{:S(2)}, u32[]{:S(2)}) collective-permute-start(bf16[384,128]{1,0:T(8,128)(2,1)S(1)} %get-tuple-element.60), channel_id=1, source_target_pairs={{0,6},{1,7},{2,4},{3,5},{4,2},{5,3},{6,0},{7,1},{8,14},{9,15},{10,... | collective-permute-start | bytes 294920 | tf_op jit(solution)/shard_map/ppermute | solution.py:64
  28.9 1.2 %collective-permute-done.8._.refs_1_ = bf16[384,128]{1,0:T(8,128)(2,1)S(1)} collective-permute-done((bf16[384,128]{1,0:T(8,128)(2,1)S(1)}, bf16[384,128]{1,0:T(8,128)(2,1)S(1)}, u32[]{:S(2)}, u32[]{:S(2)}) %collective-permute-start.8) | collective-permute-done | bytes 98336 | tf_op jit(solution)/shard_map/ppermute | solution.py:64
  30.0 1.0 %outputs.1 = (bf16[16,64,128]{2,1,0:T(8,128)(2,1)}, f32[8,128]{1,0:T(8,128)S(1)}) custom-call(bf16[8,128,128]{2,1,0:T(8,128)(2,1)S(1)} %get-tuple-element.51.hidden, bf16[128,1024]{1,0:T(8,128)(2,1)S(1)} %get-tuple-element.52.mixed_t, bf16[4,128,128]{2,1,0:T(8,128)(2,1)S(1)} %copy-done.3, bf16[384,128]{1,0:T(8,128)(2,1)S(1)} %collective-permute-done.8._.refs_1_), custom_call_target="tpu_custom_call" | custom-call | flops 1000000000 | bytes 2097152 | tf_op jit(solution)/shard_map/outputs/pallas_call | solution.py:41
  31.0 0.9 %collective-permute-done.10.refs_3_ = bf16[384,128]{1,0:T(8,128)(2,1)S(1)} collective-permute-done((bf16[384,128]{1,0:T(8,128)(2,1)S(1)}, bf16[384,128]{1,0:T(8,128)(2,1)S(1)}, u32[]{:S(2)}, u32[]{:S(2)}) %collective-permute-start.10) | collective-permute-done | bytes 98336 | tf_op jit(solution)/shard_map/ppermute | solution.py:64
  31.9 0.4 sage_back.1
  32.4 0.1 collective-permute-start.12
  32.4 0.5 %collective-permute-start.13 = (bf16[4,2,8,128]{3,2,1,0:T(8,128)(2,1)S(1)}, bf16[4,2,8,128]{3,2,1,0:T(8,128)(2,1)S(1)}, u32[]{:S(2)}, u32[]{:S(2)}) collective-permute-start(bf16[4,2,8,128]{3,2,1,0:T(8,128)(2,1)S(1)} %get-tuple-element.68), channel_id=1, source_target_pairs={{0,1},{1,0},{2,3},{3,2},{4,5},{5,4},{6,7},{7,6},{8,9},{9,8},{10,11... | collective-permute-start | bytes 49160 | tf_op jit(solution)/shard_map/ppermute | solution.py:64
  32.9 0.8 %collective-permute-done.13.refs_3_ = bf16[4,2,8,128]{3,2,1,0:T(8,128)(2,1)S(1)} collective-permute-done((bf16[4,2,8,128]{3,2,1,0:T(8,128)(2,1)S(1)}, bf16[4,2,8,128]{3,2,1,0:T(8,128)(2,1)S(1)}, u32[]{:S(2)}, u32[]{:S(2)}) %collective-permute-start.13) | collective-permute-done | bytes 16416 | tf_op jit(solution)/shard_map/ppermute | solution.py:64
  33.8 2.1 %collective-permute-start.14 = (bf16[2,2,8,128]{3,2,1,0:T(8,128)(2,1)S(1)}, bf16[2,2,8,128]{3,2,1,0:T(8,128)(2,1)S(1)}, u32[]{:S(2)}, u32[]{:S(2)}) collective-permute-start(bf16[2,2,8,128]{3,2,1,0:T(8,128)(2,1)S(1)} %slice.10), channel_id=1, source_target_pairs={{0,16},{8,24},{16,0},{24,8},{1,17},{9,25},{17,1},{25,9},{2,18},{10... | collective-permute-start | bytes 24584 | tf_op jit(solution)/shard_map/ppermute | solution.py:64
  35.9 0.1 collective-permute-start.11
  36.0 2.4 %collective-permute-start.18 = (bf16[384,128]{1,0:T(8,128)(2,1)S(1)}, bf16[384,128]{1,0:T(8,128)(2,1)S(1)}, u32[]{:S(2)}, u32[]{:S(2)}) collective-permute-start(bf16[384,128]{1,0:T(8,128)(2,1)S(1)} %get-tuple-element.70.refs_0_), channel_id=1, source_target_pairs={{0,6},{1,7},{2,4},{3,5},{4,2},{5,3},{6,0},{7,1},{8,14},{9,15},{10,... | collective-permute-start | bytes 294920 | tf_op jit(solution)/shard_map/ppermute | solution.py:64
  38.4 0.5 %collective-permute-start.17 = (bf16[384,128]{1,0:T(8,128)(2,1)S(1)}, bf16[384,128]{1,0:T(8,128)(2,1)S(1)}, u32[]{:S(2)}, u32[]{:S(2)}) collective-permute-start(bf16[384,128]{1,0:T(8,128)(2,1)S(1)} %get-tuple-element.70.refs_0_), channel_id=1, source_target_pairs={{0,4},{1,5},{2,6},{3,7},{4,0},{5,1},{6,2},{7,3},{8,12},{9,13},{10,... | collective-permute-start | bytes 294920 | tf_op jit(solution)/shard_map/ppermute | solution.py:64
  38.9 0.5 %collective-permute-start.16 = (bf16[384,128]{1,0:T(8,128)(2,1)S(1)}, bf16[384,128]{1,0:T(8,128)(2,1)S(1)}, u32[]{:S(2)}, u32[]{:S(2)}) collective-permute-start(bf16[384,128]{1,0:T(8,128)(2,1)S(1)} %get-tuple-element.70.refs_0_), channel_id=1, source_target_pairs={{0,2},{1,3},{2,0},{3,1},{4,6},{5,7},{6,4},{7,5},{8,10},{9,11},{10,... | collective-permute-start | bytes 294920 | tf_op jit(solution)/shard_map/ppermute | solution.py:64
  39.5 0.5 %collective-permute-start.15 = (bf16[1,2,8,128]{3,2,1,0:T(8,128)(2,1)S(1)}, bf16[1,2,8,128]{3,2,1,0:T(8,128)(2,1)S(1)}, u32[]{:S(2)}, u32[]{:S(2)}) collective-permute-start(bf16[1,2,8,128]{3,2,1,0:T(8,128)(2,1)S(1)} %slice.12), channel_id=1, source_target_pairs={{0,8},{8,0},{16,24},{24,16},{1,9},{9,1},{17,25},{25,17},{2,10},{10... | collective-permute-start | bytes 12296 | tf_op jit(solution)/shard_map/ppermute | solution.py:64
  40.0 0.5 %tile_back.1.totals = f32[2,512,128]{2,1,0:T(8,128)S(1)} custom-call(bf16[512,512]{1,0:T(8,128)(2,1)S(1)} %get-tuple-element.56.adj_t, bf16[128,256]{1,0:T(8,128)(2,1)S(1)} %get-tuple-element.57.refs_6_.w_back, bf16[2,256,128]{2,1,0:T(8,128)(2,1)S(1)} %get-tuple-element.64.mine, bf16[2,256,128]{2,1,0:T(8,128)(2,1)S(1)} %collective-permute-done.11.theirs), custom_call_target="tpu_custom_call" | custom-call | flops 1000000000 | bytes 2097152 | tf_op jit(solution)/shard_map/tile_back/pallas_call | solution.py:41
  40.5 1.6 %collective-permute-done.18.refs_3_ = bf16[384,128]{1,0:T(8,128)(2,1)S(1)} collective-permute-done((bf16[384,128]{1,0:T(8,128)(2,1)S(1)}, bf16[384,128]{1,0:T(8,128)(2,1)S(1)}, u32[]{:S(2)}, u32[]{:S(2)}) %collective-permute-start.18) | collective-permute-done | bytes 98336 | tf_op jit(solution)/shard_map/ppermute | solution.py:64
  42.1 2.0 %collective-permute-done.17.refs_2_ = bf16[384,128]{1,0:T(8,128)(2,1)S(1)} collective-permute-done((bf16[384,128]{1,0:T(8,128)(2,1)S(1)}, bf16[384,128]{1,0:T(8,128)(2,1)S(1)}, u32[]{:S(2)}, u32[]{:S(2)}) %collective-permute-start.17) | collective-permute-done | bytes 98336 | tf_op jit(solution)/shard_map/ppermute | solution.py:64
  44.1 0.1 collective-permute-done.16.refs_1_
  44.2 0.8 %weights_out.1 = (f32[768,128]{1,0:T(8,128)}, f32[8,128]{1,0:T(8,128)S(1)}) custom-call(bf16[384,128]{1,0:T(8,128)(2,1)S(1)} %get-tuple-element.70.refs_0_, bf16[384,128]{1,0:T(8,128)(2,1)S(1)} %collective-permute-done.16.refs_1_, bf16[384,128]{1,0:T(8,128)(2,1)S(1)} %collective-permute-done.17.refs_2_, bf16[384,128]{1,0:T(8,128)(2,1)S(1)} %collective-permute-done.18.refs_3_), custom_call_target="tpu_custom_call" | custom-call | flops 1000000000 | bytes 2097152 | tf_op jit(solution)/shard_map/weights_out/pallas_call | solution.py:41
  45.0 1.0 %finish.1 = bf16[2,512,128]{2,1,0:T(8,128)(2,1)} custom-call(bf16[8,512]{1,0:T(8,128)(2,1)S(1)} %get-tuple-element.55.hot, f32[2,512,128]{2,1,0:T(8,128)S(1)} %tile_back.1.totals, bf16[2,2,8,128]{3,2,1,0:T(8,128)(2,1)S(1)} %slice_add_fusion.hub_own, bf16[1,2,8,128]{3,2,1,0:T(8,128)(2,1)S(1)} %collective-permute-done.15.hub_in, f32[8,128]{1,0:T(8,128)S(1)} %get-tuple-element.71._), custom_call_target="tpu_custom_call" | custom-call | flops 1000000000 | bytes 2097152 | tf_op jit(solution)/shard_map/finish/pallas_call | solution.py:41
  (25 shorter events, 0.1 us)
Async XLA Ops:
  0.6 8.5 %copy-start.1 = (bf16[2,512,128]{2,1,0:T(8,128)(2,1)S(1)}, bf16[2,512,128]{2,1,0:T(8,128)(2,1)}, u32[]{:S(2)}) copy-start(bf16[2,512,128]{2,1,0:T(8,128)(2,1)} %feats.1) | copy-start | bytes 786436
  0.6 8.5 %copy-start.4 = (bf16[2,128,128]{2,1,0:T(8,128)(2,1)S(1)}, bf16[2,128,128]{2,1,0:T(8,128)(2,1)}, u32[]{:S(2)}) copy-start(bf16[2,128,128]{2,1,0:T(8,128)(2,1)} %weight.3) | copy-start | bytes 196612
  0.7 8.5 %copy-start = (bf16[12,128,128]{2,1,0:T(8,128)(2,1)S(1)}, bf16[12,128,128]{2,1,0:T(8,128)(2,1)}, u32[]{:S(2)}) copy-start(bf16[12,128,128]{2,1,0:T(8,128)(2,1)} %tiles.1) | copy-start | bytes 1179652
  0.7 8.5 %collective-permute-start = (bf16[2,512,128]{2,1,0:T(8,128)(2,1)}, bf16[2,512,128]{2,1,0:T(8,128)(2,1)S(1)}, u32[]{:S(2)}, u32[]{:S(2)}) collective-permute-start(bf16[2,512,128]{2,1,0:T(8,128)(2,1)} %feats.1), channel_id=1, source_target_pairs={{0,1},{1,0},{2,3},{3,2},{4,5},{5,4},{6,7},{7,6},{8,9},{9,8},{10,11... | collective-permute-start | bytes 786440 | tf_op jit(solution)/shard_map/ppermute | solution.py:64
  3.0 6.1 %copy-start.6 = (s32[12]{0:T(128)S(1)}, s32[12]{0:T(128)}, u32[]{:S(2)}) copy-start(s32[12]{0:T(128)} %param.16) | copy-start | bytes 148
  3.0 6.1 %copy-start.7 = (s32[12]{0:T(128)S(1)}, s32[12]{0:T(128)}, u32[]{:S(2)}) copy-start(s32[12]{0:T(128)} %param.15) | copy-start | bytes 148
  3.0 6.1 %copy-start.8 = (s32[8]{0:T(128)S(1)}, s32[8]{0:T(128)}, u32[]{:S(2)}) copy-start(s32[8]{0:T(128)} %ids.1) | copy-start | bytes 100
  3.0 7.4 %collective-permute-start.3 = (bf16[2,8,128]{2,1,0:T(8,128)(2,1)}, bf16[2,8,128]{2,1,0:T(8,128)(2,1)S(1)}, u32[]{:S(2)}, u32[]{:S(2)}) collective-permute-start(bf16[2,8,128]{2,1,0:T(8,128)(2,1)} %hub_pick.1), channel_id=1, source_target_pairs={{0,24},{8,16},{16,8},{24,0},{1,25},{9,17},{17,9},{25,1},{2,26},{10... | collective-permute-start | bytes 12296 | tf_op jit(solution)/shard_map/ppermute | solution.py:64
  7.8 4.7 %collective-permute-start.2 = (bf16[2,8,128]{2,1,0:T(8,128)(2,1)}, bf16[2,8,128]{2,1,0:T(8,128)(2,1)S(1)}, u32[]{:S(2)}, u32[]{:S(2)}) collective-permute-start(bf16[2,8,128]{2,1,0:T(8,128)(2,1)} %hub_pick.1), channel_id=1, source_target_pairs={{0,16},{8,24},{16,0},{24,8},{1,17},{9,25},{17,1},{25,9},{2,18},{10... | collective-permute-start | bytes 12296 | tf_op jit(solution)/shard_map/ppermute | solution.py:64
  7.8 4.7 %collective-permute-start.1 = (bf16[2,8,128]{2,1,0:T(8,128)(2,1)}, bf16[2,8,128]{2,1,0:T(8,128)(2,1)S(1)}, u32[]{:S(2)}, u32[]{:S(2)}) collective-permute-start(bf16[2,8,128]{2,1,0:T(8,128)(2,1)} %hub_pick.1), channel_id=1, source_target_pairs={{0,8},{8,0},{16,24},{24,16},{1,9},{9,1},{17,25},{25,17},{2,10},{10... | collective-permute-start | bytes 12296 | tf_op jit(solution)/shard_map/ppermute | solution.py:64
  12.5 0.8 %copy-start.5 = (bf16[512,32]{0,1:T(8,128)(2,1)S(1)}, bf16[512,32]{0,1:T(8,128)(2,1)}, u32[]{:S(2)}) copy-start(bf16[512,32]{0,1:T(8,128)(2,1)} %param.19) | copy-start | bytes 98308
  12.5 1.2 %collective-permute-start.4 = (bf16[32,256]{1,0:T(8,128)(2,1)S(1)}, bf16[32,256]{1,0:T(8,128)(2,1)S(1)}, u32[]{:S(2)}, u32[]{:S(2)}) collective-permute-start(bf16[32,256]{1,0:T(8,128)(2,1)S(1)} %by_slab.1.refs_0_), channel_id=1, source_target_pairs={{0,1},{1,0},{2,3},{3,2},{4,5},{5,4},{6,7},{7,6},{8,9},{9,8},{10,11... | collective-permute-start | bytes 49160 | tf_op jit(solution)/shard_map/ppermute | solution.py:64
  13.8 4.0 %copy-start.2 = (bf16[16,64,128]{2,1,0:T(8,128)(2,1)S(1)}, bf16[16,64,128]{2,1,0:T(8,128)(2,1)}, u32[]{:S(2)}) copy-start(bf16[16,64,128]{2,1,0:T(8,128)(2,1)} %cot.1) | copy-start | bytes 786436
  13.8 4.0 %copy-start.3 = (bf16[4,128,128]{2,1,0:T(8,128)(2,1)S(1)}, bf16[4,128,128]{2,1,0:T(8,128)(2,1)}, u32[]{:S(2)}) copy-start(bf16[4,128,128]{2,1,0:T(8,128)(2,1)} %attn.3) | copy-start | bytes 393220
  14.2 4.3 %collective-permute-start.5 = (bf16[8,32,128]{2,1,0:T(8,128)(2,1)S(1)}, bf16[8,32,128]{2,1,0:T(8,128)(2,1)S(1)}, u32[]{:S(2)}, u32[]{:S(2)}) collective-permute-start(bf16[8,32,128]{2,1,0:T(8,128)(2,1)S(1)} %get-tuple-element.42), channel_id=1, source_target_pairs={{0,2},{1,3},{2,0},{3,1},{4,6},{5,7},{6,4},{7,5},{8,10},{9,11},{10,... | collective-permute-start | bytes 196616 | tf_op jit(solution)/shard_map/ppermute | solution.py:64
  15.8 4.3 %collective-permute-start.6 = (bf16[8,32,128]{2,1,0:T(8,128)(2,1)S(1)}, bf16[8,32,128]{2,1,0:T(8,128)(2,1)S(1)}, u32[]{:S(2)}, u32[]{:S(2)}) collective-permute-start(bf16[8,32,128]{2,1,0:T(8,128)(2,1)S(1)} %get-tuple-element.43), channel_id=1, source_target_pairs={{0,4},{1,5},{2,6},{3,7},{4,0},{5,1},{6,2},{7,3},{8,12},{9,13},{10,... | collective-permute-start | bytes 196616 | tf_op jit(solution)/shard_map/ppermute | solution.py:64
  17.3 5.2 %collective-permute-start.7 = (bf16[8,32,128]{2,1,0:T(8,128)(2,1)S(1)}, bf16[8,32,128]{2,1,0:T(8,128)(2,1)S(1)}, u32[]{:S(2)}, u32[]{:S(2)}) collective-permute-start(bf16[8,32,128]{2,1,0:T(8,128)(2,1)S(1)} %get-tuple-element.44), channel_id=1, source_target_pairs={{0,6},{1,7},{2,4},{3,5},{4,2},{5,3},{6,0},{7,1},{8,14},{9,15},{10,... | collective-permute-start | bytes 196616 | tf_op jit(solution)/shard_map/ppermute | solution.py:64
  25.3 4.7 %collective-permute-start.8 = (bf16[384,128]{1,0:T(8,128)(2,1)S(1)}, bf16[384,128]{1,0:T(8,128)(2,1)S(1)}, u32[]{:S(2)}, u32[]{:S(2)}) collective-permute-start(bf16[384,128]{1,0:T(8,128)(2,1)S(1)} %get-tuple-element.53), channel_id=1, source_target_pairs={{0,2},{1,3},{2,0},{3,1},{4,6},{5,7},{6,4},{7,5},{8,10},{9,11},{10,... | collective-permute-start | bytes 294920 | tf_op jit(solution)/shard_map/ppermute | solution.py:64
  25.9 5.1 %collective-permute-start.9 = (bf16[384,128]{1,0:T(8,128)(2,1)S(1)}, bf16[384,128]{1,0:T(8,128)(2,1)S(1)}, u32[]{:S(2)}, u32[]{:S(2)}) collective-permute-start(bf16[384,128]{1,0:T(8,128)(2,1)S(1)} %get-tuple-element.59), channel_id=1, source_target_pairs={{0,4},{1,5},{2,6},{3,7},{4,0},{5,1},{6,2},{7,3},{8,12},{9,13},{10,... | collective-permute-start | bytes 294920 | tf_op jit(solution)/shard_map/ppermute | solution.py:64
  26.4 5.5 %collective-permute-start.10 = (bf16[384,128]{1,0:T(8,128)(2,1)S(1)}, bf16[384,128]{1,0:T(8,128)(2,1)S(1)}, u32[]{:S(2)}, u32[]{:S(2)}) collective-permute-start(bf16[384,128]{1,0:T(8,128)(2,1)S(1)} %get-tuple-element.60), channel_id=1, source_target_pairs={{0,6},{1,7},{2,4},{3,5},{4,2},{5,3},{6,0},{7,1},{8,14},{9,15},{10,... | collective-permute-start | bytes 294920 | tf_op jit(solution)/shard_map/ppermute | solution.py:64
  32.4 1.4 %collective-permute-start.12 = (bf16[384,128]{1,0:T(8,128)(2,1)S(1)}, bf16[384,128]{1,0:T(8,128)(2,1)S(1)}, u32[]{:S(2)}, u32[]{:S(2)}) collective-permute-start(bf16[384,128]{1,0:T(8,128)(2,1)S(1)} %get-tuple-element.66.refs_0_), channel_id=1, source_target_pairs={{0,1},{1,0},{2,3},{3,2},{4,5},{5,4},{6,7},{7,6},{8,9},{9,8},{10,11... | collective-permute-start | bytes 294920 | tf_op jit(solution)/shard_map/ppermute | solution.py:64
  32.4 1.3 %collective-permute-start.13 = (bf16[4,2,8,128]{3,2,1,0:T(8,128)(2,1)S(1)}, bf16[4,2,8,128]{3,2,1,0:T(8,128)(2,1)S(1)}, u32[]{:S(2)}, u32[]{:S(2)}) collective-permute-start(bf16[4,2,8,128]{3,2,1,0:T(8,128)(2,1)S(1)} %get-tuple-element.68), channel_id=1, source_target_pairs={{0,1},{1,0},{2,3},{3,2},{4,5},{5,4},{6,7},{7,6},{8,9},{9,8},{10,11... | collective-permute-start | bytes 49160 | tf_op jit(solution)/shard_map/ppermute | solution.py:64
  33.8 5.6 %collective-permute-start.14 = (bf16[2,2,8,128]{3,2,1,0:T(8,128)(2,1)S(1)}, bf16[2,2,8,128]{3,2,1,0:T(8,128)(2,1)S(1)}, u32[]{:S(2)}, u32[]{:S(2)}) collective-permute-start(bf16[2,2,8,128]{3,2,1,0:T(8,128)(2,1)S(1)} %slice.10), channel_id=1, source_target_pairs={{0,16},{8,24},{16,0},{24,8},{1,17},{9,25},{17,1},{25,9},{2,18},{10... | collective-permute-start | bytes 24584 | tf_op jit(solution)/shard_map/ppermute | solution.py:64
  35.9 4.1 %collective-permute-start.11 = (bf16[2,256,128]{2,1,0:T(8,128)(2,1)S(1)}, bf16[2,256,128]{2,1,0:T(8,128)(2,1)S(1)}, u32[]{:S(2)}, u32[]{:S(2)}) collective-permute-start(bf16[2,256,128]{2,1,0:T(8,128)(2,1)S(1)} %get-tuple-element.65), channel_id=1, source_target_pairs={{0,1},{1,0},{2,3},{3,2},{4,5},{5,4},{6,7},{7,6},{8,9},{9,8},{10,11... | collective-permute-start | bytes 393224 | tf_op jit(solution)/shard_map/ppermute | solution.py:64
  36.0 6.1 %collective-permute-start.18 = (bf16[384,128]{1,0:T(8,128)(2,1)S(1)}, bf16[384,128]{1,0:T(8,128)(2,1)S(1)}, u32[]{:S(2)}, u32[]{:S(2)}) collective-permute-start(bf16[384,128]{1,0:T(8,128)(2,1)S(1)} %get-tuple-element.70.refs_0_), channel_id=1, source_target_pairs={{0,6},{1,7},{2,4},{3,5},{4,2},{5,3},{6,0},{7,1},{8,14},{9,15},{10,... | collective-permute-start | bytes 294920 | tf_op jit(solution)/shard_map/ppermute | solution.py:64
  38.4 5.7 %collective-permute-start.17 = (bf16[384,128]{1,0:T(8,128)(2,1)S(1)}, bf16[384,128]{1,0:T(8,128)(2,1)S(1)}, u32[]{:S(2)}, u32[]{:S(2)}) collective-permute-start(bf16[384,128]{1,0:T(8,128)(2,1)S(1)} %get-tuple-element.70.refs_0_), channel_id=1, source_target_pairs={{0,4},{1,5},{2,6},{3,7},{4,0},{5,1},{6,2},{7,3},{8,12},{9,13},{10,... | collective-permute-start | bytes 294920 | tf_op jit(solution)/shard_map/ppermute | solution.py:64
  38.9 5.3 %collective-permute-start.16 = (bf16[384,128]{1,0:T(8,128)(2,1)S(1)}, bf16[384,128]{1,0:T(8,128)(2,1)S(1)}, u32[]{:S(2)}, u32[]{:S(2)}) collective-permute-start(bf16[384,128]{1,0:T(8,128)(2,1)S(1)} %get-tuple-element.70.refs_0_), channel_id=1, source_target_pairs={{0,2},{1,3},{2,0},{3,1},{4,6},{5,7},{6,4},{7,5},{8,10},{9,11},{10,... | collective-permute-start | bytes 294920 | tf_op jit(solution)/shard_map/ppermute | solution.py:64
  39.5 5.5 %collective-permute-start.15 = (bf16[1,2,8,128]{3,2,1,0:T(8,128)(2,1)S(1)}, bf16[1,2,8,128]{3,2,1,0:T(8,128)(2,1)S(1)}, u32[]{:S(2)}, u32[]{:S(2)}) collective-permute-start(bf16[1,2,8,128]{3,2,1,0:T(8,128)(2,1)S(1)} %slice.12), channel_id=1, source_target_pairs={{0,8},{8,0},{16,24},{24,16},{1,9},{9,1},{17,25},{25,17},{2,10},{10... | collective-permute-start | bytes 12296 | tf_op jit(solution)/shard_map/ppermute | solution.py:64

commit v5 on v4

--- a/solution.py
+++ b/solution.py
@@ -327,7 +327,7 @@
     rows[...] = work[...].astype(BF)
 
 
-def finish(hot, totals, hub_own, hub_in, _, out, work, sems):
+def finish(hot, totals, hub_own, hub_in, out, work, sems):
     layouts, nodes, width = totals.shape
     summed = [hub_own[0, l].astype(F32) + hub_in[0, l].astype(F32) for l in range(layouts)]
     upper = [x.astype(BF) for x in summed]
@@ -344,8 +344,7 @@
 
 
 def weights_out(scale, *refs):
-    sums, (out, done, work) = refs[:-3], refs[-3:]
-    done[...] = jnp.zeros(done.shape, F32)
+    sums, (out, work) = refs[:-2], refs[-2:]
     width = out.shape[1]
     first = 2 * width
     share = sums[0].shape[0] - first
@@ -525,9 +524,9 @@
         hub_sum = hub_sum[:keep] + swapped(hub_sum[keep:], "graph", keep)
     hub_in = swapped(hub_sum[1:], "graph", 1)
     count = sage_weight.shape[0] + attn_weight.shape[0]
-    weights, summed = call(
+    weights = call(
         functools.partial(weights_out, 1.0 / math.sqrt(layouts * node_dev)),
-        (shape((count * width, width), F32), token),
+        shape((count * width, width), F32),
         sums,
         [VMEM] * chips,
         [pltpu.VMEM((chips, 2 * width, width), F32)],
@@ -536,8 +535,8 @@
     grad_features = call(
         finish,
         shape(slab),
-        (hot, totals, hub_sum, hub_in, summed),
-        [VMEM] * 4 + [ANY],
+        (hot, totals, hub_sum, hub_in),
+        [VMEM] * 4,
         [pltpu.VMEM(slab, BF), dma((layout_dev,))],
         outs_at=HBM,
         name="finish",

time: 46.2 us -> 45.2 us (0.978)
  waiting for transfers between devices: 13.3 us -> 12.3 us
    ppermute x19, waiting for transfers between devices: 13.3 us -> 12.3 us  [swapped(): return lax.ppermute(x, axis, [(i, i ^ mask) for i in range(count)])]
  transfers between devices with their start and end apart: 19 -> 19, of which waited for: 11 -> 9; matrix products, arithmetic and copies ran while one was open for 0% -> 0% of each run, Pallas kernels for 13% -> 13%
where the time goes in v5:
time: 45.2 us; the launch traced here: 45 us
  starting transfers between devices  19.8 us (44%)
  waiting for transfers between devices  12.3 us (27%)
  Pallas kernels  10.5 us (23%)
  between operations  1.5 us (3%)
  local copies, waits for them, and re-layouts  0.82 us (2%)
    ppermute x19, starting transfers between devices, swapped(): return lax.ppermute(x, axis, [(i, i ^ mask) for i in range(count)])  19.8 us
    ppermute x19, waiting for transfers between devices, swapped(): return lax.ppermute(x, axis, [(i, i ^ mask) for i in range(count)])  12.3 us
    pallas_call x12, Pallas kernels, call(): pl.pallas_call(kernel, out_shape=outs, in_specs=specs, out_specs=jax.tree...  10.5 us
  transfers between devices with their start and end apart: 19, of which 9 were waited for; matrix products, arithmetic and copies ran while one was open for 0% of the time, Pallas kernels for 13%

profile of v5, /device:TPU:0, one launch (start us, length us, event | category | flops | bytes accessed | tf_op | source)
XLA Modules:
  0.0 45.0 jit_solution(14215078830434549055)
XLA Ops:
  0.7 0.5 %collective-permute-start = (bf16[2,512,128]{2,1,0:T(8,128)(2,1)}, bf16[2,512,128]{2,1,0:T(8,128)(2,1)S(1)}, u32[]{:S(2)}, u32[]{:S(2)}) collective-permute-start(bf16[2,512,128]{2,1,0:T(8,128)(2,1)} %feats.1), channel_id=1, source_target_pairs={{0,1},{1,0},{2,3},{3,2},{4,5},{5,4},{6,7},{7,6},{8,9},{9,8},{10,11... | collective-permute-start | bytes 786440 | tf_op jit(solution)/shard_map/ppermute | solution.py:64
  1.2 1.8 %hub_pick.1 = bf16[2,8,128]{2,1,0:T(8,128)(2,1)} custom-call(s32[8]{0:T(128)} %ids.1, bf16[2,512,128]{2,1,0:T(8,128)(2,1)} %feats.1), custom_call_target="tpu_custom_call" | custom-call | flops 1000000000 | bytes 2097152 | tf_op jit(solution)/shard_map/hub_pick/pallas_call | solution.py:41
  3.0 0.0 copy-start.6
  3.0 0.0 copy-start.7
  3.0 0.0 copy-start.8
  3.0 4.7 %collective-permute-start.3 = (bf16[2,8,128]{2,1,0:T(8,128)(2,1)}, bf16[2,8,128]{2,1,0:T(8,128)(2,1)S(1)}, u32[]{:S(2)}, u32[]{:S(2)}) collective-permute-start(bf16[2,8,128]{2,1,0:T(8,128)(2,1)} %hub_pick.1), channel_id=1, source_target_pairs={{0,24},{8,16},{16,8},{24,0},{1,25},{9,17},{17,9},{25,1},{2,26},{10... | collective-permute-start | bytes 12296 | tf_op jit(solution)/shard_map/ppermute | solution.py:64
  7.8 0.0 collective-permute-start.2
  7.8 0.6 %collective-permute-start.1 = (bf16[2,8,128]{2,1,0:T(8,128)(2,1)}, bf16[2,8,128]{2,1,0:T(8,128)(2,1)S(1)}, u32[]{:S(2)}, u32[]{:S(2)}) collective-permute-start(bf16[2,8,128]{2,1,0:T(8,128)(2,1)} %hub_pick.1), channel_id=1, source_target_pairs={{0,8},{8,0},{16,24},{24,16},{1,9},{9,1},{17,25},{25,17},{2,10},{10... | collective-permute-start | bytes 12296 | tf_op jit(solution)/shard_map/ppermute | solution.py:64
  9.1 0.1 pad_add_fusion.ints
  9.2 0.0 collective-permute-done
  9.2 1.2 %adjacency.1 = (bf16[512,512]{1,0:T(8,128)(2,1)S(1)}, f32[256,512]{1,0:T(8,128)S(1)}, f32[4,256,128]{2,1,0:T(8,128)S(1)}, bf16[4,256,128]{2,1,0:T(8,128)(2,1)S(1...) custom-call(s32[33]{0:T(128)S(1)} %pad_add_fusion.ints, bf16[12,128,128]{2,1,0:T(8,128)(2,1)S(1)} %copy-done, ...), custom_call_target="tpu_custom_call" | custom-call | flops 1000000000 | bytes 2097152 | tf_op jit(solution)/shard_map/adjacency/pallas_call | solution.py:41
  10.4 2.1 %collective-permute-done.2.refs_2_ = bf16[2,8,128]{2,1,0:T(8,128)(2,1)S(1)} collective-permute-done((bf16[2,8,128]{2,1,0:T(8,128)(2,1)}, bf16[2,8,128]{2,1,0:T(8,128)(2,1)S(1)}, u32[]{:S(2)}, u32[]{:S(2)}) %collective-permute-start.2) | collective-permute-done | bytes 4128 | tf_op jit(solution)/shard_map/ppermute | solution.py:64
  12.5 0.1 collective-permute-start.4
  12.6 0.7 %copy-done.5 = bf16[512,32]{0,1:T(8,128)(2,1)S(1)} copy-done((bf16[512,32]{0,1:T(8,128)(2,1)S(1)}, bf16[512,32]{0,1:T(8,128)(2,1)}, u32[]{:S(2)}) %copy-start.5) | copy-done | bytes 32792
  13.2 0.1 copy.13
  13.4 0.4 collective-permute-done.4.refs_1_
  13.8 0.4 sage_out.1
  14.2 1.6 %collective-permute-start.5 = (bf16[8,32,128]{2,1,0:T(8,128)(2,1)S(1)}, bf16[8,32,128]{2,1,0:T(8,128)(2,1)S(1)}, u32[]{:S(2)}, u32[]{:S(2)}) collective-permute-start(bf16[8,32,128]{2,1,0:T(8,128)(2,1)S(1)} %get-tuple-element.40), channel_id=1, source_target_pairs={{0,2},{1,3},{2,0},{3,1},{4,6},{5,7},{6,4},{7,5},{8,10},{9,11},{10,... | collective-permute-start | bytes 196616 | tf_op jit(solution)/shard_map/ppermute | solution.py:64
  15.8 1.5 %collective-permute-start.6 = (bf16[8,32,128]{2,1,0:T(8,128)(2,1)S(1)}, bf16[8,32,128]{2,1,0:T(8,128)(2,1)S(1)}, u32[]{:S(2)}, u32[]{:S(2)}) collective-permute-start(bf16[8,32,128]{2,1,0:T(8,128)(2,1)S(1)} %get-tuple-element.41), channel_id=1, source_target_pairs={{0,4},{1,5},{2,6},{3,7},{4,0},{5,1},{6,2},{7,3},{8,12},{9,13},{10,... | collective-permute-start | bytes 196616 | tf_op jit(solution)/shard_map/ppermute | solution.py:64
  17.3 0.5 %collective-permute-start.7 = (bf16[8,32,128]{2,1,0:T(8,128)(2,1)S(1)}, bf16[8,32,128]{2,1,0:T(8,128)(2,1)S(1)}, u32[]{:S(2)}, u32[]{:S(2)}) collective-permute-start(bf16[8,32,128]{2,1,0:T(8,128)(2,1)S(1)} %get-tuple-element.42), channel_id=1, source_target_pairs={{0,6},{1,7},{2,4},{3,5},{4,2},{5,3},{6,0},{7,1},{8,14},{9,15},{10,... | collective-permute-start | bytes 196616 | tf_op jit(solution)/shard_map/ppermute | solution.py:64
  17.8 0.5 %prepare.1 = (bf16[8,128,128]{2,1,0:T(8,128)(2,1)S(1)}, bf16[8,128,128]{2,1,0:T(8,128)(2,1)S(1)}, f32[4,256,128]{2,1,0:T(8,128)S(1)}, bf16[256,1024]{1,0:T(8,128...) custom-call(bf16[16,64,128]{2,1,0:T(8,128)(2,1)S(1)} %copy-done.2, ...), custom_call_target="tpu_custom_call" | custom-call | flops 1000000000 | bytes 2097152 | tf_op jit(solution)/shard_map/prepare/pallas_call | solution.py:41
  18.3 0.3 collective-permute-done.5.refs_1_
  18.5 1.5 %collective-permute-done.6.refs_2_ = bf16[8,32,128]{2,1,0:T(8,128)(2,1)S(1)} collective-permute-done((bf16[8,32,128]{2,1,0:T(8,128)(2,1)S(1)}, bf16[8,32,128]{2,1,0:T(8,128)(2,1)S(1)}, u32[]{:S(2)}, u32[]{:S(2)}) %collective-permute-start.6) | collective-permute-done | bytes 65568 | tf_op jit(solution)/shard_map/ppermute | solution.py:64
  20.0 2.4 %collective-permute-done.7.refs_3_ = bf16[8,32,128]{2,1,0:T(8,128)(2,1)S(1)} collective-permute-done((bf16[8,32,128]{2,1,0:T(8,128)(2,1)S(1)}, bf16[8,32,128]{2,1,0:T(8,128)(2,1)S(1)}, u32[]{:S(2)}, u32[]{:S(2)}) %collective-permute-start.7) | collective-permute-done | bytes 65568 | tf_op jit(solution)/shard_map/ppermute | solution.py:64
  22.4 2.8 %attend.1 = (bf16[384,128]{1,0:T(8,128)(2,1)S(1)}, bf16[384,128]{1,0:T(8,128)(2,1)S(1)}, bf16[384,128]{1,0:T(8,128)(2,1)S(1)}, bf16[384,128]{1,0:T(8,128)(2,1)S(...) custom-call(bf16[8,32,128]{2,1,0:T(8,128)(2,1)S(1)} %get-tuple-element.39.refs_0_, ...), custom_call_target="tpu_custom_call" | custom-call | flops 4000000000 | bytes 8388608 | tf_op jit(solution)/shard_map/attend/pallas_call | solution.py:41
  25.3 0.6 %collective-permute-start.8 = (bf16[384,128]{1,0:T(8,128)(2,1)S(1)}, bf16[384,128]{1,0:T(8,128)(2,1)S(1)}, u32[]{:S(2)}, u32[]{:S(2)}) collective-permute-start(bf16[384,128]{1,0:T(8,128)(2,1)S(1)} %get-tuple-element.51), channel_id=1, source_target_pairs={{0,2},{1,3},{2,0},{3,1},{4,6},{5,7},{6,4},{7,5},{8,10},{9,11},{10,... | collective-permute-start | bytes 294920 | tf_op jit(solution)/shard_map/ppermute | solution.py:64
  25.9 0.5 %collective-permute-start.9 = (bf16[384,128]{1,0:T(8,128)(2,1)S(1)}, bf16[384,128]{1,0:T(8,128)(2,1)S(1)}, u32[]{:S(2)}, u32[]{:S(2)}) collective-permute-start(bf16[384,128]{1,0:T(8,128)(2,1)S(1)} %get-tuple-element.57), channel_id=1, source_target_pairs={{0,4},{1,5},{2,6},{3,7},{4,0},{5,1},{6,2},{7,3},{8,12},{9,13},{10,... | collective-permute-start | bytes 294920 | tf_op jit(solution)/shard_map/ppermute | solution.py:64
  26.4 2.4 %collective-permute-start.10 = (bf16[384,128]{1,0:T(8,128)(2,1)S(1)}, bf16[384,128]{1,0:T(8,128)(2,1)S(1)}, u32[]{:S(2)}, u32[]{:S(2)}) collective-permute-start(bf16[384,128]{1,0:T(8,128)(2,1)S(1)} %get-tuple-element.58), channel_id=1, source_target_pairs={{0,6},{1,7},{2,4},{3,5},{4,2},{5,3},{6,0},{7,1},{8,14},{9,15},{10,... | collective-permute-start | bytes 294920 | tf_op jit(solution)/shard_map/ppermute | solution.py:64
  28.9 1.2 %collective-permute-done.8._.refs_1_ = bf16[384,128]{1,0:T(8,128)(2,1)S(1)} collective-permute-done((bf16[384,128]{1,0:T(8,128)(2,1)S(1)}, bf16[384,128]{1,0:T(8,128)(2,1)S(1)}, u32[]{:S(2)}, u32[]{:S(2)}) %collective-permute-start.8) | collective-permute-done | bytes 98336 | tf_op jit(solution)/shard_map/ppermute | solution.py:64
  30.0 1.0 %outputs.1 = (bf16[16,64,128]{2,1,0:T(8,128)(2,1)}, f32[8,128]{1,0:T(8,128)S(1)}) custom-call(bf16[8,128,128]{2,1,0:T(8,128)(2,1)S(1)} %get-tuple-element.49.hidden, bf16[128,1024]{1,0:T(8,128)(2,1)S(1)} %get-tuple-element.50.mixed_t, bf16[4,128,128]{2,1,0:T(8,128)(2,1)S(1)} %copy-done.3, bf16[384,128]{1,0:T(8,128)(2,1)S(1)} %collective-permute-done.8._.refs_1_), custom_call_target="tpu_custom_call" | custom-call | flops 1000000000 | bytes 2097152 | tf_op jit(solution)/shard_map/outputs/pallas_call | solution.py:41
  31.0 0.9 %collective-permute-done.10.refs_3_ = bf16[384,128]{1,0:T(8,128)(2,1)S(1)} collective-permute-done((bf16[384,128]{1,0:T(8,128)(2,1)S(1)}, bf16[384,128]{1,0:T(8,128)(2,1)S(1)}, u32[]{:S(2)}, u32[]{:S(2)}) %collective-permute-start.10) | collective-permute-done | bytes 98336 | tf_op jit(solution)/shard_map/ppermute | solution.py:64
  31.9 0.4 sage_back.1
  32.4 0.1 collective-permute-start.12
  32.4 0.5 %collective-permute-start.13 = (bf16[4,2,8,128]{3,2,1,0:T(8,128)(2,1)S(1)}, bf16[4,2,8,128]{3,2,1,0:T(8,128)(2,1)S(1)}, u32[]{:S(2)}, u32[]{:S(2)}) collective-permute-start(bf16[4,2,8,128]{3,2,1,0:T(8,128)(2,1)S(1)} %get-tuple-element.66), channel_id=1, source_target_pairs={{0,1},{1,0},{2,3},{3,2},{4,5},{5,4},{6,7},{7,6},{8,9},{9,8},{10,11... | collective-permute-start | bytes 49160 | tf_op jit(solution)/shard_map/ppermute | solution.py:64
  32.9 0.8 %collective-permute-done.13.refs_3_ = bf16[4,2,8,128]{3,2,1,0:T(8,128)(2,1)S(1)} collective-permute-done((bf16[4,2,8,128]{3,2,1,0:T(8,128)(2,1)S(1)}, bf16[4,2,8,128]{3,2,1,0:T(8,128)(2,1)S(1)}, u32[]{:S(2)}, u32[]{:S(2)}) %collective-permute-start.13) | collective-permute-done | bytes 16416 | tf_op jit(solution)/shard_map/ppermute | solution.py:64
  33.8 2.1 %collective-permute-start.14 = (bf16[2,2,8,128]{3,2,1,0:T(8,128)(2,1)S(1)}, bf16[2,2,8,128]{3,2,1,0:T(8,128)(2,1)S(1)}, u32[]{:S(2)}, u32[]{:S(2)}) collective-permute-start(bf16[2,2,8,128]{3,2,1,0:T(8,128)(2,1)S(1)} %slice.10), channel_id=1, source_target_pairs={{0,16},{8,24},{16,0},{24,8},{1,17},{9,25},{17,1},{25,9},{2,18},{10... | collective-permute-start | bytes 24584 | tf_op jit(solution)/shard_map/ppermute | solution.py:64
  35.9 0.1 collective-permute-start.11
  36.0 2.4 %collective-permute-start.18 = (bf16[384,128]{1,0:T(8,128)(2,1)S(1)}, bf16[384,128]{1,0:T(8,128)(2,1)S(1)}, u32[]{:S(2)}, u32[]{:S(2)}) collective-permute-start(bf16[384,128]{1,0:T(8,128)(2,1)S(1)} %get-tuple-element.68.refs_0_), channel_id=1, source_target_pairs={{0,6},{1,7},{2,4},{3,5},{4,2},{5,3},{6,0},{7,1},{8,14},{9,15},{10,... | collective-permute-start | bytes 294920 | tf_op jit(solution)/shard_map/ppermute | solution.py:64
  38.4 0.5 %collective-permute-start.17 = (bf16[384,128]{1,0:T(8,128)(2,1)S(1)}, bf16[384,128]{1,0:T(8,128)(2,1)S(1)}, u32[]{:S(2)}, u32[]{:S(2)}) collective-permute-start(bf16[384,128]{1,0:T(8,128)(2,1)S(1)} %get-tuple-element.68.refs_0_), channel_id=1, source_target_pairs={{0,4},{1,5},{2,6},{3,7},{4,0},{5,1},{6,2},{7,3},{8,12},{9,13},{10,... | collective-permute-start | bytes 294920 | tf_op jit(solution)/shard_map/ppermute | solution.py:64
  38.9 0.5 %collective-permute-start.16 = (bf16[384,128]{1,0:T(8,128)(2,1)S(1)}, bf16[384,128]{1,0:T(8,128)(2,1)S(1)}, u32[]{:S(2)}, u32[]{:S(2)}) collective-permute-start(bf16[384,128]{1,0:T(8,128)(2,1)S(1)} %get-tuple-element.68.refs_0_), channel_id=1, source_target_pairs={{0,2},{1,3},{2,0},{3,1},{4,6},{5,7},{6,4},{7,5},{8,10},{9,11},{10,... | collective-permute-start | bytes 294920 | tf_op jit(solution)/shard_map/ppermute | solution.py:64
  39.5 0.5 %collective-permute-start.15 = (bf16[1,2,8,128]{3,2,1,0:T(8,128)(2,1)S(1)}, bf16[1,2,8,128]{3,2,1,0:T(8,128)(2,1)S(1)}, u32[]{:S(2)}, u32[]{:S(2)}) collective-permute-start(bf16[1,2,8,128]{3,2,1,0:T(8,128)(2,1)S(1)} %slice.12), channel_id=1, source_target_pairs={{0,8},{8,0},{16,24},{24,16},{1,9},{9,1},{17,25},{25,17},{2,10},{10... | collective-permute-start | bytes 12296 | tf_op jit(solution)/shard_map/ppermute | solution.py:64
  39.9 0.0 collective-permute-done.11.theirs
  40.0 0.5 %tile_back.1.totals = f32[2,512,128]{2,1,0:T(8,128)S(1)} custom-call(bf16[512,512]{1,0:T(8,128)(2,1)S(1)} %get-tuple-element.54.adj_t, bf16[128,256]{1,0:T(8,128)(2,1)S(1)} %get-tuple-element.55.refs_6_.w_back, bf16[2,256,128]{2,1,0:T(8,128)(2,1)S(1)} %get-tuple-element.62.mine, bf16[2,256,128]{2,1,0:T(8,128)(2,1)S(1)} %collective-permute-done.11.theirs), custom_call_target="tpu_custom_call" | custom-call | flops 1000000000 | bytes 2097152 | tf_op jit(solution)/shard_map/tile_back/pallas_call | solution.py:41
  40.5 2.6 %collective-permute-done.15.hub_in = bf16[1,2,8,128]{3,2,1,0:T(8,128)(2,1)S(1)} collective-permute-done((bf16[1,2,8,128]{3,2,1,0:T(8,128)(2,1)S(1)}, bf16[1,2,8,128]{3,2,1,0:T(8,128)(2,1)S(1)}, u32[]{:S(2)}, u32[]{:S(2)}) %collective-permute-start.15) | collective-permute-done | bytes 4128 | tf_op jit(solution)/shard_map/ppermute | solution.py:64
  43.1 1.0 %finish.1 = bf16[2,512,128]{2,1,0:T(8,128)(2,1)} custom-call(bf16[8,512]{1,0:T(8,128)(2,1)S(1)} %get-tuple-element.53.hot, f32[2,512,128]{2,1,0:T(8,128)S(1)} %tile_back.1.totals, bf16[2,2,8,128]{3,2,1,0:T(8,128)(2,1)S(1)} %slice_add_fusion.hub_own, bf16[1,2,8,128]{3,2,1,0:T(8,128)(2,1)S(1)} %collective-permute-done.15.hub_in), custom_call_target="tpu_custom_call" | custom-call | flops 1000000000 | bytes 2097152 | tf_op jit(solution)/shard_map/finish/pallas_call | solution.py:41
  44.1 0.0 collective-permute-done.17.refs_2_
  44.1 0.0 collective-permute-done.16.refs_1_
  44.2 0.8 %weights_out.1 = f32[768,128]{1,0:T(8,128)} custom-call(bf16[384,128]{1,0:T(8,128)(2,1)S(1)} %get-tuple-element.68.refs_0_, bf16[384,128]{1,0:T(8,128)(2,1)S(1)} %collective-permute-done.16.refs_1_, bf16[384,128]{1,0:T(8,128)(2,1)S(1)} %collective-permute-done.17.refs_2_, bf16[384,128]{1,0:T(8,128)(2,1)S(1)} %collective-permute-done.18.refs_3_), custom_call_target="tpu_custom_call" | custom-call | flops 1000000000 | bytes 2097152 | tf_op jit(solution)/shard_map/weights_out/pallas_call | solution.py:41
  (25 shorter events, 0.1 us)
Async XLA Ops:
  0.6 8.5 %copy-start.1 = (bf16[2,512,128]{2,1,0:T(8,128)(2,1)S(1)}, bf16[2,512,128]{2,1,0:T(8,128)(2,1)}, u32[]{:S(2)}) copy-start(bf16[2,512,128]{2,1,0:T(8,128)(2,1)} %feats.1) | copy-start | bytes 786436
  0.6 8.5 %copy-start.4 = (bf16[2,128,128]{2,1,0:T(8,128)(2,1)S(1)}, bf16[2,128,128]{2,1,0:T(8,128)(2,1)}, u32[]{:S(2)}) copy-start(bf16[2,128,128]{2,1,0:T(8,128)(2,1)} %weight.3) | copy-start | bytes 196612
  0.7 8.5 %copy-start = (bf16[12,128,128]{2,1,0:T(8,128)(2,1)S(1)}, bf16[12,128,128]{2,1,0:T(8,128)(2,1)}, u32[]{:S(2)}) copy-start(bf16[12,128,128]{2,1,0:T(8,128)(2,1)} %tiles.1) | copy-start | bytes 1179652
  0.7 8.5 %collective-permute-start = (bf16[2,512,128]{2,1,0:T(8,128)(2,1)}, bf16[2,512,128]{2,1,0:T(8,128)(2,1)S(1)}, u32[]{:S(2)}, u32[]{:S(2)}) collective-permute-start(bf16[2,512,128]{2,1,0:T(8,128)(2,1)} %feats.1), channel_id=1, source_target_pairs={{0,1},{1,0},{2,3},{3,2},{4,5},{5,4},{6,7},{7,6},{8,9},{9,8},{10,11... | collective-permute-start | bytes 786440 | tf_op jit(solution)/shard_map/ppermute | solution.py:64
  3.0 6.1 %copy-start.6 = (s32[12]{0:T(128)S(1)}, s32[12]{0:T(128)}, u32[]{:S(2)}) copy-start(s32[12]{0:T(128)} %param.16) | copy-start | bytes 148
  3.0 6.1 %copy-start.7 = (s32[12]{0:T(128)S(1)}, s32[12]{0:T(128)}, u32[]{:S(2)}) copy-start(s32[12]{0:T(128)} %param.15) | copy-start | bytes 148
  3.0 6.1 %copy-start.8 = (s32[8]{0:T(128)S(1)}, s32[8]{0:T(128)}, u32[]{:S(2)}) copy-start(s32[8]{0:T(128)} %ids.1) | copy-start | bytes 100
  3.0 7.4 %collective-permute-start.3 = (bf16[2,8,128]{2,1,0:T(8,128)(2,1)}, bf16[2,8,128]{2,1,0:T(8,128)(2,1)S(1)}, u32[]{:S(2)}, u32[]{:S(2)}) collective-permute-start(bf16[2,8,128]{2,1,0:T(8,128)(2,1)} %hub_pick.1), channel_id=1, source_target_pairs={{0,24},{8,16},{16,8},{24,0},{1,25},{9,17},{17,9},{25,1},{2,26},{10... | collective-permute-start | bytes 12296 | tf_op jit(solution)/shard_map/ppermute | solution.py:64
  7.8 4.7 %collective-permute-start.2 = (bf16[2,8,128]{2,1,0:T(8,128)(2,1)}, bf16[2,8,128]{2,1,0:T(8,128)(2,1)S(1)}, u32[]{:S(2)}, u32[]{:S(2)}) collective-permute-start(bf16[2,8,128]{2,1,0:T(8,128)(2,1)} %hub_pick.1), channel_id=1, source_target_pairs={{0,16},{8,24},{16,0},{24,8},{1,17},{9,25},{17,1},{25,9},{2,18},{10... | collective-permute-start | bytes 12296 | tf_op jit(solution)/shard_map/ppermute | solution.py:64
  7.8 4.7 %collective-permute-start.1 = (bf16[2,8,128]{2,1,0:T(8,128)(2,1)}, bf16[2,8,128]{2,1,0:T(8,128)(2,1)S(1)}, u32[]{:S(2)}, u32[]{:S(2)}) collective-permute-start(bf16[2,8,128]{2,1,0:T(8,128)(2,1)} %hub_pick.1), channel_id=1, source_target_pairs={{0,8},{8,0},{16,24},{24,16},{1,9},{9,1},{17,25},{25,17},{2,10},{10... | collective-permute-start | bytes 12296 | tf_op jit(solution)/shard_map/ppermute | solution.py:64
  12.5 0.8 %copy-start.5 = (bf16[512,32]{0,1:T(8,128)(2,1)S(1)}, bf16[512,32]{0,1:T(8,128)(2,1)}, u32[]{:S(2)}) copy-start(bf16[512,32]{0,1:T(8,128)(2,1)} %param.19) | copy-start | bytes 98308
  12.5 1.2 %collective-permute-start.4 = (bf16[32,256]{1,0:T(8,128)(2,1)S(1)}, bf16[32,256]{1,0:T(8,128)(2,1)S(1)}, u32[]{:S(2)}, u32[]{:S(2)}) collective-permute-start(bf16[32,256]{1,0:T(8,128)(2,1)S(1)} %by_slab.1.refs_0_), channel_id=1, source_target_pairs={{0,1},{1,0},{2,3},{3,2},{4,5},{5,4},{6,7},{7,6},{8,9},{9,8},{10,11... | collective-permute-start | bytes 49160 | tf_op jit(solution)/shard_map/ppermute | solution.py:64
  13.8 4.0 %copy-start.2 = (bf16[16,64,128]{2,1,0:T(8,128)(2,1)S(1)}, bf16[16,64,128]{2,1,0:T(8,128)(2,1)}, u32[]{:S(2)}) copy-start(bf16[16,64,128]{2,1,0:T(8,128)(2,1)} %cot.1) | copy-start | bytes 786436
  13.8 4.0 %copy-start.3 = (bf16[4,128,128]{2,1,0:T(8,128)(2,1)S(1)}, bf16[4,128,128]{2,1,0:T(8,128)(2,1)}, u32[]{:S(2)}) copy-start(bf16[4,128,128]{2,1,0:T(8,128)(2,1)} %attn.3) | copy-start | bytes 393220
  14.2 4.3 %collective-permute-start.5 = (bf16[8,32,128]{2,1,0:T(8,128)(2,1)S(1)}, bf16[8,32,128]{2,1,0:T(8,128)(2,1)S(1)}, u32[]{:S(2)}, u32[]{:S(2)}) collective-permute-start(bf16[8,32,128]{2,1,0:T(8,128)(2,1)S(1)} %get-tuple-element.40), channel_id=1, source_target_pairs={{0,2},{1,3},{2,0},{3,1},{4,6},{5,7},{6,4},{7,5},{8,10},{9,11},{10,... | collective-permute-start | bytes 196616 | tf_op jit(solution)/shard_map/ppermute | solution.py:64
  15.8 4.3 %collective-permute-start.6 = (bf16[8,32,128]{2,1,0:T(8,128)(2,1)S(1)}, bf16[8,32,128]{2,1,0:T(8,128)(2,1)S(1)}, u32[]{:S(2)}, u32[]{:S(2)}) collective-permute-start(bf16[8,32,128]{2,1,0:T(8,128)(2,1)S(1)} %get-tuple-element.41), channel_id=1, source_target_pairs={{0,4},{1,5},{2,6},{3,7},{4,0},{5,1},{6,2},{7,3},{8,12},{9,13},{10,... | collective-permute-start | bytes 196616 | tf_op jit(solution)/shard_map/ppermute | solution.py:64
  17.3 5.2 %collective-permute-start.7 = (bf16[8,32,128]{2,1,0:T(8,128)(2,1)S(1)}, bf16[8,32,128]{2,1,0:T(8,128)(2,1)S(1)}, u32[]{:S(2)}, u32[]{:S(2)}) collective-permute-start(bf16[8,32,128]{2,1,0:T(8,128)(2,1)S(1)} %get-tuple-element.42), channel_id=1, source_target_pairs={{0,6},{1,7},{2,4},{3,5},{4,2},{5,3},{6,0},{7,1},{8,14},{9,15},{10,... | collective-permute-start | bytes 196616 | tf_op jit(solution)/shard_map/ppermute | solution.py:64
  25.3 4.7 %collective-permute-start.8 = (bf16[384,128]{1,0:T(8,128)(2,1)S(1)}, bf16[384,128]{1,0:T(8,128)(2,1)S(1)}, u32[]{:S(2)}, u32[]{:S(2)}) collective-permute-start(bf16[384,128]{1,0:T(8,128)(2,1)S(1)} %get-tuple-element.51), channel_id=1, source_target_pairs={{0,2},{1,3},{2,0},{3,1},{4,6},{5,7},{6,4},{7,5},{8,10},{9,11},{10,... | collective-permute-start | bytes 294920 | tf_op jit(solution)/shard_map/ppermute | solution.py:64
  25.9 5.1 %collective-permute-start.9 = (bf16[384,128]{1,0:T(8,128)(2,1)S(1)}, bf16[384,128]{1,0:T(8,128)(2,1)S(1)}, u32[]{:S(2)}, u32[]{:S(2)}) collective-permute-start(bf16[384,128]{1,0:T(8,128)(2,1)S(1)} %get-tuple-element.57), channel_id=1, source_target_pairs={{0,4},{1,5},{2,6},{3,7},{4,0},{5,1},{6,2},{7,3},{8,12},{9,13},{10,... | collective-permute-start | bytes 294920 | tf_op jit(solution)/shard_map/ppermute | solution.py:64
  26.4 5.5 %collective-permute-start.10 = (bf16[384,128]{1,0:T(8,128)(2,1)S(1)}, bf16[384,128]{1,0:T(8,128)(2,1)S(1)}, u32[]{:S(2)}, u32[]{:S(2)}) collective-permute-start(bf16[384,128]{1,0:T(8,128)(2,1)S(1)} %get-tuple-element.58), channel_id=1, source_target_pairs={{0,6},{1,7},{2,4},{3,5},{4,2},{5,3},{6,0},{7,1},{8,14},{9,15},{10,... | collective-permute-start | bytes 294920 | tf_op jit(solution)/shard_map/ppermute | solution.py:64
  32.4 1.4 %collective-permute-start.12 = (bf16[384,128]{1,0:T(8,128)(2,1)S(1)}, bf16[384,128]{1,0:T(8,128)(2,1)S(1)}, u32[]{:S(2)}, u32[]{:S(2)}) collective-permute-start(bf16[384,128]{1,0:T(8,128)(2,1)S(1)} %get-tuple-element.64.refs_0_), channel_id=1, source_target_pairs={{0,1},{1,0},{2,3},{3,2},{4,5},{5,4},{6,7},{7,6},{8,9},{9,8},{10,11... | collective-permute-start | bytes 294920 | tf_op jit(solution)/shard_map/ppermute | solution.py:64
  32.4 1.3 %collective-permute-start.13 = (bf16[4,2,8,128]{3,2,1,0:T(8,128)(2,1)S(1)}, bf16[4,2,8,128]{3,2,1,0:T(8,128)(2,1)S(1)}, u32[]{:S(2)}, u32[]{:S(2)}) collective-permute-start(bf16[4,2,8,128]{3,2,1,0:T(8,128)(2,1)S(1)} %get-tuple-element.66), channel_id=1, source_target_pairs={{0,1},{1,0},{2,3},{3,2},{4,5},{5,4},{6,7},{7,6},{8,9},{9,8},{10,11... | collective-permute-start | bytes 49160 | tf_op jit(solution)/shard_map/ppermute | solution.py:64
  33.8 5.6 %collective-permute-start.14 = (bf16[2,2,8,128]{3,2,1,0:T(8,128)(2,1)S(1)}, bf16[2,2,8,128]{3,2,1,0:T(8,128)(2,1)S(1)}, u32[]{:S(2)}, u32[]{:S(2)}) collective-permute-start(bf16[2,2,8,128]{3,2,1,0:T(8,128)(2,1)S(1)} %slice.10), channel_id=1, source_target_pairs={{0,16},{8,24},{16,0},{24,8},{1,17},{9,25},{17,1},{25,9},{2,18},{10... | collective-permute-start | bytes 24584 | tf_op jit(solution)/shard_map/ppermute | solution.py:64
  35.9 4.1 %collective-permute-start.11 = (bf16[2,256,128]{2,1,0:T(8,128)(2,1)S(1)}, bf16[2,256,128]{2,1,0:T(8,128)(2,1)S(1)}, u32[]{:S(2)}, u32[]{:S(2)}) collective-permute-start(bf16[2,256,128]{2,1,0:T(8,128)(2,1)S(1)} %get-tuple-element.63), channel_id=1, source_target_pairs={{0,1},{1,0},{2,3},{3,2},{4,5},{5,4},{6,7},{7,6},{8,9},{9,8},{10,11... | collective-permute-start | bytes 393224 | tf_op jit(solution)/shard_map/ppermute | solution.py:64
  36.0 8.2 %collective-permute-start.18 = (bf16[384,128]{1,0:T(8,128)(2,1)S(1)}, bf16[384,128]{1,0:T(8,128)(2,1)S(1)}, u32[]{:S(2)}, u32[]{:S(2)}) collective-permute-start(bf16[384,128]{1,0:T(8,128)(2,1)S(1)} %get-tuple-element.68.refs_0_), channel_id=1, source_target_pairs={{0,6},{1,7},{2,4},{3,5},{4,2},{5,3},{6,0},{7,1},{8,14},{9,15},{10,... | collective-permute-start | bytes 294920 | tf_op jit(solution)/shard_map/ppermute | solution.py:64
  38.4 5.7 %collective-permute-start.17 = (bf16[384,128]{1,0:T(8,128)(2,1)S(1)}, bf16[384,128]{1,0:T(8,128)(2,1)S(1)}, u32[]{:S(2)}, u32[]{:S(2)}) collective-permute-start(bf16[384,128]{1,0:T(8,128)(2,1)S(1)} %get-tuple-element.68.refs_0_), channel_id=1, source_target_pairs={{0,4},{1,5},{2,6},{3,7},{4,0},{5,1},{6,2},{7,3},{8,12},{9,13},{10,... | collective-permute-start | bytes 294920 | tf_op jit(solution)/shard_map/ppermute | solution.py:64
  38.9 5.3 %collective-permute-start.16 = (bf16[384,128]{1,0:T(8,128)(2,1)S(1)}, bf16[384,128]{1,0:T(8,128)(2,1)S(1)}, u32[]{:S(2)}, u32[]{:S(2)}) collective-permute-start(bf16[384,128]{1,0:T(8,128)(2,1)S(1)} %get-tuple-element.68.refs_0_), channel_id=1, source_target_pairs={{0,2},{1,3},{2,0},{3,1},{4,6},{5,7},{6,4},{7,5},{8,10},{9,11},{10,... | collective-permute-start | bytes 294920 | tf_op jit(solution)/shard_map/ppermute | solution.py:64
  39.5 3.7 %collective-permute-start.15 = (bf16[1,2,8,128]{3,2,1,0:T(8,128)(2,1)S(1)}, bf16[1,2,8,128]{3,2,1,0:T(8,128)(2,1)S(1)}, u32[]{:S(2)}, u32[]{:S(2)}) collective-permute-start(bf16[1,2,8,128]{3,2,1,0:T(8,128)(2,1)S(1)} %slice.12), channel_id=1, source_target_pairs={{0,8},{8,0},{16,24},{24,16},{1,9},{9,1},{17,25},{25,17},{2,10},{10... | collective-permute-start | bytes 12296 | tf_op jit(solution)/shard_map/ppermute | solution.py:64

commit v6 on v5

--- a/solution.py
+++ b/solution.py
@@ -64,6 +64,14 @@
     return lax.ppermute(x, axis, [(i, i ^ mask) for i in range(count)])
 
 
+def steps(count, first):
+    return [0] + [s for s in first if s < count] + [s for s in range(1, count) if s not in first]
+
+
+SLABS = (2, 3, 1)
+CHIPS = (1, 2, 3)
+
+
 def one_hot(ids, hubs, nodes):
     row = lax.broadcasted_iota(jnp.int32, (hubs, nodes), 0)
     col = lax.broadcasted_iota(jnp.int32, (hubs, nodes), 1)
@@ -73,14 +81,17 @@
     return jnp.where(col == want, 1.0, 0.0).astype(BF)
 
 
-def hub_pick(ids, feats, out, ids_s, feats_v, sems):
+def hub_pick(ids, feats, *refs):
+    outs, (ids_s, feats_v, sems) = refs[:-3], refs[-3:]
     layouts, nodes, _ = feats.shape
     copies = fetch([(ids, ids_s)] + [(feats.at[l], feats_v.at[l]) for l in range(layouts)], sems)
     copies[0].wait()
-    hot = one_hot(ids_s, out.shape[1], nodes)
+    hot = one_hot(ids_s, outs[0].shape[1], nodes)
     for l in range(layouts):
         copies[1 + l].wait()
-        out[l] = dot(hot, feats_v[l]).astype(BF)
+        picked = dot(hot, feats_v[l]).astype(BF)
+        for out in outs:
+            out[l] = picked
 
 
 def core_rows(ref, lead, core):
@@ -138,7 +149,7 @@
         act = value / (1.0 + jnp.exp(-value))
         acts.append(act.reshape(chips, groups, SUB, width))
     ready[...] = jnp.concatenate(acts, axis=2).astype(BF)
-    for s, block in enumerate(blocks):
+    for s, block in zip(steps(chips, CHIPS), blocks):
         block[...] = ready[lax.bitwise_xor(me // 2, s)]
 
 
@@ -173,7 +184,7 @@
     rows = shares * depth
     head = width // HEADS
     scale = 1.0 / math.sqrt(head)
-    for s, block in enumerate(blocks):
+    for s, block in zip(steps(chips, CHIPS), blocks):
         for core in range(2):
             hidden[:, lax.bitwise_xor(me, 2 * s + core)] = block[:, core * depth : (core + 1) * depth]
     w_all = jnp.concatenate([attn[0], attn[1], attn[2]], axis=1)
@@ -231,7 +242,7 @@
     shared = grads[...].reshape(chips, -1, width)
     pieces[...] = shared
     count = groups * 2 * depth
-    for s, block in enumerate(outs):
+    for s, block in zip(steps(chips, CHIPS), outs):
         pair = [ready[lax.bitwise_xor(me, 2 * s + core)] for core in range(2)]
         block[0:count] = jnp.concatenate(pair, axis=1).reshape(count, width)
         block[count:] = pieces[lax.bitwise_xor(me // 2, s)]
@@ -258,7 +269,7 @@
     me = lax.axis_index("config")
     nodes = slope.shape[1]
     count = parts.shape[1] * layouts * SUB
-    for s, block in enumerate(blocks):
+    for s, block in zip(steps(chips, CHIPS), blocks):
         parts[lax.bitwise_xor(me // 2, s)] = block[0:count].astype(F32).reshape(parts.shape[1:])
     sums[2 * width :] = sum(block[count:].astype(F32) for block in blocks).astype(BF)
     half = layouts // 2
@@ -320,7 +331,7 @@
     pieces, (rows, work) = refs[:-2], refs[-2:]
     layouts, hubs, width = pieces[0].shape
     slab = lax.axis_index("graph")
-    for s, piece in enumerate(pieces):
+    for s, piece in zip(steps(len(pieces), SLABS), pieces):
         at = pl.ds(pl.multiple_of(lax.bitwise_xor(slab, s) * hubs, hubs), hubs)
         for l in range(layouts):
             work[at, l * width : (l + 1) * width] = piece[l].astype(F32)
@@ -349,7 +360,7 @@
     first = 2 * width
     share = sums[0].shape[0] - first
     chip = lax.axis_index("config") // 2
-    for s, part in enumerate(sums):
+    for s, part in zip(steps(len(sums), CHIPS), sums):
         at = lax.bitwise_xor(chip, s)
         work[at] = part[0:first].astype(F32)
         out[pl.ds(pl.multiple_of(first + at * share, share), share)] = part[first:].astype(F32) * scale
@@ -360,7 +371,8 @@
 
 
 def exchange(blocks):
-    return [swapped(block, "config", 2 * s) if s else block for s, block in enumerate(blocks)]
+    masks = steps(len(blocks), CHIPS)
+    return [swapped(block, "config", 2 * s) if s else block for s, block in zip(masks, blocks)]
 
 
 def local(
@@ -395,16 +407,17 @@
     hub_weight = hub_weight.reshape(chips, 2, share, hubs)
     by_core = (layout_dev, chips, 2, share, width)
 
-    mine = call(
+    picked_shape = (layout_dev, hub_dev, width)
+    picked = call(
         hub_pick,
-        shape((layout_dev, hub_dev, width)),
+        [shape(picked_shape)] * (ranks - 1),
         (hub_ids, features),
         [HBM] * 2,
         [pltpu.SMEM((hub_dev,), jnp.int32), pltpu.VMEM(slab, BF), dma((1 + layout_dev,))],
         limit=WHOLE,
         name="hub_pick",
     )
-    pieces = [swapped(mine, "graph", s) for s in range(1, ranks)]
+    pieces = [swapped(x, "graph", s) for s, x in zip(steps(ranks, SLABS)[1:], picked)]
     other = swapped(features, "config", 1)
 
     adj, summed, pre_self, feats, mine, hot = call(
@@ -414,7 +427,7 @@
             shape((part[1], part[0] * width), F32),
             shape(part, F32),
             shape(part),
-            shape(mine.shape),
+            shape(picked_shape),
             shape((hub_dev, node_dev)),
         ),
         (ints, tile_vals, sage_weight, features.reshape(by_core), other.reshape(by_core)),
@@ -510,7 +523,7 @@
     hub_in = swapped(hub_theirs, "config", 1)
     theirs = swapped(theirs, "config", 1)
     sums, hub_sum = joined(sums, swapped(sums, "config", 1), hub_sum, hub_in)
-    sums = [swapped(sums, "config", 2 * s) if s else sums for s in range(chips)]
+    sums = exchange([sums] * chips)
     totals = call(
         tile_back,
         shape(slab, F32),

time: 45.2 us -> 44.1 us (0.976)
  waiting for transfers between devices: 12.3 us -> 11.3 us
    ppermute x19, waiting for transfers between devices: 12.3 us -> 11.3 us  [swapped(): return lax.ppermute(x, axis, [(i, i ^ mask) for i in range(count)])]
  transfers between devices with their start and end apart: 19 -> 19, of which waited for: 9 -> 9; matrix products, arithmetic and copies ran while one was open for 0% -> 0% of each run, Pallas kernels for 13% -> 14%
where the time goes in v6:
time: 44.1 us; the launch traced here: 43.9 us
  starting transfers between devices  19.8 us (45%)
  waiting for transfers between devices  11.3 us (26%)
  Pallas kernels  10.5 us (24%)
  between operations  1.49 us (3%)
  local copies, waits for them, and re-layouts  0.82 us (2%)
    ppermute x19, starting transfers between devices, swapped(): return lax.ppermute(x, axis, [(i, i ^ mask) for i in range(count)])  19.8 us
    ppermute x19, waiting for transfers between devices, swapped(): return lax.ppermute(x, axis, [(i, i ^ mask) for i in range(count)])  11.3 us
    pallas_call x12, Pallas kernels, call(): pl.pallas_call(kernel, out_shape=outs, in_specs=specs, out_specs=jax.tree...  10.5 us
  transfers between devices with their start and end apart: 19, of which 9 were waited for; matrix products, arithmetic and copies ran while one was open for 0% of the time, Pallas kernels for 14%

profile of v6, /device:TPU:0, one launch (start us, length us, event | category | flops | bytes accessed | tf_op | source)
XLA Modules:
  0.0 43.9 jit_solution(7763077211164859904)
XLA Ops:
  0.7 0.5 %collective-permute-start = (bf16[2,512,128]{2,1,0:T(8,128)(2,1)}, bf16[2,512,128]{2,1,0:T(8,128)(2,1)S(1)}, u32[]{:S(2)}, u32[]{:S(2)}) collective-permute-start(bf16[2,512,128]{2,1,0:T(8,128)(2,1)} %feats.1), channel_id=1, source_target_pairs={{0,1},{1,0},{2,3},{3,2},{4,5},{5,4},{6,7},{7,6},{8,9},{9,8},{10,11... | collective-permute-start | bytes 786440 | tf_op jit(solution)/shard_map/ppermute | solution.py:64
  1.2 1.8 %hub_pick.1 = (bf16[2,8,128]{2,1,0:T(8,128)(2,1)}, bf16[2,8,128]{2,1,0:T(8,128)(2,1)}, bf16[2,8,128]{2,1,0:T(8,128)(2,1)}) custom-call(s32[8]{0:T(128)} %ids.1, bf16[2,512,128]{2,1,0:T(8,128)(2,1)} %feats.1), custom_call_target="tpu_custom_call" | custom-call | flops 1000000000 | bytes 2097152 | tf_op jit(solution)/shard_map/hub_pick/pallas_call | solution.py:41
  3.0 0.0 copy-start.9
  3.0 3.7 %collective-permute-start.1 = (bf16[2,8,128]{2,1,0:T(8,128)(2,1)}, bf16[2,8,128]{2,1,0:T(8,128)(2,1)S(1)}, u32[]{:S(2)}, u32[]{:S(2)}) collective-permute-start(bf16[2,8,128]{2,1,0:T(8,128)(2,1)} %get-tuple-element.40), channel_id=1, source_target_pairs={{0,16},{8,24},{16,0},{24,8},{1,17},{9,25},{17,1},{25,9},{2,18},{10... | collective-permute-start | bytes 12296 | tf_op jit(solution)/shard_map/ppermute | solution.py:64
  6.7 1.3 %collective-permute-start.2 = (bf16[2,8,128]{2,1,0:T(8,128)(2,1)}, bf16[2,8,128]{2,1,0:T(8,128)(2,1)S(1)}, u32[]{:S(2)}, u32[]{:S(2)}) collective-permute-start(bf16[2,8,128]{2,1,0:T(8,128)(2,1)} %get-tuple-element.41), channel_id=1, source_target_pairs={{0,24},{8,16},{16,8},{24,0},{1,25},{9,17},{17,9},{25,1},{2,26},{10... | collective-permute-start | bytes 12296 | tf_op jit(solution)/shard_map/ppermute | solution.py:64
  8.1 0.3 collective-permute-start.3
  9.1 0.1 pad_add_fusion.ints
  9.2 0.0 collective-permute-done
  9.2 1.2 %adjacency.1 = (bf16[512,512]{1,0:T(8,128)(2,1)S(1)}, f32[256,512]{1,0:T(8,128)S(1)}, f32[4,256,128]{2,1,0:T(8,128)S(1)}, bf16[4,256,128]{2,1,0:T(8,128)(2,1)S(1...) custom-call(s32[33]{0:T(128)S(1)} %pad_add_fusion.ints, bf16[12,128,128]{2,1,0:T(8,128)(2,1)S(1)} %copy-done, ...), custom_call_target="tpu_custom_call" | custom-call | flops 1000000000 | bytes 2097152 | tf_op jit(solution)/shard_map/adjacency/pallas_call | solution.py:41
  10.4 2.0 %collective-permute-done.2.refs_2_ = bf16[2,8,128]{2,1,0:T(8,128)(2,1)S(1)} collective-permute-done((bf16[2,8,128]{2,1,0:T(8,128)(2,1)}, bf16[2,8,128]{2,1,0:T(8,128)(2,1)S(1)}, u32[]{:S(2)}, u32[]{:S(2)}) %collective-permute-start.2) | collective-permute-done | bytes 4128 | tf_op jit(solution)/shard_map/ppermute | solution.py:64
  12.4 0.0 collective-permute-done.3.refs_3_
  12.4 0.1 collective-permute-start.4
  12.5 0.7 %copy-done.5 = bf16[512,32]{0,1:T(8,128)(2,1)S(1)} copy-done((bf16[512,32]{0,1:T(8,128)(2,1)S(1)}, bf16[512,32]{0,1:T(8,128)(2,1)}, u32[]{:S(2)}) %copy-start.5) | copy-done | bytes 32792
  13.1 0.1 copy.13
  13.2 0.4 collective-permute-done.4.refs_1_
  13.6 0.4 sage_out.1
  14.1 1.6 %collective-permute-start.5 = (bf16[8,32,128]{2,1,0:T(8,128)(2,1)S(1)}, bf16[8,32,128]{2,1,0:T(8,128)(2,1)S(1)}, u32[]{:S(2)}, u32[]{:S(2)}) collective-permute-start(bf16[8,32,128]{2,1,0:T(8,128)(2,1)S(1)} %get-tuple-element.46), channel_id=1, source_target_pairs={{0,2},{1,3},{2,0},{3,1},{4,6},{5,7},{6,4},{7,5},{8,10},{9,11},{10,... | collective-permute-start | bytes 196616 | tf_op jit(solution)/shard_map/ppermute | solution.py:64
  15.6 1.5 %collective-permute-start.6 = (bf16[8,32,128]{2,1,0:T(8,128)(2,1)S(1)}, bf16[8,32,128]{2,1,0:T(8,128)(2,1)S(1)}, u32[]{:S(2)}, u32[]{:S(2)}) collective-permute-start(bf16[8,32,128]{2,1,0:T(8,128)(2,1)S(1)} %get-tuple-element.47), channel_id=1, source_target_pairs={{0,4},{1,5},{2,6},{3,7},{4,0},{5,1},{6,2},{7,3},{8,12},{9,13},{10,... | collective-permute-start | bytes 196616 | tf_op jit(solution)/shard_map/ppermute | solution.py:64
  17.2 0.5 %collective-permute-start.7 = (bf16[8,32,128]{2,1,0:T(8,128)(2,1)S(1)}, bf16[8,32,128]{2,1,0:T(8,128)(2,1)S(1)}, u32[]{:S(2)}, u32[]{:S(2)}) collective-permute-start(bf16[8,32,128]{2,1,0:T(8,128)(2,1)S(1)} %get-tuple-element.48), channel_id=1, source_target_pairs={{0,6},{1,7},{2,4},{3,5},{4,2},{5,3},{6,0},{7,1},{8,14},{9,15},{10,... | collective-permute-start | bytes 196616 | tf_op jit(solution)/shard_map/ppermute | solution.py:64
  17.6 0.5 %prepare.1 = (bf16[8,128,128]{2,1,0:T(8,128)(2,1)S(1)}, bf16[8,128,128]{2,1,0:T(8,128)(2,1)S(1)}, f32[4,256,128]{2,1,0:T(8,128)S(1)}, bf16[256,1024]{1,0:T(8,128...) custom-call(bf16[16,64,128]{2,1,0:T(8,128)(2,1)S(1)} %copy-done.2, ...), custom_call_target="tpu_custom_call" | custom-call | flops 1000000000 | bytes 2097152 | tf_op jit(solution)/shard_map/prepare/pallas_call | solution.py:41
  18.1 0.3 collective-permute-done.5.refs_1_
  18.4 1.5 %collective-permute-done.6.refs_2_ = bf16[8,32,128]{2,1,0:T(8,128)(2,1)S(1)} collective-permute-done((bf16[8,32,128]{2,1,0:T(8,128)(2,1)S(1)}, bf16[8,32,128]{2,1,0:T(8,128)(2,1)S(1)}, u32[]{:S(2)}, u32[]{:S(2)}) %collective-permute-start.6) | collective-permute-done | bytes 65568 | tf_op jit(solution)/shard_map/ppermute | solution.py:64
  19.9 2.4 %collective-permute-done.7.refs_3_ = bf16[8,32,128]{2,1,0:T(8,128)(2,1)S(1)} collective-permute-done((bf16[8,32,128]{2,1,0:T(8,128)(2,1)S(1)}, bf16[8,32,128]{2,1,0:T(8,128)(2,1)S(1)}, u32[]{:S(2)}, u32[]{:S(2)}) %collective-permute-start.7) | collective-permute-done | bytes 65568 | tf_op jit(solution)/shard_map/ppermute | solution.py:64
  22.3 2.8 %attend.1 = (bf16[384,128]{1,0:T(8,128)(2,1)S(1)}, bf16[384,128]{1,0:T(8,128)(2,1)S(1)}, bf16[384,128]{1,0:T(8,128)(2,1)S(1)}, bf16[384,128]{1,0:T(8,128)(2,1)S(...) custom-call(bf16[8,32,128]{2,1,0:T(8,128)(2,1)S(1)} %get-tuple-element.45.refs_0_, ...), custom_call_target="tpu_custom_call" | custom-call | flops 4000000000 | bytes 8388608 | tf_op jit(solution)/shard_map/attend/pallas_call | solution.py:41
  25.2 0.6 %collective-permute-start.8 = (bf16[384,128]{1,0:T(8,128)(2,1)S(1)}, bf16[384,128]{1,0:T(8,128)(2,1)S(1)}, u32[]{:S(2)}, u32[]{:S(2)}) collective-permute-start(bf16[384,128]{1,0:T(8,128)(2,1)S(1)} %get-tuple-element.57), channel_id=1, source_target_pairs={{0,2},{1,3},{2,0},{3,1},{4,6},{5,7},{6,4},{7,5},{8,10},{9,11},{10,... | collective-permute-start | bytes 294920 | tf_op jit(solution)/shard_map/ppermute | solution.py:64
  25.7 0.5 %collective-permute-start.9 = (bf16[384,128]{1,0:T(8,128)(2,1)S(1)}, bf16[384,128]{1,0:T(8,128)(2,1)S(1)}, u32[]{:S(2)}, u32[]{:S(2)}) collective-permute-start(bf16[384,128]{1,0:T(8,128)(2,1)S(1)} %get-tuple-element.63), channel_id=1, source_target_pairs={{0,4},{1,5},{2,6},{3,7},{4,0},{5,1},{6,2},{7,3},{8,12},{9,13},{10,... | collective-permute-start | bytes 294920 | tf_op jit(solution)/shard_map/ppermute | solution.py:64
  26.3 2.5 %collective-permute-start.10 = (bf16[384,128]{1,0:T(8,128)(2,1)S(1)}, bf16[384,128]{1,0:T(8,128)(2,1)S(1)}, u32[]{:S(2)}, u32[]{:S(2)}) collective-permute-start(bf16[384,128]{1,0:T(8,128)(2,1)S(1)} %get-tuple-element.64), channel_id=1, source_target_pairs={{0,6},{1,7},{2,4},{3,5},{4,2},{5,3},{6,0},{7,1},{8,14},{9,15},{10,... | collective-permute-start | bytes 294920 | tf_op jit(solution)/shard_map/ppermute | solution.py:64
  28.7 1.2 %collective-permute-done.8._.refs_1_ = bf16[384,128]{1,0:T(8,128)(2,1)S(1)} collective-permute-done((bf16[384,128]{1,0:T(8,128)(2,1)S(1)}, bf16[384,128]{1,0:T(8,128)(2,1)S(1)}, u32[]{:S(2)}, u32[]{:S(2)}) %collective-permute-start.8) | collective-permute-done | bytes 98336 | tf_op jit(solution)/shard_map/ppermute | solution.py:64
  29.9 1.0 %outputs.1 = (bf16[16,64,128]{2,1,0:T(8,128)(2,1)}, f32[8,128]{1,0:T(8,128)S(1)}) custom-call(bf16[8,128,128]{2,1,0:T(8,128)(2,1)S(1)} %get-tuple-element.55.hidden, bf16[128,1024]{1,0:T(8,128)(2,1)S(1)} %get-tuple-element.56.mixed_t, bf16[4,128,128]{2,1,0:T(8,128)(2,1)S(1)} %copy-done.3, bf16[384,128]{1,0:T(8,128)(2,1)S(1)} %collective-permute-done.8._.refs_1_), custom_call_target="tpu_custom_call" | custom-call | flops 1000000000 | bytes 2097152 | tf_op jit(solution)/shard_map/outputs/pallas_call | solution.py:41
  30.9 0.0 collective-permute-done.9.refs_2_
  30.9 0.9 %collective-permute-done.10.refs_3_ = bf16[384,128]{1,0:T(8,128)(2,1)S(1)} collective-permute-done((bf16[384,128]{1,0:T(8,128)(2,1)S(1)}, bf16[384,128]{1,0:T(8,128)(2,1)S(1)}, u32[]{:S(2)}, u32[]{:S(2)}) %collective-permute-start.10) | collective-permute-done | bytes 98336 | tf_op jit(solution)/shard_map/ppermute | solution.py:64
  31.8 0.4 sage_back.1
  32.2 0.1 collective-permute-start.12
  32.3 0.5 %collective-permute-start.13 = (bf16[4,2,8,128]{3,2,1,0:T(8,128)(2,1)S(1)}, bf16[4,2,8,128]{3,2,1,0:T(8,128)(2,1)S(1)}, u32[]{:S(2)}, u32[]{:S(2)}) collective-permute-start(bf16[4,2,8,128]{3,2,1,0:T(8,128)(2,1)S(1)} %get-tuple-element.72), channel_id=1, source_target_pairs={{0,1},{1,0},{2,3},{3,2},{4,5},{5,4},{6,7},{7,6},{8,9},{9,8},{10,11... | collective-permute-start | bytes 49160 | tf_op jit(solution)/shard_map/ppermute | solution.py:64
  32.8 0.8 %collective-permute-done.13.refs_3_ = bf16[4,2,8,128]{3,2,1,0:T(8,128)(2,1)S(1)} collective-permute-done((bf16[4,2,8,128]{3,2,1,0:T(8,128)(2,1)S(1)}, bf16[4,2,8,128]{3,2,1,0:T(8,128)(2,1)S(1)}, u32[]{:S(2)}, u32[]{:S(2)}) %collective-permute-start.13) | collective-permute-done | bytes 16416 | tf_op jit(solution)/shard_map/ppermute | solution.py:64
  33.6 1.2 %collective-permute-start.14 = (bf16[2,2,8,128]{3,2,1,0:T(8,128)(2,1)S(1)}, bf16[2,2,8,128]{3,2,1,0:T(8,128)(2,1)S(1)}, u32[]{:S(2)}, u32[]{:S(2)}) collective-permute-start(bf16[2,2,8,128]{3,2,1,0:T(8,128)(2,1)S(1)} %slice.10), channel_id=1, source_target_pairs={{0,16},{8,24},{16,0},{24,8},{1,17},{9,25},{17,1},{25,9},{2,18},{10... | collective-permute-start | bytes 24584 | tf_op jit(solution)/shard_map/ppermute | solution.py:64
  34.8 0.1 collective-permute-start.11
  34.9 2.4 %collective-permute-start.18 = (bf16[384,128]{1,0:T(8,128)(2,1)S(1)}, bf16[384,128]{1,0:T(8,128)(2,1)S(1)}, u32[]{:S(2)}, u32[]{:S(2)}) collective-permute-start(bf16[384,128]{1,0:T(8,128)(2,1)S(1)} %get-tuple-element.74.refs_0_), channel_id=1, source_target_pairs={{0,6},{1,7},{2,4},{3,5},{4,2},{5,3},{6,0},{7,1},{8,14},{9,15},{10,... | collective-permute-start | bytes 294920 | tf_op jit(solution)/shard_map/ppermute | solution.py:64
  37.3 0.5 %collective-permute-start.17 = (bf16[384,128]{1,0:T(8,128)(2,1)S(1)}, bf16[384,128]{1,0:T(8,128)(2,1)S(1)}, u32[]{:S(2)}, u32[]{:S(2)}) collective-permute-start(bf16[384,128]{1,0:T(8,128)(2,1)S(1)} %get-tuple-element.74.refs_0_), channel_id=1, source_target_pairs={{0,4},{1,5},{2,6},{3,7},{4,0},{5,1},{6,2},{7,3},{8,12},{9,13},{10,... | collective-permute-start | bytes 294920 | tf_op jit(solution)/shard_map/ppermute | solution.py:64
  37.8 0.5 %collective-permute-start.16 = (bf16[384,128]{1,0:T(8,128)(2,1)S(1)}, bf16[384,128]{1,0:T(8,128)(2,1)S(1)}, u32[]{:S(2)}, u32[]{:S(2)}) collective-permute-start(bf16[384,128]{1,0:T(8,128)(2,1)S(1)} %get-tuple-element.74.refs_0_), channel_id=1, source_target_pairs={{0,2},{1,3},{2,0},{3,1},{4,6},{5,7},{6,4},{7,5},{8,10},{9,11},{10,... | collective-permute-start | bytes 294920 | tf_op jit(solution)/shard_map/ppermute | solution.py:64
  38.4 0.0 collective-permute-done.14
  38.4 1.4 %collective-permute-start.15 = (bf16[1,2,8,128]{3,2,1,0:T(8,128)(2,1)S(1)}, bf16[1,2,8,128]{3,2,1,0:T(8,128)(2,1)S(1)}, u32[]{:S(2)}, u32[]{:S(2)}) collective-permute-start(bf16[1,2,8,128]{3,2,1,0:T(8,128)(2,1)S(1)} %slice.12), channel_id=1, source_target_pairs={{0,8},{8,0},{16,24},{24,16},{1,9},{9,1},{17,25},{25,17},{2,10},{10... | collective-permute-start | bytes 12296 | tf_op jit(solution)/shard_map/ppermute | solution.py:64
  39.8 0.0 collective-permute-done.11.theirs
  39.8 0.5 %tile_back.1.totals = f32[2,512,128]{2,1,0:T(8,128)S(1)} custom-call(bf16[512,512]{1,0:T(8,128)(2,1)S(1)} %get-tuple-element.60.adj_t, bf16[128,256]{1,0:T(8,128)(2,1)S(1)} %get-tuple-element.61.refs_6_.w_back, bf16[2,256,128]{2,1,0:T(8,128)(2,1)S(1)} %get-tuple-element.68.mine, bf16[2,256,128]{2,1,0:T(8,128)(2,1)S(1)} %collective-permute-done.11.theirs), custom_call_target="tpu_custom_call" | custom-call | flops 1000000000 | bytes 2097152 | tf_op jit(solution)/shard_map/tile_back/pallas_call | solution.py:41
  40.4 1.7 %collective-permute-done.15.hub_in = bf16[1,2,8,128]{3,2,1,0:T(8,128)(2,1)S(1)} collective-permute-done((bf16[1,2,8,128]{3,2,1,0:T(8,128)(2,1)S(1)}, bf16[1,2,8,128]{3,2,1,0:T(8,128)(2,1)S(1)}, u32[]{:S(2)}, u32[]{:S(2)}) %collective-permute-start.15) | collective-permute-done | bytes 4128 | tf_op jit(solution)/shard_map/ppermute | solution.py:64
  42.1 1.0 %finish.1 = bf16[2,512,128]{2,1,0:T(8,128)(2,1)} custom-call(bf16[8,512]{1,0:T(8,128)(2,1)S(1)} %get-tuple-element.59.hot, f32[2,512,128]{2,1,0:T(8,128)S(1)} %tile_back.1.totals, bf16[2,2,8,128]{3,2,1,0:T(8,128)(2,1)S(1)} %slice_add_fusion.hub_own, bf16[1,2,8,128]{3,2,1,0:T(8,128)(2,1)S(1)} %collective-permute-done.15.hub_in), custom_call_target="tpu_custom_call" | custom-call | flops 1000000000 | bytes 2097152 | tf_op jit(solution)/shard_map/finish/pallas_call | solution.py:41
  43.0 0.0 collective-permute-done.16.refs_1_
  43.1 0.8 %weights_out.1 = f32[768,128]{1,0:T(8,128)} custom-call(bf16[384,128]{1,0:T(8,128)(2,1)S(1)} %get-tuple-element.74.refs_0_, bf16[384,128]{1,0:T(8,128)(2,1)S(1)} %collective-permute-done.16.refs_1_, bf16[384,128]{1,0:T(8,128)(2,1)S(1)} %collective-permute-done.17.refs_2_, bf16[384,128]{1,0:T(8,128)(2,1)S(1)} %collective-permute-done.18.refs_3_), custom_call_target="tpu_custom_call" | custom-call | flops 1000000000 | bytes 2097152 | tf_op jit(solution)/shard_map/weights_out/pallas_call | solution.py:41
  (27 shorter events, 0.1 us)
Async XLA Ops:
  0.6 8.5 %copy-start.1 = (bf16[2,512,128]{2,1,0:T(8,128)(2,1)S(1)}, bf16[2,512,128]{2,1,0:T(8,128)(2,1)}, u32[]{:S(2)}) copy-start(bf16[2,512,128]{2,1,0:T(8,128)(2,1)} %feats.1) | copy-start | bytes 786436
  0.6 8.5 %copy-start.4 = (bf16[2,128,128]{2,1,0:T(8,128)(2,1)S(1)}, bf16[2,128,128]{2,1,0:T(8,128)(2,1)}, u32[]{:S(2)}) copy-start(bf16[2,128,128]{2,1,0:T(8,128)(2,1)} %weight.3) | copy-start | bytes 196612
  0.7 8.5 %copy-start = (bf16[12,128,128]{2,1,0:T(8,128)(2,1)S(1)}, bf16[12,128,128]{2,1,0:T(8,128)(2,1)}, u32[]{:S(2)}) copy-start(bf16[12,128,128]{2,1,0:T(8,128)(2,1)} %tiles.1) | copy-start | bytes 1179652
  0.7 8.5 %collective-permute-start = (bf16[2,512,128]{2,1,0:T(8,128)(2,1)}, bf16[2,512,128]{2,1,0:T(8,128)(2,1)S(1)}, u32[]{:S(2)}, u32[]{:S(2)}) collective-permute-start(bf16[2,512,128]{2,1,0:T(8,128)(2,1)} %feats.1), channel_id=1, source_target_pairs={{0,1},{1,0},{2,3},{3,2},{4,5},{5,4},{6,7},{7,6},{8,9},{9,8},{10,11... | collective-permute-start | bytes 786440 | tf_op jit(solution)/shard_map/ppermute | solution.py:64
  3.0 5.1 %copy-start.9 = (bf16[2,8,128]{2,1,0:T(8,128)(2,1)S(1)}, bf16[2,8,128]{2,1,0:T(8,128)(2,1)}, u32[]{:S(2)}) copy-start(bf16[2,8,128]{2,1,0:T(8,128)(2,1)} %get-tuple-element.42) | copy-start | bytes 12292
  3.0 7.4 %collective-permute-start.1 = (bf16[2,8,128]{2,1,0:T(8,128)(2,1)}, bf16[2,8,128]{2,1,0:T(8,128)(2,1)S(1)}, u32[]{:S(2)}, u32[]{:S(2)}) collective-permute-start(bf16[2,8,128]{2,1,0:T(8,128)(2,1)} %get-tuple-element.40), channel_id=1, source_target_pairs={{0,16},{8,24},{16,0},{24,8},{1,17},{9,25},{17,1},{25,9},{2,18},{10... | collective-permute-start | bytes 12296 | tf_op jit(solution)/shard_map/ppermute | solution.py:64
  6.7 5.6 %collective-permute-start.2 = (bf16[2,8,128]{2,1,0:T(8,128)(2,1)}, bf16[2,8,128]{2,1,0:T(8,128)(2,1)S(1)}, u32[]{:S(2)}, u32[]{:S(2)}) collective-permute-start(bf16[2,8,128]{2,1,0:T(8,128)(2,1)} %get-tuple-element.41), channel_id=1, source_target_pairs={{0,24},{8,16},{16,8},{24,0},{1,25},{9,17},{17,9},{25,1},{2,26},{10... | collective-permute-start | bytes 12296 | tf_op jit(solution)/shard_map/ppermute | solution.py:64
  8.1 1.0 %copy-start.6 = (s32[12]{0:T(128)S(1)}, s32[12]{0:T(128)}, u32[]{:S(2)}) copy-start(s32[12]{0:T(128)} %param.16) | copy-start | bytes 148
  8.1 1.0 %copy-start.7 = (s32[12]{0:T(128)S(1)}, s32[12]{0:T(128)}, u32[]{:S(2)}) copy-start(s32[12]{0:T(128)} %param.15) | copy-start | bytes 148
  8.1 1.0 %copy-start.8 = (s32[8]{0:T(128)S(1)}, s32[8]{0:T(128)}, u32[]{:S(2)}) copy-start(s32[8]{0:T(128)} %ids.1) | copy-start | bytes 100
  8.1 4.3 %collective-permute-start.3 = (bf16[2,8,128]{2,1,0:T(8,128)(2,1)S(1)}, bf16[2,8,128]{2,1,0:T(8,128)(2,1)S(1)}, u32[]{:S(2)}, u32[]{:S(2)}) collective-permute-start(bf16[2,8,128]{2,1,0:T(8,128)(2,1)S(1)} %copy-done.9), channel_id=1, source_target_pairs={{0,8},{8,0},{16,24},{24,16},{1,9},{9,1},{17,25},{25,17},{2,10},{10... | collective-permute-start | bytes 12296 | tf_op jit(solution)/shard_map/ppermute | solution.py:64
  12.4 0.8 %copy-start.5 = (bf16[512,32]{0,1:T(8,128)(2,1)S(1)}, bf16[512,32]{0,1:T(8,128)(2,1)}, u32[]{:S(2)}) copy-start(bf16[512,32]{0,1:T(8,128)(2,1)} %param.19) | copy-start | bytes 98308
  12.4 1.2 %collective-permute-start.4 = (bf16[32,256]{1,0:T(8,128)(2,1)S(1)}, bf16[32,256]{1,0:T(8,128)(2,1)S(1)}, u32[]{:S(2)}, u32[]{:S(2)}) collective-permute-start(bf16[32,256]{1,0:T(8,128)(2,1)S(1)} %by_slab.1.refs_0_), channel_id=1, source_target_pairs={{0,1},{1,0},{2,3},{3,2},{4,5},{5,4},{6,7},{7,6},{8,9},{9,8},{10,11... | collective-permute-start | bytes 49160 | tf_op jit(solution)/shard_map/ppermute | solution.py:64
  13.6 4.0 %copy-start.2 = (bf16[16,64,128]{2,1,0:T(8,128)(2,1)S(1)}, bf16[16,64,128]{2,1,0:T(8,128)(2,1)}, u32[]{:S(2)}) copy-start(bf16[16,64,128]{2,1,0:T(8,128)(2,1)} %cot.1) | copy-start | bytes 786436
  13.6 4.0 %copy-start.3 = (bf16[4,128,128]{2,1,0:T(8,128)(2,1)S(1)}, bf16[4,128,128]{2,1,0:T(8,128)(2,1)}, u32[]{:S(2)}) copy-start(bf16[4,128,128]{2,1,0:T(8,128)(2,1)} %attn.3) | copy-start | bytes 393220
  14.1 4.3 %collective-permute-start.5 = (bf16[8,32,128]{2,1,0:T(8,128)(2,1)S(1)}, bf16[8,32,128]{2,1,0:T(8,128)(2,1)S(1)}, u32[]{:S(2)}, u32[]{:S(2)}) collective-permute-start(bf16[8,32,128]{2,1,0:T(8,128)(2,1)S(1)} %get-tuple-element.46), channel_id=1, source_target_pairs={{0,2},{1,3},{2,0},{3,1},{4,6},{5,7},{6,4},{7,5},{8,10},{9,11},{10,... | collective-permute-start | bytes 196616 | tf_op jit(solution)/shard_map/ppermute | solution.py:64
  15.6 4.3 %collective-permute-start.6 = (bf16[8,32,128]{2,1,0:T(8,128)(2,1)S(1)}, bf16[8,32,128]{2,1,0:T(8,128)(2,1)S(1)}, u32[]{:S(2)}, u32[]{:S(2)}) collective-permute-start(bf16[8,32,128]{2,1,0:T(8,128)(2,1)S(1)} %get-tuple-element.47), channel_id=1, source_target_pairs={{0,4},{1,5},{2,6},{3,7},{4,0},{5,1},{6,2},{7,3},{8,12},{9,13},{10,... | collective-permute-start | bytes 196616 | tf_op jit(solution)/shard_map/ppermute | solution.py:64
  17.2 5.2 %collective-permute-start.7 = (bf16[8,32,128]{2,1,0:T(8,128)(2,1)S(1)}, bf16[8,32,128]{2,1,0:T(8,128)(2,1)S(1)}, u32[]{:S(2)}, u32[]{:S(2)}) collective-permute-start(bf16[8,32,128]{2,1,0:T(8,128)(2,1)S(1)} %get-tuple-element.48), channel_id=1, source_target_pairs={{0,6},{1,7},{2,4},{3,5},{4,2},{5,3},{6,0},{7,1},{8,14},{9,15},{10,... | collective-permute-start | bytes 196616 | tf_op jit(solution)/shard_map/ppermute | solution.py:64
  25.2 4.7 %collective-permute-start.8 = (bf16[384,128]{1,0:T(8,128)(2,1)S(1)}, bf16[384,128]{1,0:T(8,128)(2,1)S(1)}, u32[]{:S(2)}, u32[]{:S(2)}) collective-permute-start(bf16[384,128]{1,0:T(8,128)(2,1)S(1)} %get-tuple-element.57), channel_id=1, source_target_pairs={{0,2},{1,3},{2,0},{3,1},{4,6},{5,7},{6,4},{7,5},{8,10},{9,11},{10,... | collective-permute-start | bytes 294920 | tf_op jit(solution)/shard_map/ppermute | solution.py:64
  25.7 5.1 %collective-permute-start.9 = (bf16[384,128]{1,0:T(8,128)(2,1)S(1)}, bf16[384,128]{1,0:T(8,128)(2,1)S(1)}, u32[]{:S(2)}, u32[]{:S(2)}) collective-permute-start(bf16[384,128]{1,0:T(8,128)(2,1)S(1)} %get-tuple-element.63), channel_id=1, source_target_pairs={{0,4},{1,5},{2,6},{3,7},{4,0},{5,1},{6,2},{7,3},{8,12},{9,13},{10,... | collective-permute-start | bytes 294920 | tf_op jit(solution)/shard_map/ppermute | solution.py:64
  26.3 5.5 %collective-permute-start.10 = (bf16[384,128]{1,0:T(8,128)(2,1)S(1)}, bf16[384,128]{1,0:T(8,128)(2,1)S(1)}, u32[]{:S(2)}, u32[]{:S(2)}) collective-permute-start(bf16[384,128]{1,0:T(8,128)(2,1)S(1)} %get-tuple-element.64), channel_id=1, source_target_pairs={{0,6},{1,7},{2,4},{3,5},{4,2},{5,3},{6,0},{7,1},{8,14},{9,15},{10,... | collective-permute-start | bytes 294920 | tf_op jit(solution)/shard_map/ppermute | solution.py:64
  32.2 1.4 %collective-permute-start.12 = (bf16[384,128]{1,0:T(8,128)(2,1)S(1)}, bf16[384,128]{1,0:T(8,128)(2,1)S(1)}, u32[]{:S(2)}, u32[]{:S(2)}) collective-permute-start(bf16[384,128]{1,0:T(8,128)(2,1)S(1)} %get-tuple-element.70.refs_0_), channel_id=1, source_target_pairs={{0,1},{1,0},{2,3},{3,2},{4,5},{5,4},{6,7},{7,6},{8,9},{9,8},{10,11... | collective-permute-start | bytes 294920 | tf_op jit(solution)/shard_map/ppermute | solution.py:64
  32.3 1.3 %collective-permute-start.13 = (bf16[4,2,8,128]{3,2,1,0:T(8,128)(2,1)S(1)}, bf16[4,2,8,128]{3,2,1,0:T(8,128)(2,1)S(1)}, u32[]{:S(2)}, u32[]{:S(2)}) collective-permute-start(bf16[4,2,8,128]{3,2,1,0:T(8,128)(2,1)S(1)} %get-tuple-element.72), channel_id=1, source_target_pairs={{0,1},{1,0},{2,3},{3,2},{4,5},{5,4},{6,7},{7,6},{8,9},{9,8},{10,11... | collective-permute-start | bytes 49160 | tf_op jit(solution)/shard_map/ppermute | solution.py:64
  33.6 4.7 %collective-permute-start.14 = (bf16[2,2,8,128]{3,2,1,0:T(8,128)(2,1)S(1)}, bf16[2,2,8,128]{3,2,1,0:T(8,128)(2,1)S(1)}, u32[]{:S(2)}, u32[]{:S(2)}) collective-permute-start(bf16[2,2,8,128]{3,2,1,0:T(8,128)(2,1)S(1)} %slice.10), channel_id=1, source_target_pairs={{0,16},{8,24},{16,0},{24,8},{1,17},{9,25},{17,1},{25,9},{2,18},{10... | collective-permute-start | bytes 24584 | tf_op jit(solution)/shard_map/ppermute | solution.py:64
  34.8 5.0 %collective-permute-start.11 = (bf16[2,256,128]{2,1,0:T(8,128)(2,1)S(1)}, bf16[2,256,128]{2,1,0:T(8,128)(2,1)S(1)}, u32[]{:S(2)}, u32[]{:S(2)}) collective-permute-start(bf16[2,256,128]{2,1,0:T(8,128)(2,1)S(1)} %get-tuple-element.69), channel_id=1, source_target_pairs={{0,1},{1,0},{2,3},{3,2},{4,5},{5,4},{6,7},{7,6},{8,9},{9,8},{10,11... | collective-permute-start | bytes 393224 | tf_op jit(solution)/shard_map/ppermute | solution.py:64
  34.9 8.2 %collective-permute-start.18 = (bf16[384,128]{1,0:T(8,128)(2,1)S(1)}, bf16[384,128]{1,0:T(8,128)(2,1)S(1)}, u32[]{:S(2)}, u32[]{:S(2)}) collective-permute-start(bf16[384,128]{1,0:T(8,128)(2,1)S(1)} %get-tuple-element.74.refs_0_), channel_id=1, source_target_pairs={{0,6},{1,7},{2,4},{3,5},{4,2},{5,3},{6,0},{7,1},{8,14},{9,15},{10,... | collective-permute-start | bytes 294920 | tf_op jit(solution)/shard_map/ppermute | solution.py:64
  37.3 5.7 %collective-permute-start.17 = (bf16[384,128]{1,0:T(8,128)(2,1)S(1)}, bf16[384,128]{1,0:T(8,128)(2,1)S(1)}, u32[]{:S(2)}, u32[]{:S(2)}) collective-permute-start(bf16[384,128]{1,0:T(8,128)(2,1)S(1)} %get-tuple-element.74.refs_0_), channel_id=1, source_target_pairs={{0,4},{1,5},{2,6},{3,7},{4,0},{5,1},{6,2},{7,3},{8,12},{9,13},{10,... | collective-permute-start | bytes 294920 | tf_op jit(solution)/shard_map/ppermute | solution.py:64
  37.8 5.3 %collective-permute-start.16 = (bf16[384,128]{1,0:T(8,128)(2,1)S(1)}, bf16[384,128]{1,0:T(8,128)(2,1)S(1)}, u32[]{:S(2)}, u32[]{:S(2)}) collective-permute-start(bf16[384,128]{1,0:T(8,128)(2,1)S(1)} %get-tuple-element.74.refs_0_), channel_id=1, source_target_pairs={{0,2},{1,3},{2,0},{3,1},{4,6},{5,7},{6,4},{7,5},{8,10},{9,11},{10,... | collective-permute-start | bytes 294920 | tf_op jit(solution)/shard_map/ppermute | solution.py:64
  38.4 3.7 %collective-permute-start.15 = (bf16[1,2,8,128]{3,2,1,0:T(8,128)(2,1)S(1)}, bf16[1,2,8,128]{3,2,1,0:T(8,128)(2,1)S(1)}, u32[]{:S(2)}, u32[]{:S(2)}) collective-permute-start(bf16[1,2,8,128]{3,2,1,0:T(8,128)(2,1)S(1)} %slice.12), channel_id=1, source_target_pairs={{0,8},{8,0},{16,24},{24,16},{1,9},{9,1},{17,25},{25,17},{2,10},{10... | collective-permute-start | bytes 12296 | tf_op jit(solution)/shard_map/ppermute | solution.py:64

commit v7 on v6

--- a/solution.py
+++ b/solution.py
@@ -265,13 +265,14 @@
     parts, hub_sum = refs[-2:]
     chips, _, layouts, _, width = parts.shape
     blocks, (slope, rows_t, w_back, hub_weight) = refs[:chips], refs[chips : chips + 4]
-    mine, theirs, sums, hub_mine, hub_theirs = refs[chips + 5 : -2]
+    mine, theirs, sums, hub_mine = refs[chips + 5 : -2]
     me = lax.axis_index("config")
     nodes = slope.shape[1]
     count = parts.shape[1] * layouts * SUB
     for s, block in zip(steps(chips, CHIPS), blocks):
         parts[lax.bitwise_xor(me // 2, s)] = block[0:count].astype(F32).reshape(parts.shape[1:])
-    sums[2 * width :] = sum(block[count:].astype(F32) for block in blocks).astype(BF)
+    share = blocks[0].shape[0] - count
+    sums[2 * width : 2 * width + share] = sum(block[count:].astype(F32) for block in blocks).astype(BF)
     half = layouts // 2
     grad_pre, grad_agg = [], []
     for l in range(layouts):
@@ -284,10 +285,16 @@
     hub_sum[...] = dot_tn(core_rows(hub_weight, (), lax.rem(me, 2)), jnp.concatenate(grad_agg, axis=1))
     slab = lax.axis_index("graph")
     ranks, _, hubs, _ = hub_mine.shape
+    pieces = []
     for s in range(ranks):
         at = pl.ds(pl.multiple_of(lax.bitwise_xor(slab, s) * hubs, hubs), hubs)
         for l in range(layouts):
-            (hub_mine, hub_theirs)[l // half][s, l % half] = hub_sum[at, l * width : (l + 1) * width].astype(BF)
+            piece = hub_sum[at, l * width : (l + 1) * width]
+            if l < half:
+                hub_mine[s, l] = piece.astype(BF)
+            else:
+                pieces.append(piece)
+    sums[2 * width + share :] = jnp.concatenate(pieces, axis=0).astype(BF)
 
 
 def tile_back(adj_t, w_back, mine, theirs, totals, whole):
@@ -310,21 +317,11 @@
     return (a[...].astype(F32) + b[...].astype(F32)).astype(BF)
 
 
-def join(*refs):
-    pairs = len(refs) // 3
-    for i in range(pairs):
-        refs[2 * pairs + i][...] = add(refs[2 * i], refs[2 * i + 1])
-
-
-def joined(*operands):
-    return call(
-        join,
-        [shape(x.shape) for x in operands[::2]],
-        operands,
-        [VMEM] * len(operands),
-        micros=0.1,
-        name="join",
-    )
+def join(sums, sums_in, hub_mine, sums_out, hub_out):
+    count = sums_out.shape[0]
+    sums_out[...] = (sums[0:count].astype(F32) + sums_in[0:count].astype(F32)).astype(BF)
+    received = sums_in[count:].astype(F32).reshape(hub_out.shape)
+    hub_out[...] = (hub_mine[...].astype(F32) + received).astype(BF)
 
 
 def by_slab(*refs):
@@ -509,9 +506,15 @@
 
     hub_shape = (ranks, layout_dev, hub_dev, width)
     mine = (layout_dev, node_dev // 2, width)
-    mine, theirs, sums, hub_sum, hub_theirs = call(
+    hub_rows = ranks * layout_dev * hub_dev
+    mine, theirs, sums, hub_sum = call(
         sage_back,
-        (shape(mine), shape(mine), shape((2 * width + share_rows, width)), shape(hub_shape), shape(hub_shape)),
+        (
+            shape(mine),
+            shape(mine),
+            shape((2 * width + share_rows + hub_rows, width)),
+            shape(hub_shape),
+        ),
         (*grad_in, slope, rows_t, w_back, hub_weight, shown),
         [VMEM] * (chips + 4) + [ANY],
         [
@@ -520,9 +523,15 @@
         ],
         name="sage_back",
     )
-    hub_in = swapped(hub_theirs, "config", 1)
     theirs = swapped(theirs, "config", 1)
-    sums, hub_sum = joined(sums, swapped(sums, "config", 1), hub_sum, hub_in)
+    sums, hub_sum = call(
+        join,
+        (shape((2 * width + share_rows, width)), shape(hub_shape)),
+        (sums, swapped(sums, "config", 1), hub_sum),
+        [VMEM] * 3,
+        micros=0.1,
+        name="join",
+    )
     sums = exchange([sums] * chips)
     totals = call(
         tile_back,

time: 44.1 us -> 44.1 us (level)
  starting transfers between devices: 19.8 us -> 19.2 us
    ppermute x19 -> x18, starting transfers between devices: 19.8 us -> 19.2 us  [swapped(): return lax.ppermute(x, axis, [(i, i ^ mask) for i in range(count)])]
    ppermute x19 -> x18, waiting for transfers between devices: 11.3 us -> 11.6 us  [swapped(): return lax.ppermute(x, axis, [(i, i ^ mask) for i in range(count)])]
  transfers between devices with their start and end apart: 19 -> 18, of which waited for: 9 -> 10; matrix products, arithmetic and copies ran while one was open for 0% -> 0% of each run, Pallas kernels for 14% -> 14%
where the time goes in v7:
time: 44.1 us; the launch traced here: 43.9 us
  starting transfers between devices  19.2 us (44%)
  waiting for transfers between devices  11.6 us (26%)
  Pallas kernels  10.7 us (24%)
  between operations  1.48 us (3%)
  local copies, waits for them, and re-layouts  0.82 us (2%)
    ppermute x18, starting transfers between devices, swapped(): return lax.ppermute(x, axis, [(i, i ^ mask) for i in range(count)])  19.2 us
    ppermute x18, waiting for transfers between devices, swapped(): return lax.ppermute(x, axis, [(i, i ^ mask) for i in range(count)])  11.6 us
    pallas_call x12, Pallas kernels, call(): pl.pallas_call(kernel, out_shape=outs, in_specs=specs, out_specs=jax.tree...  10.7 us
  transfers between devices with their start and end apart: 18, of which 10 were waited for; matrix products, arithmetic and copies ran while one was open for 0% of the time, Pallas kernels for 14%

profile of v7, /device:TPU:0, one launch (start us, length us, event | category | flops | bytes accessed | tf_op | source)
XLA Modules:
  0.0 43.9 jit_solution(12590216260306439860)
XLA Ops:
  0.7 0.5 %collective-permute-start = (bf16[2,512,128]{2,1,0:T(8,128)(2,1)}, bf16[2,512,128]{2,1,0:T(8,128)(2,1)S(1)}, u32[]{:S(2)}, u32[]{:S(2)}) collective-permute-start(bf16[2,512,128]{2,1,0:T(8,128)(2,1)} %feats.1), channel_id=1, source_target_pairs={{0,1},{1,0},{2,3},{3,2},{4,5},{5,4},{6,7},{7,6},{8,9},{9,8},{10,11... | collective-permute-start | bytes 786440 | tf_op jit(solution)/shard_map/ppermute | solution.py:64
  1.2 1.8 %hub_pick.1 = (bf16[2,8,128]{2,1,0:T(8,128)(2,1)}, bf16[2,8,128]{2,1,0:T(8,128)(2,1)}, bf16[2,8,128]{2,1,0:T(8,128)(2,1)}) custom-call(s32[8]{0:T(128)} %ids.1, bf16[2,512,128]{2,1,0:T(8,128)(2,1)} %feats.1), custom_call_target="tpu_custom_call" | custom-call | flops 1000000000 | bytes 2097152 | tf_op jit(solution)/shard_map/hub_pick/pallas_call | solution.py:41
  3.0 0.0 copy-start.9
  3.0 3.7 %collective-permute-start.1 = (bf16[2,8,128]{2,1,0:T(8,128)(2,1)}, bf16[2,8,128]{2,1,0:T(8,128)(2,1)S(1)}, u32[]{:S(2)}, u32[]{:S(2)}) collective-permute-start(bf16[2,8,128]{2,1,0:T(8,128)(2,1)} %get-tuple-element.39), channel_id=1, source_target_pairs={{0,16},{8,24},{16,0},{24,8},{1,17},{9,25},{17,1},{25,9},{2,18},{10... | collective-permute-start | bytes 12296 | tf_op jit(solution)/shard_map/ppermute | solution.py:64
  6.7 1.3 %collective-permute-start.2 = (bf16[2,8,128]{2,1,0:T(8,128)(2,1)}, bf16[2,8,128]{2,1,0:T(8,128)(2,1)S(1)}, u32[]{:S(2)}, u32[]{:S(2)}) collective-permute-start(bf16[2,8,128]{2,1,0:T(8,128)(2,1)} %get-tuple-element.40), channel_id=1, source_target_pairs={{0,24},{8,16},{16,8},{24,0},{1,25},{9,17},{17,9},{25,1},{2,26},{10... | collective-permute-start | bytes 12296 | tf_op jit(solution)/shard_map/ppermute | solution.py:64
  8.1 0.3 collective-permute-start.3
  9.1 0.1 pad_add_fusion.ints
  9.2 0.0 collective-permute-done
  9.2 1.4 %adjacency.1 = (bf16[512,512]{1,0:T(8,128)(2,1)S(1)}, f32[256,512]{1,0:T(8,128)S(1)}, f32[4,256,128]{2,1,0:T(8,128)S(1)}, bf16[4,256,128]{2,1,0:T(8,128)(2,1)S(1...) custom-call(s32[33]{0:T(128)S(1)} %pad_add_fusion.ints, bf16[12,128,128]{2,1,0:T(8,128)(2,1)S(1)} %copy-done, ...), custom_call_target="tpu_custom_call" | custom-call | flops 1000000000 | bytes 2097152 | tf_op jit(solution)/shard_map/adjacency/pallas_call | solution.py:41
  10.6 0.0 collective-permute-done.1.refs_1_
  10.6 1.8 %collective-permute-done.2.refs_2_ = bf16[2,8,128]{2,1,0:T(8,128)(2,1)S(1)} collective-permute-done((bf16[2,8,128]{2,1,0:T(8,128)(2,1)}, bf16[2,8,128]{2,1,0:T(8,128)(2,1)S(1)}, u32[]{:S(2)}, u32[]{:S(2)}) %collective-permute-start.2) | collective-permute-done | bytes 4128 | tf_op jit(solution)/shard_map/ppermute | solution.py:64
  12.4 0.0 collective-permute-done.3.refs_3_
  12.4 0.1 collective-permute-start.4
  12.5 0.7 %copy-done.5 = bf16[512,32]{0,1:T(8,128)(2,1)S(1)} copy-done((bf16[512,32]{0,1:T(8,128)(2,1)S(1)}, bf16[512,32]{0,1:T(8,128)(2,1)}, u32[]{:S(2)}) %copy-start.5) | copy-done | bytes 32792
  13.1 0.1 copy.13
  13.2 0.4 collective-permute-done.4.refs_1_
  13.6 0.4 sage_out.1
  14.1 1.6 %collective-permute-start.5 = (bf16[8,32,128]{2,1,0:T(8,128)(2,1)S(1)}, bf16[8,32,128]{2,1,0:T(8,128)(2,1)S(1)}, u32[]{:S(2)}, u32[]{:S(2)}) collective-permute-start(bf16[8,32,128]{2,1,0:T(8,128)(2,1)S(1)} %get-tuple-element.45), channel_id=1, source_target_pairs={{0,2},{1,3},{2,0},{3,1},{4,6},{5,7},{6,4},{7,5},{8,10},{9,11},{10,... | collective-permute-start | bytes 196616 | tf_op jit(solution)/shard_map/ppermute | solution.py:64
  15.6 1.5 %collective-permute-start.6 = (bf16[8,32,128]{2,1,0:T(8,128)(2,1)S(1)}, bf16[8,32,128]{2,1,0:T(8,128)(2,1)S(1)}, u32[]{:S(2)}, u32[]{:S(2)}) collective-permute-start(bf16[8,32,128]{2,1,0:T(8,128)(2,1)S(1)} %get-tuple-element.46), channel_id=1, source_target_pairs={{0,4},{1,5},{2,6},{3,7},{4,0},{5,1},{6,2},{7,3},{8,12},{9,13},{10,... | collective-permute-start | bytes 196616 | tf_op jit(solution)/shard_map/ppermute | solution.py:64
  17.2 0.5 %collective-permute-start.7 = (bf16[8,32,128]{2,1,0:T(8,128)(2,1)S(1)}, bf16[8,32,128]{2,1,0:T(8,128)(2,1)S(1)}, u32[]{:S(2)}, u32[]{:S(2)}) collective-permute-start(bf16[8,32,128]{2,1,0:T(8,128)(2,1)S(1)} %get-tuple-element.47), channel_id=1, source_target_pairs={{0,6},{1,7},{2,4},{3,5},{4,2},{5,3},{6,0},{7,1},{8,14},{9,15},{10,... | collective-permute-start | bytes 196616 | tf_op jit(solution)/shard_map/ppermute | solution.py:64
  17.6 0.5 %prepare.1 = (bf16[8,128,128]{2,1,0:T(8,128)(2,1)S(1)}, bf16[8,128,128]{2,1,0:T(8,128)(2,1)S(1)}, f32[4,256,128]{2,1,0:T(8,128)S(1)}, bf16[256,1024]{1,0:T(8,128...) custom-call(bf16[16,64,128]{2,1,0:T(8,128)(2,1)S(1)} %copy-done.2, ...), custom_call_target="tpu_custom_call" | custom-call | flops 1000000000 | bytes 2097152 | tf_op jit(solution)/shard_map/prepare/pallas_call | solution.py:41
  18.1 0.3 collective-permute-done.5.refs_1_
  18.4 1.5 %collective-permute-done.6.refs_2_ = bf16[8,32,128]{2,1,0:T(8,128)(2,1)S(1)} collective-permute-done((bf16[8,32,128]{2,1,0:T(8,128)(2,1)S(1)}, bf16[8,32,128]{2,1,0:T(8,128)(2,1)S(1)}, u32[]{:S(2)}, u32[]{:S(2)}) %collective-permute-start.6) | collective-permute-done | bytes 65568 | tf_op jit(solution)/shard_map/ppermute | solution.py:64
  19.9 2.4 %collective-permute-done.7.refs_3_ = bf16[8,32,128]{2,1,0:T(8,128)(2,1)S(1)} collective-permute-done((bf16[8,32,128]{2,1,0:T(8,128)(2,1)S(1)}, bf16[8,32,128]{2,1,0:T(8,128)(2,1)S(1)}, u32[]{:S(2)}, u32[]{:S(2)}) %collective-permute-start.7) | collective-permute-done | bytes 65568 | tf_op jit(solution)/shard_map/ppermute | solution.py:64
  22.3 2.8 %attend.1 = (bf16[384,128]{1,0:T(8,128)(2,1)S(1)}, bf16[384,128]{1,0:T(8,128)(2,1)S(1)}, bf16[384,128]{1,0:T(8,128)(2,1)S(1)}, bf16[384,128]{1,0:T(8,128)(2,1)S(...) custom-call(bf16[8,32,128]{2,1,0:T(8,128)(2,1)S(1)} %get-tuple-element.44.refs_0_, ...), custom_call_target="tpu_custom_call" | custom-call | flops 4000000000 | bytes 8388608 | tf_op jit(solution)/shard_map/attend/pallas_call | solution.py:41
  25.2 0.6 %collective-permute-start.8 = (bf16[384,128]{1,0:T(8,128)(2,1)S(1)}, bf16[384,128]{1,0:T(8,128)(2,1)S(1)}, u32[]{:S(2)}, u32[]{:S(2)}) collective-permute-start(bf16[384,128]{1,0:T(8,128)(2,1)S(1)} %get-tuple-element.56), channel_id=1, source_target_pairs={{0,2},{1,3},{2,0},{3,1},{4,6},{5,7},{6,4},{7,5},{8,10},{9,11},{10,... | collective-permute-start | bytes 294920 | tf_op jit(solution)/shard_map/ppermute | solution.py:64
  25.7 0.5 %collective-permute-start.9 = (bf16[384,128]{1,0:T(8,128)(2,1)S(1)}, bf16[384,128]{1,0:T(8,128)(2,1)S(1)}, u32[]{:S(2)}, u32[]{:S(2)}) collective-permute-start(bf16[384,128]{1,0:T(8,128)(2,1)S(1)} %get-tuple-element.62), channel_id=1, source_target_pairs={{0,4},{1,5},{2,6},{3,7},{4,0},{5,1},{6,2},{7,3},{8,12},{9,13},{10,... | collective-permute-start | bytes 294920 | tf_op jit(solution)/shard_map/ppermute | solution.py:64
  26.3 2.5 %collective-permute-start.10 = (bf16[384,128]{1,0:T(8,128)(2,1)S(1)}, bf16[384,128]{1,0:T(8,128)(2,1)S(1)}, u32[]{:S(2)}, u32[]{:S(2)}) collective-permute-start(bf16[384,128]{1,0:T(8,128)(2,1)S(1)} %get-tuple-element.63), channel_id=1, source_target_pairs={{0,6},{1,7},{2,4},{3,5},{4,2},{5,3},{6,0},{7,1},{8,14},{9,15},{10,... | collective-permute-start | bytes 294920 | tf_op jit(solution)/shard_map/ppermute | solution.py:64
  28.7 1.2 %collective-permute-done.8._.refs_1_ = bf16[384,128]{1,0:T(8,128)(2,1)S(1)} collective-permute-done((bf16[384,128]{1,0:T(8,128)(2,1)S(1)}, bf16[384,128]{1,0:T(8,128)(2,1)S(1)}, u32[]{:S(2)}, u32[]{:S(2)}) %collective-permute-start.8) | collective-permute-done | bytes 98336 | tf_op jit(solution)/shard_map/ppermute | solution.py:64
  29.9 1.0 %outputs.1 = (bf16[16,64,128]{2,1,0:T(8,128)(2,1)}, f32[8,128]{1,0:T(8,128)S(1)}) custom-call(bf16[8,128,128]{2,1,0:T(8,128)(2,1)S(1)} %get-tuple-element.54.hidden, bf16[128,1024]{1,0:T(8,128)(2,1)S(1)} %get-tuple-element.55.mixed_t, bf16[4,128,128]{2,1,0:T(8,128)(2,1)S(1)} %copy-done.3, bf16[384,128]{1,0:T(8,128)(2,1)S(1)} %collective-permute-done.8._.refs_1_), custom_call_target="tpu_custom_call" | custom-call | flops 1000000000 | bytes 2097152 | tf_op jit(solution)/shard_map/outputs/pallas_call | solution.py:41
  30.9 0.0 collective-permute-done.9.refs_2_
  30.9 0.9 %collective-permute-done.10.refs_3_ = bf16[384,128]{1,0:T(8,128)(2,1)S(1)} collective-permute-done((bf16[384,128]{1,0:T(8,128)(2,1)S(1)}, bf16[384,128]{1,0:T(8,128)(2,1)S(1)}, u32[]{:S(2)}, u32[]{:S(2)}) %collective-permute-start.10) | collective-permute-done | bytes 98336 | tf_op jit(solution)/shard_map/ppermute | solution.py:64
  31.8 0.4 sage_back.1
  32.2 0.1 collective-permute-start.12
  32.3 1.3 %collective-permute-done.12.sums_in = bf16[448,128]{1,0:T(8,128)(2,1)S(1)} collective-permute-done((bf16[448,128]{1,0:T(8,128)(2,1)S(1)}, bf16[448,128]{1,0:T(8,128)(2,1)S(1)}, u32[]{:S(2)}, u32[]{:S(2)}) %collective-permute-start.12) | collective-permute-done | bytes 114720 | tf_op jit(solution)/shard_map/ppermute | solution.py:64
  33.6 1.2 %collective-permute-start.13 = (bf16[2,2,8,128]{3,2,1,0:T(8,128)(2,1)S(1)}, bf16[2,2,8,128]{3,2,1,0:T(8,128)(2,1)S(1)}, u32[]{:S(2)}, u32[]{:S(2)}) collective-permute-start(bf16[2,2,8,128]{3,2,1,0:T(8,128)(2,1)S(1)} %slice.10), channel_id=1, source_target_pairs={{0,16},{8,24},{16,0},{24,8},{1,17},{9,25},{17,1},{25,9},{2,18},{10... | collective-permute-start | bytes 24584 | tf_op jit(solution)/shard_map/ppermute | solution.py:64
  34.8 0.0 collective-permute-start.11
  34.8 2.4 %collective-permute-start.17 = (bf16[384,128]{1,0:T(8,128)(2,1)S(1)}, bf16[384,128]{1,0:T(8,128)(2,1)S(1)}, u32[]{:S(2)}, u32[]{:S(2)}) collective-permute-start(bf16[384,128]{1,0:T(8,128)(2,1)S(1)} %get-tuple-element.72.refs_0_), channel_id=1, source_target_pairs={{0,6},{1,7},{2,4},{3,5},{4,2},{5,3},{6,0},{7,1},{8,14},{9,15},{10,... | collective-permute-start | bytes 294920 | tf_op jit(solution)/shard_map/ppermute | solution.py:64
  37.2 0.5 %collective-permute-start.16 = (bf16[384,128]{1,0:T(8,128)(2,1)S(1)}, bf16[384,128]{1,0:T(8,128)(2,1)S(1)}, u32[]{:S(2)}, u32[]{:S(2)}) collective-permute-start(bf16[384,128]{1,0:T(8,128)(2,1)S(1)} %get-tuple-element.72.refs_0_), channel_id=1, source_target_pairs={{0,4},{1,5},{2,6},{3,7},{4,0},{5,1},{6,2},{7,3},{8,12},{9,13},{10,... | collective-permute-start | bytes 294920 | tf_op jit(solution)/shard_map/ppermute | solution.py:64
  37.8 0.5 %collective-permute-start.15 = (bf16[384,128]{1,0:T(8,128)(2,1)S(1)}, bf16[384,128]{1,0:T(8,128)(2,1)S(1)}, u32[]{:S(2)}, u32[]{:S(2)}) collective-permute-start(bf16[384,128]{1,0:T(8,128)(2,1)S(1)} %get-tuple-element.72.refs_0_), channel_id=1, source_target_pairs={{0,2},{1,3},{2,0},{3,1},{4,6},{5,7},{6,4},{7,5},{8,10},{9,11},{10,... | collective-permute-start | bytes 294920 | tf_op jit(solution)/shard_map/ppermute | solution.py:64
  38.3 0.0 collective-permute-done.13
  38.3 1.4 %collective-permute-start.14 = (bf16[1,2,8,128]{3,2,1,0:T(8,128)(2,1)S(1)}, bf16[1,2,8,128]{3,2,1,0:T(8,128)(2,1)S(1)}, u32[]{:S(2)}, u32[]{:S(2)}) collective-permute-start(bf16[1,2,8,128]{3,2,1,0:T(8,128)(2,1)S(1)} %slice.12), channel_id=1, source_target_pairs={{0,8},{8,0},{16,24},{24,16},{1,9},{9,1},{17,25},{25,17},{2,10},{10... | collective-permute-start | bytes 12296 | tf_op jit(solution)/shard_map/ppermute | solution.py:64
  39.7 0.5 %tile_back.1.totals = f32[2,512,128]{2,1,0:T(8,128)S(1)} custom-call(bf16[512,512]{1,0:T(8,128)(2,1)S(1)} %get-tuple-element.59.adj_t, bf16[128,256]{1,0:T(8,128)(2,1)S(1)} %get-tuple-element.60.refs_6_.w_back, bf16[2,256,128]{2,1,0:T(8,128)(2,1)S(1)} %get-tuple-element.67.mine, bf16[2,256,128]{2,1,0:T(8,128)(2,1)S(1)} %collective-permute-done.11.theirs), custom_call_target="tpu_custom_call" | custom-call | flops 1000000000 | bytes 2097152 | tf_op jit(solution)/shard_map/tile_back/pallas_call | solution.py:41
  40.3 1.7 %collective-permute-done.14.hub_in = bf16[1,2,8,128]{3,2,1,0:T(8,128)(2,1)S(1)} collective-permute-done((bf16[1,2,8,128]{3,2,1,0:T(8,128)(2,1)S(1)}, bf16[1,2,8,128]{3,2,1,0:T(8,128)(2,1)S(1)}, u32[]{:S(2)}, u32[]{:S(2)}) %collective-permute-start.14) | collective-permute-done | bytes 4128 | tf_op jit(solution)/shard_map/ppermute | solution.py:64
  42.0 1.0 %finish.1 = bf16[2,512,128]{2,1,0:T(8,128)(2,1)} custom-call(bf16[8,512]{1,0:T(8,128)(2,1)S(1)} %get-tuple-element.58.hot, f32[2,512,128]{2,1,0:T(8,128)S(1)} %tile_back.1.totals, bf16[2,2,8,128]{3,2,1,0:T(8,128)(2,1)S(1)} %slice_add_fusion.hub_own, bf16[1,2,8,128]{3,2,1,0:T(8,128)(2,1)S(1)} %collective-permute-done.14.hub_in), custom_call_target="tpu_custom_call" | custom-call | flops 1000000000 | bytes 2097152 | tf_op jit(solution)/shard_map/finish/pallas_call | solution.py:41
  43.0 0.1 collective-permute-done.16.refs_2_
  43.0 0.1 collective-permute-done.15.refs_1_
  43.1 0.8 %weights_out.1 = f32[768,128]{1,0:T(8,128)} custom-call(bf16[384,128]{1,0:T(8,128)(2,1)S(1)} %get-tuple-element.72.refs_0_, bf16[384,128]{1,0:T(8,128)(2,1)S(1)} %collective-permute-done.15.refs_1_, bf16[384,128]{1,0:T(8,128)(2,1)S(1)} %collective-permute-done.16.refs_2_, bf16[384,128]{1,0:T(8,128)(2,1)S(1)} %collective-permute-done.17.refs_3_), custom_call_target="tpu_custom_call" | custom-call | flops 1000000000 | bytes 2097152 | tf_op jit(solution)/shard_map/weights_out/pallas_call | solution.py:41
  (25 shorter events, 0.1 us)
Async XLA Ops:
  0.6 8.5 %copy-start.1 = (bf16[2,512,128]{2,1,0:T(8,128)(2,1)S(1)}, bf16[2,512,128]{2,1,0:T(8,128)(2,1)}, u32[]{:S(2)}) copy-start(bf16[2,512,128]{2,1,0:T(8,128)(2,1)} %feats.1) | copy-start | bytes 786436
  0.6 8.5 %copy-start.4 = (bf16[2,128,128]{2,1,0:T(8,128)(2,1)S(1)}, bf16[2,128,128]{2,1,0:T(8,128)(2,1)}, u32[]{:S(2)}) copy-start(bf16[2,128,128]{2,1,0:T(8,128)(2,1)} %weight.3) | copy-start | bytes 196612
  0.7 8.5 %copy-start = (bf16[12,128,128]{2,1,0:T(8,128)(2,1)S(1)}, bf16[12,128,128]{2,1,0:T(8,128)(2,1)}, u32[]{:S(2)}) copy-start(bf16[12,128,128]{2,1,0:T(8,128)(2,1)} %tiles.1) | copy-start | bytes 1179652
  0.7 8.5 %collective-permute-start = (bf16[2,512,128]{2,1,0:T(8,128)(2,1)}, bf16[2,512,128]{2,1,0:T(8,128)(2,1)S(1)}, u32[]{:S(2)}, u32[]{:S(2)}) collective-permute-start(bf16[2,512,128]{2,1,0:T(8,128)(2,1)} %feats.1), channel_id=1, source_target_pairs={{0,1},{1,0},{2,3},{3,2},{4,5},{5,4},{6,7},{7,6},{8,9},{9,8},{10,11... | collective-permute-start | bytes 786440 | tf_op jit(solution)/shard_map/ppermute | solution.py:64
  3.0 5.1 %copy-start.9 = (bf16[2,8,128]{2,1,0:T(8,128)(2,1)S(1)}, bf16[2,8,128]{2,1,0:T(8,128)(2,1)}, u32[]{:S(2)}) copy-start(bf16[2,8,128]{2,1,0:T(8,128)(2,1)} %get-tuple-element.41) | copy-start | bytes 12292
  3.0 7.6 %collective-permute-start.1 = (bf16[2,8,128]{2,1,0:T(8,128)(2,1)}, bf16[2,8,128]{2,1,0:T(8,128)(2,1)S(1)}, u32[]{:S(2)}, u32[]{:S(2)}) collective-permute-start(bf16[2,8,128]{2,1,0:T(8,128)(2,1)} %get-tuple-element.39), channel_id=1, source_target_pairs={{0,16},{8,24},{16,0},{24,8},{1,17},{9,25},{17,1},{25,9},{2,18},{10... | collective-permute-start | bytes 12296 | tf_op jit(solution)/shard_map/ppermute | solution.py:64
  6.7 5.6 %collective-permute-start.2 = (bf16[2,8,128]{2,1,0:T(8,128)(2,1)}, bf16[2,8,128]{2,1,0:T(8,128)(2,1)S(1)}, u32[]{:S(2)}, u32[]{:S(2)}) collective-permute-start(bf16[2,8,128]{2,1,0:T(8,128)(2,1)} %get-tuple-element.40), channel_id=1, source_target_pairs={{0,24},{8,16},{16,8},{24,0},{1,25},{9,17},{17,9},{25,1},{2,26},{10... | collective-permute-start | bytes 12296 | tf_op jit(solution)/shard_map/ppermute | solution.py:64
  8.1 1.0 %copy-start.6 = (s32[12]{0:T(128)S(1)}, s32[12]{0:T(128)}, u32[]{:S(2)}) copy-start(s32[12]{0:T(128)} %param.16) | copy-start | bytes 148
  8.1 1.0 %copy-start.7 = (s32[12]{0:T(128)S(1)}, s32[12]{0:T(128)}, u32[]{:S(2)}) copy-start(s32[12]{0:T(128)} %param.15) | copy-start | bytes 148
  8.1 1.0 %copy-start.8 = (s32[8]{0:T(128)S(1)}, s32[8]{0:T(128)}, u32[]{:S(2)}) copy-start(s32[8]{0:T(128)} %ids.1) | copy-start | bytes 100
  8.1 4.3 %collective-permute-start.3 = (bf16[2,8,128]{2,1,0:T(8,128)(2,1)S(1)}, bf16[2,8,128]{2,1,0:T(8,128)(2,1)S(1)}, u32[]{:S(2)}, u32[]{:S(2)}) collective-permute-start(bf16[2,8,128]{2,1,0:T(8,128)(2,1)S(1)} %copy-done.9), channel_id=1, source_target_pairs={{0,8},{8,0},{16,24},{24,16},{1,9},{9,1},{17,25},{25,17},{2,10},{10... | collective-permute-start | bytes 12296 | tf_op jit(solution)/shard_map/ppermute | solution.py:64
  12.4 0.8 %copy-start.5 = (bf16[512,32]{0,1:T(8,128)(2,1)S(1)}, bf16[512,32]{0,1:T(8,128)(2,1)}, u32[]{:S(2)}) copy-start(bf16[512,32]{0,1:T(8,128)(2,1)} %param.19) | copy-start | bytes 98308
  12.4 1.2 %collective-permute-start.4 = (bf16[32,256]{1,0:T(8,128)(2,1)S(1)}, bf16[32,256]{1,0:T(8,128)(2,1)S(1)}, u32[]{:S(2)}, u32[]{:S(2)}) collective-permute-start(bf16[32,256]{1,0:T(8,128)(2,1)S(1)} %by_slab.1.refs_0_), channel_id=1, source_target_pairs={{0,1},{1,0},{2,3},{3,2},{4,5},{5,4},{6,7},{7,6},{8,9},{9,8},{10,11... | collective-permute-start | bytes 49160 | tf_op jit(solution)/shard_map/ppermute | solution.py:64
  13.6 4.0 %copy-start.2 = (bf16[16,64,128]{2,1,0:T(8,128)(2,1)S(1)}, bf16[16,64,128]{2,1,0:T(8,128)(2,1)}, u32[]{:S(2)}) copy-start(bf16[16,64,128]{2,1,0:T(8,128)(2,1)} %cot.1) | copy-start | bytes 786436
  13.6 4.0 %copy-start.3 = (bf16[4,128,128]{2,1,0:T(8,128)(2,1)S(1)}, bf16[4,128,128]{2,1,0:T(8,128)(2,1)}, u32[]{:S(2)}) copy-start(bf16[4,128,128]{2,1,0:T(8,128)(2,1)} %attn.3) | copy-start | bytes 393220
  14.1 4.3 %collective-permute-start.5 = (bf16[8,32,128]{2,1,0:T(8,128)(2,1)S(1)}, bf16[8,32,128]{2,1,0:T(8,128)(2,1)S(1)}, u32[]{:S(2)}, u32[]{:S(2)}) collective-permute-start(bf16[8,32,128]{2,1,0:T(8,128)(2,1)S(1)} %get-tuple-element.45), channel_id=1, source_target_pairs={{0,2},{1,3},{2,0},{3,1},{4,6},{5,7},{6,4},{7,5},{8,10},{9,11},{10,... | collective-permute-start | bytes 196616 | tf_op jit(solution)/shard_map/ppermute | solution.py:64
  15.6 4.3 %collective-permute-start.6 = (bf16[8,32,128]{2,1,0:T(8,128)(2,1)S(1)}, bf16[8,32,128]{2,1,0:T(8,128)(2,1)S(1)}, u32[]{:S(2)}, u32[]{:S(2)}) collective-permute-start(bf16[8,32,128]{2,1,0:T(8,128)(2,1)S(1)} %get-tuple-element.46), channel_id=1, source_target_pairs={{0,4},{1,5},{2,6},{3,7},{4,0},{5,1},{6,2},{7,3},{8,12},{9,13},{10,... | collective-permute-start | bytes 196616 | tf_op jit(solution)/shard_map/ppermute | solution.py:64
  17.2 5.2 %collective-permute-start.7 = (bf16[8,32,128]{2,1,0:T(8,128)(2,1)S(1)}, bf16[8,32,128]{2,1,0:T(8,128)(2,1)S(1)}, u32[]{:S(2)}, u32[]{:S(2)}) collective-permute-start(bf16[8,32,128]{2,1,0:T(8,128)(2,1)S(1)} %get-tuple-element.47), channel_id=1, source_target_pairs={{0,6},{1,7},{2,4},{3,5},{4,2},{5,3},{6,0},{7,1},{8,14},{9,15},{10,... | collective-permute-start | bytes 196616 | tf_op jit(solution)/shard_map/ppermute | solution.py:64
  25.2 4.7 %collective-permute-start.8 = (bf16[384,128]{1,0:T(8,128)(2,1)S(1)}, bf16[384,128]{1,0:T(8,128)(2,1)S(1)}, u32[]{:S(2)}, u32[]{:S(2)}) collective-permute-start(bf16[384,128]{1,0:T(8,128)(2,1)S(1)} %get-tuple-element.56), channel_id=1, source_target_pairs={{0,2},{1,3},{2,0},{3,1},{4,6},{5,7},{6,4},{7,5},{8,10},{9,11},{10,... | collective-permute-start | bytes 294920 | tf_op jit(solution)/shard_map/ppermute | solution.py:64
  25.7 5.1 %collective-permute-start.9 = (bf16[384,128]{1,0:T(8,128)(2,1)S(1)}, bf16[384,128]{1,0:T(8,128)(2,1)S(1)}, u32[]{:S(2)}, u32[]{:S(2)}) collective-permute-start(bf16[384,128]{1,0:T(8,128)(2,1)S(1)} %get-tuple-element.62), channel_id=1, source_target_pairs={{0,4},{1,5},{2,6},{3,7},{4,0},{5,1},{6,2},{7,3},{8,12},{9,13},{10,... | collective-permute-start | bytes 294920 | tf_op jit(solution)/shard_map/ppermute | solution.py:64
  26.3 5.5 %collective-permute-start.10 = (bf16[384,128]{1,0:T(8,128)(2,1)S(1)}, bf16[384,128]{1,0:T(8,128)(2,1)S(1)}, u32[]{:S(2)}, u32[]{:S(2)}) collective-permute-start(bf16[384,128]{1,0:T(8,128)(2,1)S(1)} %get-tuple-element.63), channel_id=1, source_target_pairs={{0,6},{1,7},{2,4},{3,5},{4,2},{5,3},{6,0},{7,1},{8,14},{9,15},{10,... | collective-permute-start | bytes 294920 | tf_op jit(solution)/shard_map/ppermute | solution.py:64
  32.2 1.4 %collective-permute-start.12 = (bf16[448,128]{1,0:T(8,128)(2,1)S(1)}, bf16[448,128]{1,0:T(8,128)(2,1)S(1)}, u32[]{:S(2)}, u32[]{:S(2)}) collective-permute-start(bf16[448,128]{1,0:T(8,128)(2,1)S(1)} %get-tuple-element.69.sums), channel_id=1, source_target_pairs={{0,1},{1,0},{2,3},{3,2},{4,5},{5,4},{6,7},{7,6},{8,9},{9,8},{10,11... | collective-permute-start | bytes 344072 | tf_op jit(solution)/shard_map/ppermute | solution.py:64
  33.6 4.7 %collective-permute-start.13 = (bf16[2,2,8,128]{3,2,1,0:T(8,128)(2,1)S(1)}, bf16[2,2,8,128]{3,2,1,0:T(8,128)(2,1)S(1)}, u32[]{:S(2)}, u32[]{:S(2)}) collective-permute-start(bf16[2,2,8,128]{3,2,1,0:T(8,128)(2,1)S(1)} %slice.10), channel_id=1, source_target_pairs={{0,16},{8,24},{16,0},{24,8},{1,17},{9,25},{17,1},{25,9},{2,18},{10... | collective-permute-start | bytes 24584 | tf_op jit(solution)/shard_map/ppermute | solution.py:64
  34.8 4.9 %collective-permute-start.11 = (bf16[2,256,128]{2,1,0:T(8,128)(2,1)S(1)}, bf16[2,256,128]{2,1,0:T(8,128)(2,1)S(1)}, u32[]{:S(2)}, u32[]{:S(2)}) collective-permute-start(bf16[2,256,128]{2,1,0:T(8,128)(2,1)S(1)} %get-tuple-element.68), channel_id=1, source_target_pairs={{0,1},{1,0},{2,3},{3,2},{4,5},{5,4},{6,7},{7,6},{8,9},{9,8},{10,11... | collective-permute-start | bytes 393224 | tf_op jit(solution)/shard_map/ppermute | solution.py:64
  34.8 8.2 %collective-permute-start.17 = (bf16[384,128]{1,0:T(8,128)(2,1)S(1)}, bf16[384,128]{1,0:T(8,128)(2,1)S(1)}, u32[]{:S(2)}, u32[]{:S(2)}) collective-permute-start(bf16[384,128]{1,0:T(8,128)(2,1)S(1)} %get-tuple-element.72.refs_0_), channel_id=1, source_target_pairs={{0,6},{1,7},{2,4},{3,5},{4,2},{5,3},{6,0},{7,1},{8,14},{9,15},{10,... | collective-permute-start | bytes 294920 | tf_op jit(solution)/shard_map/ppermute | solution.py:64
  37.2 5.8 %collective-permute-start.16 = (bf16[384,128]{1,0:T(8,128)(2,1)S(1)}, bf16[384,128]{1,0:T(8,128)(2,1)S(1)}, u32[]{:S(2)}, u32[]{:S(2)}) collective-permute-start(bf16[384,128]{1,0:T(8,128)(2,1)S(1)} %get-tuple-element.72.refs_0_), channel_id=1, source_target_pairs={{0,4},{1,5},{2,6},{3,7},{4,0},{5,1},{6,2},{7,3},{8,12},{9,13},{10,... | collective-permute-start | bytes 294920 | tf_op jit(solution)/shard_map/ppermute | solution.py:64
  37.8 5.3 %collective-permute-start.15 = (bf16[384,128]{1,0:T(8,128)(2,1)S(1)}, bf16[384,128]{1,0:T(8,128)(2,1)S(1)}, u32[]{:S(2)}, u32[]{:S(2)}) collective-permute-start(bf16[384,128]{1,0:T(8,128)(2,1)S(1)} %get-tuple-element.72.refs_0_), channel_id=1, source_target_pairs={{0,2},{1,3},{2,0},{3,1},{4,6},{5,7},{6,4},{7,5},{8,10},{9,11},{10,... | collective-permute-start | bytes 294920 | tf_op jit(solution)/shard_map/ppermute | solution.py:64
  38.3 3.7 %collective-permute-start.14 = (bf16[1,2,8,128]{3,2,1,0:T(8,128)(2,1)S(1)}, bf16[1,2,8,128]{3,2,1,0:T(8,128)(2,1)S(1)}, u32[]{:S(2)}, u32[]{:S(2)}) collective-permute-start(bf16[1,2,8,128]{3,2,1,0:T(8,128)(2,1)S(1)} %slice.12), channel_id=1, source_target_pairs={{0,8},{8,0},{16,24},{24,16},{1,9},{9,1},{17,25},{25,17},{2,10},{10... | collective-permute-start | bytes 12296 | tf_op jit(solution)/shard_map/ppermute | solution.py:64

commit v8 on v6

--- a/solution.py
+++ b/solution.py
@@ -66,6 +66,14 @@
 
 def steps(count, first):
     return [0] + [s for s in first if s < count] + [s for s in range(1, count) if s not in first]
+
+
+def turned(s):
+    return s if s % 4 in (0, 3) else s ^ 3
+
+
+def met(s, core):
+    return s + core * (turned(s) - s)
 
 
 SLABS = (2, 3, 1)
@@ -361,7 +369,7 @@
     share = sums[0].shape[0] - first
     chip = lax.axis_index("config") // 2
     for s, part in zip(steps(len(sums), CHIPS), sums):
-        at = lax.bitwise_xor(chip, s)
+        at = lax.bitwise_xor(chip, met(s, lax.rem(lax.axis_index("config"), 2)))
         work[at] = part[0:first].astype(F32)
         out[pl.ds(pl.multiple_of(first + at * share, share), share)] = part[first:].astype(F32) * scale
     total = work[0]
@@ -370,9 +378,15 @@
     out[0:first] = total * scale
 
 
-def exchange(blocks):
+def exchange(blocks, apart=False):
     masks = steps(len(blocks), CHIPS)
-    return [swapped(block, "config", 2 * s) if s else block for s, block in zip(masks, blocks)]
+    if not apart or len(blocks) < 4:
+        return [swapped(block, "config", 2 * s) if s else block for s, block in zip(masks, blocks)]
+    count = lax.axis_size("config")
+    return [
+        lax.ppermute(block, "config", [(i, i ^ 2 * (turned(s) if i % 2 else s)) for i in range(count)]) if s else block
+        for s, block in zip(masks, blocks)
+    ]
 
 
 def local(
@@ -523,7 +537,7 @@
     hub_in = swapped(hub_theirs, "config", 1)
     theirs = swapped(theirs, "config", 1)
     sums, hub_sum = joined(sums, swapped(sums, "config", 1), hub_sum, hub_in)
-    sums = exchange([sums] * chips)
+    sums = exchange([sums] * chips, apart=True)
     totals = call(
         tile_back,
         shape(slab, F32),

time: 44.1 us -> 44.1 us (level)
    ppermute x19 -> x16, starting transfers between devices: 19.8 us -> 16.3 us  [swapped(): return lax.ppermute(x, axis, [(i, i ^ mask) for i in range(count)])]
    ppermute x0 -> x3, starting transfers between devices: none -> 3.49 us  [exchange(): lax.ppermute(block, 'config', [(i, i ^ 2 * (turned(s) if i % 2 else s)) f...]
    ppermute x19 -> x16, waiting for transfers between devices: 11.3 us -> 11.2 us  [swapped(): return lax.ppermute(x, axis, [(i, i ^ mask) for i in range(count)])]
  transfers between devices with their start and end apart: 19 -> 19, of which waited for: 9 -> 9; matrix products, arithmetic and copies ran while one was open for 0% -> 0% of each run, Pallas kernels for 14% -> 13%
where the time goes in v8:
time: 44.1 us; the launch traced here: 43.9 us
  starting transfers between devices  19.8 us (45%)
  waiting for transfers between devices  11.3 us (26%)
  Pallas kernels  10.5 us (24%)
  between operations  1.49 us (3%)
  local copies, waits for them, and re-layouts  0.82 us (2%)
    ppermute x16, starting transfers between devices, swapped(): return lax.ppermute(x, axis, [(i, i ^ mask) for i in range(count)])  16.3 us
    ppermute x16, waiting for transfers between devices, swapped(): return lax.ppermute(x, axis, [(i, i ^ mask) for i in range(count)])  11.2 us
    pallas_call x12, Pallas kernels, call(): pl.pallas_call(kernel, out_shape=outs, in_specs=specs, out_specs=jax.tree...  10.5 us
    ppermute x3, starting transfers between devices, exchange(): lax.ppermute(block, 'config', [(i, i ^ 2 * (turned(s) if i % 2 else s)) f...  3.49 us
  transfers between devices with their start and end apart: 19, of which 9 were waited for; matrix products, arithmetic and copies ran while one was open for 0% of the time, Pallas kernels for 13%

profile of v8, /device:TPU:0, one launch (start us, length us, event | category | flops | bytes accessed | tf_op | source)
XLA Modules:
  0.0 43.9 jit_solution(8125654345665975768)
XLA Ops:
  0.7 0.5 %collective-permute-start = (bf16[2,512,128]{2,1,0:T(8,128)(2,1)}, bf16[2,512,128]{2,1,0:T(8,128)(2,1)S(1)}, u32[]{:S(2)}, u32[]{:S(2)}) collective-permute-start(bf16[2,512,128]{2,1,0:T(8,128)(2,1)} %feats.1), channel_id=1, source_target_pairs={{0,1},{1,0},{2,3},{3,2},{4,5},{5,4},{6,7},{7,6},{8,9},{9,8},{10,11... | collective-permute-start | bytes 786440 | tf_op jit(solution)/shard_map/ppermute | solution.py:64
  1.2 1.8 %hub_pick.1 = (bf16[2,8,128]{2,1,0:T(8,128)(2,1)}, bf16[2,8,128]{2,1,0:T(8,128)(2,1)}, bf16[2,8,128]{2,1,0:T(8,128)(2,1)}) custom-call(s32[8]{0:T(128)} %ids.1, bf16[2,512,128]{2,1,0:T(8,128)(2,1)} %feats.1), custom_call_target="tpu_custom_call" | custom-call | flops 1000000000 | bytes 2097152 | tf_op jit(solution)/shard_map/hub_pick/pallas_call | solution.py:41
  3.0 0.0 copy-start.9
  3.0 3.7 %collective-permute-start.1 = (bf16[2,8,128]{2,1,0:T(8,128)(2,1)}, bf16[2,8,128]{2,1,0:T(8,128)(2,1)S(1)}, u32[]{:S(2)}, u32[]{:S(2)}) collective-permute-start(bf16[2,8,128]{2,1,0:T(8,128)(2,1)} %get-tuple-element.40), channel_id=1, source_target_pairs={{0,16},{8,24},{16,0},{24,8},{1,17},{9,25},{17,1},{25,9},{2,18},{10... | collective-permute-start | bytes 12296 | tf_op jit(solution)/shard_map/ppermute | solution.py:64
  6.7 1.3 %collective-permute-start.2 = (bf16[2,8,128]{2,1,0:T(8,128)(2,1)}, bf16[2,8,128]{2,1,0:T(8,128)(2,1)S(1)}, u32[]{:S(2)}, u32[]{:S(2)}) collective-permute-start(bf16[2,8,128]{2,1,0:T(8,128)(2,1)} %get-tuple-element.41), channel_id=1, source_target_pairs={{0,24},{8,16},{16,8},{24,0},{1,25},{9,17},{17,9},{25,1},{2,26},{10... | collective-permute-start | bytes 12296 | tf_op jit(solution)/shard_map/ppermute | solution.py:64
  8.1 0.3 collective-permute-start.3
  9.1 0.1 pad_add_fusion.ints
  9.2 1.1 %adjacency.1 = (bf16[512,512]{1,0:T(8,128)(2,1)S(1)}, f32[256,512]{1,0:T(8,128)S(1)}, f32[4,256,128]{2,1,0:T(8,128)S(1)}, bf16[4,256,128]{2,1,0:T(8,128)(2,1)S(1...) custom-call(s32[33]{0:T(128)S(1)} %pad_add_fusion.ints, bf16[12,128,128]{2,1,0:T(8,128)(2,1)S(1)} %copy-done, ...), custom_call_target="tpu_custom_call" | custom-call | flops 1000000000 | bytes 2097152 | tf_op jit(solution)/shard_map/adjacency/pallas_call | solution.py:41
  10.3 0.0 collective-permute-done.1.refs_1_
  10.3 2.0 %collective-permute-done.2.refs_2_ = bf16[2,8,128]{2,1,0:T(8,128)(2,1)S(1)} collective-permute-done((bf16[2,8,128]{2,1,0:T(8,128)(2,1)}, bf16[2,8,128]{2,1,0:T(8,128)(2,1)S(1)}, u32[]{:S(2)}, u32[]{:S(2)}) %collective-permute-start.2) | collective-permute-done | bytes 4128 | tf_op jit(solution)/shard_map/ppermute | solution.py:64
  12.4 0.1 collective-permute-start.4
  12.5 0.7 %copy-done.5 = bf16[512,32]{0,1:T(8,128)(2,1)S(1)} copy-done((bf16[512,32]{0,1:T(8,128)(2,1)S(1)}, bf16[512,32]{0,1:T(8,128)(2,1)}, u32[]{:S(2)}) %copy-start.5) | copy-done | bytes 32792
  13.1 0.1 copy.13
  13.2 0.4 collective-permute-done.4.refs_1_
  13.6 0.4 sage_out.1
  14.1 1.6 %collective-permute-start.5 = (bf16[8,32,128]{2,1,0:T(8,128)(2,1)S(1)}, bf16[8,32,128]{2,1,0:T(8,128)(2,1)S(1)}, u32[]{:S(2)}, u32[]{:S(2)}) collective-permute-start(bf16[8,32,128]{2,1,0:T(8,128)(2,1)S(1)} %get-tuple-element.46), channel_id=1, source_target_pairs={{0,2},{1,3},{2,0},{3,1},{4,6},{5,7},{6,4},{7,5},{8,10},{9,11},{10,... | collective-permute-start | bytes 196616 | tf_op jit(solution)/shard_map/ppermute | solution.py:64
  15.6 1.5 %collective-permute-start.6 = (bf16[8,32,128]{2,1,0:T(8,128)(2,1)S(1)}, bf16[8,32,128]{2,1,0:T(8,128)(2,1)S(1)}, u32[]{:S(2)}, u32[]{:S(2)}) collective-permute-start(bf16[8,32,128]{2,1,0:T(8,128)(2,1)S(1)} %get-tuple-element.47), channel_id=1, source_target_pairs={{0,4},{1,5},{2,6},{3,7},{4,0},{5,1},{6,2},{7,3},{8,12},{9,13},{10,... | collective-permute-start | bytes 196616 | tf_op jit(solution)/shard_map/ppermute | solution.py:64
  17.2 0.5 %collective-permute-start.7 = (bf16[8,32,128]{2,1,0:T(8,128)(2,1)S(1)}, bf16[8,32,128]{2,1,0:T(8,128)(2,1)S(1)}, u32[]{:S(2)}, u32[]{:S(2)}) collective-permute-start(bf16[8,32,128]{2,1,0:T(8,128)(2,1)S(1)} %get-tuple-element.48), channel_id=1, source_target_pairs={{0,6},{1,7},{2,4},{3,5},{4,2},{5,3},{6,0},{7,1},{8,14},{9,15},{10,... | collective-permute-start | bytes 196616 | tf_op jit(solution)/shard_map/ppermute | solution.py:64
  17.6 0.5 %prepare.1 = (bf16[8,128,128]{2,1,0:T(8,128)(2,1)S(1)}, bf16[8,128,128]{2,1,0:T(8,128)(2,1)S(1)}, f32[4,256,128]{2,1,0:T(8,128)S(1)}, bf16[256,1024]{1,0:T(8,128...) custom-call(bf16[16,64,128]{2,1,0:T(8,128)(2,1)S(1)} %copy-done.2, ...), custom_call_target="tpu_custom_call" | custom-call | flops 1000000000 | bytes 2097152 | tf_op jit(solution)/shard_map/prepare/pallas_call | solution.py:41
  18.1 0.3 collective-permute-done.5.refs_1_
  18.4 1.5 %collective-permute-done.6.refs_2_ = bf16[8,32,128]{2,1,0:T(8,128)(2,1)S(1)} collective-permute-done((bf16[8,32,128]{2,1,0:T(8,128)(2,1)S(1)}, bf16[8,32,128]{2,1,0:T(8,128)(2,1)S(1)}, u32[]{:S(2)}, u32[]{:S(2)}) %collective-permute-start.6) | collective-permute-done | bytes 65568 | tf_op jit(solution)/shard_map/ppermute | solution.py:64
  19.9 2.4 %collective-permute-done.7.refs_3_ = bf16[8,32,128]{2,1,0:T(8,128)(2,1)S(1)} collective-permute-done((bf16[8,32,128]{2,1,0:T(8,128)(2,1)S(1)}, bf16[8,32,128]{2,1,0:T(8,128)(2,1)S(1)}, u32[]{:S(2)}, u32[]{:S(2)}) %collective-permute-start.7) | collective-permute-done | bytes 65568 | tf_op jit(solution)/shard_map/ppermute | solution.py:64
  22.3 2.8 %attend.1 = (bf16[384,128]{1,0:T(8,128)(2,1)S(1)}, bf16[384,128]{1,0:T(8,128)(2,1)S(1)}, bf16[384,128]{1,0:T(8,128)(2,1)S(1)}, bf16[384,128]{1,0:T(8,128)(2,1)S(...) custom-call(bf16[8,32,128]{2,1,0:T(8,128)(2,1)S(1)} %get-tuple-element.45.refs_0_, ...), custom_call_target="tpu_custom_call" | custom-call | flops 4000000000 | bytes 8388608 | tf_op jit(solution)/shard_map/attend/pallas_call | solution.py:41
  25.2 0.6 %collective-permute-start.8 = (bf16[384,128]{1,0:T(8,128)(2,1)S(1)}, bf16[384,128]{1,0:T(8,128)(2,1)S(1)}, u32[]{:S(2)}, u32[]{:S(2)}) collective-permute-start(bf16[384,128]{1,0:T(8,128)(2,1)S(1)} %get-tuple-element.57), channel_id=1, source_target_pairs={{0,2},{1,3},{2,0},{3,1},{4,6},{5,7},{6,4},{7,5},{8,10},{9,11},{10,... | collective-permute-start | bytes 294920 | tf_op jit(solution)/shard_map/ppermute | solution.py:64
  25.7 0.5 %collective-permute-start.9 = (bf16[384,128]{1,0:T(8,128)(2,1)S(1)}, bf16[384,128]{1,0:T(8,128)(2,1)S(1)}, u32[]{:S(2)}, u32[]{:S(2)}) collective-permute-start(bf16[384,128]{1,0:T(8,128)(2,1)S(1)} %get-tuple-element.63), channel_id=1, source_target_pairs={{0,4},{1,5},{2,6},{3,7},{4,0},{5,1},{6,2},{7,3},{8,12},{9,13},{10,... | collective-permute-start | bytes 294920 | tf_op jit(solution)/shard_map/ppermute | solution.py:64
  26.3 2.5 %collective-permute-start.10 = (bf16[384,128]{1,0:T(8,128)(2,1)S(1)}, bf16[384,128]{1,0:T(8,128)(2,1)S(1)}, u32[]{:S(2)}, u32[]{:S(2)}) collective-permute-start(bf16[384,128]{1,0:T(8,128)(2,1)S(1)} %get-tuple-element.64), channel_id=1, source_target_pairs={{0,6},{1,7},{2,4},{3,5},{4,2},{5,3},{6,0},{7,1},{8,14},{9,15},{10,... | collective-permute-start | bytes 294920 | tf_op jit(solution)/shard_map/ppermute | solution.py:64
  28.7 1.2 %collective-permute-done.8._.refs_1_ = bf16[384,128]{1,0:T(8,128)(2,1)S(1)} collective-permute-done((bf16[384,128]{1,0:T(8,128)(2,1)S(1)}, bf16[384,128]{1,0:T(8,128)(2,1)S(1)}, u32[]{:S(2)}, u32[]{:S(2)}) %collective-permute-start.8) | collective-permute-done | bytes 98336 | tf_op jit(solution)/shard_map/ppermute | solution.py:64
  29.9 1.0 %outputs.1 = (bf16[16,64,128]{2,1,0:T(8,128)(2,1)}, f32[8,128]{1,0:T(8,128)S(1)}) custom-call(bf16[8,128,128]{2,1,0:T(8,128)(2,1)S(1)} %get-tuple-element.55.hidden, bf16[128,1024]{1,0:T(8,128)(2,1)S(1)} %get-tuple-element.56.mixed_t, bf16[4,128,128]{2,1,0:T(8,128)(2,1)S(1)} %copy-done.3, bf16[384,128]{1,0:T(8,128)(2,1)S(1)} %collective-permute-done.8._.refs_1_), custom_call_target="tpu_custom_call" | custom-call | flops 1000000000 | bytes 2097152 | tf_op jit(solution)/shard_map/outputs/pallas_call | solution.py:41
  30.9 0.0 collective-permute-done.9.refs_2_
  30.9 0.9 %collective-permute-done.10.refs_3_ = bf16[384,128]{1,0:T(8,128)(2,1)S(1)} collective-permute-done((bf16[384,128]{1,0:T(8,128)(2,1)S(1)}, bf16[384,128]{1,0:T(8,128)(2,1)S(1)}, u32[]{:S(2)}, u32[]{:S(2)}) %collective-permute-start.10) | collective-permute-done | bytes 98336 | tf_op jit(solution)/shard_map/ppermute | solution.py:64
  31.8 0.4 sage_back.1
  32.2 0.1 collective-permute-start.12
  32.3 0.5 %collective-permute-start.13 = (bf16[4,2,8,128]{3,2,1,0:T(8,128)(2,1)S(1)}, bf16[4,2,8,128]{3,2,1,0:T(8,128)(2,1)S(1)}, u32[]{:S(2)}, u32[]{:S(2)}) collective-permute-start(bf16[4,2,8,128]{3,2,1,0:T(8,128)(2,1)S(1)} %get-tuple-element.72), channel_id=1, source_target_pairs={{0,1},{1,0},{2,3},{3,2},{4,5},{5,4},{6,7},{7,6},{8,9},{9,8},{10,11... | collective-permute-start | bytes 49160 | tf_op jit(solution)/shard_map/ppermute | solution.py:64
  32.8 0.8 %collective-permute-done.13.refs_3_ = bf16[4,2,8,128]{3,2,1,0:T(8,128)(2,1)S(1)} collective-permute-done((bf16[4,2,8,128]{3,2,1,0:T(8,128)(2,1)S(1)}, bf16[4,2,8,128]{3,2,1,0:T(8,128)(2,1)S(1)}, u32[]{:S(2)}, u32[]{:S(2)}) %collective-permute-start.13) | collective-permute-done | bytes 16416 | tf_op jit(solution)/shard_map/ppermute | solution.py:64
  33.6 0.0 collective-permute-done.12.refs_1_
  33.6 1.2 %collective-permute-start.14 = (bf16[2,2,8,128]{3,2,1,0:T(8,128)(2,1)S(1)}, bf16[2,2,8,128]{3,2,1,0:T(8,128)(2,1)S(1)}, u32[]{:S(2)}, u32[]{:S(2)}) collective-permute-start(bf16[2,2,8,128]{3,2,1,0:T(8,128)(2,1)S(1)} %slice.10), channel_id=1, source_target_pairs={{0,16},{8,24},{16,0},{24,8},{1,17},{9,25},{17,1},{25,9},{2,18},{10... | collective-permute-start | bytes 24584 | tf_op jit(solution)/shard_map/ppermute | solution.py:64
  34.8 0.1 collective-permute-start.11
  34.9 2.4 %collective-permute-start.18 = (bf16[384,128]{1,0:T(8,128)(2,1)S(1)}, bf16[384,128]{1,0:T(8,128)(2,1)S(1)}, u32[]{:S(2)}, u32[]{:S(2)}) collective-permute-start(bf16[384,128]{1,0:T(8,128)(2,1)S(1)} %get-tuple-element.74.refs_0_), channel_id=1, source_target_pairs={{0,6},{1,7},{2,4},{3,5},{4,2},{5,3},{6,0},{7,1},{8,14},{9,15},{10,... | collective-permute-start | bytes 294920 | tf_op jit(solution)/shard_map/ppermute | solution.py:387
  37.3 0.5 %collective-permute-start.17 = (bf16[384,128]{1,0:T(8,128)(2,1)S(1)}, bf16[384,128]{1,0:T(8,128)(2,1)S(1)}, u32[]{:S(2)}, u32[]{:S(2)}) collective-permute-start(bf16[384,128]{1,0:T(8,128)(2,1)S(1)} %get-tuple-element.74.refs_0_), channel_id=1, source_target_pairs={{0,4},{1,3},{2,6},{3,1},{4,0},{5,7},{6,2},{7,5},{8,12},{9,11},{10,... | collective-permute-start | bytes 294920 | tf_op jit(solution)/shard_map/ppermute | solution.py:387
  37.8 0.5 %collective-permute-start.16 = (bf16[384,128]{1,0:T(8,128)(2,1)S(1)}, bf16[384,128]{1,0:T(8,128)(2,1)S(1)}, u32[]{:S(2)}, u32[]{:S(2)}) collective-permute-start(bf16[384,128]{1,0:T(8,128)(2,1)S(1)} %get-tuple-element.74.refs_0_), channel_id=1, source_target_pairs={{0,2},{1,5},{2,0},{3,7},{4,6},{5,1},{6,4},{7,3},{8,10},{9,13},{10,... | collective-permute-start | bytes 294920 | tf_op jit(solution)/shard_map/ppermute | solution.py:387
  38.4 0.0 collective-permute-done.14
  38.4 1.4 %collective-permute-start.15 = (bf16[1,2,8,128]{3,2,1,0:T(8,128)(2,1)S(1)}, bf16[1,2,8,128]{3,2,1,0:T(8,128)(2,1)S(1)}, u32[]{:S(2)}, u32[]{:S(2)}) collective-permute-start(bf16[1,2,8,128]{3,2,1,0:T(8,128)(2,1)S(1)} %slice.12), channel_id=1, source_target_pairs={{0,8},{8,0},{16,24},{24,16},{1,9},{9,1},{17,25},{25,17},{2,10},{10... | collective-permute-start | bytes 12296 | tf_op jit(solution)/shard_map/ppermute | solution.py:64
  39.8 0.0 collective-permute-done.11.theirs
  39.8 0.5 %tile_back.1.totals = f32[2,512,128]{2,1,0:T(8,128)S(1)} custom-call(bf16[512,512]{1,0:T(8,128)(2,1)S(1)} %get-tuple-element.60.adj_t, bf16[128,256]{1,0:T(8,128)(2,1)S(1)} %get-tuple-element.61.refs_6_.w_back, bf16[2,256,128]{2,1,0:T(8,128)(2,1)S(1)} %get-tuple-element.68.mine, bf16[2,256,128]{2,1,0:T(8,128)(2,1)S(1)} %collective-permute-done.11.theirs), custom_call_target="tpu_custom_call" | custom-call | flops 1000000000 | bytes 2097152 | tf_op jit(solution)/shard_map/tile_back/pallas_call | solution.py:41
  40.4 1.7 %collective-permute-done.15.hub_in = bf16[1,2,8,128]{3,2,1,0:T(8,128)(2,1)S(1)} collective-permute-done((bf16[1,2,8,128]{3,2,1,0:T(8,128)(2,1)S(1)}, bf16[1,2,8,128]{3,2,1,0:T(8,128)(2,1)S(1)}, u32[]{:S(2)}, u32[]{:S(2)}) %collective-permute-start.15) | collective-permute-done | bytes 4128 | tf_op jit(solution)/shard_map/ppermute | solution.py:64
  42.1 1.0 %finish.1 = bf16[2,512,128]{2,1,0:T(8,128)(2,1)} custom-call(bf16[8,512]{1,0:T(8,128)(2,1)S(1)} %get-tuple-element.59.hot, f32[2,512,128]{2,1,0:T(8,128)S(1)} %tile_back.1.totals, bf16[2,2,8,128]{3,2,1,0:T(8,128)(2,1)S(1)} %slice_add_fusion.hub_own, bf16[1,2,8,128]{3,2,1,0:T(8,128)(2,1)S(1)} %collective-permute-done.15.hub_in), custom_call_target="tpu_custom_call" | custom-call | flops 1000000000 | bytes 2097152 | tf_op jit(solution)/shard_map/finish/pallas_call | solution.py:41
  43.0 0.0 collective-permute-done.16.refs_1_
  43.1 0.8 %weights_out.1 = f32[768,128]{1,0:T(8,128)} custom-call(bf16[384,128]{1,0:T(8,128)(2,1)S(1)} %get-tuple-element.74.refs_0_, bf16[384,128]{1,0:T(8,128)(2,1)S(1)} %collective-permute-done.16.refs_1_, bf16[384,128]{1,0:T(8,128)(2,1)S(1)} %collective-permute-done.17.refs_2_, bf16[384,128]{1,0:T(8,128)(2,1)S(1)} %collective-permute-done.18.refs_3_), custom_call_target="tpu_custom_call" | custom-call | flops 1000000000 | bytes 2097152 | tf_op jit(solution)/shard_map/weights_out/pallas_call | solution.py:41
  (27 shorter events, 0.1 us)
Async XLA Ops:
  0.6 8.5 %copy-start.1 = (bf16[2,512,128]{2,1,0:T(8,128)(2,1)S(1)}, bf16[2,512,128]{2,1,0:T(8,128)(2,1)}, u32[]{:S(2)}) copy-start(bf16[2,512,128]{2,1,0:T(8,128)(2,1)} %feats.1) | copy-start | bytes 786436
  0.6 8.5 %copy-start.4 = (bf16[2,128,128]{2,1,0:T(8,128)(2,1)S(1)}, bf16[2,128,128]{2,1,0:T(8,128)(2,1)}, u32[]{:S(2)}) copy-start(bf16[2,128,128]{2,1,0:T(8,128)(2,1)} %weight.3) | copy-start | bytes 196612
  0.7 8.5 %copy-start = (bf16[12,128,128]{2,1,0:T(8,128)(2,1)S(1)}, bf16[12,128,128]{2,1,0:T(8,128)(2,1)}, u32[]{:S(2)}) copy-start(bf16[12,128,128]{2,1,0:T(8,128)(2,1)} %tiles.1) | copy-start | bytes 1179652
  0.7 8.5 %collective-permute-start = (bf16[2,512,128]{2,1,0:T(8,128)(2,1)}, bf16[2,512,128]{2,1,0:T(8,128)(2,1)S(1)}, u32[]{:S(2)}, u32[]{:S(2)}) collective-permute-start(bf16[2,512,128]{2,1,0:T(8,128)(2,1)} %feats.1), channel_id=1, source_target_pairs={{0,1},{1,0},{2,3},{3,2},{4,5},{5,4},{6,7},{7,6},{8,9},{9,8},{10,11... | collective-permute-start | bytes 786440 | tf_op jit(solution)/shard_map/ppermute | solution.py:64
  3.0 5.1 %copy-start.9 = (bf16[2,8,128]{2,1,0:T(8,128)(2,1)S(1)}, bf16[2,8,128]{2,1,0:T(8,128)(2,1)}, u32[]{:S(2)}) copy-start(bf16[2,8,128]{2,1,0:T(8,128)(2,1)} %get-tuple-element.42) | copy-start | bytes 12292
  3.0 7.3 %collective-permute-start.1 = (bf16[2,8,128]{2,1,0:T(8,128)(2,1)}, bf16[2,8,128]{2,1,0:T(8,128)(2,1)S(1)}, u32[]{:S(2)}, u32[]{:S(2)}) collective-permute-start(bf16[2,8,128]{2,1,0:T(8,128)(2,1)} %get-tuple-element.40), channel_id=1, source_target_pairs={{0,16},{8,24},{16,0},{24,8},{1,17},{9,25},{17,1},{25,9},{2,18},{10... | collective-permute-start | bytes 12296 | tf_op jit(solution)/shard_map/ppermute | solution.py:64
  6.7 5.6 %collective-permute-start.2 = (bf16[2,8,128]{2,1,0:T(8,128)(2,1)}, bf16[2,8,128]{2,1,0:T(8,128)(2,1)S(1)}, u32[]{:S(2)}, u32[]{:S(2)}) collective-permute-start(bf16[2,8,128]{2,1,0:T(8,128)(2,1)} %get-tuple-element.41), channel_id=1, source_target_pairs={{0,24},{8,16},{16,8},{24,0},{1,25},{9,17},{17,9},{25,1},{2,26},{10... | collective-permute-start | bytes 12296 | tf_op jit(solution)/shard_map/ppermute | solution.py:64
  8.1 1.0 %copy-start.6 = (s32[12]{0:T(128)S(1)}, s32[12]{0:T(128)}, u32[]{:S(2)}) copy-start(s32[12]{0:T(128)} %param.16) | copy-start | bytes 148
  8.1 1.0 %copy-start.7 = (s32[12]{0:T(128)S(1)}, s32[12]{0:T(128)}, u32[]{:S(2)}) copy-start(s32[12]{0:T(128)} %param.15) | copy-start | bytes 148
  8.1 1.0 %copy-start.8 = (s32[8]{0:T(128)S(1)}, s32[8]{0:T(128)}, u32[]{:S(2)}) copy-start(s32[8]{0:T(128)} %ids.1) | copy-start | bytes 100
  8.1 4.3 %collective-permute-start.3 = (bf16[2,8,128]{2,1,0:T(8,128)(2,1)S(1)}, bf16[2,8,128]{2,1,0:T(8,128)(2,1)S(1)}, u32[]{:S(2)}, u32[]{:S(2)}) collective-permute-start(bf16[2,8,128]{2,1,0:T(8,128)(2,1)S(1)} %copy-done.9), channel_id=1, source_target_pairs={{0,8},{8,0},{16,24},{24,16},{1,9},{9,1},{17,25},{25,17},{2,10},{10... | collective-permute-start | bytes 12296 | tf_op jit(solution)/shard_map/ppermute | solution.py:64
  12.4 0.8 %copy-start.5 = (bf16[512,32]{0,1:T(8,128)(2,1)S(1)}, bf16[512,32]{0,1:T(8,128)(2,1)}, u32[]{:S(2)}) copy-start(bf16[512,32]{0,1:T(8,128)(2,1)} %param.19) | copy-start | bytes 98308
  12.4 1.2 %collective-permute-start.4 = (bf16[32,256]{1,0:T(8,128)(2,1)S(1)}, bf16[32,256]{1,0:T(8,128)(2,1)S(1)}, u32[]{:S(2)}, u32[]{:S(2)}) collective-permute-start(bf16[32,256]{1,0:T(8,128)(2,1)S(1)} %by_slab.1.refs_0_), channel_id=1, source_target_pairs={{0,1},{1,0},{2,3},{3,2},{4,5},{5,4},{6,7},{7,6},{8,9},{9,8},{10,11... | collective-permute-start | bytes 49160 | tf_op jit(solution)/shard_map/ppermute | solution.py:64
  13.6 4.0 %copy-start.2 = (bf16[16,64,128]{2,1,0:T(8,128)(2,1)S(1)}, bf16[16,64,128]{2,1,0:T(8,128)(2,1)}, u32[]{:S(2)}) copy-start(bf16[16,64,128]{2,1,0:T(8,128)(2,1)} %cot.1) | copy-start | bytes 786436
  13.6 4.0 %copy-start.3 = (bf16[4,128,128]{2,1,0:T(8,128)(2,1)S(1)}, bf16[4,128,128]{2,1,0:T(8,128)(2,1)}, u32[]{:S(2)}) copy-start(bf16[4,128,128]{2,1,0:T(8,128)(2,1)} %attn.3) | copy-start | bytes 393220
  14.1 4.3 %collective-permute-start.5 = (bf16[8,32,128]{2,1,0:T(8,128)(2,1)S(1)}, bf16[8,32,128]{2,1,0:T(8,128)(2,1)S(1)}, u32[]{:S(2)}, u32[]{:S(2)}) collective-permute-start(bf16[8,32,128]{2,1,0:T(8,128)(2,1)S(1)} %get-tuple-element.46), channel_id=1, source_target_pairs={{0,2},{1,3},{2,0},{3,1},{4,6},{5,7},{6,4},{7,5},{8,10},{9,11},{10,... | collective-permute-start | bytes 196616 | tf_op jit(solution)/shard_map/ppermute | solution.py:64
  15.6 4.3 %collective-permute-start.6 = (bf16[8,32,128]{2,1,0:T(8,128)(2,1)S(1)}, bf16[8,32,128]{2,1,0:T(8,128)(2,1)S(1)}, u32[]{:S(2)}, u32[]{:S(2)}) collective-permute-start(bf16[8,32,128]{2,1,0:T(8,128)(2,1)S(1)} %get-tuple-element.47), channel_id=1, source_target_pairs={{0,4},{1,5},{2,6},{3,7},{4,0},{5,1},{6,2},{7,3},{8,12},{9,13},{10,... | collective-permute-start | bytes 196616 | tf_op jit(solution)/shard_map/ppermute | solution.py:64
  17.2 5.2 %collective-permute-start.7 = (bf16[8,32,128]{2,1,0:T(8,128)(2,1)S(1)}, bf16[8,32,128]{2,1,0:T(8,128)(2,1)S(1)}, u32[]{:S(2)}, u32[]{:S(2)}) collective-permute-start(bf16[8,32,128]{2,1,0:T(8,128)(2,1)S(1)} %get-tuple-element.48), channel_id=1, source_target_pairs={{0,6},{1,7},{2,4},{3,5},{4,2},{5,3},{6,0},{7,1},{8,14},{9,15},{10,... | collective-permute-start | bytes 196616 | tf_op jit(solution)/shard_map/ppermute | solution.py:64
  25.2 4.7 %collective-permute-start.8 = (bf16[384,128]{1,0:T(8,128)(2,1)S(1)}, bf16[384,128]{1,0:T(8,128)(2,1)S(1)}, u32[]{:S(2)}, u32[]{:S(2)}) collective-permute-start(bf16[384,128]{1,0:T(8,128)(2,1)S(1)} %get-tuple-element.57), channel_id=1, source_target_pairs={{0,2},{1,3},{2,0},{3,1},{4,6},{5,7},{6,4},{7,5},{8,10},{9,11},{10,... | collective-permute-start | bytes 294920 | tf_op jit(solution)/shard_map/ppermute | solution.py:64
  25.7 5.1 %collective-permute-start.9 = (bf16[384,128]{1,0:T(8,128)(2,1)S(1)}, bf16[384,128]{1,0:T(8,128)(2,1)S(1)}, u32[]{:S(2)}, u32[]{:S(2)}) collective-permute-start(bf16[384,128]{1,0:T(8,128)(2,1)S(1)} %get-tuple-element.63), channel_id=1, source_target_pairs={{0,4},{1,5},{2,6},{3,7},{4,0},{5,1},{6,2},{7,3},{8,12},{9,13},{10,... | collective-permute-start | bytes 294920 | tf_op jit(solution)/shard_map/ppermute | solution.py:64
  26.3 5.5 %collective-permute-start.10 = (bf16[384,128]{1,0:T(8,128)(2,1)S(1)}, bf16[384,128]{1,0:T(8,128)(2,1)S(1)}, u32[]{:S(2)}, u32[]{:S(2)}) collective-permute-start(bf16[384,128]{1,0:T(8,128)(2,1)S(1)} %get-tuple-element.64), channel_id=1, source_target_pairs={{0,6},{1,7},{2,4},{3,5},{4,2},{5,3},{6,0},{7,1},{8,14},{9,15},{10,... | collective-permute-start | bytes 294920 | tf_op jit(solution)/shard_map/ppermute | solution.py:64
  32.2 1.4 %collective-permute-start.12 = (bf16[384,128]{1,0:T(8,128)(2,1)S(1)}, bf16[384,128]{1,0:T(8,128)(2,1)S(1)}, u32[]{:S(2)}, u32[]{:S(2)}) collective-permute-start(bf16[384,128]{1,0:T(8,128)(2,1)S(1)} %get-tuple-element.70.refs_0_), channel_id=1, source_target_pairs={{0,1},{1,0},{2,3},{3,2},{4,5},{5,4},{6,7},{7,6},{8,9},{9,8},{10,11... | collective-permute-start | bytes 294920 | tf_op jit(solution)/shard_map/ppermute | solution.py:64
  32.3 1.3 %collective-permute-start.13 = (bf16[4,2,8,128]{3,2,1,0:T(8,128)(2,1)S(1)}, bf16[4,2,8,128]{3,2,1,0:T(8,128)(2,1)S(1)}, u32[]{:S(2)}, u32[]{:S(2)}) collective-permute-start(bf16[4,2,8,128]{3,2,1,0:T(8,128)(2,1)S(1)} %get-tuple-element.72), channel_id=1, source_target_pairs={{0,1},{1,0},{2,3},{3,2},{4,5},{5,4},{6,7},{7,6},{8,9},{9,8},{10,11... | collective-permute-start | bytes 49160 | tf_op jit(solution)/shard_map/ppermute | solution.py:64
  33.6 4.7 %collective-permute-start.14 = (bf16[2,2,8,128]{3,2,1,0:T(8,128)(2,1)S(1)}, bf16[2,2,8,128]{3,2,1,0:T(8,128)(2,1)S(1)}, u32[]{:S(2)}, u32[]{:S(2)}) collective-permute-start(bf16[2,2,8,128]{3,2,1,0:T(8,128)(2,1)S(1)} %slice.10), channel_id=1, source_target_pairs={{0,16},{8,24},{16,0},{24,8},{1,17},{9,25},{17,1},{25,9},{2,18},{10... | collective-permute-start | bytes 24584 | tf_op jit(solution)/shard_map/ppermute | solution.py:64
  34.8 5.0 %collective-permute-start.11 = (bf16[2,256,128]{2,1,0:T(8,128)(2,1)S(1)}, bf16[2,256,128]{2,1,0:T(8,128)(2,1)S(1)}, u32[]{:S(2)}, u32[]{:S(2)}) collective-permute-start(bf16[2,256,128]{2,1,0:T(8,128)(2,1)S(1)} %get-tuple-element.69), channel_id=1, source_target_pairs={{0,1},{1,0},{2,3},{3,2},{4,5},{5,4},{6,7},{7,6},{8,9},{9,8},{10,11... | collective-permute-start | bytes 393224 | tf_op jit(solution)/shard_map/ppermute | solution.py:64
  34.9 8.2 %collective-permute-start.18 = (bf16[384,128]{1,0:T(8,128)(2,1)S(1)}, bf16[384,128]{1,0:T(8,128)(2,1)S(1)}, u32[]{:S(2)}, u32[]{:S(2)}) collective-permute-start(bf16[384,128]{1,0:T(8,128)(2,1)S(1)} %get-tuple-element.74.refs_0_), channel_id=1, source_target_pairs={{0,6},{1,7},{2,4},{3,5},{4,2},{5,3},{6,0},{7,1},{8,14},{9,15},{10,... | collective-permute-start | bytes 294920 | tf_op jit(solution)/shard_map/ppermute | solution.py:387
  37.3 5.7 %collective-permute-start.17 = (bf16[384,128]{1,0:T(8,128)(2,1)S(1)}, bf16[384,128]{1,0:T(8,128)(2,1)S(1)}, u32[]{:S(2)}, u32[]{:S(2)}) collective-permute-start(bf16[384,128]{1,0:T(8,128)(2,1)S(1)} %get-tuple-element.74.refs_0_), channel_id=1, source_target_pairs={{0,4},{1,3},{2,6},{3,1},{4,0},{5,7},{6,2},{7,5},{8,12},{9,11},{10,... | collective-permute-start | bytes 294920 | tf_op jit(solution)/shard_map/ppermute | solution.py:387
  37.8 5.3 %collective-permute-start.16 = (bf16[384,128]{1,0:T(8,128)(2,1)S(1)}, bf16[384,128]{1,0:T(8,128)(2,1)S(1)}, u32[]{:S(2)}, u32[]{:S(2)}) collective-permute-start(bf16[384,128]{1,0:T(8,128)(2,1)S(1)} %get-tuple-element.74.refs_0_), channel_id=1, source_target_pairs={{0,2},{1,5},{2,0},{3,7},{4,6},{5,1},{6,4},{7,3},{8,10},{9,13},{10,... | collective-permute-start | bytes 294920 | tf_op jit(solution)/shard_map/ppermute | solution.py:387
  38.4 3.7 %collective-permute-start.15 = (bf16[1,2,8,128]{3,2,1,0:T(8,128)(2,1)S(1)}, bf16[1,2,8,128]{3,2,1,0:T(8,128)(2,1)S(1)}, u32[]{:S(2)}, u32[]{:S(2)}) collective-permute-start(bf16[1,2,8,128]{3,2,1,0:T(8,128)(2,1)S(1)} %slice.12), channel_id=1, source_target_pairs={{0,8},{8,0},{16,24},{24,16},{1,9},{9,1},{17,25},{25,17},{2,10},{10... | collective-permute-start | bytes 12296 | tf_op jit(solution)/shard_map/ppermute | solution.py:64
